TPU v7x, 32 devices: a whole 2x2x4 slice. The times are simulated.
32 devices in a mesh: slab: 16 (over z, x, core), ang: 2 (over y).
Axes of the slice: x: 2, y: 2, z: 4, core: 2. Of those that a mesh axis runs over, the one named last changes fastest.
Arguments:
- volume: float32 [128, 256, 4096], P('slab', 'ang'), may hold values from 0.1 to 3
- measured: bfloat16 [8, 512, 4096], P('ang', 'slab'), may hold values from 0 to 2
- foot_start: int32 [16, 8], P('slab', 'ang'), may hold values from 0 to 480, as said below
- foot_len: int32 [16, 8], P('slab', 'ang'), may hold values from 32 to 96
- order: int32 [64], replicated, may hold values from 0 to 63, each once
- ray_table: float32 [64, 256], replicated, may hold values from 0.001953125 to 0.0078125
Outputs:
- updated: float32 [128, 256, 4096], P('slab', 'ang')
- residual: float32 [8, 512, 4096], P('ang', 'slab')
Inputs may be any that keep to these rules, and one draw needn't show every extreme that they name: foot_start[s, j] + foot_len[s, j] <= 512; the footprint of slab s lies within rows (s - 2) * 32 to (s + 3) * 32.
All inputs are finite; a program needn't handle non-finite values.
Results may differ from a plain program's by a relative error of at most 0.0003.
Values sent between devices are 32-bit elements; how exact they have to be, the bound alone decides.
No kernel may reach another device: no remote copies, remote signals or barrier semaphores. Data moves between devices by JAX's collectives and lax.ppermute only.
A program may use at most 128 MiB of HBM per device.

v0:
```python
import functools

import jax
import jax.numpy as jnp
from jax import lax
from jax.experimental import pallas as pl
from jax.experimental.pallas import tpu as pltpu
from jax.sharding import PartitionSpec as P

F32, BF16 = jnp.float32, jnp.bfloat16
CHUNKS = 2
TILE = 512
LANES = 128
SUBLANES = 8
MIB = 1024 * 1024

IN_VMEM = pl.BlockSpec(memory_space=pltpu.VMEM)
IN_SMEM = pl.BlockSpec(memory_space=pltpu.SMEM)
ANYWHERE = pl.BlockSpec(memory_space=pl.ANY)


def split(value):
    high = value.astype(BF16)
    return high, (value - high.astype(F32)).astype(BF16)


def dot(a, b):
    return jnp.dot(a, b, preferred_element_type=F32)


def dot3(a, b):
    return dot(a[0], b[0]) + (dot(a[0], b[1]) + dot(a[1], b[0]))


def iota(shape, dim):
    return lax.broadcasted_iota(jnp.int32, shape, dim)


def low_bits(value, size):
    assert size & (size - 1) == 0
    return value & (size - 1)


def over(value, size):
    assert size & (size - 1) == 0
    return value >> (size.bit_length() - 1)


def pick(index, values):
    out = jnp.zeros(index.shape, values[0].dtype)
    for at, value in enumerate(values):
        out = jnp.where(index == at, value, out)
    return out


def tiles(width):
    step = min(TILE, width)
    return [(at, min(step, width - at)) for at in range(0, width, step)]


def slice_weights(dims, sign, order_ref, table_ref, rows_ref):
    per, groups, zb, cells = dims
    ang = lax.axis_index("ang")
    for d in range(groups):
        group = lax.rem(ang + sign * d + groups, groups)
        for z in range(zb):
            for a in range(per):
                at = (d * zb + z) * per + a
                rows_ref[at:at + 1, :] = table_ref[pl.ds(order_ref[group * per + a], 1), :]
    wide = rows_ref[...]
    total = wide.shape[1]
    row_slice = low_bits(over(iota(wide.shape, 0), per), zb)
    lane_slice = over(iota(wide.shape, 1), cells)
    out = jnp.zeros_like(wide)
    for z in range(zb):
        shift = lax.rem(z * cells - ang * cells + total, total)
        here = jnp.logical_and(row_slice == z, lane_slice == z)
        out = jnp.where(here, pltpu.roll(wide, shift, 1), out)
    return out


def volume_pieces(dims, zdev, half, offset):
    odd = lax.rem(lax.axis_index("slab"), 2)
    zb = dims[2]
    for h in range(2):
        start = pl.multiple_of(lax.rem(odd + h, 2) * half + offset, LANES)
        for zp in range(zdev // zb):
            yield h, zp, slice(zp * zb, (zp + 1) * zb), start


def rays_kernel(dims, first, last, half, offset, width, *refs):
    per, groups, zb, cells = dims
    count = groups * SUBLANES
    if first:
        order_ref, start_ref, len_ref, table_ref, vol_ref, *refs = refs
    else:
        given_ref, vol_ref, *refs = refs
    outs, refs = refs[:2 * groups], refs[2 * groups:]
    if first:
        left_ref, buf, sems, table_buf, rows_ref, table_sem = refs
    elif last:
        kept_ref, sems, rest_sems = refs
    else:
        buf, sems = refs
    zdev = vol_ref.shape[0]
    copies, rest = [], []
    if first:
        table_copy = pltpu.make_async_copy(table_ref, table_buf, table_sem)
        table_copy.start()
    for h, zp, slices, start in volume_pieces(dims, zdev, half, offset):
        columns = pl.ds(start, width)
        to = kept_ref.at[slices, :, columns] if last else buf.at[h, slices]
        copies.append((h, zp, start, pltpu.make_async_copy(vol_ref.at[slices, :, columns], to, sems.at[h, zp])))
        copies[-1][-1].start()
    if last:
        for h in range(2):
            columns = pl.ds(h * half, offset)
            rest.append(pltpu.make_async_copy(vol_ref.at[:, :, columns], kept_ref.at[:, :, columns], rest_sems.at[h]))
            rest[h].start()
    if first:
        shape = (zdev * per, LANES)
        angle, lane = low_bits(iota(shape, 0), per), iota(shape, 1)
        starts = pick(angle, [start_ref[0, a].astype(F32) for a in range(per)])
        lengths = pick(angle, [len_ref[0, a].astype(F32) for a in range(per)])
        for d in range(groups):
            foot = jnp.where(lane == 2 * d, starts, jnp.where(lane == 2 * d + 1, lengths, 0.0))
            for h in range(2):
                outs[h * groups + d][:, width:] = foot
        table_copy.wait()
        both = jnp.concatenate(split(slice_weights(dims, 1, order_ref, table_buf, rows_ref)), axis=0)
        left = jnp.concatenate([both, both], axis=1)
        left_ref[...] = left
    else:
        left = given_ref[...]
    for h, zp, start, copy in copies:
        copy.wait()
        for at, size in tiles(width):
            parts = []
            for z in range(zb):
                if last:
                    cells_at = kept_ref[zp * zb + z, :, pl.ds(pl.multiple_of(start + at, LANES), size)]
                else:
                    cells_at = buf[h, zp * zb + z, :, at:at + size]
                parts.append(split(cells_at))
            product = dot(left, jnp.concatenate([p[0] for p in parts] + [p[1] for p in parts], axis=0))
            sums = product[:count] + product[count:]
            for d in range(groups):
                outs[h * groups + d][zp * SUBLANES:(zp + 1) * SUBLANES, at:at + size] = (
                    sums[d * SUBLANES:(d + 1) * SUBLANES]
                )
    for copy in rest:
        copy.wait()


def ray_sums(dims, chunk, offset, width, given, small, table, volume):
    per, groups, zb, cells = dims
    zdev, _, total = volume.shape
    first, last = chunk == 0, chunk == CHUNKS - 1
    count, all_cells = groups * SUBLANES, table.shape[1]
    out = jax.ShapeDtypeStruct((zdev * per, width + (LANES if first else 0)), F32)
    left = jax.ShapeDtypeStruct((2 * count, 2 * zb * cells), BF16)
    assert zb * cells == all_cells and not (first and last)
    sems = pltpu.SemaphoreType.DMA((2, zdev // zb))
    shapes = [out] * (2 * groups)
    scratch = [pltpu.VMEM((2, zdev, cells, width), F32), sems]
    args, specs, limit = [given, volume], [IN_VMEM, ANYWHERE], 50
    if first:
        scratch += [pltpu.VMEM(table.shape, F32), pltpu.VMEM((count, all_cells), F32), pltpu.SemaphoreType.DMA]
        args, specs, limit = [*small, table, volume], [IN_SMEM] * 3 + [ANYWHERE, ANYWHERE], 58
        shapes += [left]
    if last:
        scratch = [sems, pltpu.SemaphoreType.DMA((2,))]
        shapes += [jax.ShapeDtypeStruct(volume.shape, F32)]
        limit = 28
    size = zdev * cells * width * 2
    return pl.pallas_call(
        functools.partial(rays_kernel, dims, first, last, total // 2, offset, width),
        in_specs=specs,
        out_specs=[IN_VMEM] * len(shapes),
        out_shape=shapes,
        scratch_shapes=scratch,
        compiler_params=pltpu.CompilerParams(vmem_limit_bytes=limit * MIB),
        cost_estimate=pl.CostEstimate(flops=2 * size * 16, bytes_accessed=size * 4, transcendentals=0),
        name=f"ray_sums_{chunk}",
    )(*args)


def hat_weights(dims, zdev, start, length, row):
    per, groups, zb, cells = dims
    at = low_bits(iota(start.shape, 0), zdev * per)
    slice_at = over(at, zb * per) * zb + low_bits(over(at, per), zb)
    span = jnp.where(length > 0.0, length, 1.0) / zdev
    centre = start + (slice_at.astype(F32) + 0.5) * span
    hat = jnp.maximum(0.0, 1.0 - jnp.abs(row + 0.5 - centre) / span)
    return jnp.where(jnp.logical_and(row >= start, row < start + length), hat, 0.0)


def footprint_matrix(dims, zdev, rdev, foot):
    per = dims[0]
    rows = 2 * per * rdev
    slab = lax.axis_index("slab")
    sibling = slab + 1 - 2 * lax.rem(slab, 2)
    row_id = iota((1, rows), 1)
    row_slab = jnp.where(row_id < per * rdev, slab, sibling)
    row = (row_slab * rdev + low_bits(row_id, rdev)).astype(F32)
    shape = (foot.shape[0], rows)
    same_angle = low_bits(iota(shape, 0), per) == low_bits(over(iota(shape, 1), rdev), per)
    beyond = slab + jnp.where(low_bits(slab, 4) < 2, -2, 2)
    there = jnp.logical_and(beyond >= 0, beyond < lax.axis_size("slab"))
    known = jnp.where(there, foot.shape[0], foot.shape[0] // 3 * 2)
    meets = jnp.logical_and(same_angle, iota(shape, 0) < known)
    return jnp.where(meets, hat_weights(dims, zdev, foot[:, 0:1], foot[:, 1:2], row), 0.0)


def update_weights(dims, zdev, rdev, foot, order_ref, table_ref, rows_ref, out_ref):
    per, groups, zb, cells = dims
    count = groups * SUBLANES
    weights = slice_weights(dims, -1, order_ref, table_ref, rows_ref)
    window = -(-5 * rdev // LANES) * LANES
    row = ((lax.axis_index("slab") - 2) * rdev + iota((1, window), 1)).astype(F32)
    sums = [
        jnp.sum(hat_weights(dims, zdev, foot[:, 2 * d:2 * d + 1], foot[:, 2 * d + 1:2 * d + 2], row), axis=1, keepdims=True)
        for d in range(groups)
    ]
    pad = jnp.zeros((out_ref.shape[2] - 3 * count, weights.shape[1]), F32)
    for zp in range(zdev // zb):
        slices = jnp.concatenate([s[zp * SUBLANES:(zp + 1) * SUBLANES] for s in sums], axis=0)
        scaled = weights / jnp.sum(weights * slices, axis=0, keepdims=True)
        high = scaled.astype(BF16).astype(F32)
        stacked = jnp.concatenate([high, high, scaled - high, pad], axis=0)
        out_ref[zp] = stacked.T.astype(BF16)


def residual_kernel(dims, first, last, half, rdev, zdev, offset, width, *refs):
    per, groups, zb, cells = dims
    block = zdev * per
    if first or last:
        order_ref, table_ref, *refs = refs
    if last:
        foot_ref, *refs = refs
    if not first:
        mats, inverse_ref, refs = refs[:4], refs[4], refs[5:]
    sums_refs, (mine_ref, theirs_ref), refs = refs[:3], refs[3:5], refs[5:]
    if not first:
        mine_before, sent_before, *refs = refs
    mine_out, sent_out, *refs = refs
    if not first:
        mine_out[:, :, :offset] = mine_before[...]
        sent_out[:, :, :offset] = sent_before[...]
    outs, refs = refs[:3], refs[3:]
    if first:
        foot = jnp.concatenate([r[i, :, width:] for r in sums_refs for i in range(2)], axis=0)
        refs[5][...] = sums_refs[0][0, :, width:]
        kernel = footprint_matrix(dims, zdev, rdev, foot)
        count, rows = kernel.shape
        kernel_t = kernel.T
        cover = jnp.sum(kernel_t, axis=1, keepdims=True)
        angle = low_bits(over(iota((rows, 1), 0), rdev), per)
        path = jnp.zeros((rows, 1), F32)
        for a in range(per):
            at = order_ref[lax.axis_index("ang") * per + a]
            path = jnp.where(angle == a, jnp.sum(table_ref[pl.ds(at, 1), :], axis=1, keepdims=True), path)
        inverse = 1.0 / jnp.maximum(path * cover, 0.25)
        ahead, back = split(kernel_t), split(kernel)
        for ref, value in zip(refs, (*ahead, *back)):
            ref[...] = value
        refs[4][...] = jnp.broadcast_to(inverse, (rows, LANES))
    else:
        ahead, back = (mats[0][...], mats[1][...]), (mats[2][...], mats[3][...])
        inverse = inverse_ref[:, 0:1]
    start = lax.rem(lax.axis_index("slab"), 2) * half + offset
    for at, size in tiles(width):
        columns = slice(at, at + size)
        mine = mine_ref[:, :, pl.ds(pl.multiple_of(start + at, LANES), size)].astype(F32)
        theirs = theirs_ref[:, :, offset + at:offset + at + size]
        measured = jnp.concatenate([m.reshape(per * rdev, size) for m in (mine, theirs)], axis=0)
        sums = jnp.concatenate([r[i, :, columns] for r in sums_refs for i in range(2)], axis=0)
        residual = (measured - dot3(ahead, split(sums))) * inverse
        placed = slice(offset + at, offset + at + size)
        mine_out[:, :, placed] = residual[:per * rdev].reshape(per, rdev, size)
        sent_out[:, :, placed] = residual[per * rdev:].reshape(per, rdev, size)
        given = dot3(back, split(residual))
        for i, ref in enumerate(outs):
            for j in range(2):
                ref[j, :, columns] = given[(2 * i + j) * block:(2 * i + j + 1) * block]
    if last:
        update_weights(dims, zdev, rdev, foot_ref[...], order_ref, table_ref, refs[1], refs[0])


def residual_step(dims, zdev, chunk, offset, width, mats, before, order, table, sums, measured, theirs):
    per, groups, zb, cells = dims
    _, rdev, total = measured.shape
    first = chunk == 0
    block = zdev * per
    count, rows = 6 * block, 2 * per * rdev
    last = chunk == CHUNKS - 1
    assert not (first and last)
    given = jax.ShapeDtypeStruct((2, block, width), F32)
    piece = jax.ShapeDtypeStruct((per, rdev, offset + width), F32)
    shapes = [piece, piece, given, given, given]
    args, specs, scratch = [], [], []
    if first or last:
        args, specs = [order, table], [IN_SMEM, IN_VMEM]
    if last:
        depth = -(-3 * groups * SUBLANES // LANES) * LANES
        shapes.append(jax.ShapeDtypeStruct((zdev // zb, zb * cells, depth), BF16))
        scratch.append(pltpu.VMEM((groups * SUBLANES, table.shape[1]), F32))
        args += [mats[5]]
        specs += [IN_VMEM]
    if first:
        ahead, back = jax.ShapeDtypeStruct((rows, count), BF16), jax.ShapeDtypeStruct((count, rows), BF16)
        shapes += [ahead, ahead, back, back, jax.ShapeDtypeStruct((rows, LANES), F32)]
        shapes += [jax.ShapeDtypeStruct((block, LANES), F32)]
    else:
        args += mats[:5]
        specs += [IN_VMEM] * 5
    args += [*sums, measured, theirs, *before]
    specs += [IN_VMEM] * (5 + len(before))
    return pl.pallas_call(
        functools.partial(residual_kernel, dims, first, last, total // 2, rdev, zdev, offset, width),
        in_specs=specs,
        out_specs=[IN_VMEM] * len(shapes),
        out_shape=shapes,
        scratch_shapes=scratch,
        compiler_params=pltpu.CompilerParams(vmem_limit_bytes=16 * MIB),
        cost_estimate=pl.CostEstimate(
            flops=12 * count * rows * width, bytes_accessed=8 * width * (count + rows), transcendentals=0
        ),
        name=f"residual_{chunk}",
    )(*args)


def update_kernel(dims, first, last, half, offset, width, *refs):
    per, groups, zb, cells = dims
    count = groups * SUBLANES
    left_ref, backs, vol_ref, refs = refs[0], refs[1:1 + 2 * groups], refs[1 + 2 * groups], refs[2 + 2 * groups:]
    backs = [backs[-1], *backs[groups:-1], *backs[:groups]]
    zdev, depth = vol_ref.shape[0], left_ref.shape[2]
    if last:
        pieces, refs = refs[:2], refs[2:]
    if not first:
        refs = refs[1:]
    if last:
        out_ref, res_ref, buf, sems, res_sems = refs
    else:
        out_ref, buf, sems = refs
    odd = lax.rem(lax.axis_index("slab"), 2)
    leaving = []
    for h, zp, slices, start in volume_pieces(dims, zdev, half, offset):
        rows = slice(zp * SUBLANES, (zp + 1) * SUBLANES)
        left = left_ref[zp]
        for at, size in tiles(width):
            piece = slice(at, at + size)
            source = pl.ds(pl.multiple_of(start + at, LANES), size)
            back = jnp.concatenate([backs[h * groups + d][rows, piece] for d in range(groups)], axis=0)
            high, low = split(back)
            pad = jnp.zeros((depth - 3 * count, size), BF16)
            change = dot(left, jnp.concatenate([high, low, high, pad], axis=0))
            for z in range(zb):
                buf[h, zp * zb + z, :, piece] = (
                    vol_ref[zp * zb + z, :, source] + change[z * cells:(z + 1) * cells]
                )
        leaving.append(
            pltpu.make_async_copy(buf.at[h, slices], out_ref.at[slices, :, pl.ds(start, width)], sems.at[h, zp])
        )
        leaving[-1].start()
    if last:
        for h, ref in enumerate(pieces):
            columns = pl.ds(pl.multiple_of(lax.rem(odd + h, 2) * half, LANES), half)
            leaving.append(pltpu.make_async_copy(ref, res_ref.at[:, :, columns], res_sems.at[h]))
            leaving[-1].start()
    for copy in leaving:
        copy.wait()


def update_step(dims, chunk, offset, width, left, backs, pieces, volume, out):
    per, groups, zb, cells = dims
    zdev, _, total = volume.shape
    first, last = chunk == 0, chunk == CHUNKS - 1
    args = [left, *backs[groups:], *backs[1:groups], backs[0], volume]
    shapes = [jax.ShapeDtypeStruct(volume.shape, F32)]
    scratch = [pltpu.VMEM((2, zdev, cells, width), F32), pltpu.SemaphoreType.DMA((2, zdev // zb))]
    if last:
        args += pieces
        shapes += [jax.ShapeDtypeStruct((*pieces[0].shape[:2], total), F32)]
        scratch += [pltpu.SemaphoreType.DMA((2,))]
    specs = [IN_VMEM] * len(args)
    aliases = {}
    if not first:
        aliases = {len(args): 0}
        args += [out]
        specs += [ANYWHERE]
    size = zdev * cells * width * 2
    return pl.pallas_call(
        functools.partial(update_kernel, dims, first, last, total // 2, offset, width),
        in_specs=specs,
        out_specs=[ANYWHERE] * len(shapes),
        out_shape=shapes,
        scratch_shapes=scratch,
        input_output_aliases=aliases,
        compiler_params=pltpu.CompilerParams(vmem_limit_bytes=20 * MIB),
        cost_estimate=pl.CostEstimate(flops=2 * size * 48, bytes_accessed=size * 4, transcendentals=0),
        name=f"update_{chunk}",
    )(*args)


def body(volume, measured, foot_start, foot_len, order, table):
    slabs, groups = lax.axis_size("slab"), lax.axis_size("ang")
    per, rdev, total = measured.shape
    zdev, cells, _ = volume.shape
    half = total // 2
    zb = SUBLANES // per
    dims = (per, groups, zb, cells)
    each = half // CHUNKS
    widths = [each - LANES] + [each] * (CHUNKS - 2) + [each + LANES]
    offsets = [sum(widths[:c]) for c in range(CHUNKS)]

    def along(value, to):
        pairs = [(s, to(s)) for s in range(slabs)]
        return lax.ppermute(value, "slab", pairs)

    def spread(value, other, d):
        if not (other or d):
            return value
        pairs = [
            (s * groups + a, (s ^ other) * groups + (a + d) % groups) for s in range(slabs) for a in range(groups)
        ]
        return lax.ppermute(value, ("slab", "ang"), pairs)

    def facing(s):
        return s ^ 2

    def within(to, s):
        return to if 0 <= to < slabs else facing(s)

    def beyond(s):
        return within(s - 4 if s & 2 else s + 4, s)

    def back_from_beyond(s):
        return within(s + 4 if s & 2 else s - 4, s)

    odd = lax.rem(lax.axis_index("slab"), 2)
    theirs = along(
        lax.dynamic_slice_in_dim(measured, (1 - odd) * half, half, 2).astype(F32), lambda s: s ^ 1
    )

    sums, left = [], None
    for c in range(CHUNKS):
        parts = ray_sums(
            dims, c, offsets[c], widths[c], left, (order, foot_start, foot_len), table, volume
        )
        if c == 0:
            left = parts[2 * groups]
        kept = parts[-1]
        parts = [spread(parts[h * groups + d], h, d) for h in range(2) for d in range(groups)]
        own = jnp.stack([sum(parts[:groups]), sum(parts[groups:])])
        near = along(own, facing)
        far = along(near, beyond)
        sums.append((own, near, far))
    pieces, given, mats = [], [], None
    for c in range(CHUNKS):
        mine, sent, own, near, far, *rest = residual_step(
            dims, zdev, c, offsets[c], widths[c], mats, pieces, order, table, sums[c], measured, theirs
        )
        pieces = [mine, sent]
        mats = rest if c == 0 else mats
        left = rest[0]
        near = near + along(far, back_from_beyond)
        arrived = along(near, facing)
        halves = [own[i] + arrived[i] for i in range(2)]
        given.append([spread(halves[h], h, d) for h in range(2) for d in range(groups)])
    pieces = [mine, along(sent, lambda s: s ^ 1)]
    out = None
    for c in range(CHUNKS):
        out, *res = update_step(dims, c, offsets[c], widths[c], left, given[c], pieces, kept, out)
    return out, res[0]


def solution(mesh):
    return jax.shard_map(
        body,
        mesh=mesh,
        in_specs=(
            P("slab", "ang", None),
            P("ang", "slab", None),
            P("slab", "ang"),
            P("slab", "ang"),
            P(),
            P(),
        ),
        out_specs=(P("slab", "ang", None), P("ang", "slab", None)),
        check_vma=False,
    )
```

profile of v0, /device:TPU:0, one launch (start us, length us, event | category | flops | bytes accessed | tf_op | source)
XLA Modules:
  0.0 80.1 jit_solution(14613252909657863806)
XLA Ops:
  0.6 0.0 copy-start.1
  0.6 0.0 copy-start.3
  0.7 0.0 copy-start
  0.7 5.9 %ray_sums_0.1 = (f32[32,1024]{1,0:T(8,128)}, f32[32,1024]{1,0:T(8,128)}, f32[32,1024]{1,0:T(8,128)}, f32[32,1024]{1,0:T(8,128)}, bf16[32,512]{1,0:T(8,128)(2,1)}) custom-call(s32[64]{0:T(128)} %refs_0_.5, s32[1,4]{1,0:T(1,128)} %refs_1_.4, s32[1,4]{1,0:T(1,128)} %refs_2_.1, f32[64,256]{1,0:T(8,128)} %refs_1_.7, f32[8,128,4096]{2,1,0:T(8,128)} %refs_1_.6), custom_call_target="tpu_custom_call" | custom-call | flops 58720256 | bytes 7340032 | tf_op jit(solution)/shard_map/ray_sums_0/pallas_call | solution.py:176
  6.5 0.0 copy-start.4
  6.6 3.0 %collective-permute-start = (f32[32,1024]{1,0:T(8,128)}, f32[32,1024]{1,0:T(8,128)S(1)}, u32[]{:S(2)}, u32[]{:S(2)}) collective-permute-start(f32[32,1024]{1,0:T(8,128)} %get-tuple-element.30), channel_id=1, source_target_pairs={{0,1},{1,0},{2,3},{3,2},{4,5},{5,4},{6,7},{7,6},{8,9},{9,8},{10,11... | collective-permute-start | bytes 393224 | tf_op jit(solution)/shard_map/ppermute | solution.py:428
  9.6 0.0 collective-permute-start.1
  9.6 0.2 collective-permute-start.2
  9.8 0.0 copy-done
  9.8 0.1 dynamic-slice_convert_fusion
  9.9 0.4 collective-permute-start.5
  10.3 0.0 copy-start.2
  10.3 0.8 copy-done.2
  11.0 6.0 %ray_sums_1.1 = (f32[32,1152]{1,0:T(8,128)S(1)}, f32[32,1152]{1,0:T(8,128)S(1)}, f32[32,1152]{1,0:T(8,128)S(1)}, f32[32,1152]{1,0:T(8,128)S(1)}, f32[8,128,4096]{2,1,0:T(8,128)S(1)}) custom-call(bf16[32,512]{1,0:T(8,128)(2,1)S(1)} %copy-done.2, f32[8,128,4096]{2,1,0:T(8,128)} %refs_1_.6), custom_call_target="tpu_custom_call" | custom-call | flops 75497472 | bytes 9437184 | tf_op jit(solution)/shard_map/ray_sums_1/pallas_call | solution.py:176
  17.0 1.7 %collective-permute-start.6 = (f32[32,1152]{1,0:T(8,128)S(1)}, f32[32,1152]{1,0:T(8,128)S(1)}, u32[]{:S(2)}, u32[]{:S(2)}) collective-permute-start(f32[32,1152]{1,0:T(8,128)S(1)} %get-tuple-element.41), channel_id=1, source_target_pairs={{0,1},{1,0},{2,3},{3,2},{4,5},{5,4},{6,7},{7,6},{8,9},{9,8},{10,11... | collective-permute-start | bytes 442376 | tf_op jit(solution)/shard_map/ppermute | solution.py:428
  18.7 0.0 collective-permute-done
  18.7 0.2 collective-permute-start.7
  18.9 0.0 copy-done.4
  19.0 0.0 collective-permute-done.1
  19.0 0.3 collective-permute-start.8
  19.3 0.0 collective-permute-done.2
  19.4 1.7 %collective-permute-start.3 = (f32[2,32,1024]{2,1,0:T(8,128)S(1)}, f32[2,32,1024]{2,1,0:T(8,128)S(1)}, u32[]{:S(2)}, u32[]{:S(2)}) collective-permute-start(f32[2,32,1024]{2,1,0:T(8,128)S(1)} %pad_maximum_fusion.1.refs_2_), channel_id=1, source_target_pairs={{0,4},{2,6},{4,0},{6,2},{8,12},{10,14},{12,8},{14,10},{16,20},{18,... | collective-permute-start | bytes 786440 | tf_op jit(solution)/shard_map/ppermute | solution.py:420
  21.1 2.7 %collective-permute-done.6 = f32[32,1152]{1,0:T(8,128)S(1)} collective-permute-done((f32[32,1152]{1,0:T(8,128)S(1)}, f32[32,1152]{1,0:T(8,128)S(1)}, u32[]{:S(2)}, u32[]{:S(2)}) %collective-permute-start.6) | collective-permute-done | bytes 147488 | tf_op jit(solution)/shard_map/ppermute | solution.py:428
  23.8 0.0 collective-permute-done.7
  23.8 2.1 %collective-permute-done.8 = f32[32,1152]{1,0:T(8,128)S(1)} collective-permute-done((f32[32,1152]{1,0:T(8,128)S(1)}, f32[32,1152]{1,0:T(8,128)S(1)}, u32[]{:S(2)}, u32[]{:S(2)}) %collective-permute-start.8) | collective-permute-done | bytes 147488 | tf_op jit(solution)/shard_map/ppermute | solution.py:428
  25.9 1.9 %collective-permute-start.9 = (f32[2,32,1152]{2,1,0:T(8,128)S(1)}, f32[2,32,1152]{2,1,0:T(8,128)S(1)}, u32[]{:S(2)}, u32[]{:S(2)}) collective-permute-start(f32[2,32,1152]{2,1,0:T(8,128)S(1)} %pad_maximum_fusion.refs_8_), channel_id=1, source_target_pairs={{0,4},{2,6},{4,0},{6,2},{8,12},{10,14},{12,8},{14,10},{16,20},{18,... | collective-permute-start | bytes 884744 | tf_op jit(solution)/shard_map/ppermute | solution.py:420
  27.8 0.0 collective-permute-done.3.refs_3_
  27.8 1.7 %collective-permute-start.4 = (f32[2,32,1024]{2,1,0:T(8,128)S(1)}, f32[2,32,1024]{2,1,0:T(8,128)S(1)}, u32[]{:S(2)}, u32[]{:S(2)}) collective-permute-start(f32[2,32,1024]{2,1,0:T(8,128)S(1)} %collective-permute-done.3.refs_3_), channel_id=1, source_target_pairs={{0,8},{2,10},{4,0},{6,2},{8,16},{10,18},{12,4},{14,6},{16,24},{18,... | collective-permute-start | bytes 786440 | tf_op jit(solution)/shard_map/ppermute | solution.py:420
  29.6 6.3 %collective-permute-done.9.refs_9_ = f32[2,32,1152]{2,1,0:T(8,128)S(1)} collective-permute-done((f32[2,32,1152]{2,1,0:T(8,128)S(1)}, f32[2,32,1152]{2,1,0:T(8,128)S(1)}, u32[]{:S(2)}, u32[]{:S(2)}) %collective-permute-start.9) | collective-permute-done | bytes 294944 | tf_op jit(solution)/shard_map/ppermute | solution.py:420
  35.9 1.5 %collective-permute-start.10 = (f32[2,32,1152]{2,1,0:T(8,128)S(1)}, f32[2,32,1152]{2,1,0:T(8,128)S(1)}, u32[]{:S(2)}, u32[]{:S(2)}) collective-permute-start(f32[2,32,1152]{2,1,0:T(8,128)S(1)} %collective-permute-done.9.refs_9_), channel_id=1, source_target_pairs={{0,8},{2,10},{4,0},{6,2},{8,16},{10,18},{12,4},{14,6},{16,24},{18,... | collective-permute-start | bytes 884744 | tf_op jit(solution)/shard_map/ppermute | solution.py:420
  37.3 4.2 %collective-permute-done.4.refs_4_ = f32[2,32,1024]{2,1,0:T(8,128)S(1)} collective-permute-done((f32[2,32,1024]{2,1,0:T(8,128)S(1)}, f32[2,32,1024]{2,1,0:T(8,128)S(1)}, u32[]{:S(2)}, u32[]{:S(2)}) %collective-permute-start.4) | collective-permute-done | bytes 262176 | tf_op jit(solution)/shard_map/ppermute | solution.py:420
  41.5 0.0 collective-permute-done.5.refs_6_.refs_12_
  41.5 0.0 copy-done.1
  41.5 0.0 copy-done.3
  41.5 2.1 %residual_0.1 = (f32[4,32,896]{2,1,0:T(8,128)S(1)}, f32[4,32,896]{2,1,0:T(8,128)S(1)}, f32[2,32,896]{2,1,0:T(8,128)S(1)}, f32[2,32,896]{2,1,0:T(8,128)S(1)}, f32...) custom-call(s32[64]{0:T(128)S(1)} %copy-done.3, ...), custom_call_target="tpu_custom_call" | custom-call | flops 528482304 | bytes 3211264 | tf_op jit(solution)/shard_map/residual_0/pallas_call | solution.py:319
  43.6 0.1 collective-permute-start.17
  43.7 3.8 %collective-permute-done.10.refs_10_ = f32[2,32,1152]{2,1,0:T(8,128)S(1)} collective-permute-done((f32[2,32,1152]{2,1,0:T(8,128)S(1)}, f32[2,32,1152]{2,1,0:T(8,128)S(1)}, u32[]{:S(2)}, u32[]{:S(2)}) %collective-permute-start.10) | collective-permute-done | bytes 294944 | tf_op jit(solution)/shard_map/ppermute | solution.py:420
  47.5 2.2 %residual_1.1 = (f32[4,32,2048]{2,1,0:T(8,128)S(1)}, f32[4,32,2048]{2,1,0:T(8,128)S(1)}, f32[2,32,1152]{2,1,0:T(8,128)S(1)}, f32[2,32,1152]{2,1,0:T(8,128)S(1)},...) custom-call(s32[64]{0:T(128)S(1)} %copy-done.3, f32[64,256]{1,0:T(8,128)S(1)} %copy-done.1, ...), custom_call_target="tpu_custom_call" | custom-call | flops 679477248 | bytes 4128768 | tf_op jit(solution)/shard_map/residual_1/pallas_call | solution.py:319
  49.7 0.1 collective-permute-start.11
  49.8 0.8 %collective-permute-done.17 = f32[2,32,896]{2,1,0:T(8,128)S(1)} collective-permute-done((f32[2,32,896]{2,1,0:T(8,128)S(1)}, f32[2,32,896]{2,1,0:T(8,128)S(1)}, u32[]{:S(2)}, u32[]{:S(2)}) %collective-permute-start.17) | collective-permute-done | bytes 229408 | tf_op jit(solution)/shard_map/ppermute | solution.py:420
  50.6 0.4 collective-permute-start.18
  51.0 0.0 collective-permute-start.16
  51.0 7.4 %collective-permute-done.11 = f32[2,32,1152]{2,1,0:T(8,128)S(1)} collective-permute-done((f32[2,32,1152]{2,1,0:T(8,128)S(1)}, f32[2,32,1152]{2,1,0:T(8,128)S(1)}, u32[]{:S(2)}, u32[]{:S(2)}) %collective-permute-start.11) | collective-permute-done | bytes 294944 | tf_op jit(solution)/shard_map/ppermute | solution.py:420
  58.5 1.3 %collective-permute-start.12 = (f32[2,32,1152]{2,1,0:T(8,128)S(1)}, f32[2,32,1152]{2,1,0:T(8,128)S(1)}, u32[]{:S(2)}, u32[]{:S(2)}) collective-permute-start(f32[2,32,1152]{2,1,0:T(8,128)S(1)} %add.48), channel_id=1, source_target_pairs={{0,4},{2,6},{4,0},{6,2},{8,12},{10,14},{12,8},{14,10},{16,20},{18,... | collective-permute-start | bytes 884744 | tf_op jit(solution)/shard_map/ppermute | solution.py:420
  59.7 2.3 %collective-permute-done.18 = f32[2,32,896]{2,1,0:T(8,128)S(1)} collective-permute-done((f32[2,32,896]{2,1,0:T(8,128)S(1)}, f32[2,32,896]{2,1,0:T(8,128)S(1)}, u32[]{:S(2)}, u32[]{:S(2)}) %collective-permute-start.18) | collective-permute-done | bytes 229408 | tf_op jit(solution)/shard_map/ppermute | solution.py:420
  62.1 1.8 %collective-permute-start.21 = (f32[32,896]{1,0:T(8,128)S(1)}, f32[32,896]{1,0:T(8,128)S(1)}, u32[]{:S(2)}, u32[]{:S(2)}) collective-permute-start(f32[32,896]{1,0:T(8,128)S(1)} %get-tuple-element.58.refs_4_), channel_id=1, source_target_pairs={{0,1},{1,0},{2,3},{3,2},{4,5},{5,4},{6,7},{7,6},{8,9},{9,8},{10,11... | collective-permute-start | bytes 344072 | tf_op jit(solution)/shard_map/ppermute | solution.py:428
  63.9 0.0 collective-permute-start.20
  63.9 3.6 %collective-permute-done.12 = f32[2,32,1152]{2,1,0:T(8,128)S(1)} collective-permute-done((f32[2,32,1152]{2,1,0:T(8,128)S(1)}, f32[2,32,1152]{2,1,0:T(8,128)S(1)}, u32[]{:S(2)}, u32[]{:S(2)}) %collective-permute-start.12) | collective-permute-done | bytes 294944 | tf_op jit(solution)/shard_map/ppermute | solution.py:420
  67.5 1.8 %collective-permute-start.15 = (f32[32,1152]{1,0:T(8,128)S(1)}, f32[32,1152]{1,0:T(8,128)S(1)}, u32[]{:S(2)}, u32[]{:S(2)}) collective-permute-start(f32[32,1152]{1,0:T(8,128)S(1)} %get-tuple-element.56.refs_4_), channel_id=1, source_target_pairs={{0,1},{1,0},{2,3},{3,2},{4,5},{5,4},{6,7},{7,6},{8,9},{9,8},{10,11... | collective-permute-start | bytes 442376 | tf_op jit(solution)/shard_map/ppermute | solution.py:428
  69.3 0.0 collective-permute-start.14
  69.3 0.0 collective-permute-done.21.refs_3_
  69.3 0.4 collective-permute-start.13
  69.7 0.0 collective-permute-done.20.refs_2_
  69.7 0.1 collective-permute-start.19
  69.8 1.2 %collective-permute-done.19.refs_1_ = f32[32,896]{1,0:T(8,128)S(1)} collective-permute-done((f32[32,896]{1,0:T(8,128)S(1)}, f32[32,896]{1,0:T(8,128)S(1)}, u32[]{:S(2)}, u32[]{:S(2)}) %collective-permute-start.19) | collective-permute-done | bytes 114720 | tf_op jit(solution)/shard_map/ppermute | solution.py:428
  71.0 3.3 %update_0.1.refs_8_ = f32[8,128,4096]{2,1,0:T(8,128)} custom-call(bf16[4,256,128]{2,1,0:T(8,128)(2,1)S(1)} %get-tuple-element.46.refs_0_, f32[32,896]{1,0:T(8,128)S(1)} %collective-permute-done.19.refs_1_, f32[32,896]{1,0:T(8,128)S(1)} %collective-permute-done.20.refs_2_, f32[32,896]{1,0:T(8,128)S(1)} %collective-permute-done.21.refs_3_, ...), custom_call_target="tpu_custom_call" | custom-call | flops 176160768 | bytes 7340032 | tf_op jit(solution)/shard_map/update_0/pallas_call | solution.py:394
  74.4 0.0 collective-permute-done.15.refs_3_
  74.4 1.0 %collective-permute-done.14.refs_2_ = f32[32,1152]{1,0:T(8,128)S(1)} collective-permute-done((f32[32,1152]{1,0:T(8,128)S(1)}, f32[32,1152]{1,0:T(8,128)S(1)}, u32[]{:S(2)}, u32[]{:S(2)}) %collective-permute-start.14) | collective-permute-done | bytes 147488 | tf_op jit(solution)/shard_map/ppermute | solution.py:428
  75.4 0.0 collective-permute-done.13.refs_1_
  75.4 0.0 collective-permute-done.16.refs_7_
  75.4 4.7 %update_1.1 = (f32[8,128,4096]{2,1,0:T(8,128)}, f32[4,32,4096]{2,1,0:T(8,128)}) custom-call(bf16[4,256,128]{2,1,0:T(8,128)(2,1)S(1)} %get-tuple-element.46.refs_0_, f32[32,1152]{1,0:T(8,128)S(1)} %collective-permute-done.13.refs_1_, f32[32,1152]{1,0:T(8,128)S(1)} %collective-permute-done.14.refs_2_, ...), custom_call_target="tpu_custom_call", output_to_operand_aliasing={{0}: (8, {})} | custom-call | flops 226492416 | bytes 9437184 | tf_op jit(solution)/shard_map/update_1/pallas_call | solution.py:394
  (10 shorter events, 0.2 us)
Async XLA Ops:
  0.6 40.9 %copy-start.1 = (f32[64,256]{1,0:T(8,128)S(1)}, f32[64,256]{1,0:T(8,128)}, u32[]{:S(2)}) copy-start(f32[64,256]{1,0:T(8,128)} %refs_1_.7) | copy-start | bytes 196612
  0.6 40.9 %copy-start.3 = (s32[64]{0:T(128)S(1)}, s32[64]{0:T(128)}, u32[]{:S(2)}) copy-start(s32[64]{0:T(128)} %refs_0_.5) | copy-start | bytes 772
  0.7 9.1 %copy-start = (bf16[4,32,4096]{2,1,0:T(8,128)(2,1)S(1)}, bf16[4,32,4096]{2,1,0:T(8,128)(2,1)}, u32[]{:S(2)}) copy-start(bf16[4,32,4096]{2,1,0:T(8,128)(2,1)} %refs_11_.1) | copy-start | bytes 3145732
  6.5 12.4 %copy-start.4 = (f32[32,1024]{1,0:T(8,128)S(1)}, f32[32,1024]{1,0:T(8,128)}, u32[]{:S(2)}) copy-start(f32[32,1024]{1,0:T(8,128)} %get-tuple-element.29) | copy-start | bytes 393220
  6.6 12.2 %collective-permute-start = (f32[32,1024]{1,0:T(8,128)}, f32[32,1024]{1,0:T(8,128)S(1)}, u32[]{:S(2)}, u32[]{:S(2)}) collective-permute-start(f32[32,1024]{1,0:T(8,128)} %get-tuple-element.30), channel_id=1, source_target_pairs={{0,1},{1,0},{2,3},{3,2},{4,5},{5,4},{6,7},{7,6},{8,9},{9,8},{10,11... | collective-permute-start | bytes 393224 | tf_op jit(solution)/shard_map/ppermute | solution.py:428
  9.6 9.4 %collective-permute-start.1 = (f32[32,1024]{1,0:T(8,128)}, f32[32,1024]{1,0:T(8,128)S(1)}, u32[]{:S(2)}, u32[]{:S(2)}) collective-permute-start(f32[32,1024]{1,0:T(8,128)} %get-tuple-element.31), channel_id=1, source_target_pairs={{0,2},{1,3},{2,0},{3,1},{4,6},{5,7},{6,4},{7,5},{8,10},{9,11},{10,... | collective-permute-start | bytes 393224 | tf_op jit(solution)/shard_map/ppermute | solution.py:428
  9.6 9.7 %collective-permute-start.2 = (f32[32,1024]{1,0:T(8,128)}, f32[32,1024]{1,0:T(8,128)S(1)}, u32[]{:S(2)}, u32[]{:S(2)}) collective-permute-start(f32[32,1024]{1,0:T(8,128)} %get-tuple-element.32), channel_id=1, source_target_pairs={{0,3},{1,2},{2,1},{3,0},{4,7},{5,6},{6,5},{7,4},{8,11},{9,10},{10,... | collective-permute-start | bytes 393224 | tf_op jit(solution)/shard_map/ppermute | solution.py:428
  9.9 31.6 %collective-permute-start.5 = (f32[4,32,2048]{2,1,0:T(8,128)S(1)}, f32[4,32,2048]{2,1,0:T(8,128)S(1)}, u32[]{:S(2)}, u32[]{:S(2)}) collective-permute-start(f32[4,32,2048]{2,1,0:T(8,128)S(1)} %dynamic-slice_convert_fusion), channel_id=1, source_target_pairs={{0,2},{2,0},{4,6},{6,4},{8,10},{10,8},{12,14},{14,12},{16,18},{18,... | collective-permute-start | bytes 3145736 | tf_op jit(solution)/shard_map/ppermute | solution.py:420
  10.3 0.8 copy-start.2
  17.0 6.7 %collective-permute-start.6 = (f32[32,1152]{1,0:T(8,128)S(1)}, f32[32,1152]{1,0:T(8,128)S(1)}, u32[]{:S(2)}, u32[]{:S(2)}) collective-permute-start(f32[32,1152]{1,0:T(8,128)S(1)} %get-tuple-element.41), channel_id=1, source_target_pairs={{0,1},{1,0},{2,3},{3,2},{4,5},{5,4},{6,7},{7,6},{8,9},{9,8},{10,11... | collective-permute-start | bytes 442376 | tf_op jit(solution)/shard_map/ppermute | solution.py:428
  18.7 5.0 %collective-permute-start.7 = (f32[32,1152]{1,0:T(8,128)S(1)}, f32[32,1152]{1,0:T(8,128)S(1)}, u32[]{:S(2)}, u32[]{:S(2)}) collective-permute-start(f32[32,1152]{1,0:T(8,128)S(1)} %get-tuple-element.42), channel_id=1, source_target_pairs={{0,2},{1,3},{2,0},{3,1},{4,6},{5,7},{6,4},{7,5},{8,10},{9,11},{10,... | collective-permute-start | bytes 442376 | tf_op jit(solution)/shard_map/ppermute | solution.py:428
  19.0 6.9 %collective-permute-start.8 = (f32[32,1152]{1,0:T(8,128)S(1)}, f32[32,1152]{1,0:T(8,128)S(1)}, u32[]{:S(2)}, u32[]{:S(2)}) collective-permute-start(f32[32,1152]{1,0:T(8,128)S(1)} %get-tuple-element.43), channel_id=1, source_target_pairs={{0,3},{1,2},{2,1},{3,0},{4,7},{5,6},{6,5},{7,4},{8,11},{9,10},{10,... | collective-permute-start | bytes 442376 | tf_op jit(solution)/shard_map/ppermute | solution.py:428
  19.4 8.5 %collective-permute-start.3 = (f32[2,32,1024]{2,1,0:T(8,128)S(1)}, f32[2,32,1024]{2,1,0:T(8,128)S(1)}, u32[]{:S(2)}, u32[]{:S(2)}) collective-permute-start(f32[2,32,1024]{2,1,0:T(8,128)S(1)} %pad_maximum_fusion.1.refs_2_), channel_id=1, source_target_pairs={{0,4},{2,6},{4,0},{6,2},{8,12},{10,14},{12,8},{14,10},{16,20},{18,... | collective-permute-start | bytes 786440 | tf_op jit(solution)/shard_map/ppermute | solution.py:420
  25.9 9.9 %collective-permute-start.9 = (f32[2,32,1152]{2,1,0:T(8,128)S(1)}, f32[2,32,1152]{2,1,0:T(8,128)S(1)}, u32[]{:S(2)}, u32[]{:S(2)}) collective-permute-start(f32[2,32,1152]{2,1,0:T(8,128)S(1)} %pad_maximum_fusion.refs_8_), channel_id=1, source_target_pairs={{0,4},{2,6},{4,0},{6,2},{8,12},{10,14},{12,8},{14,10},{16,20},{18,... | collective-permute-start | bytes 884744 | tf_op jit(solution)/shard_map/ppermute | solution.py:420
  27.8 13.6 %collective-permute-start.4 = (f32[2,32,1024]{2,1,0:T(8,128)S(1)}, f32[2,32,1024]{2,1,0:T(8,128)S(1)}, u32[]{:S(2)}, u32[]{:S(2)}) collective-permute-start(f32[2,32,1024]{2,1,0:T(8,128)S(1)} %collective-permute-done.3.refs_3_), channel_id=1, source_target_pairs={{0,8},{2,10},{4,0},{6,2},{8,16},{10,18},{12,4},{14,6},{16,24},{18,... | collective-permute-start | bytes 786440 | tf_op jit(solution)/shard_map/ppermute | solution.py:420
  35.9 11.6 %collective-permute-start.10 = (f32[2,32,1152]{2,1,0:T(8,128)S(1)}, f32[2,32,1152]{2,1,0:T(8,128)S(1)}, u32[]{:S(2)}, u32[]{:S(2)}) collective-permute-start(f32[2,32,1152]{2,1,0:T(8,128)S(1)} %collective-permute-done.9.refs_9_), channel_id=1, source_target_pairs={{0,8},{2,10},{4,0},{6,2},{8,16},{10,18},{12,4},{14,6},{16,24},{18,... | collective-permute-start | bytes 884744 | tf_op jit(solution)/shard_map/ppermute | solution.py:420
  43.6 7.0 %collective-permute-start.17 = (f32[2,32,896]{2,1,0:T(8,128)S(1)}, f32[2,32,896]{2,1,0:T(8,128)S(1)}, u32[]{:S(2)}, u32[]{:S(2)}) collective-permute-start(f32[2,32,896]{2,1,0:T(8,128)S(1)} %get-tuple-element.55), channel_id=1, source_target_pairs={{0,4},{2,6},{4,12},{6,14},{8,0},{10,2},{12,20},{14,22},{16,8},{18,... | collective-permute-start | bytes 688136 | tf_op jit(solution)/shard_map/ppermute | solution.py:420
  49.7 8.7 %collective-permute-start.11 = (f32[2,32,1152]{2,1,0:T(8,128)S(1)}, f32[2,32,1152]{2,1,0:T(8,128)S(1)}, u32[]{:S(2)}, u32[]{:S(2)}) collective-permute-start(f32[2,32,1152]{2,1,0:T(8,128)S(1)} %get-tuple-element.49), channel_id=1, source_target_pairs={{0,4},{2,6},{4,12},{6,14},{8,0},{10,2},{12,20},{14,22},{16,8},{18,... | collective-permute-start | bytes 884744 | tf_op jit(solution)/shard_map/ppermute | solution.py:420
  50.6 11.4 %collective-permute-start.18 = (f32[2,32,896]{2,1,0:T(8,128)S(1)}, f32[2,32,896]{2,1,0:T(8,128)S(1)}, u32[]{:S(2)}, u32[]{:S(2)}) collective-permute-start(f32[2,32,896]{2,1,0:T(8,128)S(1)} %add.53), channel_id=1, source_target_pairs={{0,4},{2,6},{4,0},{6,2},{8,12},{10,14},{12,8},{14,10},{16,20},{18,... | collective-permute-start | bytes 688136 | tf_op jit(solution)/shard_map/ppermute | solution.py:420
  51.0 24.5 %collective-permute-start.16 = (f32[4,32,2048]{2,1,0:T(8,128)S(1)}, f32[4,32,2048]{2,1,0:T(8,128)S(1)}, u32[]{:S(2)}, u32[]{:S(2)}) collective-permute-start(f32[4,32,2048]{2,1,0:T(8,128)S(1)} %get-tuple-element.52), channel_id=1, source_target_pairs={{0,2},{2,0},{4,6},{6,4},{8,10},{10,8},{12,14},{14,12},{16,18},{18,... | collective-permute-start | bytes 3145736 | tf_op jit(solution)/shard_map/ppermute | solution.py:420
  58.5 9.0 %collective-permute-start.12 = (f32[2,32,1152]{2,1,0:T(8,128)S(1)}, f32[2,32,1152]{2,1,0:T(8,128)S(1)}, u32[]{:S(2)}, u32[]{:S(2)}) collective-permute-start(f32[2,32,1152]{2,1,0:T(8,128)S(1)} %add.48), channel_id=1, source_target_pairs={{0,4},{2,6},{4,0},{6,2},{8,12},{10,14},{12,8},{14,10},{16,20},{18,... | collective-permute-start | bytes 884744 | tf_op jit(solution)/shard_map/ppermute | solution.py:420
  62.1 7.2 %collective-permute-start.21 = (f32[32,896]{1,0:T(8,128)S(1)}, f32[32,896]{1,0:T(8,128)S(1)}, u32[]{:S(2)}, u32[]{:S(2)}) collective-permute-start(f32[32,896]{1,0:T(8,128)S(1)} %get-tuple-element.58.refs_4_), channel_id=1, source_target_pairs={{0,1},{1,0},{2,3},{3,2},{4,5},{5,4},{6,7},{7,6},{8,9},{9,8},{10,11... | collective-permute-start | bytes 344072 | tf_op jit(solution)/shard_map/ppermute | solution.py:428
  63.9 5.8 %collective-permute-start.20 = (f32[32,896]{1,0:T(8,128)S(1)}, f32[32,896]{1,0:T(8,128)S(1)}, u32[]{:S(2)}, u32[]{:S(2)}) collective-permute-start(f32[32,896]{1,0:T(8,128)S(1)} %get-tuple-element.59), channel_id=1, source_target_pairs={{0,3},{1,2},{2,1},{3,0},{4,7},{5,6},{6,5},{7,4},{8,11},{9,10},{10,... | collective-permute-start | bytes 344072 | tf_op jit(solution)/shard_map/ppermute | solution.py:428
  67.5 6.9 %collective-permute-start.15 = (f32[32,1152]{1,0:T(8,128)S(1)}, f32[32,1152]{1,0:T(8,128)S(1)}, u32[]{:S(2)}, u32[]{:S(2)}) collective-permute-start(f32[32,1152]{1,0:T(8,128)S(1)} %get-tuple-element.56.refs_4_), channel_id=1, source_target_pairs={{0,1},{1,0},{2,3},{3,2},{4,5},{5,4},{6,7},{7,6},{8,9},{9,8},{10,11... | collective-permute-start | bytes 442376 | tf_op jit(solution)/shard_map/ppermute | solution.py:428
  69.3 6.2 %collective-permute-start.14 = (f32[32,1152]{1,0:T(8,128)S(1)}, f32[32,1152]{1,0:T(8,128)S(1)}, u32[]{:S(2)}, u32[]{:S(2)}) collective-permute-start(f32[32,1152]{1,0:T(8,128)S(1)} %get-tuple-element.57), channel_id=1, source_target_pairs={{0,3},{1,2},{2,1},{3,0},{4,7},{5,6},{6,5},{7,4},{8,11},{9,10},{10,... | collective-permute-start | bytes 442376 | tf_op jit(solution)/shard_map/ppermute | solution.py:428
  69.3 6.2 %collective-permute-start.13 = (f32[32,1152]{1,0:T(8,128)S(1)}, f32[32,1152]{1,0:T(8,128)S(1)}, u32[]{:S(2)}, u32[]{:S(2)}) collective-permute-start(f32[32,1152]{1,0:T(8,128)S(1)} %get-tuple-element.57), channel_id=1, source_target_pairs={{0,2},{1,3},{2,0},{3,1},{4,6},{5,7},{6,4},{7,5},{8,10},{9,11},{10,... | collective-permute-start | bytes 442376 | tf_op jit(solution)/shard_map/ppermute | solution.py:428
  69.7 1.3 %collective-permute-start.19 = (f32[32,896]{1,0:T(8,128)S(1)}, f32[32,896]{1,0:T(8,128)S(1)}, u32[]{:S(2)}, u32[]{:S(2)}) collective-permute-start(f32[32,896]{1,0:T(8,128)S(1)} %get-tuple-element.59), channel_id=1, source_target_pairs={{0,2},{1,3},{2,0},{3,1},{4,6},{5,7},{6,4},{7,5},{8,10},{9,11},{10,... | collective-permute-start | bytes 344072 | tf_op jit(solution)/shard_map/ppermute | solution.py:428
where the time goes:
time: 81.4 us; the launch traced here: 80.1 us
  waiting for transfers between devices  35.6 us (44%)
  Pallas kernels  24.1 us (30%)
  starting transfers between devices  18.4 us (23%)
    ppermute x10, waiting for transfers between devices, along(): return lax.ppermute(value, 'slab', pairs)  28.5 us
    pallas_call x2, Pallas kernels, ray_sums(): pl.pallas_call(functools.partial(rays_kernel, dims, first, last, total //...  11.8 us
    ppermute x12, starting transfers between devices, spread(): return lax.ppermute(value, ('slab', 'ang'), pairs)  9.6 us
    ppermute x10, starting transfers between devices, along(): return lax.ppermute(value, 'slab', pairs)  8.84 us
    pallas_call x2, Pallas kernels, update_step(): pl.pallas_call(functools.partial(update_kernel, dims, first, last, total...  7.99 us
    ppermute x12, waiting for transfers between devices, spread(): return lax.ppermute(value, ('slab', 'ang'), pairs)  7.1 us
    pallas_call x2, Pallas kernels, residual_step(): pl.pallas_call(functools.partial(residual_kernel, dims, first, last, tota...  4.3 us
  transfers between devices with their start and end apart: 22, of which 11 were waited for; matrix products, arithmetic and copies ran while one was open for 0% of the time, Pallas kernels for 17%

commit v1 on v0

--- a/solution.py
+++ b/solution.py
@@ -97,7 +97,7 @@
         given_ref, vol_ref, *refs = refs
     outs, refs = refs[:2 * groups], refs[2 * groups:]
     if first:
-        left_ref, buf, sems, table_buf, rows_ref, table_sem = refs
+        left_ref, buf, sems, table_buf, order_buf, start_buf, len_buf, rows_ref, small_sems = refs
     elif last:
         kept_ref, sems, rest_sems = refs
     else:
@@ -105,8 +105,14 @@
     zdev = vol_ref.shape[0]
     copies, rest = [], []
     if first:
-        table_copy = pltpu.make_async_copy(table_ref, table_buf, table_sem)
-        table_copy.start()
+        small = [
+            pltpu.make_async_copy(source, to, small_sems.at[i])
+            for i, (source, to) in enumerate(
+                [(order_ref, order_buf), (table_ref, table_buf), (start_ref, start_buf), (len_ref, len_buf)]
+            )
+        ]
+        for copy in small:
+            copy.start()
     for h, zp, slices, start in volume_pieces(dims, zdev, half, offset):
         columns = pl.ds(start, width)
         to = kept_ref.at[slices, :, columns] if last else buf.at[h, slices]
@@ -118,18 +124,21 @@
             rest.append(pltpu.make_async_copy(vol_ref.at[:, :, columns], kept_ref.at[:, :, columns], rest_sems.at[h]))
             rest[h].start()
     if first:
+        small[0].wait()
+        small[1].wait()
+        both = jnp.concatenate(split(slice_weights(dims, 1, order_buf, table_buf, rows_ref)), axis=0)
+        left = jnp.concatenate([both, both], axis=1)
+        left_ref[...] = left
+        small[2].wait()
+        small[3].wait()
         shape = (zdev * per, LANES)
         angle, lane = low_bits(iota(shape, 0), per), iota(shape, 1)
-        starts = pick(angle, [start_ref[0, a].astype(F32) for a in range(per)])
-        lengths = pick(angle, [len_ref[0, a].astype(F32) for a in range(per)])
+        starts = pick(angle, [start_buf[0, a].astype(F32) for a in range(per)])
+        lengths = pick(angle, [len_buf[0, a].astype(F32) for a in range(per)])
         for d in range(groups):
             foot = jnp.where(lane == 2 * d, starts, jnp.where(lane == 2 * d + 1, lengths, 0.0))
             for h in range(2):
                 outs[h * groups + d][:, width:] = foot
-        table_copy.wait()
-        both = jnp.concatenate(split(slice_weights(dims, 1, order_ref, table_buf, rows_ref)), axis=0)
-        left = jnp.concatenate([both, both], axis=1)
-        left_ref[...] = left
     else:
         left = given_ref[...]
     for h, zp, start, copy in copies:
@@ -165,8 +174,9 @@
     scratch = [pltpu.VMEM((2, zdev, cells, width), F32), sems]
     args, specs, limit = [given, volume], [IN_VMEM, ANYWHERE], 50
     if first:
-        scratch += [pltpu.VMEM(table.shape, F32), pltpu.VMEM((count, all_cells), F32), pltpu.SemaphoreType.DMA]
-        args, specs, limit = [*small, table, volume], [IN_SMEM] * 3 + [ANYWHERE, ANYWHERE], 58
+        scratch += [pltpu.VMEM(table.shape, F32)] + [pltpu.SMEM(a.shape, a.dtype) for a in small]
+        scratch += [pltpu.VMEM((count, all_cells), F32), pltpu.SemaphoreType.DMA((4,))]
+        args, specs, limit = [*small, table, volume], [ANYWHERE] * 5, 58
         shapes += [left]
     if last:
         scratch = [sems, pltpu.SemaphoreType.DMA((2,))]
@@ -430,14 +440,19 @@
     def facing(s):
         return s ^ 2
 
-    def within(to, s):
-        return to if 0 <= to < slabs else facing(s)
-
-    def beyond(s):
-        return within(s - 4 if s & 2 else s + 4, s)
-
-    def back_from_beyond(s):
-        return within(s + 4 if s & 2 else s - 4, s)
+    def step(up, busy):
+        def to(s):
+            there = s + 4 if up(s) else s - 4
+            if 0 <= there < slabs:
+                return there
+            return there % slabs if busy else facing(s)
+        return to
+
+    def beyond(c):
+        return step(lambda s: not s & 2, c < CHUNKS - 1)
+
+    def back_from_beyond(c):
+        return step(lambda s: s & 2, c > 0)
 
     odd = lax.rem(lax.axis_index("slab"), 2)
     theirs = along(
@@ -455,7 +470,7 @@
         parts = [spread(parts[h * groups + d], h, d) for h in range(2) for d in range(groups)]
         own = jnp.stack([sum(parts[:groups]), sum(parts[groups:])])
         near = along(own, facing)
-        far = along(near, beyond)
+        far = along(near, beyond(c))
         sums.append((own, near, far))
     pieces, given, mats = [], [], None
     for c in range(CHUNKS):
@@ -465,7 +480,7 @@
         pieces = [mine, sent]
         mats = rest if c == 0 else mats
         left = rest[0]
-        near = near + along(far, back_from_beyond)
+        near = near + along(far, back_from_beyond(c))
         arrived = along(near, facing)
         halves = [own[i] + arrived[i] for i in range(2)]
         given.append([spread(halves[h], h, d) for h in range(2) for d in range(groups)])

time: 81.4 us -> 74.2 us (0.912); the launches traced: 80.1 us -> 74 us
  waiting for transfers between devices: 35.6 us -> 26.3 us
  starting transfers between devices: 18.4 us -> 23.2 us
  Pallas kernels: 24.1 us -> 22.6 us
    ppermute x10, waiting for transfers between devices: 28.5 us -> 19.3 us  [along(): return lax.ppermute(value, 'slab', pairs)]
    ppermute x10, starting transfers between devices: 8.84 us -> 13.9 us  [along(): return lax.ppermute(value, 'slab', pairs)]
    pallas_call x2, Pallas kernels: 11.8 us -> 10.3 us  [ray_sums(): pl.pallas_call(functools.partial(rays_kernel, dims, first, last, total //...]
  transfers between devices with their start and end apart: 22 -> 22, of which waited for: 11 -> 10; matrix products, arithmetic and copies ran while one was open for 0% -> 0% of each run, Pallas kernels for 17% -> 18%
where the time goes in v1:
time: 74.2 us; the launch traced here: 74 us
  waiting for transfers between devices  26.3 us (35%)
  starting transfers between devices  23.2 us (31%)
  Pallas kernels  22.6 us (30%)
  between operations  0.81 us (1%)
  local copies, waits for them, and re-layouts  0.78 us (1%)
    ppermute x10, waiting for transfers between devices, along(): return lax.ppermute(value, 'slab', pairs)  19.3 us
    ppermute x10, starting transfers between devices, along(): return lax.ppermute(value, 'slab', pairs)  13.9 us
    pallas_call x2, Pallas kernels, ray_sums(): pl.pallas_call(functools.partial(rays_kernel, dims, first, last, total //...  10.3 us
    ppermute x12, starting transfers between devices, spread(): return lax.ppermute(value, ('slab', 'ang'), pairs)  9.31 us
    pallas_call x2, Pallas kernels, update_step(): pl.pallas_call(functools.partial(update_kernel, dims, first, last, total...  7.98 us
    ppermute x12, waiting for transfers between devices, spread(): return lax.ppermute(value, ('slab', 'ang'), pairs)  6.99 us
    pallas_call x2, Pallas kernels, residual_step(): pl.pallas_call(functools.partial(residual_kernel, dims, first, last, tota...  4.28 us
  transfers between devices with their start and end apart: 22, of which 10 were waited for; matrix products, arithmetic and copies ran while one was open for 0% of the time, Pallas kernels for 18%

profile of v1, /device:TPU:0, one launch (start us, length us, event | category | flops | bytes accessed | tf_op | source)
XLA Modules:
  0.0 74.0 jit_solution(1146158264813343383)
XLA Ops:
  0.6 0.0 copy-start.1
  0.6 0.0 copy-start.3
  0.7 0.0 copy-start
  0.7 4.3 %ray_sums_0.1 = (f32[32,1024]{1,0:T(8,128)}, f32[32,1024]{1,0:T(8,128)}, f32[32,1024]{1,0:T(8,128)}, f32[32,1024]{1,0:T(8,128)}, bf16[32,512]{1,0:T(8,128)(2,1)}) custom-call(s32[64]{0:T(128)} %refs_0_.5, s32[1,4]{1,0:T(1,128)} %refs_1_.4, s32[1,4]{1,0:T(1,128)} %refs_2_.1, f32[64,256]{1,0:T(8,128)} %refs_1_.7, f32[8,128,4096]{2,1,0:T(8,128)} %refs_1_.6), custom_call_target="tpu_custom_call" | custom-call | flops 58720256 | bytes 7340032 | tf_op jit(solution)/shard_map/ray_sums_0/pallas_call | solution.py:186
  5.0 0.0 copy-start.4
  5.0 3.0 %collective-permute-start = (f32[32,1024]{1,0:T(8,128)}, f32[32,1024]{1,0:T(8,128)S(1)}, u32[]{:S(2)}, u32[]{:S(2)}) collective-permute-start(f32[32,1024]{1,0:T(8,128)} %get-tuple-element.30), channel_id=1, source_target_pairs={{0,1},{1,0},{2,3},{3,2},{4,5},{5,4},{6,7},{7,6},{8,9},{9,8},{10,11... | collective-permute-start | bytes 393224 | tf_op jit(solution)/shard_map/ppermute | solution.py:438
  8.1 0.0 collective-permute-start.1
  8.1 0.2 collective-permute-start.2
  8.3 0.0 copy-done
  8.3 0.1 dynamic-slice_convert_fusion
  8.4 0.4 collective-permute-start.5
  8.7 0.0 copy-start.2
  8.7 0.8 %copy-done.2 = bf16[32,512]{1,0:T(8,128)(2,1)S(1)} copy-done((bf16[32,512]{1,0:T(8,128)(2,1)S(1)}, bf16[32,512]{1,0:T(8,128)(2,1)}, u32[]{:S(2)}) %copy-start.2) | copy-done | bytes 32792
  9.5 6.0 %ray_sums_1.1 = (f32[32,1152]{1,0:T(8,128)S(1)}, f32[32,1152]{1,0:T(8,128)S(1)}, f32[32,1152]{1,0:T(8,128)S(1)}, f32[32,1152]{1,0:T(8,128)S(1)}, f32[8,128,4096]{2,1,0:T(8,128)S(1)}) custom-call(bf16[32,512]{1,0:T(8,128)(2,1)S(1)} %copy-done.2, f32[8,128,4096]{2,1,0:T(8,128)} %refs_1_.6), custom_call_target="tpu_custom_call" | custom-call | flops 75497472 | bytes 9437184 | tf_op jit(solution)/shard_map/ray_sums_1/pallas_call | solution.py:186
  15.5 1.7 %collective-permute-start.6 = (f32[32,1152]{1,0:T(8,128)S(1)}, f32[32,1152]{1,0:T(8,128)S(1)}, u32[]{:S(2)}, u32[]{:S(2)}) collective-permute-start(f32[32,1152]{1,0:T(8,128)S(1)} %get-tuple-element.41), channel_id=1, source_target_pairs={{0,1},{1,0},{2,3},{3,2},{4,5},{5,4},{6,7},{7,6},{8,9},{9,8},{10,11... | collective-permute-start | bytes 442376 | tf_op jit(solution)/shard_map/ppermute | solution.py:438
  17.2 0.0 collective-permute-done
  17.2 0.2 collective-permute-start.7
  17.4 0.0 copy-done.4
  17.4 0.0 collective-permute-done.1
  17.4 0.3 collective-permute-start.8
  17.8 0.0 collective-permute-done.2
  17.8 1.7 %collective-permute-start.3 = (f32[2,32,1024]{2,1,0:T(8,128)S(1)}, f32[2,32,1024]{2,1,0:T(8,128)S(1)}, u32[]{:S(2)}, u32[]{:S(2)}) collective-permute-start(f32[2,32,1024]{2,1,0:T(8,128)S(1)} %pad_maximum_fusion.1.refs_2_), channel_id=1, source_target_pairs={{0,4},{2,6},{4,0},{6,2},{8,12},{10,14},{12,8},{14,10},{16,20},{18,... | collective-permute-start | bytes 786440 | tf_op jit(solution)/shard_map/ppermute | solution.py:430
  19.5 2.7 %collective-permute-done.6 = f32[32,1152]{1,0:T(8,128)S(1)} collective-permute-done((f32[32,1152]{1,0:T(8,128)S(1)}, f32[32,1152]{1,0:T(8,128)S(1)}, u32[]{:S(2)}, u32[]{:S(2)}) %collective-permute-start.6) | collective-permute-done | bytes 147488 | tf_op jit(solution)/shard_map/ppermute | solution.py:438
  22.2 0.0 collective-permute-done.7
  22.2 2.1 %collective-permute-done.8 = f32[32,1152]{1,0:T(8,128)S(1)} collective-permute-done((f32[32,1152]{1,0:T(8,128)S(1)}, f32[32,1152]{1,0:T(8,128)S(1)}, u32[]{:S(2)}, u32[]{:S(2)}) %collective-permute-start.8) | collective-permute-done | bytes 147488 | tf_op jit(solution)/shard_map/ppermute | solution.py:438
  24.4 1.9 %collective-permute-start.9 = (f32[2,32,1152]{2,1,0:T(8,128)S(1)}, f32[2,32,1152]{2,1,0:T(8,128)S(1)}, u32[]{:S(2)}, u32[]{:S(2)}) collective-permute-start(f32[2,32,1152]{2,1,0:T(8,128)S(1)} %pad_maximum_fusion.refs_8_), channel_id=1, source_target_pairs={{0,4},{2,6},{4,0},{6,2},{8,12},{10,14},{12,8},{14,10},{16,20},{18,... | collective-permute-start | bytes 884744 | tf_op jit(solution)/shard_map/ppermute | solution.py:430
  26.3 0.0 collective-permute-done.3.refs_3_
  26.3 1.7 %collective-permute-start.4 = (f32[2,32,1024]{2,1,0:T(8,128)S(1)}, f32[2,32,1024]{2,1,0:T(8,128)S(1)}, u32[]{:S(2)}, u32[]{:S(2)}) collective-permute-start(f32[2,32,1024]{2,1,0:T(8,128)S(1)} %collective-permute-done.3.refs_3_), channel_id=1, source_target_pairs={{0,8},{2,10},{4,28},{6,30},{8,16},{10,18},{12,4},{14,6},{16,24},{1... | collective-permute-start | bytes 786440 | tf_op jit(solution)/shard_map/ppermute | solution.py:430
  28.0 6.0 %collective-permute-done.9.refs_9_ = f32[2,32,1152]{2,1,0:T(8,128)S(1)} collective-permute-done((f32[2,32,1152]{2,1,0:T(8,128)S(1)}, f32[2,32,1152]{2,1,0:T(8,128)S(1)}, u32[]{:S(2)}, u32[]{:S(2)}) %collective-permute-start.9) | collective-permute-done | bytes 294944 | tf_op jit(solution)/shard_map/ppermute | solution.py:430
  34.0 1.8 %collective-permute-start.10 = (f32[2,32,1152]{2,1,0:T(8,128)S(1)}, f32[2,32,1152]{2,1,0:T(8,128)S(1)}, u32[]{:S(2)}, u32[]{:S(2)}) collective-permute-start(f32[2,32,1152]{2,1,0:T(8,128)S(1)} %collective-permute-done.9.refs_9_), channel_id=1, source_target_pairs={{0,8},{2,10},{4,0},{6,2},{8,16},{10,18},{12,4},{14,6},{16,24},{18,... | collective-permute-start | bytes 884744 | tf_op jit(solution)/shard_map/ppermute | solution.py:430
  35.8 0.8 %collective-permute-done.4.refs_4_ = f32[2,32,1024]{2,1,0:T(8,128)S(1)} collective-permute-done((f32[2,32,1024]{2,1,0:T(8,128)S(1)}, f32[2,32,1024]{2,1,0:T(8,128)S(1)}, u32[]{:S(2)}, u32[]{:S(2)}) %collective-permute-start.4) | collective-permute-done | bytes 262176 | tf_op jit(solution)/shard_map/ppermute | solution.py:430
  36.6 0.0 collective-permute-done.5.refs_6_.refs_12_
  36.6 0.0 copy-done.1
  36.6 0.0 copy-done.3
  36.6 2.1 %residual_0.1 = (f32[4,32,896]{2,1,0:T(8,128)S(1)}, f32[4,32,896]{2,1,0:T(8,128)S(1)}, f32[2,32,896]{2,1,0:T(8,128)S(1)}, f32[2,32,896]{2,1,0:T(8,128)S(1)}, f32...) custom-call(s32[64]{0:T(128)S(1)} %copy-done.3, ...), custom_call_target="tpu_custom_call" | custom-call | flops 528482304 | bytes 3211264 | tf_op jit(solution)/shard_map/residual_0/pallas_call | solution.py:329
  38.7 0.1 collective-permute-start.17
  38.8 3.9 %collective-permute-done.10.refs_10_ = f32[2,32,1152]{2,1,0:T(8,128)S(1)} collective-permute-done((f32[2,32,1152]{2,1,0:T(8,128)S(1)}, f32[2,32,1152]{2,1,0:T(8,128)S(1)}, u32[]{:S(2)}, u32[]{:S(2)}) %collective-permute-start.10) | collective-permute-done | bytes 294944 | tf_op jit(solution)/shard_map/ppermute | solution.py:430
  42.7 2.2 %residual_1.1 = (f32[4,32,2048]{2,1,0:T(8,128)S(1)}, f32[4,32,2048]{2,1,0:T(8,128)S(1)}, f32[2,32,1152]{2,1,0:T(8,128)S(1)}, f32[2,32,1152]{2,1,0:T(8,128)S(1)},...) custom-call(s32[64]{0:T(128)S(1)} %copy-done.3, f32[64,256]{1,0:T(8,128)S(1)} %copy-done.1, ...), custom_call_target="tpu_custom_call" | custom-call | flops 679477248 | bytes 4128768 | tf_op jit(solution)/shard_map/residual_1/pallas_call | solution.py:329
  44.9 3.8 %collective-permute-start.11 = (f32[2,32,1152]{2,1,0:T(8,128)S(1)}, f32[2,32,1152]{2,1,0:T(8,128)S(1)}, u32[]{:S(2)}, u32[]{:S(2)}) collective-permute-start(f32[2,32,1152]{2,1,0:T(8,128)S(1)} %get-tuple-element.49), channel_id=1, source_target_pairs={{0,24},{2,26},{4,12},{6,14},{8,0},{10,2},{12,20},{14,22},{16,8},{1... | collective-permute-start | bytes 884744 | tf_op jit(solution)/shard_map/ppermute | solution.py:430
  48.7 0.0 collective-permute-done.17
  48.8 0.1 collective-permute-start.18
  48.8 0.1 collective-permute-start.16
  48.9 5.1 %collective-permute-done.11 = f32[2,32,1152]{2,1,0:T(8,128)S(1)} collective-permute-done((f32[2,32,1152]{2,1,0:T(8,128)S(1)}, f32[2,32,1152]{2,1,0:T(8,128)S(1)}, u32[]{:S(2)}, u32[]{:S(2)}) %collective-permute-start.11) | collective-permute-done | bytes 294944 | tf_op jit(solution)/shard_map/ppermute | solution.py:430
  54.1 2.3 %collective-permute-start.12 = (f32[2,32,1152]{2,1,0:T(8,128)S(1)}, f32[2,32,1152]{2,1,0:T(8,128)S(1)}, u32[]{:S(2)}, u32[]{:S(2)}) collective-permute-start(f32[2,32,1152]{2,1,0:T(8,128)S(1)} %add.48), channel_id=1, source_target_pairs={{0,4},{2,6},{4,0},{6,2},{8,12},{10,14},{12,8},{14,10},{16,20},{18,... | collective-permute-start | bytes 884744 | tf_op jit(solution)/shard_map/ppermute | solution.py:430
  56.4 0.0 collective-permute-done.18
  56.4 1.6 %collective-permute-start.21 = (f32[32,896]{1,0:T(8,128)S(1)}, f32[32,896]{1,0:T(8,128)S(1)}, u32[]{:S(2)}, u32[]{:S(2)}) collective-permute-start(f32[32,896]{1,0:T(8,128)S(1)} %get-tuple-element.58.refs_4_), channel_id=1, source_target_pairs={{0,1},{1,0},{2,3},{3,2},{4,5},{5,4},{6,7},{7,6},{8,9},{9,8},{10,11... | collective-permute-start | bytes 344072 | tf_op jit(solution)/shard_map/ppermute | solution.py:438
  58.0 0.0 collective-permute-start.20
  58.0 3.5 %collective-permute-done.12 = f32[2,32,1152]{2,1,0:T(8,128)S(1)} collective-permute-done((f32[2,32,1152]{2,1,0:T(8,128)S(1)}, f32[2,32,1152]{2,1,0:T(8,128)S(1)}, u32[]{:S(2)}, u32[]{:S(2)}) %collective-permute-start.12) | collective-permute-done | bytes 294944 | tf_op jit(solution)/shard_map/ppermute | solution.py:430
  61.6 1.6 %collective-permute-start.15 = (f32[32,1152]{1,0:T(8,128)S(1)}, f32[32,1152]{1,0:T(8,128)S(1)}, u32[]{:S(2)}, u32[]{:S(2)}) collective-permute-start(f32[32,1152]{1,0:T(8,128)S(1)} %get-tuple-element.56.refs_4_), channel_id=1, source_target_pairs={{0,1},{1,0},{2,3},{3,2},{4,5},{5,4},{6,7},{7,6},{8,9},{9,8},{10,11... | collective-permute-start | bytes 442376 | tf_op jit(solution)/shard_map/ppermute | solution.py:438
  63.1 0.0 collective-permute-start.14
  63.2 0.0 collective-permute-done.21.refs_3_
  63.2 0.6 collective-permute-start.13
  63.8 0.2 collective-permute-done.20.refs_2_
  64.0 0.0 collective-permute-start.19
  64.0 1.3 %collective-permute-done.19.refs_1_ = f32[32,896]{1,0:T(8,128)S(1)} collective-permute-done((f32[32,896]{1,0:T(8,128)S(1)}, f32[32,896]{1,0:T(8,128)S(1)}, u32[]{:S(2)}, u32[]{:S(2)}) %collective-permute-start.19) | collective-permute-done | bytes 114720 | tf_op jit(solution)/shard_map/ppermute | solution.py:438
  65.3 3.3 %update_0.1.refs_8_ = f32[8,128,4096]{2,1,0:T(8,128)} custom-call(bf16[4,256,128]{2,1,0:T(8,128)(2,1)S(1)} %get-tuple-element.46.refs_0_, f32[32,896]{1,0:T(8,128)S(1)} %collective-permute-done.19.refs_1_, f32[32,896]{1,0:T(8,128)S(1)} %collective-permute-done.20.refs_2_, f32[32,896]{1,0:T(8,128)S(1)} %collective-permute-done.21.refs_3_, ...), custom_call_target="tpu_custom_call" | custom-call | flops 176160768 | bytes 7340032 | tf_op jit(solution)/shard_map/update_0/pallas_call | solution.py:404
  68.6 0.0 collective-permute-done.15.refs_3_
  68.6 0.6 collective-permute-done.14.refs_2_
  69.3 0.0 collective-permute-done.13.refs_1_
  69.3 0.0 collective-permute-done.16.refs_7_
  69.3 4.7 %update_1.1 = (f32[8,128,4096]{2,1,0:T(8,128)}, f32[4,32,4096]{2,1,0:T(8,128)}) custom-call(bf16[4,256,128]{2,1,0:T(8,128)(2,1)S(1)} %get-tuple-element.46.refs_0_, f32[32,1152]{1,0:T(8,128)S(1)} %collective-permute-done.13.refs_1_, f32[32,1152]{1,0:T(8,128)S(1)} %collective-permute-done.14.refs_2_, ...), custom_call_target="tpu_custom_call", output_to_operand_aliasing={{0}: (8, {})} | custom-call | flops 226492416 | bytes 9437184 | tf_op jit(solution)/shard_map/update_1/pallas_call | solution.py:404
  (10 shorter events, 0.2 us)
Async XLA Ops:
  0.6 36.0 %copy-start.1 = (f32[64,256]{1,0:T(8,128)S(1)}, f32[64,256]{1,0:T(8,128)}, u32[]{:S(2)}) copy-start(f32[64,256]{1,0:T(8,128)} %refs_1_.7) | copy-start | bytes 196612
  0.6 36.0 %copy-start.3 = (s32[64]{0:T(128)S(1)}, s32[64]{0:T(128)}, u32[]{:S(2)}) copy-start(s32[64]{0:T(128)} %refs_0_.5) | copy-start | bytes 772
  0.7 7.6 %copy-start = (bf16[4,32,4096]{2,1,0:T(8,128)(2,1)S(1)}, bf16[4,32,4096]{2,1,0:T(8,128)(2,1)}, u32[]{:S(2)}) copy-start(bf16[4,32,4096]{2,1,0:T(8,128)(2,1)} %refs_11_.1) | copy-start | bytes 3145732
  5.0 12.4 %copy-start.4 = (f32[32,1024]{1,0:T(8,128)S(1)}, f32[32,1024]{1,0:T(8,128)}, u32[]{:S(2)}) copy-start(f32[32,1024]{1,0:T(8,128)} %get-tuple-element.29) | copy-start | bytes 393220
  5.0 12.2 %collective-permute-start = (f32[32,1024]{1,0:T(8,128)}, f32[32,1024]{1,0:T(8,128)S(1)}, u32[]{:S(2)}, u32[]{:S(2)}) collective-permute-start(f32[32,1024]{1,0:T(8,128)} %get-tuple-element.30), channel_id=1, source_target_pairs={{0,1},{1,0},{2,3},{3,2},{4,5},{5,4},{6,7},{7,6},{8,9},{9,8},{10,11... | collective-permute-start | bytes 393224 | tf_op jit(solution)/shard_map/ppermute | solution.py:438
  8.1 9.4 %collective-permute-start.1 = (f32[32,1024]{1,0:T(8,128)}, f32[32,1024]{1,0:T(8,128)S(1)}, u32[]{:S(2)}, u32[]{:S(2)}) collective-permute-start(f32[32,1024]{1,0:T(8,128)} %get-tuple-element.31), channel_id=1, source_target_pairs={{0,2},{1,3},{2,0},{3,1},{4,6},{5,7},{6,4},{7,5},{8,10},{9,11},{10,... | collective-permute-start | bytes 393224 | tf_op jit(solution)/shard_map/ppermute | solution.py:438
  8.1 9.7 %collective-permute-start.2 = (f32[32,1024]{1,0:T(8,128)}, f32[32,1024]{1,0:T(8,128)S(1)}, u32[]{:S(2)}, u32[]{:S(2)}) collective-permute-start(f32[32,1024]{1,0:T(8,128)} %get-tuple-element.32), channel_id=1, source_target_pairs={{0,3},{1,2},{2,1},{3,0},{4,7},{5,6},{6,5},{7,4},{8,11},{9,10},{10,... | collective-permute-start | bytes 393224 | tf_op jit(solution)/shard_map/ppermute | solution.py:438
  8.4 28.2 %collective-permute-start.5 = (f32[4,32,2048]{2,1,0:T(8,128)S(1)}, f32[4,32,2048]{2,1,0:T(8,128)S(1)}, u32[]{:S(2)}, u32[]{:S(2)}) collective-permute-start(f32[4,32,2048]{2,1,0:T(8,128)S(1)} %dynamic-slice_convert_fusion), channel_id=1, source_target_pairs={{0,2},{2,0},{4,6},{6,4},{8,10},{10,8},{12,14},{14,12},{16,18},{18,... | collective-permute-start | bytes 3145736 | tf_op jit(solution)/shard_map/ppermute | solution.py:430
  8.7 0.8 %copy-start.2 = (bf16[32,512]{1,0:T(8,128)(2,1)S(1)}, bf16[32,512]{1,0:T(8,128)(2,1)}, u32[]{:S(2)}) copy-start(bf16[32,512]{1,0:T(8,128)(2,1)} %get-tuple-element.39.refs_0_) | copy-start | bytes 98308
  15.5 6.7 %collective-permute-start.6 = (f32[32,1152]{1,0:T(8,128)S(1)}, f32[32,1152]{1,0:T(8,128)S(1)}, u32[]{:S(2)}, u32[]{:S(2)}) collective-permute-start(f32[32,1152]{1,0:T(8,128)S(1)} %get-tuple-element.41), channel_id=1, source_target_pairs={{0,1},{1,0},{2,3},{3,2},{4,5},{5,4},{6,7},{7,6},{8,9},{9,8},{10,11... | collective-permute-start | bytes 442376 | tf_op jit(solution)/shard_map/ppermute | solution.py:438
  17.2 5.0 %collective-permute-start.7 = (f32[32,1152]{1,0:T(8,128)S(1)}, f32[32,1152]{1,0:T(8,128)S(1)}, u32[]{:S(2)}, u32[]{:S(2)}) collective-permute-start(f32[32,1152]{1,0:T(8,128)S(1)} %get-tuple-element.42), channel_id=1, source_target_pairs={{0,2},{1,3},{2,0},{3,1},{4,6},{5,7},{6,4},{7,5},{8,10},{9,11},{10,... | collective-permute-start | bytes 442376 | tf_op jit(solution)/shard_map/ppermute | solution.py:438
  17.4 6.9 %collective-permute-start.8 = (f32[32,1152]{1,0:T(8,128)S(1)}, f32[32,1152]{1,0:T(8,128)S(1)}, u32[]{:S(2)}, u32[]{:S(2)}) collective-permute-start(f32[32,1152]{1,0:T(8,128)S(1)} %get-tuple-element.43), channel_id=1, source_target_pairs={{0,3},{1,2},{2,1},{3,0},{4,7},{5,6},{6,5},{7,4},{8,11},{9,10},{10,... | collective-permute-start | bytes 442376 | tf_op jit(solution)/shard_map/ppermute | solution.py:438
  17.8 8.5 %collective-permute-start.3 = (f32[2,32,1024]{2,1,0:T(8,128)S(1)}, f32[2,32,1024]{2,1,0:T(8,128)S(1)}, u32[]{:S(2)}, u32[]{:S(2)}) collective-permute-start(f32[2,32,1024]{2,1,0:T(8,128)S(1)} %pad_maximum_fusion.1.refs_2_), channel_id=1, source_target_pairs={{0,4},{2,6},{4,0},{6,2},{8,12},{10,14},{12,8},{14,10},{16,20},{18,... | collective-permute-start | bytes 786440 | tf_op jit(solution)/shard_map/ppermute | solution.py:430
  24.4 9.6 %collective-permute-start.9 = (f32[2,32,1152]{2,1,0:T(8,128)S(1)}, f32[2,32,1152]{2,1,0:T(8,128)S(1)}, u32[]{:S(2)}, u32[]{:S(2)}) collective-permute-start(f32[2,32,1152]{2,1,0:T(8,128)S(1)} %pad_maximum_fusion.refs_8_), channel_id=1, source_target_pairs={{0,4},{2,6},{4,0},{6,2},{8,12},{10,14},{12,8},{14,10},{16,20},{18,... | collective-permute-start | bytes 884744 | tf_op jit(solution)/shard_map/ppermute | solution.py:430
  26.3 10.3 %collective-permute-start.4 = (f32[2,32,1024]{2,1,0:T(8,128)S(1)}, f32[2,32,1024]{2,1,0:T(8,128)S(1)}, u32[]{:S(2)}, u32[]{:S(2)}) collective-permute-start(f32[2,32,1024]{2,1,0:T(8,128)S(1)} %collective-permute-done.3.refs_3_), channel_id=1, source_target_pairs={{0,8},{2,10},{4,28},{6,30},{8,16},{10,18},{12,4},{14,6},{16,24},{1... | collective-permute-start | bytes 786440 | tf_op jit(solution)/shard_map/ppermute | solution.py:430
  34.0 8.7 %collective-permute-start.10 = (f32[2,32,1152]{2,1,0:T(8,128)S(1)}, f32[2,32,1152]{2,1,0:T(8,128)S(1)}, u32[]{:S(2)}, u32[]{:S(2)}) collective-permute-start(f32[2,32,1152]{2,1,0:T(8,128)S(1)} %collective-permute-done.9.refs_9_), channel_id=1, source_target_pairs={{0,8},{2,10},{4,0},{6,2},{8,16},{10,18},{12,4},{14,6},{16,24},{18,... | collective-permute-start | bytes 884744 | tf_op jit(solution)/shard_map/ppermute | solution.py:430
  38.7 10.1 %collective-permute-start.17 = (f32[2,32,896]{2,1,0:T(8,128)S(1)}, f32[2,32,896]{2,1,0:T(8,128)S(1)}, u32[]{:S(2)}, u32[]{:S(2)}) collective-permute-start(f32[2,32,896]{2,1,0:T(8,128)S(1)} %get-tuple-element.55), channel_id=1, source_target_pairs={{0,4},{2,6},{4,12},{6,14},{8,0},{10,2},{12,20},{14,22},{16,8},{18,... | collective-permute-start | bytes 688136 | tf_op jit(solution)/shard_map/ppermute | solution.py:430
  44.9 9.1 %collective-permute-start.11 = (f32[2,32,1152]{2,1,0:T(8,128)S(1)}, f32[2,32,1152]{2,1,0:T(8,128)S(1)}, u32[]{:S(2)}, u32[]{:S(2)}) collective-permute-start(f32[2,32,1152]{2,1,0:T(8,128)S(1)} %get-tuple-element.49), channel_id=1, source_target_pairs={{0,24},{2,26},{4,12},{6,14},{8,0},{10,2},{12,20},{14,22},{16,8},{1... | collective-permute-start | bytes 884744 | tf_op jit(solution)/shard_map/ppermute | solution.py:430
  48.8 7.6 %collective-permute-start.18 = (f32[2,32,896]{2,1,0:T(8,128)S(1)}, f32[2,32,896]{2,1,0:T(8,128)S(1)}, u32[]{:S(2)}, u32[]{:S(2)}) collective-permute-start(f32[2,32,896]{2,1,0:T(8,128)S(1)} %add.53), channel_id=1, source_target_pairs={{0,4},{2,6},{4,0},{6,2},{8,12},{10,14},{12,8},{14,10},{16,20},{18,... | collective-permute-start | bytes 688136 | tf_op jit(solution)/shard_map/ppermute | solution.py:430
  48.8 20.4 %collective-permute-start.16 = (f32[4,32,2048]{2,1,0:T(8,128)S(1)}, f32[4,32,2048]{2,1,0:T(8,128)S(1)}, u32[]{:S(2)}, u32[]{:S(2)}) collective-permute-start(f32[4,32,2048]{2,1,0:T(8,128)S(1)} %get-tuple-element.52), channel_id=1, source_target_pairs={{0,2},{2,0},{4,6},{6,4},{8,10},{10,8},{12,14},{14,12},{16,18},{18,... | collective-permute-start | bytes 3145736 | tf_op jit(solution)/shard_map/ppermute | solution.py:430
  54.1 7.5 %collective-permute-start.12 = (f32[2,32,1152]{2,1,0:T(8,128)S(1)}, f32[2,32,1152]{2,1,0:T(8,128)S(1)}, u32[]{:S(2)}, u32[]{:S(2)}) collective-permute-start(f32[2,32,1152]{2,1,0:T(8,128)S(1)} %add.48), channel_id=1, source_target_pairs={{0,4},{2,6},{4,0},{6,2},{8,12},{10,14},{12,8},{14,10},{16,20},{18,... | collective-permute-start | bytes 884744 | tf_op jit(solution)/shard_map/ppermute | solution.py:430
  56.4 6.8 %collective-permute-start.21 = (f32[32,896]{1,0:T(8,128)S(1)}, f32[32,896]{1,0:T(8,128)S(1)}, u32[]{:S(2)}, u32[]{:S(2)}) collective-permute-start(f32[32,896]{1,0:T(8,128)S(1)} %get-tuple-element.58.refs_4_), channel_id=1, source_target_pairs={{0,1},{1,0},{2,3},{3,2},{4,5},{5,4},{6,7},{7,6},{8,9},{9,8},{10,11... | collective-permute-start | bytes 344072 | tf_op jit(solution)/shard_map/ppermute | solution.py:438
  58.0 6.0 %collective-permute-start.20 = (f32[32,896]{1,0:T(8,128)S(1)}, f32[32,896]{1,0:T(8,128)S(1)}, u32[]{:S(2)}, u32[]{:S(2)}) collective-permute-start(f32[32,896]{1,0:T(8,128)S(1)} %get-tuple-element.59), channel_id=1, source_target_pairs={{0,3},{1,2},{2,1},{3,0},{4,7},{5,6},{6,5},{7,4},{8,11},{9,10},{10,... | collective-permute-start | bytes 344072 | tf_op jit(solution)/shard_map/ppermute | solution.py:438
  61.6 7.1 %collective-permute-start.15 = (f32[32,1152]{1,0:T(8,128)S(1)}, f32[32,1152]{1,0:T(8,128)S(1)}, u32[]{:S(2)}, u32[]{:S(2)}) collective-permute-start(f32[32,1152]{1,0:T(8,128)S(1)} %get-tuple-element.56.refs_4_), channel_id=1, source_target_pairs={{0,1},{1,0},{2,3},{3,2},{4,5},{5,4},{6,7},{7,6},{8,9},{9,8},{10,11... | collective-permute-start | bytes 442376 | tf_op jit(solution)/shard_map/ppermute | solution.py:438
  63.1 6.1 %collective-permute-start.14 = (f32[32,1152]{1,0:T(8,128)S(1)}, f32[32,1152]{1,0:T(8,128)S(1)}, u32[]{:S(2)}, u32[]{:S(2)}) collective-permute-start(f32[32,1152]{1,0:T(8,128)S(1)} %get-tuple-element.57), channel_id=1, source_target_pairs={{0,3},{1,2},{2,1},{3,0},{4,7},{5,6},{6,5},{7,4},{8,11},{9,10},{10,... | collective-permute-start | bytes 442376 | tf_op jit(solution)/shard_map/ppermute | solution.py:438
  63.2 6.1 %collective-permute-start.13 = (f32[32,1152]{1,0:T(8,128)S(1)}, f32[32,1152]{1,0:T(8,128)S(1)}, u32[]{:S(2)}, u32[]{:S(2)}) collective-permute-start(f32[32,1152]{1,0:T(8,128)S(1)} %get-tuple-element.57), channel_id=1, source_target_pairs={{0,2},{1,3},{2,0},{3,1},{4,6},{5,7},{6,4},{7,5},{8,10},{9,11},{10,... | collective-permute-start | bytes 442376 | tf_op jit(solution)/shard_map/ppermute | solution.py:438
  64.0 1.3 %collective-permute-start.19 = (f32[32,896]{1,0:T(8,128)S(1)}, f32[32,896]{1,0:T(8,128)S(1)}, u32[]{:S(2)}, u32[]{:S(2)}) collective-permute-start(f32[32,896]{1,0:T(8,128)S(1)} %get-tuple-element.59), channel_id=1, source_target_pairs={{0,2},{1,3},{2,0},{3,1},{4,6},{5,7},{6,4},{7,5},{8,10},{9,11},{10,... | collective-permute-start | bytes 344072 | tf_op jit(solution)/shard_map/ppermute | solution.py:438

commit v2 on v1

--- a/solution.py
+++ b/solution.py
@@ -88,7 +88,7 @@
             yield h, zp, slice(zp * zb, (zp + 1) * zb), start
 
 
-def rays_kernel(dims, first, last, half, offset, width, *refs):
+def rays_kernel(dims, first, half, offset, width, *refs):
     per, groups, zb, cells = dims
     count = groups * SUBLANES
     if first:
@@ -98,12 +98,10 @@
     outs, refs = refs[:2 * groups], refs[2 * groups:]
     if first:
         left_ref, buf, sems, table_buf, order_buf, start_buf, len_buf, rows_ref, small_sems = refs
-    elif last:
-        kept_ref, sems, rest_sems = refs
     else:
         buf, sems = refs
     zdev = vol_ref.shape[0]
-    copies, rest = [], []
+    copies = []
     if first:
         small = [
             pltpu.make_async_copy(source, to, small_sems.at[i])
@@ -114,15 +112,9 @@
         for copy in small:
             copy.start()
     for h, zp, slices, start in volume_pieces(dims, zdev, half, offset):
-        columns = pl.ds(start, width)
-        to = kept_ref.at[slices, :, columns] if last else buf.at[h, slices]
-        copies.append((h, zp, start, pltpu.make_async_copy(vol_ref.at[slices, :, columns], to, sems.at[h, zp])))
+        source = vol_ref.at[slices, :, pl.ds(start, width)]
+        copies.append((h, zp, pltpu.make_async_copy(source, buf.at[h, slices], sems.at[h, zp])))
         copies[-1][-1].start()
-    if last:
-        for h in range(2):
-            columns = pl.ds(h * half, offset)
-            rest.append(pltpu.make_async_copy(vol_ref.at[:, :, columns], kept_ref.at[:, :, columns], rest_sems.at[h]))
-            rest[h].start()
     if first:
         small[0].wait()
         small[1].wait()
@@ -141,50 +133,41 @@
                 outs[h * groups + d][:, width:] = foot
     else:
         left = given_ref[...]
-    for h, zp, start, copy in copies:
+    for h, zp, copy in copies:
         copy.wait()
         for at, size in tiles(width):
-            parts = []
-            for z in range(zb):
-                if last:
-                    cells_at = kept_ref[zp * zb + z, :, pl.ds(pl.multiple_of(start + at, LANES), size)]
-                else:
-                    cells_at = buf[h, zp * zb + z, :, at:at + size]
-                parts.append(split(cells_at))
+            parts = [split(buf[h, zp * zb + z, :, at:at + size]) for z in range(zb)]
             product = dot(left, jnp.concatenate([p[0] for p in parts] + [p[1] for p in parts], axis=0))
             sums = product[:count] + product[count:]
             for d in range(groups):
                 outs[h * groups + d][zp * SUBLANES:(zp + 1) * SUBLANES, at:at + size] = (
                     sums[d * SUBLANES:(d + 1) * SUBLANES]
                 )
-    for copy in rest:
-        copy.wait()
 
 
 def ray_sums(dims, chunk, offset, width, given, small, table, volume):
     per, groups, zb, cells = dims
     zdev, _, total = volume.shape
-    first, last = chunk == 0, chunk == CHUNKS - 1
+    first = chunk == 0
     count, all_cells = groups * SUBLANES, table.shape[1]
     out = jax.ShapeDtypeStruct((zdev * per, width + (LANES if first else 0)), F32)
     left = jax.ShapeDtypeStruct((2 * count, 2 * zb * cells), BF16)
-    assert zb * cells == all_cells and not (first and last)
+    assert zb * cells == all_cells
     sems = pltpu.SemaphoreType.DMA((2, zdev // zb))
     shapes = [out] * (2 * groups)
     scratch = [pltpu.VMEM((2, zdev, cells, width), F32), sems]
-    args, specs, limit = [given, volume], [IN_VMEM, ANYWHERE], 50
+    args, specs, limit = [given, volume], [IN_VMEM, ANYWHERE], 40
     if first:
         scratch += [pltpu.VMEM(table.shape, F32)] + [pltpu.SMEM(a.shape, a.dtype) for a in small]
         scratch += [pltpu.VMEM((count, all_cells), F32), pltpu.SemaphoreType.DMA((4,))]
         args, specs, limit = [*small, table, volume], [ANYWHERE] * 5, 58
         shapes += [left]
-    if last:
-        scratch = [sems, pltpu.SemaphoreType.DMA((2,))]
-        shapes += [jax.ShapeDtypeStruct(volume.shape, F32)]
-        limit = 28
+    if not first:
+        scratch = [sems]
+        shapes += [jax.ShapeDtypeStruct((2, zdev, cells, width), F32)]
     size = zdev * cells * width * 2
     return pl.pallas_call(
-        functools.partial(rays_kernel, dims, first, last, total // 2, offset, width),
+        functools.partial(rays_kernel, dims, first, total // 2, offset, width),
         in_specs=specs,
         out_specs=[IN_VMEM] * len(shapes),
         out_shape=shapes,
@@ -244,8 +227,9 @@
 def residual_kernel(dims, first, last, half, rdev, zdev, offset, width, *refs):
     per, groups, zb, cells = dims
     block = zdev * per
+    load = None
     if first or last:
-        order_ref, table_ref, *refs = refs
+        order_ref, table_ref, vol_ref, *refs, sem = refs
     if last:
         foot_ref, *refs = refs
     if not first:
@@ -253,6 +237,12 @@
     sums_refs, (mine_ref, theirs_ref), refs = refs[:3], refs[3:5], refs[5:]
     if not first:
         mine_before, sent_before, *refs = refs
+    if first or last:
+        kept_ref, *refs = refs
+        start = lax.rem(lax.axis_index("slab") + (0 if first else 1), 2) * half
+        columns = pl.ds(pl.multiple_of(start, LANES), kept_ref.shape[2])
+        load = pltpu.make_async_copy(vol_ref.at[:, :, columns], kept_ref, sem)
+        load.start()
     mine_out, sent_out, *refs = refs
     if not first:
         mine_out[:, :, :offset] = mine_before[...]
@@ -295,10 +285,13 @@
                 ref[j, :, columns] = given[(2 * i + j) * block:(2 * i + j + 1) * block]
     if last:
         update_weights(dims, zdev, rdev, foot_ref[...], order_ref, table_ref, refs[1], refs[0])
-
-
-def residual_step(dims, zdev, chunk, offset, width, mats, before, order, table, sums, measured, theirs):
-    per, groups, zb, cells = dims
+    if load is not None:
+        load.wait()
+
+
+def residual_step(dims, chunk, offset, width, load_width, mats, before, order, table, volume, sums, measured, theirs):
+    per, groups, zb, cells = dims
+    zdev = volume.shape[0]
     _, rdev, total = measured.shape
     first = chunk == 0
     block = zdev * per
@@ -310,7 +303,8 @@
     shapes = [piece, piece, given, given, given]
     args, specs, scratch = [], [], []
     if first or last:
-        args, specs = [order, table], [IN_SMEM, IN_VMEM]
+        args, specs = [order, table, volume], [IN_SMEM, IN_VMEM, ANYWHERE]
+        shapes = [jax.ShapeDtypeStruct((zdev, cells, load_width), F32)] + shapes
     if last:
         depth = -(-3 * groups * SUBLANES // LANES) * LANES
         shapes.append(jax.ShapeDtypeStruct((zdev // zb, zb * cells, depth), BF16))
@@ -324,6 +318,8 @@
     else:
         args += mats[:5]
         specs += [IN_VMEM] * 5
+    if first or last:
+        scratch.append(pltpu.SemaphoreType.DMA)
     args += [*sums, measured, theirs, *before]
     specs += [IN_VMEM] * (5 + len(before))
     return pl.pallas_call(
@@ -332,7 +328,7 @@
         out_specs=[IN_VMEM] * len(shapes),
         out_shape=shapes,
         scratch_shapes=scratch,
-        compiler_params=pltpu.CompilerParams(vmem_limit_bytes=16 * MIB),
+        compiler_params=pltpu.CompilerParams(vmem_limit_bytes=30 * MIB),
         cost_estimate=pl.CostEstimate(
             flops=12 * count * rows * width, bytes_accessed=8 * width * (count + rows), transcendentals=0
         ),
@@ -343,9 +339,13 @@
 def update_kernel(dims, first, last, half, offset, width, *refs):
     per, groups, zb, cells = dims
     count = groups * SUBLANES
-    left_ref, backs, vol_ref, refs = refs[0], refs[1:1 + 2 * groups], refs[1 + 2 * groups], refs[2 + 2 * groups:]
+    left_ref, backs, refs = refs[0], refs[1:1 + 2 * groups], refs[1 + 2 * groups:]
     backs = [backs[-1], *backs[groups:-1], *backs[:groups]]
-    zdev, depth = vol_ref.shape[0], left_ref.shape[2]
+    if first:
+        vols, refs = refs[:2], refs[2:]
+    else:
+        vols, refs = [refs[0].at[0], refs[0].at[1]], refs[1:]
+    zdev, depth = vols[0].shape[0], left_ref.shape[2]
     if last:
         pieces, refs = refs[:2], refs[2:]
     if not first:
@@ -361,14 +361,13 @@
         left = left_ref[zp]
         for at, size in tiles(width):
             piece = slice(at, at + size)
-            source = pl.ds(pl.multiple_of(start + at, LANES), size)
             back = jnp.concatenate([backs[h * groups + d][rows, piece] for d in range(groups)], axis=0)
             high, low = split(back)
             pad = jnp.zeros((depth - 3 * count, size), BF16)
             change = dot(left, jnp.concatenate([high, low, high, pad], axis=0))
             for z in range(zb):
                 buf[h, zp * zb + z, :, piece] = (
-                    vol_ref[zp * zb + z, :, source] + change[z * cells:(z + 1) * cells]
+                    vols[h][zp * zb + z, :, piece] + change[z * cells:(z + 1) * cells]
                 )
         leaving.append(
             pltpu.make_async_copy(buf.at[h, slices], out_ref.at[slices, :, pl.ds(start, width)], sems.at[h, zp])
@@ -383,11 +382,11 @@
         copy.wait()
 
 
-def update_step(dims, chunk, offset, width, left, backs, pieces, volume, out):
+def update_step(dims, chunk, offset, width, left, backs, pieces, kept, volume, out):
     per, groups, zb, cells = dims
     zdev, _, total = volume.shape
     first, last = chunk == 0, chunk == CHUNKS - 1
-    args = [left, *backs[groups:], *backs[1:groups], backs[0], volume]
+    args = [left, *backs[groups:], *backs[1:groups], backs[0], *kept]
     shapes = [jax.ShapeDtypeStruct(volume.shape, F32)]
     scratch = [pltpu.VMEM((2, zdev, cells, width), F32), pltpu.SemaphoreType.DMA((2, zdev // zb))]
     if last:
@@ -422,7 +421,7 @@
     zb = SUBLANES // per
     dims = (per, groups, zb, cells)
     each = half // CHUNKS
-    widths = [each - LANES] + [each] * (CHUNKS - 2) + [each + LANES]
+    widths = [each - LANES] + [each + LANES]
     offsets = [sum(widths[:c]) for c in range(CHUNKS)]
 
     def along(value, to):
@@ -459,24 +458,28 @@
         lax.dynamic_slice_in_dim(measured, (1 - odd) * half, half, 2).astype(F32), lambda s: s ^ 1
     )
 
-    sums, left = [], None
+    sums, kept, left = [], [[] for _ in range(CHUNKS)], None
     for c in range(CHUNKS):
         parts = ray_sums(
             dims, c, offsets[c], widths[c], left, (order, foot_start, foot_len), table, volume
         )
         if c == 0:
             left = parts[2 * groups]
-        kept = parts[-1]
+        else:
+            kept[c].append(parts[2 * groups])
         parts = [spread(parts[h * groups + d], h, d) for h in range(2) for d in range(groups)]
+        if c:
+            parts, _ = lax.optimization_barrier((parts, sums[-1][0]))
         own = jnp.stack([sum(parts[:groups]), sum(parts[groups:])])
         near = along(own, facing)
         far = along(near, beyond(c))
         sums.append((own, near, far))
     pieces, given, mats = [], [], None
     for c in range(CHUNKS):
-        mine, sent, own, near, far, *rest = residual_step(
-            dims, zdev, c, offsets[c], widths[c], mats, pieces, order, table, sums[c], measured, theirs
+        loaded, mine, sent, own, near, far, *rest = residual_step(
+            dims, c, offsets[c], widths[c], widths[0], mats, pieces, order, table, volume, sums[c], measured, theirs
         )
+        kept[0].append(loaded)
         pieces = [mine, sent]
         mats = rest if c == 0 else mats
         left = rest[0]
@@ -487,7 +490,7 @@
     pieces = [mine, along(sent, lambda s: s ^ 1)]
     out = None
     for c in range(CHUNKS):
-        out, *res = update_step(dims, c, offsets[c], widths[c], left, given[c], pieces, kept, out)
+        out, *res = update_step(dims, c, offsets[c], widths[c], left, given[c], pieces, kept[c], volume, out)
     return out, res[0]
 
 

time: 74.2 us -> 74.3 us (level)
  waiting for transfers between devices: 26.3 us -> 24.9 us
  Pallas kernels: 22.6 us -> 24 us
    pallas_call x2, Pallas kernels: 4.28 us -> 7.49 us  [residual_step(): pl.pallas_call(functools.partial(residual_kernel, dims, first, last, tota...]
    pallas_call x2, Pallas kernels: 10.3 us -> 8.48 us  [ray_sums(): pl.pallas_call(functools.partial(rays_kernel, dims, first, total // 2, of...]
    ppermute x10, waiting for transfers between devices: 19.3 us -> 17.9 us  [along(): return lax.ppermute(value, 'slab', pairs)]
  transfers between devices with their start and end apart: 22 -> 22, of which waited for: 10 -> 10; matrix products, arithmetic and copies ran while one was open for 0% -> 0% of each run, Pallas kernels for 18% -> 20%
where the time goes in v2:
time: 74.3 us; the launch traced here: 73.9 us
  waiting for transfers between devices  24.9 us (34%)
  Pallas kernels  24 us (32%)
  starting transfers between devices  23.1 us (31%)
  between operations  0.79 us (1%)
  local copies, waits for them, and re-layouts  0.78 us (1%)
    ppermute x10, waiting for transfers between devices, along(): return lax.ppermute(value, 'slab', pairs)  17.9 us
    ppermute x10, starting transfers between devices, along(): return lax.ppermute(value, 'slab', pairs)  13.8 us
    ppermute x12, starting transfers between devices, spread(): return lax.ppermute(value, ('slab', 'ang'), pairs)  9.31 us
    pallas_call x2, Pallas kernels, ray_sums(): pl.pallas_call(functools.partial(rays_kernel, dims, first, total // 2, of...  8.48 us
    pallas_call x2, Pallas kernels, update_step(): pl.pallas_call(functools.partial(update_kernel, dims, first, last, total...  7.99 us
    pallas_call x2, Pallas kernels, residual_step(): pl.pallas_call(functools.partial(residual_kernel, dims, first, last, tota...  7.49 us
    ppermute x12, waiting for transfers between devices, spread(): return lax.ppermute(value, ('slab', 'ang'), pairs)  7 us
  transfers between devices with their start and end apart: 22, of which 10 were waited for; matrix products, arithmetic and copies ran while one was open for 0% of the time, Pallas kernels for 20%

profile of v2, /device:TPU:0, one launch (start us, length us, event | category | flops | bytes accessed | tf_op | source)
XLA Modules:
  0.0 73.9 jit_solution(12056494713445279793)
XLA Ops:
  0.6 0.0 copy-start
  0.6 4.3 %ray_sums_0.1 = (f32[32,1024]{1,0:T(8,128)}, f32[32,1024]{1,0:T(8,128)}, f32[32,1024]{1,0:T(8,128)}, f32[32,1024]{1,0:T(8,128)}, bf16[32,512]{1,0:T(8,128)(2,1)}) custom-call(s32[64]{0:T(128)} %refs_0_.5, s32[1,4]{1,0:T(1,128)} %refs_1_.4, s32[1,4]{1,0:T(1,128)} %refs_2_.3, f32[64,256]{1,0:T(8,128)} %refs_1_.7, f32[8,128,4096]{2,1,0:T(8,128)} %refs_2_.5), custom_call_target="tpu_custom_call" | custom-call | flops 58720256 | bytes 7340032 | tf_op jit(solution)/shard_map/ray_sums_0/pallas_call | solution.py:169
  5.0 0.0 copy-start.4
  5.0 3.0 %collective-permute-start = (f32[32,1024]{1,0:T(8,128)}, f32[32,1024]{1,0:T(8,128)S(1)}, u32[]{:S(2)}, u32[]{:S(2)}) collective-permute-start(f32[32,1024]{1,0:T(8,128)} %get-tuple-element.36), channel_id=1, source_target_pairs={{0,1},{1,0},{2,3},{3,2},{4,5},{5,4},{6,7},{7,6},{8,9},{9,8},{10,11... | collective-permute-start | bytes 393224 | tf_op jit(solution)/shard_map/ppermute | solution.py:437
  8.0 0.0 collective-permute-start.1
  8.0 0.2 collective-permute-start.2
  8.2 0.0 copy-done
  8.2 0.1 dynamic-slice_convert_fusion
  8.3 0.4 collective-permute-start.5
  8.7 0.0 copy-start.2
  8.7 0.8 %copy-done.2 = bf16[32,512]{1,0:T(8,128)(2,1)S(1)} copy-done((bf16[32,512]{1,0:T(8,128)(2,1)S(1)}, bf16[32,512]{1,0:T(8,128)(2,1)}, u32[]{:S(2)}) %copy-start.2) | copy-done | bytes 32792
  9.5 0.0 copy-start.1
  9.5 0.0 copy-start.3
  9.5 4.2 %ray_sums_1.1 = (f32[32,1152]{1,0:T(8,128)S(1)}, f32[32,1152]{1,0:T(8,128)S(1)}, f32[32,1152]{1,0:T(8,128)S(1)}, f32[32,1152]{1,0:T(8,128)S(1)}, f32[2,8,128,1152]{3,2,1,0:T(8,128)S(1)}) custom-call(bf16[32,512]{1,0:T(8,128)(2,1)S(1)} %copy-done.2, f32[8,128,4096]{2,1,0:T(8,128)} %refs_2_.5), custom_call_target="tpu_custom_call" | custom-call | flops 75497472 | bytes 9437184 | tf_op jit(solution)/shard_map/ray_sums_1/pallas_call | solution.py:169
  13.6 1.7 %collective-permute-start.6 = (f32[32,1152]{1,0:T(8,128)S(1)}, f32[32,1152]{1,0:T(8,128)S(1)}, u32[]{:S(2)}, u32[]{:S(2)}) collective-permute-start(f32[32,1152]{1,0:T(8,128)S(1)} %get-tuple-element.47), channel_id=1, source_target_pairs={{0,1},{1,0},{2,3},{3,2},{4,5},{5,4},{6,7},{7,6},{8,9},{9,8},{10,11... | collective-permute-start | bytes 442376 | tf_op jit(solution)/shard_map/ppermute | solution.py:437
  15.3 0.0 collective-permute-done
  15.3 0.2 collective-permute-start.7
  15.6 0.0 copy-done.4
  15.6 0.0 collective-permute-done.1
  15.6 0.3 collective-permute-start.8
  15.9 0.0 collective-permute-done.2
  16.0 1.7 %collective-permute-start.3 = (f32[2,32,1024]{2,1,0:T(8,128)S(1)}, f32[2,32,1024]{2,1,0:T(8,128)S(1)}, u32[]{:S(2)}, u32[]{:S(2)}) collective-permute-start(f32[2,32,1024]{2,1,0:T(8,128)S(1)} %pad_maximum_fusion.1.refs_3_), channel_id=1, source_target_pairs={{0,4},{2,6},{4,0},{6,2},{8,12},{10,14},{12,8},{14,10},{16,20},{18,... | collective-permute-start | bytes 786440 | tf_op jit(solution)/shard_map/ppermute | solution.py:429
  17.7 2.7 %collective-permute-done.6 = f32[32,1152]{1,0:T(8,128)S(1)} collective-permute-done((f32[32,1152]{1,0:T(8,128)S(1)}, f32[32,1152]{1,0:T(8,128)S(1)}, u32[]{:S(2)}, u32[]{:S(2)}) %collective-permute-start.6) | collective-permute-done | bytes 147488 | tf_op jit(solution)/shard_map/ppermute | solution.py:437
  20.4 0.0 collective-permute-done.7
  20.4 2.1 %collective-permute-done.8 = f32[32,1152]{1,0:T(8,128)S(1)} collective-permute-done((f32[32,1152]{1,0:T(8,128)S(1)}, f32[32,1152]{1,0:T(8,128)S(1)}, u32[]{:S(2)}, u32[]{:S(2)}) %collective-permute-start.8) | collective-permute-done | bytes 147488 | tf_op jit(solution)/shard_map/ppermute | solution.py:437
  22.6 1.9 %collective-permute-start.9 = (f32[2,32,1152]{2,1,0:T(8,128)S(1)}, f32[2,32,1152]{2,1,0:T(8,128)S(1)}, u32[]{:S(2)}, u32[]{:S(2)}) collective-permute-start(f32[2,32,1152]{2,1,0:T(8,128)S(1)} %pad_maximum_fusion.refs_9_), channel_id=1, source_target_pairs={{0,4},{2,6},{4,0},{6,2},{8,12},{10,14},{12,8},{14,10},{16,20},{18,... | collective-permute-start | bytes 884744 | tf_op jit(solution)/shard_map/ppermute | solution.py:429
  24.4 0.0 collective-permute-done.3.refs_4_
  24.5 1.7 %collective-permute-start.4 = (f32[2,32,1024]{2,1,0:T(8,128)S(1)}, f32[2,32,1024]{2,1,0:T(8,128)S(1)}, u32[]{:S(2)}, u32[]{:S(2)}) collective-permute-start(f32[2,32,1024]{2,1,0:T(8,128)S(1)} %collective-permute-done.3.refs_4_), channel_id=1, source_target_pairs={{0,8},{2,10},{4,28},{6,30},{8,16},{10,18},{12,4},{14,6},{16,24},{1... | collective-permute-start | bytes 786440 | tf_op jit(solution)/shard_map/ppermute | solution.py:429
  26.2 6.0 %collective-permute-done.9.refs_10_ = f32[2,32,1152]{2,1,0:T(8,128)S(1)} collective-permute-done((f32[2,32,1152]{2,1,0:T(8,128)S(1)}, f32[2,32,1152]{2,1,0:T(8,128)S(1)}, u32[]{:S(2)}, u32[]{:S(2)}) %collective-permute-start.9) | collective-permute-done | bytes 294944 | tf_op jit(solution)/shard_map/ppermute | solution.py:429
  32.2 1.8 %collective-permute-start.10 = (f32[2,32,1152]{2,1,0:T(8,128)S(1)}, f32[2,32,1152]{2,1,0:T(8,128)S(1)}, u32[]{:S(2)}, u32[]{:S(2)}) collective-permute-start(f32[2,32,1152]{2,1,0:T(8,128)S(1)} %collective-permute-done.9.refs_10_), channel_id=1, source_target_pairs={{0,8},{2,10},{4,0},{6,2},{8,16},{10,18},{12,4},{14,6},{16,24},{18,... | collective-permute-start | bytes 884744 | tf_op jit(solution)/shard_map/ppermute | solution.py:429
  34.0 0.8 %collective-permute-done.4.refs_5_ = f32[2,32,1024]{2,1,0:T(8,128)S(1)} collective-permute-done((f32[2,32,1024]{2,1,0:T(8,128)S(1)}, f32[2,32,1024]{2,1,0:T(8,128)S(1)}, u32[]{:S(2)}, u32[]{:S(2)}) %collective-permute-start.4) | collective-permute-done | bytes 262176 | tf_op jit(solution)/shard_map/ppermute | solution.py:429
  34.8 0.0 collective-permute-done.5.refs_7_.refs_13_
  34.8 0.0 copy-done.1
  34.8 0.0 copy-done.3
  34.8 3.5 %residual_0.1 = (f32[8,128,896]{2,1,0:T(8,128)S(1)}, f32[4,32,896]{2,1,0:T(8,128)S(1)}, f32[4,32,896]{2,1,0:T(8,128)S(1)}, f32[2,32,896]{2,1,0:T(8,128)S(1)}, f3...) custom-call(s32[64]{0:T(128)S(1)} %copy-done.3, ...), custom_call_target="tpu_custom_call" | custom-call | flops 528482304 | bytes 3211264 | tf_op jit(solution)/shard_map/residual_0/pallas_call | solution.py:325
  38.3 0.1 collective-permute-start.17
  38.4 2.5 %collective-permute-done.10.refs_11_ = f32[2,32,1152]{2,1,0:T(8,128)S(1)} collective-permute-done((f32[2,32,1152]{2,1,0:T(8,128)S(1)}, f32[2,32,1152]{2,1,0:T(8,128)S(1)}, u32[]{:S(2)}, u32[]{:S(2)}) %collective-permute-start.10) | collective-permute-done | bytes 294944 | tf_op jit(solution)/shard_map/ppermute | solution.py:429
  40.9 4.0 %residual_1.1 = (f32[8,128,896]{2,1,0:T(8,128)S(1)}, f32[4,32,2048]{2,1,0:T(8,128)S(1)}, f32[4,32,2048]{2,1,0:T(8,128)S(1)}, f32[2,32,1152]{2,1,0:T(8,128)S(1)},...) custom-call(s32[64]{0:T(128)S(1)} %copy-done.3, ...), custom_call_target="tpu_custom_call" | custom-call | flops 679477248 | bytes 4128768 | tf_op jit(solution)/shard_map/residual_1/pallas_call | solution.py:325
  44.9 3.8 %collective-permute-start.11 = (f32[2,32,1152]{2,1,0:T(8,128)S(1)}, f32[2,32,1152]{2,1,0:T(8,128)S(1)}, u32[]{:S(2)}, u32[]{:S(2)}) collective-permute-start(f32[2,32,1152]{2,1,0:T(8,128)S(1)} %get-tuple-element.59), channel_id=1, source_target_pairs={{0,24},{2,26},{4,12},{6,14},{8,0},{10,2},{12,20},{14,22},{16,8},{1... | collective-permute-start | bytes 884744 | tf_op jit(solution)/shard_map/ppermute | solution.py:429
  48.7 0.0 collective-permute-done.17
  48.7 0.1 collective-permute-start.18
  48.8 0.1 collective-permute-start.16
  48.9 5.1 %collective-permute-done.11 = f32[2,32,1152]{2,1,0:T(8,128)S(1)} collective-permute-done((f32[2,32,1152]{2,1,0:T(8,128)S(1)}, f32[2,32,1152]{2,1,0:T(8,128)S(1)}, u32[]{:S(2)}, u32[]{:S(2)}) %collective-permute-start.11) | collective-permute-done | bytes 294944 | tf_op jit(solution)/shard_map/ppermute | solution.py:429
  54.0 2.3 %collective-permute-start.12 = (f32[2,32,1152]{2,1,0:T(8,128)S(1)}, f32[2,32,1152]{2,1,0:T(8,128)S(1)}, u32[]{:S(2)}, u32[]{:S(2)}) collective-permute-start(f32[2,32,1152]{2,1,0:T(8,128)S(1)} %add.48), channel_id=1, source_target_pairs={{0,4},{2,6},{4,0},{6,2},{8,12},{10,14},{12,8},{14,10},{16,20},{18,... | collective-permute-start | bytes 884744 | tf_op jit(solution)/shard_map/ppermute | solution.py:429
  56.3 0.0 collective-permute-done.18
  56.3 1.6 %collective-permute-start.21 = (f32[32,896]{1,0:T(8,128)S(1)}, f32[32,896]{1,0:T(8,128)S(1)}, u32[]{:S(2)}, u32[]{:S(2)}) collective-permute-start(f32[32,896]{1,0:T(8,128)S(1)} %get-tuple-element.70.refs_4_), channel_id=1, source_target_pairs={{0,1},{1,0},{2,3},{3,2},{4,5},{5,4},{6,7},{7,6},{8,9},{9,8},{10,11... | collective-permute-start | bytes 344072 | tf_op jit(solution)/shard_map/ppermute | solution.py:437
  57.9 0.0 collective-permute-start.20
  57.9 3.5 %collective-permute-done.12 = f32[2,32,1152]{2,1,0:T(8,128)S(1)} collective-permute-done((f32[2,32,1152]{2,1,0:T(8,128)S(1)}, f32[2,32,1152]{2,1,0:T(8,128)S(1)}, u32[]{:S(2)}, u32[]{:S(2)}) %collective-permute-start.12) | collective-permute-done | bytes 294944 | tf_op jit(solution)/shard_map/ppermute | solution.py:429
  61.5 1.6 %collective-permute-start.15 = (f32[32,1152]{1,0:T(8,128)S(1)}, f32[32,1152]{1,0:T(8,128)S(1)}, u32[]{:S(2)}, u32[]{:S(2)}) collective-permute-start(f32[32,1152]{1,0:T(8,128)S(1)} %get-tuple-element.68.refs_4_), channel_id=1, source_target_pairs={{0,1},{1,0},{2,3},{3,2},{4,5},{5,4},{6,7},{7,6},{8,9},{9,8},{10,11... | collective-permute-start | bytes 442376 | tf_op jit(solution)/shard_map/ppermute | solution.py:437
  63.1 0.0 collective-permute-start.14
  63.1 0.0 collective-permute-done.21.refs_3_
  63.1 0.6 collective-permute-start.13
  63.7 0.2 collective-permute-done.20.refs_2_
  63.9 0.0 collective-permute-start.19
  63.9 1.3 %collective-permute-done.19.refs_1_ = f32[32,896]{1,0:T(8,128)S(1)} collective-permute-done((f32[32,896]{1,0:T(8,128)S(1)}, f32[32,896]{1,0:T(8,128)S(1)}, u32[]{:S(2)}, u32[]{:S(2)}) %collective-permute-start.19) | collective-permute-done | bytes 114720 | tf_op jit(solution)/shard_map/ppermute | solution.py:437
  65.2 3.3 %update_0.1.refs_8_ = f32[8,128,4096]{2,1,0:T(8,128)} custom-call(bf16[4,256,128]{2,1,0:T(8,128)(2,1)S(1)} %get-tuple-element.56.refs_0_, f32[32,896]{1,0:T(8,128)S(1)} %collective-permute-done.19.refs_1_, f32[32,896]{1,0:T(8,128)S(1)} %collective-permute-done.20.refs_2_, f32[32,896]{1,0:T(8,128)S(1)} %collective-permute-done.21.refs_3_, ...), custom_call_target="tpu_custom_call" | custom-call | flops 176160768 | bytes 7340032 | tf_op jit(solution)/shard_map/update_0/pallas_call | solution.py:403
  68.6 0.0 collective-permute-done.15.refs_3_
  68.6 0.6 collective-permute-done.14.refs_2_
  69.2 0.0 collective-permute-done.13.refs_1_
  69.2 0.0 collective-permute-done.16.refs_7_
  69.2 4.7 %update_1.1 = (f32[8,128,4096]{2,1,0:T(8,128)}, f32[4,32,4096]{2,1,0:T(8,128)}) custom-call(bf16[4,256,128]{2,1,0:T(8,128)(2,1)S(1)} %get-tuple-element.56.refs_0_, f32[32,1152]{1,0:T(8,128)S(1)} %collective-permute-done.13.refs_1_, f32[32,1152]{1,0:T(8,128)S(1)} %collective-permute-done.14.refs_2_, ...), custom_call_target="tpu_custom_call", output_to_operand_aliasing={{0}: (8, {})} | custom-call | flops 226492416 | bytes 9437184 | tf_op jit(solution)/shard_map/update_1/pallas_call | solution.py:403
  (9 shorter events, 0.2 us)
Async XLA Ops:
  0.6 7.6 %copy-start = (bf16[4,32,4096]{2,1,0:T(8,128)(2,1)S(1)}, bf16[4,32,4096]{2,1,0:T(8,128)(2,1)}, u32[]{:S(2)}) copy-start(bf16[4,32,4096]{2,1,0:T(8,128)(2,1)} %refs_12_.1) | copy-start | bytes 3145732
  5.0 10.6 %copy-start.4 = (f32[32,1024]{1,0:T(8,128)S(1)}, f32[32,1024]{1,0:T(8,128)}, u32[]{:S(2)}) copy-start(f32[32,1024]{1,0:T(8,128)} %get-tuple-element.35) | copy-start | bytes 393220
  5.0 10.4 %collective-permute-start = (f32[32,1024]{1,0:T(8,128)}, f32[32,1024]{1,0:T(8,128)S(1)}, u32[]{:S(2)}, u32[]{:S(2)}) collective-permute-start(f32[32,1024]{1,0:T(8,128)} %get-tuple-element.36), channel_id=1, source_target_pairs={{0,1},{1,0},{2,3},{3,2},{4,5},{5,4},{6,7},{7,6},{8,9},{9,8},{10,11... | collective-permute-start | bytes 393224 | tf_op jit(solution)/shard_map/ppermute | solution.py:437
  8.0 7.6 %collective-permute-start.1 = (f32[32,1024]{1,0:T(8,128)}, f32[32,1024]{1,0:T(8,128)S(1)}, u32[]{:S(2)}, u32[]{:S(2)}) collective-permute-start(f32[32,1024]{1,0:T(8,128)} %get-tuple-element.37), channel_id=1, source_target_pairs={{0,2},{1,3},{2,0},{3,1},{4,6},{5,7},{6,4},{7,5},{8,10},{9,11},{10,... | collective-permute-start | bytes 393224 | tf_op jit(solution)/shard_map/ppermute | solution.py:437
  8.0 7.9 %collective-permute-start.2 = (f32[32,1024]{1,0:T(8,128)}, f32[32,1024]{1,0:T(8,128)S(1)}, u32[]{:S(2)}, u32[]{:S(2)}) collective-permute-start(f32[32,1024]{1,0:T(8,128)} %get-tuple-element.38), channel_id=1, source_target_pairs={{0,3},{1,2},{2,1},{3,0},{4,7},{5,6},{6,5},{7,4},{8,11},{9,10},{10,... | collective-permute-start | bytes 393224 | tf_op jit(solution)/shard_map/ppermute | solution.py:437
  8.3 26.4 %collective-permute-start.5 = (f32[4,32,2048]{2,1,0:T(8,128)S(1)}, f32[4,32,2048]{2,1,0:T(8,128)S(1)}, u32[]{:S(2)}, u32[]{:S(2)}) collective-permute-start(f32[4,32,2048]{2,1,0:T(8,128)S(1)} %dynamic-slice_convert_fusion), channel_id=1, source_target_pairs={{0,2},{2,0},{4,6},{6,4},{8,10},{10,8},{12,14},{14,12},{16,18},{18,... | collective-permute-start | bytes 3145736 | tf_op jit(solution)/shard_map/ppermute | solution.py:429
  8.7 0.8 %copy-start.2 = (bf16[32,512]{1,0:T(8,128)(2,1)S(1)}, bf16[32,512]{1,0:T(8,128)(2,1)}, u32[]{:S(2)}) copy-start(bf16[32,512]{1,0:T(8,128)(2,1)} %get-tuple-element.45.refs_0_) | copy-start | bytes 98308
  9.5 25.3 %copy-start.1 = (f32[64,256]{1,0:T(8,128)S(1)}, f32[64,256]{1,0:T(8,128)}, u32[]{:S(2)}) copy-start(f32[64,256]{1,0:T(8,128)} %refs_1_.7) | copy-start | bytes 196612
  9.5 25.3 %copy-start.3 = (s32[64]{0:T(128)S(1)}, s32[64]{0:T(128)}, u32[]{:S(2)}) copy-start(s32[64]{0:T(128)} %refs_0_.5) | copy-start | bytes 772
  13.6 6.7 %collective-permute-start.6 = (f32[32,1152]{1,0:T(8,128)S(1)}, f32[32,1152]{1,0:T(8,128)S(1)}, u32[]{:S(2)}, u32[]{:S(2)}) collective-permute-start(f32[32,1152]{1,0:T(8,128)S(1)} %get-tuple-element.47), channel_id=1, source_target_pairs={{0,1},{1,0},{2,3},{3,2},{4,5},{5,4},{6,7},{7,6},{8,9},{9,8},{10,11... | collective-permute-start | bytes 442376 | tf_op jit(solution)/shard_map/ppermute | solution.py:437
  15.3 5.0 %collective-permute-start.7 = (f32[32,1152]{1,0:T(8,128)S(1)}, f32[32,1152]{1,0:T(8,128)S(1)}, u32[]{:S(2)}, u32[]{:S(2)}) collective-permute-start(f32[32,1152]{1,0:T(8,128)S(1)} %get-tuple-element.48), channel_id=1, source_target_pairs={{0,2},{1,3},{2,0},{3,1},{4,6},{5,7},{6,4},{7,5},{8,10},{9,11},{10,... | collective-permute-start | bytes 442376 | tf_op jit(solution)/shard_map/ppermute | solution.py:437
  15.6 6.9 %collective-permute-start.8 = (f32[32,1152]{1,0:T(8,128)S(1)}, f32[32,1152]{1,0:T(8,128)S(1)}, u32[]{:S(2)}, u32[]{:S(2)}) collective-permute-start(f32[32,1152]{1,0:T(8,128)S(1)} %get-tuple-element.49), channel_id=1, source_target_pairs={{0,3},{1,2},{2,1},{3,0},{4,7},{5,6},{6,5},{7,4},{8,11},{9,10},{10,... | collective-permute-start | bytes 442376 | tf_op jit(solution)/shard_map/ppermute | solution.py:437
  16.0 8.5 %collective-permute-start.3 = (f32[2,32,1024]{2,1,0:T(8,128)S(1)}, f32[2,32,1024]{2,1,0:T(8,128)S(1)}, u32[]{:S(2)}, u32[]{:S(2)}) collective-permute-start(f32[2,32,1024]{2,1,0:T(8,128)S(1)} %pad_maximum_fusion.1.refs_3_), channel_id=1, source_target_pairs={{0,4},{2,6},{4,0},{6,2},{8,12},{10,14},{12,8},{14,10},{16,20},{18,... | collective-permute-start | bytes 786440 | tf_op jit(solution)/shard_map/ppermute | solution.py:429
  22.6 9.6 %collective-permute-start.9 = (f32[2,32,1152]{2,1,0:T(8,128)S(1)}, f32[2,32,1152]{2,1,0:T(8,128)S(1)}, u32[]{:S(2)}, u32[]{:S(2)}) collective-permute-start(f32[2,32,1152]{2,1,0:T(8,128)S(1)} %pad_maximum_fusion.refs_9_), channel_id=1, source_target_pairs={{0,4},{2,6},{4,0},{6,2},{8,12},{10,14},{12,8},{14,10},{16,20},{18,... | collective-permute-start | bytes 884744 | tf_op jit(solution)/shard_map/ppermute | solution.py:429
  24.5 10.3 %collective-permute-start.4 = (f32[2,32,1024]{2,1,0:T(8,128)S(1)}, f32[2,32,1024]{2,1,0:T(8,128)S(1)}, u32[]{:S(2)}, u32[]{:S(2)}) collective-permute-start(f32[2,32,1024]{2,1,0:T(8,128)S(1)} %collective-permute-done.3.refs_4_), channel_id=1, source_target_pairs={{0,8},{2,10},{4,28},{6,30},{8,16},{10,18},{12,4},{14,6},{16,24},{1... | collective-permute-start | bytes 786440 | tf_op jit(solution)/shard_map/ppermute | solution.py:429
  32.2 8.7 %collective-permute-start.10 = (f32[2,32,1152]{2,1,0:T(8,128)S(1)}, f32[2,32,1152]{2,1,0:T(8,128)S(1)}, u32[]{:S(2)}, u32[]{:S(2)}) collective-permute-start(f32[2,32,1152]{2,1,0:T(8,128)S(1)} %collective-permute-done.9.refs_10_), channel_id=1, source_target_pairs={{0,8},{2,10},{4,0},{6,2},{8,16},{10,18},{12,4},{14,6},{16,24},{18,... | collective-permute-start | bytes 884744 | tf_op jit(solution)/shard_map/ppermute | solution.py:429
  38.3 10.4 %collective-permute-start.17 = (f32[2,32,896]{2,1,0:T(8,128)S(1)}, f32[2,32,896]{2,1,0:T(8,128)S(1)}, u32[]{:S(2)}, u32[]{:S(2)}) collective-permute-start(f32[2,32,896]{2,1,0:T(8,128)S(1)} %get-tuple-element.65), channel_id=1, source_target_pairs={{0,4},{2,6},{4,12},{6,14},{8,0},{10,2},{12,20},{14,22},{16,8},{18,... | collective-permute-start | bytes 688136 | tf_op jit(solution)/shard_map/ppermute | solution.py:429
  44.9 9.1 %collective-permute-start.11 = (f32[2,32,1152]{2,1,0:T(8,128)S(1)}, f32[2,32,1152]{2,1,0:T(8,128)S(1)}, u32[]{:S(2)}, u32[]{:S(2)}) collective-permute-start(f32[2,32,1152]{2,1,0:T(8,128)S(1)} %get-tuple-element.59), channel_id=1, source_target_pairs={{0,24},{2,26},{4,12},{6,14},{8,0},{10,2},{12,20},{14,22},{16,8},{1... | collective-permute-start | bytes 884744 | tf_op jit(solution)/shard_map/ppermute | solution.py:429
  48.7 7.6 %collective-permute-start.18 = (f32[2,32,896]{2,1,0:T(8,128)S(1)}, f32[2,32,896]{2,1,0:T(8,128)S(1)}, u32[]{:S(2)}, u32[]{:S(2)}) collective-permute-start(f32[2,32,896]{2,1,0:T(8,128)S(1)} %add.53), channel_id=1, source_target_pairs={{0,4},{2,6},{4,0},{6,2},{8,12},{10,14},{12,8},{14,10},{16,20},{18,... | collective-permute-start | bytes 688136 | tf_op jit(solution)/shard_map/ppermute | solution.py:429
  48.8 20.4 %collective-permute-start.16 = (f32[4,32,2048]{2,1,0:T(8,128)S(1)}, f32[4,32,2048]{2,1,0:T(8,128)S(1)}, u32[]{:S(2)}, u32[]{:S(2)}) collective-permute-start(f32[4,32,2048]{2,1,0:T(8,128)S(1)} %get-tuple-element.62), channel_id=1, source_target_pairs={{0,2},{2,0},{4,6},{6,4},{8,10},{10,8},{12,14},{14,12},{16,18},{18,... | collective-permute-start | bytes 3145736 | tf_op jit(solution)/shard_map/ppermute | solution.py:429
  54.0 7.5 %collective-permute-start.12 = (f32[2,32,1152]{2,1,0:T(8,128)S(1)}, f32[2,32,1152]{2,1,0:T(8,128)S(1)}, u32[]{:S(2)}, u32[]{:S(2)}) collective-permute-start(f32[2,32,1152]{2,1,0:T(8,128)S(1)} %add.48), channel_id=1, source_target_pairs={{0,4},{2,6},{4,0},{6,2},{8,12},{10,14},{12,8},{14,10},{16,20},{18,... | collective-permute-start | bytes 884744 | tf_op jit(solution)/shard_map/ppermute | solution.py:429
  56.3 6.8 %collective-permute-start.21 = (f32[32,896]{1,0:T(8,128)S(1)}, f32[32,896]{1,0:T(8,128)S(1)}, u32[]{:S(2)}, u32[]{:S(2)}) collective-permute-start(f32[32,896]{1,0:T(8,128)S(1)} %get-tuple-element.70.refs_4_), channel_id=1, source_target_pairs={{0,1},{1,0},{2,3},{3,2},{4,5},{5,4},{6,7},{7,6},{8,9},{9,8},{10,11... | collective-permute-start | bytes 344072 | tf_op jit(solution)/shard_map/ppermute | solution.py:437
  57.9 6.0 %collective-permute-start.20 = (f32[32,896]{1,0:T(8,128)S(1)}, f32[32,896]{1,0:T(8,128)S(1)}, u32[]{:S(2)}, u32[]{:S(2)}) collective-permute-start(f32[32,896]{1,0:T(8,128)S(1)} %get-tuple-element.71), channel_id=1, source_target_pairs={{0,3},{1,2},{2,1},{3,0},{4,7},{5,6},{6,5},{7,4},{8,11},{9,10},{10,... | collective-permute-start | bytes 344072 | tf_op jit(solution)/shard_map/ppermute | solution.py:437
  61.5 7.1 %collective-permute-start.15 = (f32[32,1152]{1,0:T(8,128)S(1)}, f32[32,1152]{1,0:T(8,128)S(1)}, u32[]{:S(2)}, u32[]{:S(2)}) collective-permute-start(f32[32,1152]{1,0:T(8,128)S(1)} %get-tuple-element.68.refs_4_), channel_id=1, source_target_pairs={{0,1},{1,0},{2,3},{3,2},{4,5},{5,4},{6,7},{7,6},{8,9},{9,8},{10,11... | collective-permute-start | bytes 442376 | tf_op jit(solution)/shard_map/ppermute | solution.py:437
  63.1 6.1 %collective-permute-start.14 = (f32[32,1152]{1,0:T(8,128)S(1)}, f32[32,1152]{1,0:T(8,128)S(1)}, u32[]{:S(2)}, u32[]{:S(2)}) collective-permute-start(f32[32,1152]{1,0:T(8,128)S(1)} %get-tuple-element.69), channel_id=1, source_target_pairs={{0,3},{1,2},{2,1},{3,0},{4,7},{5,6},{6,5},{7,4},{8,11},{9,10},{10,... | collective-permute-start | bytes 442376 | tf_op jit(solution)/shard_map/ppermute | solution.py:437
  63.1 6.1 %collective-permute-start.13 = (f32[32,1152]{1,0:T(8,128)S(1)}, f32[32,1152]{1,0:T(8,128)S(1)}, u32[]{:S(2)}, u32[]{:S(2)}) collective-permute-start(f32[32,1152]{1,0:T(8,128)S(1)} %get-tuple-element.69), channel_id=1, source_target_pairs={{0,2},{1,3},{2,0},{3,1},{4,6},{5,7},{6,4},{7,5},{8,10},{9,11},{10,... | collective-permute-start | bytes 442376 | tf_op jit(solution)/shard_map/ppermute | solution.py:437
  63.9 1.3 %collective-permute-start.19 = (f32[32,896]{1,0:T(8,128)S(1)}, f32[32,896]{1,0:T(8,128)S(1)}, u32[]{:S(2)}, u32[]{:S(2)}) collective-permute-start(f32[32,896]{1,0:T(8,128)S(1)} %get-tuple-element.71), channel_id=1, source_target_pairs={{0,2},{1,3},{2,0},{3,1},{4,6},{5,7},{6,4},{7,5},{8,10},{9,11},{10,... | collective-permute-start | bytes 344072 | tf_op jit(solution)/shard_map/ppermute | solution.py:437

commit v3 on v2

--- a/solution.py
+++ b/solution.py
@@ -227,9 +227,9 @@
 def residual_kernel(dims, first, last, half, rdev, zdev, offset, width, *refs):
     per, groups, zb, cells = dims
     block = zdev * per
-    load = None
+    loads = []
     if first or last:
-        order_ref, table_ref, vol_ref, *refs, sem = refs
+        order_ref, table_ref, vol_ref, *refs, sems = refs
     if last:
         foot_ref, *refs = refs
     if not first:
@@ -241,8 +241,9 @@
         kept_ref, *refs = refs
         start = lax.rem(lax.axis_index("slab") + (0 if first else 1), 2) * half
         columns = pl.ds(pl.multiple_of(start, LANES), kept_ref.shape[2])
-        load = pltpu.make_async_copy(vol_ref.at[:, :, columns], kept_ref, sem)
-        load.start()
+        for z in range(zdev):
+            loads.append(pltpu.make_async_copy(vol_ref.at[z, :, columns], kept_ref.at[z], sems.at[z]))
+            loads[z].start()
     mine_out, sent_out, *refs = refs
     if not first:
         mine_out[:, :, :offset] = mine_before[...]
@@ -285,7 +286,7 @@
                 ref[j, :, columns] = given[(2 * i + j) * block:(2 * i + j + 1) * block]
     if last:
         update_weights(dims, zdev, rdev, foot_ref[...], order_ref, table_ref, refs[1], refs[0])
-    if load is not None:
+    for load in loads:
         load.wait()
 
 
@@ -319,7 +320,7 @@
         args += mats[:5]
         specs += [IN_VMEM] * 5
     if first or last:
-        scratch.append(pltpu.SemaphoreType.DMA)
+        scratch.append(pltpu.SemaphoreType.DMA((zdev,)))
     args += [*sums, measured, theirs, *before]
     specs += [IN_VMEM] * (5 + len(before))
     return pl.pallas_call(
@@ -421,7 +422,7 @@
     zb = SUBLANES // per
     dims = (per, groups, zb, cells)
     each = half // CHUNKS
-    widths = [each - LANES] + [each + LANES]
+    widths = [each] * CHUNKS
     offsets = [sum(widths[:c]) for c in range(CHUNKS)]
 
     def along(value, to):

time: 74.3 us -> 74.7 us (level)
    ppermute x12, starting transfers between devices: 9.31 us -> 10.2 us  [spread(): return lax.ppermute(value, ('slab', 'ang'), pairs)]
    ppermute x12, waiting for transfers between devices: 7 us -> 6.11 us  [spread(): return lax.ppermute(value, ('slab', 'ang'), pairs)]
  transfers between devices with their start and end apart: 22 -> 22, of which waited for: 10 -> 9; matrix products, arithmetic and copies ran while one was open for 0% -> 0% of each run, Pallas kernels for 20% -> 21%
where the time goes in v3:
time: 74.7 us; the launch traced here: 74.5 us
  Pallas kernels  24.4 us (33%)
  waiting for transfers between devices  24.4 us (33%)
  starting transfers between devices  23.8 us (32%)
  local copies, waits for them, and re-layouts  0.77 us (1%)
  between operations  0.77 us (1%)
    ppermute x10, waiting for transfers between devices, along(): return lax.ppermute(value, 'slab', pairs)  18.3 us
    ppermute x10, starting transfers between devices, along(): return lax.ppermute(value, 'slab', pairs)  13.6 us
    ppermute x12, starting transfers between devices, spread(): return lax.ppermute(value, ('slab', 'ang'), pairs)  10.2 us
    pallas_call x2, Pallas kernels, ray_sums(): pl.pallas_call(functools.partial(rays_kernel, dims, first, total // 2, of...  8.49 us
    pallas_call x2, Pallas kernels, residual_step(): pl.pallas_call(functools.partial(residual_kernel, dims, first, last, tota...  7.99 us
    pallas_call x2, Pallas kernels, update_step(): pl.pallas_call(functools.partial(update_kernel, dims, first, last, total...  7.93 us
    ppermute x12, waiting for transfers between devices, spread(): return lax.ppermute(value, ('slab', 'ang'), pairs)  6.11 us
  transfers between devices with their start and end apart: 22, of which 9 were waited for; matrix products, arithmetic and copies ran while one was open for 0% of the time, Pallas kernels for 21%

profile of v3, /device:TPU:0, one launch (start us, length us, event | category | flops | bytes accessed | tf_op | source)
XLA Modules:
  0.0 74.5 jit_solution(1388347450492142069)
XLA Ops:
  0.6 0.0 copy-start
  0.6 4.6 %ray_sums_0.1 = (f32[32,1152]{1,0:T(8,128)}, f32[32,1152]{1,0:T(8,128)}, f32[32,1152]{1,0:T(8,128)}, f32[32,1152]{1,0:T(8,128)}, bf16[32,512]{1,0:T(8,128)(2,1)}) custom-call(s32[64]{0:T(128)} %refs_0_.5, s32[1,4]{1,0:T(1,128)} %refs_1_.4, s32[1,4]{1,0:T(1,128)} %refs_2_.3, f32[64,256]{1,0:T(8,128)} %refs_1_.7, f32[8,128,4096]{2,1,0:T(8,128)} %refs_2_.5), custom_call_target="tpu_custom_call" | custom-call | flops 67108864 | bytes 8388608 | tf_op jit(solution)/shard_map/ray_sums_0/pallas_call | solution.py:169
  5.3 3.0 %collective-permute-start = (f32[32,1152]{1,0:T(8,128)}, f32[32,1152]{1,0:T(8,128)S(1)}, u32[]{:S(2)}, u32[]{:S(2)}) collective-permute-start(f32[32,1152]{1,0:T(8,128)} %get-tuple-element.36), channel_id=1, source_target_pairs={{0,1},{1,0},{2,3},{3,2},{4,5},{5,4},{6,7},{7,6},{8,9},{9,8},{10,11... | collective-permute-start | bytes 442376 | tf_op jit(solution)/shard_map/ppermute | solution.py:438
  8.3 0.0 collective-permute-start.1
  8.3 0.2 collective-permute-start.2
  8.5 0.0 copy-done
  8.5 0.1 dynamic-slice_convert_fusion
  8.6 0.4 collective-permute-start.5
  9.0 0.0 copy-start.2
  9.0 0.8 %copy-done.2 = bf16[32,512]{1,0:T(8,128)(2,1)S(1)} copy-done((bf16[32,512]{1,0:T(8,128)(2,1)S(1)}, bf16[32,512]{1,0:T(8,128)(2,1)}, u32[]{:S(2)}) %copy-start.2) | copy-done | bytes 32792
  9.8 0.0 copy-start.4
  9.8 0.0 copy-start.1
  9.8 0.0 copy-start.3
  9.8 3.9 %ray_sums_1.1 = (f32[32,1024]{1,0:T(8,128)S(1)}, f32[32,1024]{1,0:T(8,128)S(1)}, f32[32,1024]{1,0:T(8,128)S(1)}, f32[32,1024]{1,0:T(8,128)S(1)}, f32[2,8,128,1024]{3,2,1,0:T(8,128)S(1)}) custom-call(bf16[32,512]{1,0:T(8,128)(2,1)S(1)} %copy-done.2, f32[8,128,4096]{2,1,0:T(8,128)} %refs_2_.5), custom_call_target="tpu_custom_call" | custom-call | flops 67108864 | bytes 8388608 | tf_op jit(solution)/shard_map/ray_sums_1/pallas_call | solution.py:169
  13.6 1.7 %collective-permute-start.6 = (f32[32,1024]{1,0:T(8,128)S(1)}, f32[32,1024]{1,0:T(8,128)S(1)}, u32[]{:S(2)}, u32[]{:S(2)}) collective-permute-start(f32[32,1024]{1,0:T(8,128)S(1)} %get-tuple-element.47), channel_id=1, source_target_pairs={{0,1},{1,0},{2,3},{3,2},{4,5},{5,4},{6,7},{7,6},{8,9},{9,8},{10,11... | collective-permute-start | bytes 393224 | tf_op jit(solution)/shard_map/ppermute | solution.py:438
  15.3 0.0 collective-permute-done
  15.3 0.2 collective-permute-start.7
  15.6 0.0 copy-done.4
  15.6 0.0 collective-permute-done.1
  15.6 0.3 collective-permute-start.8
  15.9 0.0 collective-permute-done.2
  16.0 1.7 %collective-permute-start.3 = (f32[2,32,1152]{2,1,0:T(8,128)S(1)}, f32[2,32,1152]{2,1,0:T(8,128)S(1)}, u32[]{:S(2)}, u32[]{:S(2)}) collective-permute-start(f32[2,32,1152]{2,1,0:T(8,128)S(1)} %pad_maximum_fusion.refs_3_), channel_id=1, source_target_pairs={{0,4},{2,6},{4,0},{6,2},{8,12},{10,14},{12,8},{14,10},{16,20},{18,... | collective-permute-start | bytes 884744 | tf_op jit(solution)/shard_map/ppermute | solution.py:430
  17.7 2.3 %collective-permute-done.6 = f32[32,1024]{1,0:T(8,128)S(1)} collective-permute-done((f32[32,1024]{1,0:T(8,128)S(1)}, f32[32,1024]{1,0:T(8,128)S(1)}, u32[]{:S(2)}, u32[]{:S(2)}) %collective-permute-start.6) | collective-permute-done | bytes 131104 | tf_op jit(solution)/shard_map/ppermute | solution.py:438
  20.0 0.0 collective-permute-done.7
  20.0 1.8 %collective-permute-done.8 = f32[32,1024]{1,0:T(8,128)S(1)} collective-permute-done((f32[32,1024]{1,0:T(8,128)S(1)}, f32[32,1024]{1,0:T(8,128)S(1)}, u32[]{:S(2)}, u32[]{:S(2)}) %collective-permute-start.8) | collective-permute-done | bytes 131104 | tf_op jit(solution)/shard_map/ppermute | solution.py:438
  21.8 1.9 %collective-permute-start.9 = (f32[2,32,1024]{2,1,0:T(8,128)S(1)}, f32[2,32,1024]{2,1,0:T(8,128)S(1)}, u32[]{:S(2)}, u32[]{:S(2)}) collective-permute-start(f32[2,32,1024]{2,1,0:T(8,128)S(1)} %pad_maximum_fusion.1.refs_9_), channel_id=1, source_target_pairs={{0,4},{2,6},{4,0},{6,2},{8,12},{10,14},{12,8},{14,10},{16,20},{18,... | collective-permute-start | bytes 786440 | tf_op jit(solution)/shard_map/ppermute | solution.py:430
  23.7 1.4 %collective-permute-done.3.refs_4_ = f32[2,32,1152]{2,1,0:T(8,128)S(1)} collective-permute-done((f32[2,32,1152]{2,1,0:T(8,128)S(1)}, f32[2,32,1152]{2,1,0:T(8,128)S(1)}, u32[]{:S(2)}, u32[]{:S(2)}) %collective-permute-start.3) | collective-permute-done | bytes 294944 | tf_op jit(solution)/shard_map/ppermute | solution.py:430
  25.2 1.7 %collective-permute-start.4 = (f32[2,32,1152]{2,1,0:T(8,128)S(1)}, f32[2,32,1152]{2,1,0:T(8,128)S(1)}, u32[]{:S(2)}, u32[]{:S(2)}) collective-permute-start(f32[2,32,1152]{2,1,0:T(8,128)S(1)} %collective-permute-done.3.refs_4_), channel_id=1, source_target_pairs={{0,8},{2,10},{4,28},{6,30},{8,16},{10,18},{12,4},{14,6},{16,24},{1... | collective-permute-start | bytes 884744 | tf_op jit(solution)/shard_map/ppermute | solution.py:430
  26.9 3.9 %collective-permute-done.9.refs_10_ = f32[2,32,1024]{2,1,0:T(8,128)S(1)} collective-permute-done((f32[2,32,1024]{2,1,0:T(8,128)S(1)}, f32[2,32,1024]{2,1,0:T(8,128)S(1)}, u32[]{:S(2)}, u32[]{:S(2)}) %collective-permute-start.9) | collective-permute-done | bytes 262176 | tf_op jit(solution)/shard_map/ppermute | solution.py:430
  30.8 1.8 %collective-permute-start.10 = (f32[2,32,1024]{2,1,0:T(8,128)S(1)}, f32[2,32,1024]{2,1,0:T(8,128)S(1)}, u32[]{:S(2)}, u32[]{:S(2)}) collective-permute-start(f32[2,32,1024]{2,1,0:T(8,128)S(1)} %collective-permute-done.9.refs_10_), channel_id=1, source_target_pairs={{0,8},{2,10},{4,0},{6,2},{8,16},{10,18},{12,4},{14,6},{16,24},{18,... | collective-permute-start | bytes 786440 | tf_op jit(solution)/shard_map/ppermute | solution.py:430
  32.6 2.9 %collective-permute-done.4.refs_5_ = f32[2,32,1152]{2,1,0:T(8,128)S(1)} collective-permute-done((f32[2,32,1152]{2,1,0:T(8,128)S(1)}, f32[2,32,1152]{2,1,0:T(8,128)S(1)}, u32[]{:S(2)}, u32[]{:S(2)}) %collective-permute-start.4) | collective-permute-done | bytes 294944 | tf_op jit(solution)/shard_map/ppermute | solution.py:430
  35.5 0.0 collective-permute-done.5.refs_7_.refs_13_
  35.5 0.0 copy-done.1
  35.5 0.0 copy-done.3
  35.5 4.0 %residual_0.1 = (f32[8,128,1024]{2,1,0:T(8,128)S(1)}, f32[4,32,1024]{2,1,0:T(8,128)S(1)}, f32[4,32,1024]{2,1,0:T(8,128)S(1)}, f32[2,32,1024]{2,1,0:T(8,128)S(1)}...) custom-call(s32[64]{0:T(128)S(1)} %copy-done.3, ...), custom_call_target="tpu_custom_call" | custom-call | flops 603979776 | bytes 3670016 | tf_op jit(solution)/shard_map/residual_0/pallas_call | solution.py:326
  39.5 0.8 %collective-permute-start.17 = (f32[2,32,1024]{2,1,0:T(8,128)S(1)}, f32[2,32,1024]{2,1,0:T(8,128)S(1)}, u32[]{:S(2)}, u32[]{:S(2)}) collective-permute-start(f32[2,32,1024]{2,1,0:T(8,128)S(1)} %get-tuple-element.65), channel_id=1, source_target_pairs={{0,4},{2,6},{4,12},{6,14},{8,0},{10,2},{12,20},{14,22},{16,8},{18,... | collective-permute-start | bytes 786440 | tf_op jit(solution)/shard_map/ppermute | solution.py:430
  40.3 0.0 collective-permute-done.10.refs_11_
  40.3 4.0 %residual_1.1 = (f32[8,128,1024]{2,1,0:T(8,128)S(1)}, f32[4,32,2048]{2,1,0:T(8,128)S(1)}, f32[4,32,2048]{2,1,0:T(8,128)S(1)}, f32[2,32,1024]{2,1,0:T(8,128)S(1)}...) custom-call(s32[64]{0:T(128)S(1)} %copy-done.3, ...), custom_call_target="tpu_custom_call" | custom-call | flops 603979776 | bytes 3670016 | tf_op jit(solution)/shard_map/residual_1/pallas_call | solution.py:326
  44.3 0.1 collective-permute-start.16
  44.4 2.6 %collective-permute-start.11 = (f32[2,32,1024]{2,1,0:T(8,128)S(1)}, f32[2,32,1024]{2,1,0:T(8,128)S(1)}, u32[]{:S(2)}, u32[]{:S(2)}) collective-permute-start(f32[2,32,1024]{2,1,0:T(8,128)S(1)} %get-tuple-element.59), channel_id=1, source_target_pairs={{0,24},{2,26},{4,12},{6,14},{8,0},{10,2},{12,20},{14,22},{16,8},{1... | collective-permute-start | bytes 786440 | tf_op jit(solution)/shard_map/ppermute | solution.py:430
  47.0 0.0 collective-permute-done.17
  47.0 0.1 collective-permute-start.18
  47.1 6.0 %collective-permute-done.11 = f32[2,32,1024]{2,1,0:T(8,128)S(1)} collective-permute-done((f32[2,32,1024]{2,1,0:T(8,128)S(1)}, f32[2,32,1024]{2,1,0:T(8,128)S(1)}, u32[]{:S(2)}, u32[]{:S(2)}) %collective-permute-start.11) | collective-permute-done | bytes 262176 | tf_op jit(solution)/shard_map/ppermute | solution.py:430
  53.2 2.6 %collective-permute-start.12 = (f32[2,32,1024]{2,1,0:T(8,128)S(1)}, f32[2,32,1024]{2,1,0:T(8,128)S(1)}, u32[]{:S(2)}, u32[]{:S(2)}) collective-permute-start(f32[2,32,1024]{2,1,0:T(8,128)S(1)} %add.48), channel_id=1, source_target_pairs={{0,4},{2,6},{4,0},{6,2},{8,12},{10,14},{12,8},{14,10},{16,20},{18,... | collective-permute-start | bytes 786440 | tf_op jit(solution)/shard_map/ppermute | solution.py:430
  55.8 0.0 collective-permute-done.18
  55.8 0.7 collective-permute-start.20
  56.5 1.0 %collective-permute-start.19 = (f32[32,1024]{1,0:T(8,128)S(1)}, f32[32,1024]{1,0:T(8,128)S(1)}, u32[]{:S(2)}, u32[]{:S(2)}) collective-permute-start(f32[32,1024]{1,0:T(8,128)S(1)} %get-tuple-element.69), channel_id=1, source_target_pairs={{0,2},{1,3},{2,0},{3,1},{4,6},{5,7},{6,4},{7,5},{8,10},{9,11},{10,... | collective-permute-start | bytes 393224 | tf_op jit(solution)/shard_map/ppermute | solution.py:438
  57.5 0.5 collective-permute-start.21
  58.0 4.0 %collective-permute-done.12 = f32[2,32,1024]{2,1,0:T(8,128)S(1)} collective-permute-done((f32[2,32,1024]{2,1,0:T(8,128)S(1)}, f32[2,32,1024]{2,1,0:T(8,128)S(1)}, u32[]{:S(2)}, u32[]{:S(2)}) %collective-permute-start.12) | collective-permute-done | bytes 262176 | tf_op jit(solution)/shard_map/ppermute | solution.py:430
  62.0 1.6 %collective-permute-start.15 = (f32[32,1024]{1,0:T(8,128)S(1)}, f32[32,1024]{1,0:T(8,128)S(1)}, u32[]{:S(2)}, u32[]{:S(2)}) collective-permute-start(f32[32,1024]{1,0:T(8,128)S(1)} %get-tuple-element.70.refs_4_), channel_id=1, source_target_pairs={{0,1},{1,0},{2,3},{3,2},{4,5},{5,4},{6,7},{7,6},{8,9},{9,8},{10,11... | collective-permute-start | bytes 393224 | tf_op jit(solution)/shard_map/ppermute | solution.py:438
  63.6 0.9 %collective-permute-done.21.refs_3_ = f32[32,1024]{1,0:T(8,128)S(1)} collective-permute-done((f32[32,1024]{1,0:T(8,128)S(1)}, f32[32,1024]{1,0:T(8,128)S(1)}, u32[]{:S(2)}, u32[]{:S(2)}) %collective-permute-start.21) | collective-permute-done | bytes 131104 | tf_op jit(solution)/shard_map/ppermute | solution.py:438
  64.6 0.6 collective-permute-start.14
  65.1 0.0 collective-permute-done.20.refs_2_
  65.1 0.4 collective-permute-start.13
  65.5 0.0 collective-permute-done.19.refs_1_
  65.5 3.6 %update_0.1.refs_8_ = f32[8,128,4096]{2,1,0:T(8,128)} custom-call(bf16[4,256,128]{2,1,0:T(8,128)(2,1)S(1)} %get-tuple-element.56.refs_0_, f32[32,1024]{1,0:T(8,128)S(1)} %collective-permute-done.19.refs_1_, f32[32,1024]{1,0:T(8,128)S(1)} %collective-permute-done.20.refs_2_, f32[32,1024]{1,0:T(8,128)S(1)} %collective-permute-done.21.refs_3_, ...), custom_call_target="tpu_custom_call" | custom-call | flops 201326592 | bytes 8388608 | tf_op jit(solution)/shard_map/update_0/pallas_call | solution.py:404
  69.2 0.0 collective-permute-done.15.refs_3_
  69.2 1.0 %collective-permute-done.14.refs_2_ = f32[32,1024]{1,0:T(8,128)S(1)} collective-permute-done((f32[32,1024]{1,0:T(8,128)S(1)}, f32[32,1024]{1,0:T(8,128)S(1)}, u32[]{:S(2)}, u32[]{:S(2)}) %collective-permute-start.14) | collective-permute-done | bytes 131104 | tf_op jit(solution)/shard_map/ppermute | solution.py:438
  70.2 0.0 collective-permute-done.13.refs_1_
  70.2 0.0 collective-permute-done.16.refs_7_
  70.2 4.3 %update_1.1 = (f32[8,128,4096]{2,1,0:T(8,128)}, f32[4,32,4096]{2,1,0:T(8,128)}) custom-call(bf16[4,256,128]{2,1,0:T(8,128)(2,1)S(1)} %get-tuple-element.56.refs_0_, f32[32,1024]{1,0:T(8,128)S(1)} %collective-permute-done.13.refs_1_, f32[32,1024]{1,0:T(8,128)S(1)} %collective-permute-done.14.refs_2_, ...), custom_call_target="tpu_custom_call", output_to_operand_aliasing={{0}: (8, {})} | custom-call | flops 201326592 | bytes 8388608 | tf_op jit(solution)/shard_map/update_1/pallas_call | solution.py:404
  (9 shorter events, 0.2 us)
Async XLA Ops:
  0.6 7.9 %copy-start = (bf16[4,32,4096]{2,1,0:T(8,128)(2,1)S(1)}, bf16[4,32,4096]{2,1,0:T(8,128)(2,1)}, u32[]{:S(2)}) copy-start(bf16[4,32,4096]{2,1,0:T(8,128)(2,1)} %refs_12_.1) | copy-start | bytes 3145732
  5.3 10.1 %collective-permute-start = (f32[32,1152]{1,0:T(8,128)}, f32[32,1152]{1,0:T(8,128)S(1)}, u32[]{:S(2)}, u32[]{:S(2)}) collective-permute-start(f32[32,1152]{1,0:T(8,128)} %get-tuple-element.36), channel_id=1, source_target_pairs={{0,1},{1,0},{2,3},{3,2},{4,5},{5,4},{6,7},{7,6},{8,9},{9,8},{10,11... | collective-permute-start | bytes 442376 | tf_op jit(solution)/shard_map/ppermute | solution.py:438
  8.3 7.3 %collective-permute-start.1 = (f32[32,1152]{1,0:T(8,128)}, f32[32,1152]{1,0:T(8,128)S(1)}, u32[]{:S(2)}, u32[]{:S(2)}) collective-permute-start(f32[32,1152]{1,0:T(8,128)} %get-tuple-element.37), channel_id=1, source_target_pairs={{0,2},{1,3},{2,0},{3,1},{4,6},{5,7},{6,4},{7,5},{8,10},{9,11},{10,... | collective-permute-start | bytes 442376 | tf_op jit(solution)/shard_map/ppermute | solution.py:438
  8.3 7.6 %collective-permute-start.2 = (f32[32,1152]{1,0:T(8,128)}, f32[32,1152]{1,0:T(8,128)S(1)}, u32[]{:S(2)}, u32[]{:S(2)}) collective-permute-start(f32[32,1152]{1,0:T(8,128)} %get-tuple-element.38), channel_id=1, source_target_pairs={{0,3},{1,2},{2,1},{3,0},{4,7},{5,6},{6,5},{7,4},{8,11},{9,10},{10,... | collective-permute-start | bytes 442376 | tf_op jit(solution)/shard_map/ppermute | solution.py:438
  8.6 26.9 %collective-permute-start.5 = (f32[4,32,2048]{2,1,0:T(8,128)S(1)}, f32[4,32,2048]{2,1,0:T(8,128)S(1)}, u32[]{:S(2)}, u32[]{:S(2)}) collective-permute-start(f32[4,32,2048]{2,1,0:T(8,128)S(1)} %dynamic-slice_convert_fusion), channel_id=1, source_target_pairs={{0,2},{2,0},{4,6},{6,4},{8,10},{10,8},{12,14},{14,12},{16,18},{18,... | collective-permute-start | bytes 3145736 | tf_op jit(solution)/shard_map/ppermute | solution.py:430
  9.0 0.8 %copy-start.2 = (bf16[32,512]{1,0:T(8,128)(2,1)S(1)}, bf16[32,512]{1,0:T(8,128)(2,1)}, u32[]{:S(2)}) copy-start(bf16[32,512]{1,0:T(8,128)(2,1)} %get-tuple-element.45.refs_0_) | copy-start | bytes 98308
  9.8 5.8 %copy-start.4 = (f32[32,1152]{1,0:T(8,128)S(1)}, f32[32,1152]{1,0:T(8,128)}, u32[]{:S(2)}) copy-start(f32[32,1152]{1,0:T(8,128)} %get-tuple-element.35) | copy-start | bytes 442372
  9.8 25.7 %copy-start.1 = (f32[64,256]{1,0:T(8,128)S(1)}, f32[64,256]{1,0:T(8,128)}, u32[]{:S(2)}) copy-start(f32[64,256]{1,0:T(8,128)} %refs_1_.7) | copy-start | bytes 196612
  9.8 25.7 %copy-start.3 = (s32[64]{0:T(128)S(1)}, s32[64]{0:T(128)}, u32[]{:S(2)}) copy-start(s32[64]{0:T(128)} %refs_0_.5) | copy-start | bytes 772
  13.6 6.4 %collective-permute-start.6 = (f32[32,1024]{1,0:T(8,128)S(1)}, f32[32,1024]{1,0:T(8,128)S(1)}, u32[]{:S(2)}, u32[]{:S(2)}) collective-permute-start(f32[32,1024]{1,0:T(8,128)S(1)} %get-tuple-element.47), channel_id=1, source_target_pairs={{0,1},{1,0},{2,3},{3,2},{4,5},{5,4},{6,7},{7,6},{8,9},{9,8},{10,11... | collective-permute-start | bytes 393224 | tf_op jit(solution)/shard_map/ppermute | solution.py:438
  15.3 4.7 %collective-permute-start.7 = (f32[32,1024]{1,0:T(8,128)S(1)}, f32[32,1024]{1,0:T(8,128)S(1)}, u32[]{:S(2)}, u32[]{:S(2)}) collective-permute-start(f32[32,1024]{1,0:T(8,128)S(1)} %get-tuple-element.48), channel_id=1, source_target_pairs={{0,2},{1,3},{2,0},{3,1},{4,6},{5,7},{6,4},{7,5},{8,10},{9,11},{10,... | collective-permute-start | bytes 393224 | tf_op jit(solution)/shard_map/ppermute | solution.py:438
  15.6 6.2 %collective-permute-start.8 = (f32[32,1024]{1,0:T(8,128)S(1)}, f32[32,1024]{1,0:T(8,128)S(1)}, u32[]{:S(2)}, u32[]{:S(2)}) collective-permute-start(f32[32,1024]{1,0:T(8,128)S(1)} %get-tuple-element.49), channel_id=1, source_target_pairs={{0,3},{1,2},{2,1},{3,0},{4,7},{5,6},{6,5},{7,4},{8,11},{9,10},{10,... | collective-permute-start | bytes 393224 | tf_op jit(solution)/shard_map/ppermute | solution.py:438
  16.0 9.2 %collective-permute-start.3 = (f32[2,32,1152]{2,1,0:T(8,128)S(1)}, f32[2,32,1152]{2,1,0:T(8,128)S(1)}, u32[]{:S(2)}, u32[]{:S(2)}) collective-permute-start(f32[2,32,1152]{2,1,0:T(8,128)S(1)} %pad_maximum_fusion.refs_3_), channel_id=1, source_target_pairs={{0,4},{2,6},{4,0},{6,2},{8,12},{10,14},{12,8},{14,10},{16,20},{18,... | collective-permute-start | bytes 884744 | tf_op jit(solution)/shard_map/ppermute | solution.py:430
  21.8 8.9 %collective-permute-start.9 = (f32[2,32,1024]{2,1,0:T(8,128)S(1)}, f32[2,32,1024]{2,1,0:T(8,128)S(1)}, u32[]{:S(2)}, u32[]{:S(2)}) collective-permute-start(f32[2,32,1024]{2,1,0:T(8,128)S(1)} %pad_maximum_fusion.1.refs_9_), channel_id=1, source_target_pairs={{0,4},{2,6},{4,0},{6,2},{8,12},{10,14},{12,8},{14,10},{16,20},{18,... | collective-permute-start | bytes 786440 | tf_op jit(solution)/shard_map/ppermute | solution.py:430
  25.2 10.3 %collective-permute-start.4 = (f32[2,32,1152]{2,1,0:T(8,128)S(1)}, f32[2,32,1152]{2,1,0:T(8,128)S(1)}, u32[]{:S(2)}, u32[]{:S(2)}) collective-permute-start(f32[2,32,1152]{2,1,0:T(8,128)S(1)} %collective-permute-done.3.refs_4_), channel_id=1, source_target_pairs={{0,8},{2,10},{4,28},{6,30},{8,16},{10,18},{12,4},{14,6},{16,24},{1... | collective-permute-start | bytes 884744 | tf_op jit(solution)/shard_map/ppermute | solution.py:430
  30.8 9.5 %collective-permute-start.10 = (f32[2,32,1024]{2,1,0:T(8,128)S(1)}, f32[2,32,1024]{2,1,0:T(8,128)S(1)}, u32[]{:S(2)}, u32[]{:S(2)}) collective-permute-start(f32[2,32,1024]{2,1,0:T(8,128)S(1)} %collective-permute-done.9.refs_10_), channel_id=1, source_target_pairs={{0,8},{2,10},{4,0},{6,2},{8,16},{10,18},{12,4},{14,6},{16,24},{18,... | collective-permute-start | bytes 786440 | tf_op jit(solution)/shard_map/ppermute | solution.py:430
  39.5 7.4 %collective-permute-start.17 = (f32[2,32,1024]{2,1,0:T(8,128)S(1)}, f32[2,32,1024]{2,1,0:T(8,128)S(1)}, u32[]{:S(2)}, u32[]{:S(2)}) collective-permute-start(f32[2,32,1024]{2,1,0:T(8,128)S(1)} %get-tuple-element.65), channel_id=1, source_target_pairs={{0,4},{2,6},{4,12},{6,14},{8,0},{10,2},{12,20},{14,22},{16,8},{18,... | collective-permute-start | bytes 786440 | tf_op jit(solution)/shard_map/ppermute | solution.py:430
  44.3 25.9 %collective-permute-start.16 = (f32[4,32,2048]{2,1,0:T(8,128)S(1)}, f32[4,32,2048]{2,1,0:T(8,128)S(1)}, u32[]{:S(2)}, u32[]{:S(2)}) collective-permute-start(f32[4,32,2048]{2,1,0:T(8,128)S(1)} %get-tuple-element.62), channel_id=1, source_target_pairs={{0,2},{2,0},{4,6},{6,4},{8,10},{10,8},{12,14},{14,12},{16,18},{18,... | collective-permute-start | bytes 3145736 | tf_op jit(solution)/shard_map/ppermute | solution.py:430
  44.4 8.7 %collective-permute-start.11 = (f32[2,32,1024]{2,1,0:T(8,128)S(1)}, f32[2,32,1024]{2,1,0:T(8,128)S(1)}, u32[]{:S(2)}, u32[]{:S(2)}) collective-permute-start(f32[2,32,1024]{2,1,0:T(8,128)S(1)} %get-tuple-element.59), channel_id=1, source_target_pairs={{0,24},{2,26},{4,12},{6,14},{8,0},{10,2},{12,20},{14,22},{16,8},{1... | collective-permute-start | bytes 786440 | tf_op jit(solution)/shard_map/ppermute | solution.py:430
  47.0 8.8 %collective-permute-start.18 = (f32[2,32,1024]{2,1,0:T(8,128)S(1)}, f32[2,32,1024]{2,1,0:T(8,128)S(1)}, u32[]{:S(2)}, u32[]{:S(2)}) collective-permute-start(f32[2,32,1024]{2,1,0:T(8,128)S(1)} %add.53), channel_id=1, source_target_pairs={{0,4},{2,6},{4,0},{6,2},{8,12},{10,14},{12,8},{14,10},{16,20},{18,... | collective-permute-start | bytes 786440 | tf_op jit(solution)/shard_map/ppermute | solution.py:430
  53.2 8.8 %collective-permute-start.12 = (f32[2,32,1024]{2,1,0:T(8,128)S(1)}, f32[2,32,1024]{2,1,0:T(8,128)S(1)}, u32[]{:S(2)}, u32[]{:S(2)}) collective-permute-start(f32[2,32,1024]{2,1,0:T(8,128)S(1)} %add.48), channel_id=1, source_target_pairs={{0,4},{2,6},{4,0},{6,2},{8,12},{10,14},{12,8},{14,10},{16,20},{18,... | collective-permute-start | bytes 786440 | tf_op jit(solution)/shard_map/ppermute | solution.py:430
  55.8 9.3 %collective-permute-start.20 = (f32[32,1024]{1,0:T(8,128)S(1)}, f32[32,1024]{1,0:T(8,128)S(1)}, u32[]{:S(2)}, u32[]{:S(2)}) collective-permute-start(f32[32,1024]{1,0:T(8,128)S(1)} %get-tuple-element.69), channel_id=1, source_target_pairs={{0,3},{1,2},{2,1},{3,0},{4,7},{5,6},{6,5},{7,4},{8,11},{9,10},{10,... | collective-permute-start | bytes 393224 | tf_op jit(solution)/shard_map/ppermute | solution.py:438
  56.5 9.0 %collective-permute-start.19 = (f32[32,1024]{1,0:T(8,128)S(1)}, f32[32,1024]{1,0:T(8,128)S(1)}, u32[]{:S(2)}, u32[]{:S(2)}) collective-permute-start(f32[32,1024]{1,0:T(8,128)S(1)} %get-tuple-element.69), channel_id=1, source_target_pairs={{0,2},{1,3},{2,0},{3,1},{4,6},{5,7},{6,4},{7,5},{8,10},{9,11},{10,... | collective-permute-start | bytes 393224 | tf_op jit(solution)/shard_map/ppermute | solution.py:438
  57.5 7.0 %collective-permute-start.21 = (f32[32,1024]{1,0:T(8,128)S(1)}, f32[32,1024]{1,0:T(8,128)S(1)}, u32[]{:S(2)}, u32[]{:S(2)}) collective-permute-start(f32[32,1024]{1,0:T(8,128)S(1)} %get-tuple-element.68.refs_4_), channel_id=1, source_target_pairs={{0,1},{1,0},{2,3},{3,2},{4,5},{5,4},{6,7},{7,6},{8,9},{9,8},{10,11... | collective-permute-start | bytes 393224 | tf_op jit(solution)/shard_map/ppermute | solution.py:438
  62.0 7.1 %collective-permute-start.15 = (f32[32,1024]{1,0:T(8,128)S(1)}, f32[32,1024]{1,0:T(8,128)S(1)}, u32[]{:S(2)}, u32[]{:S(2)}) collective-permute-start(f32[32,1024]{1,0:T(8,128)S(1)} %get-tuple-element.70.refs_4_), channel_id=1, source_target_pairs={{0,1},{1,0},{2,3},{3,2},{4,5},{5,4},{6,7},{7,6},{8,9},{9,8},{10,11... | collective-permute-start | bytes 393224 | tf_op jit(solution)/shard_map/ppermute | solution.py:438
  64.6 5.6 %collective-permute-start.14 = (f32[32,1024]{1,0:T(8,128)S(1)}, f32[32,1024]{1,0:T(8,128)S(1)}, u32[]{:S(2)}, u32[]{:S(2)}) collective-permute-start(f32[32,1024]{1,0:T(8,128)S(1)} %get-tuple-element.71), channel_id=1, source_target_pairs={{0,3},{1,2},{2,1},{3,0},{4,7},{5,6},{6,5},{7,4},{8,11},{9,10},{10,... | collective-permute-start | bytes 393224 | tf_op jit(solution)/shard_map/ppermute | solution.py:438
  65.1 5.1 %collective-permute-start.13 = (f32[32,1024]{1,0:T(8,128)S(1)}, f32[32,1024]{1,0:T(8,128)S(1)}, u32[]{:S(2)}, u32[]{:S(2)}) collective-permute-start(f32[32,1024]{1,0:T(8,128)S(1)} %get-tuple-element.71), channel_id=1, source_target_pairs={{0,2},{1,3},{2,0},{3,1},{4,6},{5,7},{6,4},{7,5},{8,10},{9,11},{10,... | collective-permute-start | bytes 393224 | tf_op jit(solution)/shard_map/ppermute | solution.py:438

commit v4 on v3

--- a/solution.py
+++ b/solution.py
@@ -224,26 +224,50 @@
         out_ref[zp] = stacked.T.astype(BF16)
 
 
-def residual_kernel(dims, first, last, half, rdev, zdev, offset, width, *refs):
+def prepare_kernel(dims, rdev, half, width, order_ref, table_ref, foot_ref, _, vol_ref, kept_ref, left_ref, sems, rows_ref):
+    zdev = vol_ref.shape[0]
+    copies = []
+    for h, zp, slices, start in volume_pieces(dims, zdev, half, 0):
+        source = vol_ref.at[slices, :, pl.ds(start, width)]
+        copies.append(pltpu.make_async_copy(source, kept_ref.at[h, slices], sems.at[h, zp]))
+        copies[-1].start()
+    update_weights(dims, zdev, rdev, foot_ref[0, :, width:], order_ref, table_ref, rows_ref, left_ref)
+    for copy in copies:
+        copy.wait()
+
+
+def prepare_step(dims, rdev, width, order, table, own, after, volume):
+    per, groups, zb, cells = dims
+    zdev, _, total = volume.shape
+    depth = -(-3 * groups * SUBLANES // LANES) * LANES
+    return pl.pallas_call(
+        functools.partial(prepare_kernel, dims, rdev, total // 2, width),
+        in_specs=[IN_SMEM, IN_VMEM, IN_VMEM, ANYWHERE, ANYWHERE],
+        out_specs=[IN_VMEM, IN_VMEM],
+        out_shape=[
+            jax.ShapeDtypeStruct((2, zdev, cells, width), F32),
+            jax.ShapeDtypeStruct((zdev // zb, zb * cells, depth), BF16),
+        ],
+        scratch_shapes=[
+            pltpu.SemaphoreType.DMA((2, zdev // zb)),
+            pltpu.VMEM((groups * SUBLANES, table.shape[1]), F32),
+        ],
+        compiler_params=pltpu.CompilerParams(vmem_limit_bytes=40 * MIB),
+        cost_estimate=pl.CostEstimate(flops=0, bytes_accessed=8 * zdev * cells * width, transcendentals=0),
+        name="prepare",
+    )(order, table, own, after, volume)
+
+
+def residual_kernel(dims, first, half, rdev, zdev, offset, width, *refs):
     per, groups, zb, cells = dims
     block = zdev * per
-    loads = []
-    if first or last:
-        order_ref, table_ref, vol_ref, *refs, sems = refs
-    if last:
-        foot_ref, *refs = refs
-    if not first:
+    if first:
+        order_ref, table_ref, *refs = refs
+    else:
         mats, inverse_ref, refs = refs[:4], refs[4], refs[5:]
     sums_refs, (mine_ref, theirs_ref), refs = refs[:3], refs[3:5], refs[5:]
     if not first:
         mine_before, sent_before, *refs = refs
-    if first or last:
-        kept_ref, *refs = refs
-        start = lax.rem(lax.axis_index("slab") + (0 if first else 1), 2) * half
-        columns = pl.ds(pl.multiple_of(start, LANES), kept_ref.shape[2])
-        for z in range(zdev):
-            loads.append(pltpu.make_async_copy(vol_ref.at[z, :, columns], kept_ref.at[z], sems.at[z]))
-            loads[z].start()
     mine_out, sent_out, *refs = refs
     if not first:
         mine_out[:, :, :offset] = mine_before[...]
@@ -251,7 +275,6 @@
     outs, refs = refs[:3], refs[3:]
     if first:
         foot = jnp.concatenate([r[i, :, width:] for r in sums_refs for i in range(2)], axis=0)
-        refs[5][...] = sums_refs[0][0, :, width:]
         kernel = footprint_matrix(dims, zdev, rdev, foot)
         count, rows = kernel.shape
         kernel_t = kernel.T
@@ -284,51 +307,30 @@
         for i, ref in enumerate(outs):
             for j in range(2):
                 ref[j, :, columns] = given[(2 * i + j) * block:(2 * i + j + 1) * block]
-    if last:
-        update_weights(dims, zdev, rdev, foot_ref[...], order_ref, table_ref, refs[1], refs[0])
-    for load in loads:
-        load.wait()
-
-
-def residual_step(dims, chunk, offset, width, load_width, mats, before, order, table, volume, sums, measured, theirs):
-    per, groups, zb, cells = dims
-    zdev = volume.shape[0]
+
+
+def residual_step(dims, zdev, chunk, offset, width, mats, before, order, table, sums, measured, theirs):
+    per, groups, zb, cells = dims
     _, rdev, total = measured.shape
     first = chunk == 0
     block = zdev * per
     count, rows = 6 * block, 2 * per * rdev
-    last = chunk == CHUNKS - 1
-    assert not (first and last)
     given = jax.ShapeDtypeStruct((2, block, width), F32)
     piece = jax.ShapeDtypeStruct((per, rdev, offset + width), F32)
     shapes = [piece, piece, given, given, given]
-    args, specs, scratch = [], [], []
-    if first or last:
-        args, specs = [order, table, volume], [IN_SMEM, IN_VMEM, ANYWHERE]
-        shapes = [jax.ShapeDtypeStruct((zdev, cells, load_width), F32)] + shapes
-    if last:
-        depth = -(-3 * groups * SUBLANES // LANES) * LANES
-        shapes.append(jax.ShapeDtypeStruct((zdev // zb, zb * cells, depth), BF16))
-        scratch.append(pltpu.VMEM((groups * SUBLANES, table.shape[1]), F32))
-        args += [mats[5]]
-        specs += [IN_VMEM]
-    if first:
+    if first:
+        args, specs = [order, table], [IN_SMEM, IN_VMEM]
         ahead, back = jax.ShapeDtypeStruct((rows, count), BF16), jax.ShapeDtypeStruct((count, rows), BF16)
         shapes += [ahead, ahead, back, back, jax.ShapeDtypeStruct((rows, LANES), F32)]
-        shapes += [jax.ShapeDtypeStruct((block, LANES), F32)]
-    else:
-        args += mats[:5]
-        specs += [IN_VMEM] * 5
-    if first or last:
-        scratch.append(pltpu.SemaphoreType.DMA((zdev,)))
+    else:
+        args, specs = list(mats), [IN_VMEM] * len(mats)
     args += [*sums, measured, theirs, *before]
     specs += [IN_VMEM] * (5 + len(before))
     return pl.pallas_call(
-        functools.partial(residual_kernel, dims, first, last, total // 2, rdev, zdev, offset, width),
+        functools.partial(residual_kernel, dims, first, total // 2, rdev, zdev, offset, width),
         in_specs=specs,
         out_specs=[IN_VMEM] * len(shapes),
         out_shape=shapes,
-        scratch_shapes=scratch,
         compiler_params=pltpu.CompilerParams(vmem_limit_bytes=30 * MIB),
         cost_estimate=pl.CostEstimate(
             flops=12 * count * rows * width, bytes_accessed=8 * width * (count + rows), transcendentals=0
@@ -342,11 +344,8 @@
     count = groups * SUBLANES
     left_ref, backs, refs = refs[0], refs[1:1 + 2 * groups], refs[1 + 2 * groups:]
     backs = [backs[-1], *backs[groups:-1], *backs[:groups]]
-    if first:
-        vols, refs = refs[:2], refs[2:]
-    else:
-        vols, refs = [refs[0].at[0], refs[0].at[1]], refs[1:]
-    zdev, depth = vols[0].shape[0], left_ref.shape[2]
+    vol_ref, *refs = refs
+    zdev, depth = vol_ref.shape[1], left_ref.shape[2]
     if last:
         pieces, refs = refs[:2], refs[2:]
     if not first:
@@ -368,7 +367,7 @@
             change = dot(left, jnp.concatenate([high, low, high, pad], axis=0))
             for z in range(zb):
                 buf[h, zp * zb + z, :, piece] = (
-                    vols[h][zp * zb + z, :, piece] + change[z * cells:(z + 1) * cells]
+                    vol_ref[h, zp * zb + z, :, piece] + change[z * cells:(z + 1) * cells]
                 )
         leaving.append(
             pltpu.make_async_copy(buf.at[h, slices], out_ref.at[slices, :, pl.ds(start, width)], sems.at[h, zp])
@@ -387,7 +386,7 @@
     per, groups, zb, cells = dims
     zdev, _, total = volume.shape
     first, last = chunk == 0, chunk == CHUNKS - 1
-    args = [left, *backs[groups:], *backs[1:groups], backs[0], *kept]
+    args = [left, *backs[groups:], *backs[1:groups], backs[0], kept]
     shapes = [jax.ShapeDtypeStruct(volume.shape, F32)]
     scratch = [pltpu.VMEM((2, zdev, cells, width), F32), pltpu.SemaphoreType.DMA((2, zdev // zb))]
     if last:
@@ -459,7 +458,7 @@
         lax.dynamic_slice_in_dim(measured, (1 - odd) * half, half, 2).astype(F32), lambda s: s ^ 1
     )
 
-    sums, kept, left = [], [[] for _ in range(CHUNKS)], None
+    sums, kept, left = [], [], None
     for c in range(CHUNKS):
         parts = ray_sums(
             dims, c, offsets[c], widths[c], left, (order, foot_start, foot_len), table, volume
@@ -467,23 +466,26 @@
         if c == 0:
             left = parts[2 * groups]
         else:
-            kept[c].append(parts[2 * groups])
+            kept.append(parts[2 * groups])
         parts = [spread(parts[h * groups + d], h, d) for h in range(2) for d in range(groups)]
         if c:
             parts, _ = lax.optimization_barrier((parts, sums[-1][0]))
         own = jnp.stack([sum(parts[:groups]), sum(parts[groups:])])
         near = along(own, facing)
+        if c == 0:
+            first_columns, update_left = prepare_step(dims, rdev, widths[0], order, table, own, near, volume)
+            kept.append(first_columns)
+        if c == 1:
+            near, kept[0] = lax.optimization_barrier((near, kept[0]))
         far = along(near, beyond(c))
         sums.append((own, near, far))
     pieces, given, mats = [], [], None
     for c in range(CHUNKS):
-        loaded, mine, sent, own, near, far, *rest = residual_step(
-            dims, c, offsets[c], widths[c], widths[0], mats, pieces, order, table, volume, sums[c], measured, theirs
+        mine, sent, own, near, far, *rest = residual_step(
+            dims, zdev, c, offsets[c], widths[c], mats, pieces, order, table, sums[c], measured, theirs
         )
-        kept[0].append(loaded)
         pieces = [mine, sent]
         mats = rest if c == 0 else mats
-        left = rest[0]
         near = near + along(far, back_from_beyond(c))
         arrived = along(near, facing)
         halves = [own[i] + arrived[i] for i in range(2)]
@@ -491,7 +493,7 @@
     pieces = [mine, along(sent, lambda s: s ^ 1)]
     out = None
     for c in range(CHUNKS):
-        out, *res = update_step(dims, c, offsets[c], widths[c], left, given[c], pieces, kept[c], volume, out)
+        out, *res = update_step(dims, c, offsets[c], widths[c], update_left, given[c], pieces, kept[c], volume, out)
     return out, res[0]
 
 

time: 74.7 us -> 72.7 us (0.973)
  waiting for transfers between devices: 24.4 us -> 21.9 us
  starting transfers between devices: 23.8 us -> 25 us
    ppermute x10, waiting for transfers between devices: 18.3 us -> 15.5 us  [along(): return lax.ppermute(value, 'slab', pairs)]
    ppermute x10, starting transfers between devices: 13.6 us -> 14.9 us  [along(): return lax.ppermute(value, 'slab', pairs)]
    pallas_call x2 -> x3, Pallas kernels: 7.99 us -> 7.42 us  [the longest x1 4.09 us: prepare_step(): pl.pallas_call(functools.partial(prepare_kernel, dims, rdev, total // 2,...]
  transfers between devices with their start and end apart: 22 -> 22, of which waited for: 9 -> 10; matrix products, arithmetic and copies ran while one was open for 0% -> 0% of each run, Pallas kernels for 21% -> 20%
where the time goes in v4:
time: 72.7 us; the launch traced here: 72.6 us
  starting transfers between devices  25 us (34%)
  Pallas kernels  23.8 us (33%)
  waiting for transfers between devices  21.9 us (30%)
  between operations  0.81 us (1%)
  local copies, waits for them, and re-layouts  0.78 us (1%)
    ppermute x10, waiting for transfers between devices, along(): return lax.ppermute(value, 'slab', pairs)  15.5 us
    ppermute x10, starting transfers between devices, along(): return lax.ppermute(value, 'slab', pairs)  14.9 us
    ppermute x12, starting transfers between devices, spread(): return lax.ppermute(value, ('slab', 'ang'), pairs)  10.1 us
    pallas_call x2, Pallas kernels, ray_sums(): pl.pallas_call(functools.partial(rays_kernel, dims, first, total // 2, of...  8.46 us
    pallas_call x2, Pallas kernels, update_step(): pl.pallas_call(functools.partial(update_kernel, dims, first, last, total...  7.93 us
    ppermute x12, waiting for transfers between devices, spread(): return lax.ppermute(value, ('slab', 'ang'), pairs)  6.39 us
    pallas_call x1, Pallas kernels, prepare_step(): pl.pallas_call(functools.partial(prepare_kernel, dims, rdev, total // 2,...  4.09 us
    pallas_call x2, Pallas kernels, residual_step(): pl.pallas_call(functools.partial(residual_kernel, dims, first, total // 2...  3.33 us
  transfers between devices with their start and end apart: 22, of which 10 were waited for; matrix products, arithmetic and copies ran while one was open for 0% of the time, Pallas kernels for 20%

profile of v4, /device:TPU:0, one launch (start us, length us, event | category | flops | bytes accessed | tf_op | source)
XLA Modules:
  0.0 72.6 jit_solution(17582119786252755159)
XLA Ops:
  0.6 0.0 copy-start.1
  0.6 0.0 copy-start.3
  0.7 0.0 copy-start
  0.7 4.7 %ray_sums_0.1 = (f32[32,1152]{1,0:T(8,128)}, f32[32,1152]{1,0:T(8,128)}, f32[32,1152]{1,0:T(8,128)}, f32[32,1152]{1,0:T(8,128)}, bf16[32,512]{1,0:T(8,128)(2,1)}) custom-call(s32[64]{0:T(128)} %refs_0_.3, s32[1,4]{1,0:T(1,128)} %refs_1_.3, s32[1,4]{1,0:T(1,128)} %refs_2_.1, f32[64,256]{1,0:T(8,128)} %refs_1_.4, f32[8,128,4096]{2,1,0:T(8,128)} %refs_1_.5), custom_call_target="tpu_custom_call" | custom-call | flops 67108864 | bytes 8388608 | tf_op jit(solution)/shard_map/ray_sums_0/pallas_call | solution.py:169
  5.3 0.0 copy-start.4
  5.3 3.0 %collective-permute-start = (f32[32,1152]{1,0:T(8,128)}, f32[32,1152]{1,0:T(8,128)S(1)}, u32[]{:S(2)}, u32[]{:S(2)}) collective-permute-start(f32[32,1152]{1,0:T(8,128)} %get-tuple-element.36), channel_id=1, source_target_pairs={{0,1},{1,0},{2,3},{3,2},{4,5},{5,4},{6,7},{7,6},{8,9},{9,8},{10,11... | collective-permute-start | bytes 442376 | tf_op jit(solution)/shard_map/ppermute | solution.py:437
  8.4 0.0 collective-permute-start.1
  8.4 0.2 collective-permute-start.2
  8.6 0.0 copy-done
  8.6 0.1 dynamic-slice_convert_fusion
  8.7 0.4 collective-permute-start.5
  9.1 0.0 copy-start.2
  9.1 0.8 %copy-done.2 = bf16[32,512]{1,0:T(8,128)(2,1)S(1)} copy-done((bf16[32,512]{1,0:T(8,128)(2,1)S(1)}, bf16[32,512]{1,0:T(8,128)(2,1)}, u32[]{:S(2)}) %copy-start.2) | copy-done | bytes 32792
  9.8 3.8 %ray_sums_1.1 = (f32[32,1024]{1,0:T(8,128)S(1)}, f32[32,1024]{1,0:T(8,128)S(1)}, f32[32,1024]{1,0:T(8,128)S(1)}, f32[32,1024]{1,0:T(8,128)S(1)}, f32[2,8,128,1024]{3,2,1,0:T(8,128)S(1)}) custom-call(bf16[32,512]{1,0:T(8,128)(2,1)S(1)} %copy-done.2, f32[8,128,4096]{2,1,0:T(8,128)} %refs_1_.5), custom_call_target="tpu_custom_call" | custom-call | flops 67108864 | bytes 8388608 | tf_op jit(solution)/shard_map/ray_sums_1/pallas_call | solution.py:169
  13.6 1.7 %collective-permute-start.6 = (f32[32,1024]{1,0:T(8,128)S(1)}, f32[32,1024]{1,0:T(8,128)S(1)}, u32[]{:S(2)}, u32[]{:S(2)}) collective-permute-start(f32[32,1024]{1,0:T(8,128)S(1)} %get-tuple-element.47), channel_id=1, source_target_pairs={{0,1},{1,0},{2,3},{3,2},{4,5},{5,4},{6,7},{7,6},{8,9},{9,8},{10,11... | collective-permute-start | bytes 393224 | tf_op jit(solution)/shard_map/ppermute | solution.py:437
  15.3 0.0 collective-permute-done
  15.3 0.2 collective-permute-start.7
  15.6 0.0 copy-done.4
  15.6 0.0 collective-permute-done.1
  15.6 0.3 collective-permute-start.8
  15.9 0.0 collective-permute-done.2
  16.0 1.7 %collective-permute-start.3 = (f32[2,32,1152]{2,1,0:T(8,128)S(1)}, f32[2,32,1152]{2,1,0:T(8,128)S(1)}, u32[]{:S(2)}, u32[]{:S(2)}) collective-permute-start(f32[2,32,1152]{2,1,0:T(8,128)S(1)} %pad_maximum_fusion.foot_ref.refs_2_), channel_id=1, source_target_pairs={{0,4},{2,6},{4,0},{6,2},{8,12},{10,14},{12,8},{14,10},{16,20},{18,... | collective-permute-start | bytes 884744 | tf_op jit(solution)/shard_map/ppermute | solution.py:429
  17.7 2.3 %collective-permute-done.6 = f32[32,1024]{1,0:T(8,128)S(1)} collective-permute-done((f32[32,1024]{1,0:T(8,128)S(1)}, f32[32,1024]{1,0:T(8,128)S(1)}, u32[]{:S(2)}, u32[]{:S(2)}) %collective-permute-start.6) | collective-permute-done | bytes 131104 | tf_op jit(solution)/shard_map/ppermute | solution.py:437
  20.0 0.0 collective-permute-done.7
  20.0 1.8 %collective-permute-done.8 = f32[32,1024]{1,0:T(8,128)S(1)} collective-permute-done((f32[32,1024]{1,0:T(8,128)S(1)}, f32[32,1024]{1,0:T(8,128)S(1)}, u32[]{:S(2)}, u32[]{:S(2)}) %collective-permute-start.8) | collective-permute-done | bytes 131104 | tf_op jit(solution)/shard_map/ppermute | solution.py:437
  21.8 1.9 %collective-permute-start.9 = (f32[2,32,1024]{2,1,0:T(8,128)S(1)}, f32[2,32,1024]{2,1,0:T(8,128)S(1)}, u32[]{:S(2)}, u32[]{:S(2)}) collective-permute-start(f32[2,32,1024]{2,1,0:T(8,128)S(1)} %pad_maximum_fusion.1.refs_5_), channel_id=1, source_target_pairs={{0,4},{2,6},{4,0},{6,2},{8,12},{10,14},{12,8},{14,10},{16,20},{18,... | collective-permute-start | bytes 786440 | tf_op jit(solution)/shard_map/ppermute | solution.py:429
  23.7 1.4 %collective-permute-done.3._.refs_3_ = f32[2,32,1152]{2,1,0:T(8,128)S(1)} collective-permute-done((f32[2,32,1152]{2,1,0:T(8,128)S(1)}, f32[2,32,1152]{2,1,0:T(8,128)S(1)}, u32[]{:S(2)}, u32[]{:S(2)}) %collective-permute-start.3) | collective-permute-done | bytes 294944 | tf_op jit(solution)/shard_map/ppermute | solution.py:429
  25.2 1.7 %collective-permute-start.4 = (f32[2,32,1152]{2,1,0:T(8,128)S(1)}, f32[2,32,1152]{2,1,0:T(8,128)S(1)}, u32[]{:S(2)}, u32[]{:S(2)}) collective-permute-start(f32[2,32,1152]{2,1,0:T(8,128)S(1)} %collective-permute-done.3._.refs_3_), channel_id=1, source_target_pairs={{0,8},{2,10},{4,28},{6,30},{8,16},{10,18},{12,4},{14,6},{16,24},{1... | collective-permute-start | bytes 884744 | tf_op jit(solution)/shard_map/ppermute | solution.py:429
  26.9 0.0 copy-done.1
  26.9 0.0 copy-done.3
  26.9 4.1 %prepare.1 = (f32[2,8,128,1024]{3,2,1,0:T(8,128)S(1)}, bf16[4,256,128]{2,1,0:T(8,128)(2,1)S(1)}) custom-call(s32[64]{0:T(128)S(1)} %copy-done.3, f32[64,256]{1,0:T(8,128)S(1)} %copy-done.1, f32[2,32,1152]{2,1,0:T(8,128)S(1)} %pad_maximum_fusion.foot_ref.refs_2_, f32[2,32,1152]{2,1,0:T(8,128)S(1)} %collective-permute-done.3._.refs_3_, f32[8,128,4096]{2,1,0:T(8,128)} %refs_1_.5), custom_call_target="tpu_custom_call" | custom-call | bytes 8388608 | tf_op jit(solution)/shard_map/prepare/pallas_call | solution.py:243
  31.0 0.0 collective-permute-done.9.refs_6_
  31.0 1.6 %collective-permute-start.10 = (f32[2,32,1024]{2,1,0:T(8,128)S(1)}, f32[2,32,1024]{2,1,0:T(8,128)S(1)}, u32[]{:S(2)}, u32[]{:S(2)}) collective-permute-start(f32[2,32,1024]{2,1,0:T(8,128)S(1)} %collective-permute-done.9.refs_6_), channel_id=1, source_target_pairs={{0,8},{2,10},{4,0},{6,2},{8,16},{10,18},{12,4},{14,6},{16,24},{18,... | collective-permute-start | bytes 786440 | tf_op jit(solution)/shard_map/ppermute | solution.py:429
  32.6 2.9 %collective-permute-done.4.refs_4_ = f32[2,32,1152]{2,1,0:T(8,128)S(1)} collective-permute-done((f32[2,32,1152]{2,1,0:T(8,128)S(1)}, f32[2,32,1152]{2,1,0:T(8,128)S(1)}, u32[]{:S(2)}, u32[]{:S(2)}) %collective-permute-start.4) | collective-permute-done | bytes 294944 | tf_op jit(solution)/shard_map/ppermute | solution.py:429
  35.5 0.0 collective-permute-done.5.refs_6_.refs_9_
  35.5 2.1 %residual_0.1 = (f32[4,32,1024]{2,1,0:T(8,128)S(1)}, f32[4,32,1024]{2,1,0:T(8,128)S(1)}, f32[2,32,1024]{2,1,0:T(8,128)S(1)}, f32[2,32,1024]{2,1,0:T(8,128)S(1)},...) custom-call(s32[64]{0:T(128)S(1)} %copy-done.3, ...), custom_call_target="tpu_custom_call" | custom-call | flops 603979776 | bytes 3670016 | tf_op jit(solution)/shard_map/residual_0/pallas_call | solution.py:329
  37.6 0.8 %collective-permute-start.17 = (f32[2,32,1024]{2,1,0:T(8,128)S(1)}, f32[2,32,1024]{2,1,0:T(8,128)S(1)}, u32[]{:S(2)}, u32[]{:S(2)}) collective-permute-start(f32[2,32,1024]{2,1,0:T(8,128)S(1)} %get-tuple-element.66), channel_id=1, source_target_pairs={{0,4},{2,6},{4,12},{6,14},{8,0},{10,2},{12,20},{14,22},{16,8},{18,... | collective-permute-start | bytes 786440 | tf_op jit(solution)/shard_map/ppermute | solution.py:429
  38.4 1.8 %collective-permute-done.10.refs_7_ = f32[2,32,1024]{2,1,0:T(8,128)S(1)} collective-permute-done((f32[2,32,1024]{2,1,0:T(8,128)S(1)}, f32[2,32,1024]{2,1,0:T(8,128)S(1)}, u32[]{:S(2)}, u32[]{:S(2)}) %collective-permute-start.10) | collective-permute-done | bytes 262176 | tf_op jit(solution)/shard_map/ppermute | solution.py:429
  40.2 1.2 %residual_1.1 = (f32[4,32,2048]{2,1,0:T(8,128)S(1)}, f32[4,32,2048]{2,1,0:T(8,128)S(1)}, f32[2,32,1024]{2,1,0:T(8,128)S(1)}, f32[2,32,1024]{2,1,0:T(8,128)S(1)}, f32[2,32,1024]{2,1,0:T(8,128)S(1)}) custom-call(bf16[256,192]{1,0:T(8,128)(2,1)S(1)} %get-tuple-element.40.refs_0_, bf16[256,192]{1,0:T(8,128)(2,1)S(1)} %get-tuple-element.41.refs_1_, ...), custom_call_target="tpu_custom_call" | custom-call | flops 603979776 | bytes 3670016 | tf_op jit(solution)/shard_map/residual_1/pallas_call | solution.py:329
  41.4 0.1 collective-permute-start.16
  41.5 2.7 %collective-permute-start.11 = (f32[2,32,1024]{2,1,0:T(8,128)S(1)}, f32[2,32,1024]{2,1,0:T(8,128)S(1)}, u32[]{:S(2)}, u32[]{:S(2)}) collective-permute-start(f32[2,32,1024]{2,1,0:T(8,128)S(1)} %get-tuple-element.60), channel_id=1, source_target_pairs={{0,24},{2,26},{4,12},{6,14},{8,0},{10,2},{12,20},{14,22},{16,8},{1... | collective-permute-start | bytes 786440 | tf_op jit(solution)/shard_map/ppermute | solution.py:429
  44.2 0.3 collective-permute-done.17
  44.6 0.6 collective-permute-start.18
  45.2 5.2 %collective-permute-done.11 = f32[2,32,1024]{2,1,0:T(8,128)S(1)} collective-permute-done((f32[2,32,1024]{2,1,0:T(8,128)S(1)}, f32[2,32,1024]{2,1,0:T(8,128)S(1)}, u32[]{:S(2)}, u32[]{:S(2)}) %collective-permute-start.11) | collective-permute-done | bytes 262176 | tf_op jit(solution)/shard_map/ppermute | solution.py:429
  50.4 3.4 %collective-permute-start.12 = (f32[2,32,1024]{2,1,0:T(8,128)S(1)}, f32[2,32,1024]{2,1,0:T(8,128)S(1)}, u32[]{:S(2)}, u32[]{:S(2)}) collective-permute-start(f32[2,32,1024]{2,1,0:T(8,128)S(1)} %add.48), channel_id=1, source_target_pairs={{0,4},{2,6},{4,0},{6,2},{8,12},{10,14},{12,8},{14,10},{16,20},{18,... | collective-permute-start | bytes 786440 | tf_op jit(solution)/shard_map/ppermute | solution.py:429
  53.8 0.0 collective-permute-done.18
  53.9 0.6 collective-permute-start.20
  54.4 1.1 %collective-permute-start.19 = (f32[32,1024]{1,0:T(8,128)S(1)}, f32[32,1024]{1,0:T(8,128)S(1)}, u32[]{:S(2)}, u32[]{:S(2)}) collective-permute-start(f32[32,1024]{1,0:T(8,128)S(1)} %get-tuple-element.69), channel_id=1, source_target_pairs={{0,2},{1,3},{2,0},{3,1},{4,6},{5,7},{6,4},{7,5},{8,10},{9,11},{10,... | collective-permute-start | bytes 393224 | tf_op jit(solution)/shard_map/ppermute | solution.py:437
  55.6 0.5 collective-permute-start.21
  56.1 3.9 %collective-permute-done.12 = f32[2,32,1024]{2,1,0:T(8,128)S(1)} collective-permute-done((f32[2,32,1024]{2,1,0:T(8,128)S(1)}, f32[2,32,1024]{2,1,0:T(8,128)S(1)}, u32[]{:S(2)}, u32[]{:S(2)}) %collective-permute-start.12) | collective-permute-done | bytes 262176 | tf_op jit(solution)/shard_map/ppermute | solution.py:429
  60.0 1.6 %collective-permute-start.15 = (f32[32,1024]{1,0:T(8,128)S(1)}, f32[32,1024]{1,0:T(8,128)S(1)}, u32[]{:S(2)}, u32[]{:S(2)}) collective-permute-start(f32[32,1024]{1,0:T(8,128)S(1)} %get-tuple-element.70.refs_4_), channel_id=1, source_target_pairs={{0,1},{1,0},{2,3},{3,2},{4,5},{5,4},{6,7},{7,6},{8,9},{9,8},{10,11... | collective-permute-start | bytes 393224 | tf_op jit(solution)/shard_map/ppermute | solution.py:437
  61.6 1.0 %collective-permute-done.21.refs_3_ = f32[32,1024]{1,0:T(8,128)S(1)} collective-permute-done((f32[32,1024]{1,0:T(8,128)S(1)}, f32[32,1024]{1,0:T(8,128)S(1)}, u32[]{:S(2)}, u32[]{:S(2)}) %collective-permute-start.21) | collective-permute-done | bytes 131104 | tf_op jit(solution)/shard_map/ppermute | solution.py:437
  62.6 0.4 collective-permute-start.14
  63.0 0.0 collective-permute-done.20.refs_2_
  63.0 0.3 collective-permute-start.13
  63.4 0.0 collective-permute-done.19.refs_1_
  63.4 3.6 %update_0.1.refs_8_ = f32[8,128,4096]{2,1,0:T(8,128)} custom-call(bf16[4,256,128]{2,1,0:T(8,128)(2,1)S(1)} %get-tuple-element.39.refs_0_, f32[32,1024]{1,0:T(8,128)S(1)} %collective-permute-done.19.refs_1_, f32[32,1024]{1,0:T(8,128)S(1)} %collective-permute-done.20.refs_2_, f32[32,1024]{1,0:T(8,128)S(1)} %collective-permute-done.21.refs_3_, ...), custom_call_target="tpu_custom_call" | custom-call | flops 201326592 | bytes 8388608 | tf_op jit(solution)/shard_map/update_0/pallas_call | solution.py:403
  67.0 0.0 collective-permute-done.15.refs_3_
  67.0 1.2 %collective-permute-done.14.refs_2_ = f32[32,1024]{1,0:T(8,128)S(1)} collective-permute-done((f32[32,1024]{1,0:T(8,128)S(1)}, f32[32,1024]{1,0:T(8,128)S(1)}, u32[]{:S(2)}, u32[]{:S(2)}) %collective-permute-start.14) | collective-permute-done | bytes 131104 | tf_op jit(solution)/shard_map/ppermute | solution.py:437
  68.3 0.0 collective-permute-done.13.refs_1_
  68.3 0.0 collective-permute-done.16.refs_7_
  68.3 4.3 %update_1.1 = (f32[8,128,4096]{2,1,0:T(8,128)}, f32[4,32,4096]{2,1,0:T(8,128)}) custom-call(bf16[4,256,128]{2,1,0:T(8,128)(2,1)S(1)} %get-tuple-element.39.refs_0_, f32[32,1024]{1,0:T(8,128)S(1)} %collective-permute-done.13.refs_1_, f32[32,1024]{1,0:T(8,128)S(1)} %collective-permute-done.14.refs_2_, ...), custom_call_target="tpu_custom_call", output_to_operand_aliasing={{0}: (8, {})} | custom-call | flops 201326592 | bytes 8388608 | tf_op jit(solution)/shard_map/update_1/pallas_call | solution.py:403
  (9 shorter events, 0.2 us)
Async XLA Ops:
  0.6 26.3 %copy-start.1 = (f32[64,256]{1,0:T(8,128)S(1)}, f32[64,256]{1,0:T(8,128)}, u32[]{:S(2)}) copy-start(f32[64,256]{1,0:T(8,128)} %refs_1_.4) | copy-start | bytes 196612
  0.6 26.2 %copy-start.3 = (s32[64]{0:T(128)S(1)}, s32[64]{0:T(128)}, u32[]{:S(2)}) copy-start(s32[64]{0:T(128)} %refs_0_.3) | copy-start | bytes 772
  0.7 7.9 %copy-start = (bf16[4,32,4096]{2,1,0:T(8,128)(2,1)S(1)}, bf16[4,32,4096]{2,1,0:T(8,128)(2,1)}, u32[]{:S(2)}) copy-start(bf16[4,32,4096]{2,1,0:T(8,128)(2,1)} %refs_8_.1) | copy-start | bytes 3145732
  5.3 10.2 %copy-start.4 = (f32[32,1152]{1,0:T(8,128)S(1)}, f32[32,1152]{1,0:T(8,128)}, u32[]{:S(2)}) copy-start(f32[32,1152]{1,0:T(8,128)} %get-tuple-element.35) | copy-start | bytes 442372
  5.3 10.0 %collective-permute-start = (f32[32,1152]{1,0:T(8,128)}, f32[32,1152]{1,0:T(8,128)S(1)}, u32[]{:S(2)}, u32[]{:S(2)}) collective-permute-start(f32[32,1152]{1,0:T(8,128)} %get-tuple-element.36), channel_id=1, source_target_pairs={{0,1},{1,0},{2,3},{3,2},{4,5},{5,4},{6,7},{7,6},{8,9},{9,8},{10,11... | collective-permute-start | bytes 442376 | tf_op jit(solution)/shard_map/ppermute | solution.py:437
  8.4 7.2 %collective-permute-start.1 = (f32[32,1152]{1,0:T(8,128)}, f32[32,1152]{1,0:T(8,128)S(1)}, u32[]{:S(2)}, u32[]{:S(2)}) collective-permute-start(f32[32,1152]{1,0:T(8,128)} %get-tuple-element.37), channel_id=1, source_target_pairs={{0,2},{1,3},{2,0},{3,1},{4,6},{5,7},{6,4},{7,5},{8,10},{9,11},{10,... | collective-permute-start | bytes 442376 | tf_op jit(solution)/shard_map/ppermute | solution.py:437
  8.4 7.6 %collective-permute-start.2 = (f32[32,1152]{1,0:T(8,128)}, f32[32,1152]{1,0:T(8,128)S(1)}, u32[]{:S(2)}, u32[]{:S(2)}) collective-permute-start(f32[32,1152]{1,0:T(8,128)} %get-tuple-element.38), channel_id=1, source_target_pairs={{0,3},{1,2},{2,1},{3,0},{4,7},{5,6},{6,5},{7,4},{8,11},{9,10},{10,... | collective-permute-start | bytes 442376 | tf_op jit(solution)/shard_map/ppermute | solution.py:437
  8.7 26.8 %collective-permute-start.5 = (f32[4,32,2048]{2,1,0:T(8,128)S(1)}, f32[4,32,2048]{2,1,0:T(8,128)S(1)}, u32[]{:S(2)}, u32[]{:S(2)}) collective-permute-start(f32[4,32,2048]{2,1,0:T(8,128)S(1)} %dynamic-slice_convert_fusion), channel_id=1, source_target_pairs={{0,2},{2,0},{4,6},{6,4},{8,10},{10,8},{12,14},{14,12},{16,18},{18,... | collective-permute-start | bytes 3145736 | tf_op jit(solution)/shard_map/ppermute | solution.py:429
  9.1 0.8 %copy-start.2 = (bf16[32,512]{1,0:T(8,128)(2,1)S(1)}, bf16[32,512]{1,0:T(8,128)(2,1)}, u32[]{:S(2)}) copy-start(bf16[32,512]{1,0:T(8,128)(2,1)} %get-tuple-element.45.refs_0_) | copy-start | bytes 98308
  13.6 6.4 %collective-permute-start.6 = (f32[32,1024]{1,0:T(8,128)S(1)}, f32[32,1024]{1,0:T(8,128)S(1)}, u32[]{:S(2)}, u32[]{:S(2)}) collective-permute-start(f32[32,1024]{1,0:T(8,128)S(1)} %get-tuple-element.47), channel_id=1, source_target_pairs={{0,1},{1,0},{2,3},{3,2},{4,5},{5,4},{6,7},{7,6},{8,9},{9,8},{10,11... | collective-permute-start | bytes 393224 | tf_op jit(solution)/shard_map/ppermute | solution.py:437
  15.3 4.7 %collective-permute-start.7 = (f32[32,1024]{1,0:T(8,128)S(1)}, f32[32,1024]{1,0:T(8,128)S(1)}, u32[]{:S(2)}, u32[]{:S(2)}) collective-permute-start(f32[32,1024]{1,0:T(8,128)S(1)} %get-tuple-element.48), channel_id=1, source_target_pairs={{0,2},{1,3},{2,0},{3,1},{4,6},{5,7},{6,4},{7,5},{8,10},{9,11},{10,... | collective-permute-start | bytes 393224 | tf_op jit(solution)/shard_map/ppermute | solution.py:437
  15.6 6.2 %collective-permute-start.8 = (f32[32,1024]{1,0:T(8,128)S(1)}, f32[32,1024]{1,0:T(8,128)S(1)}, u32[]{:S(2)}, u32[]{:S(2)}) collective-permute-start(f32[32,1024]{1,0:T(8,128)S(1)} %get-tuple-element.49), channel_id=1, source_target_pairs={{0,3},{1,2},{2,1},{3,0},{4,7},{5,6},{6,5},{7,4},{8,11},{9,10},{10,... | collective-permute-start | bytes 393224 | tf_op jit(solution)/shard_map/ppermute | solution.py:437
  16.0 9.2 %collective-permute-start.3 = (f32[2,32,1152]{2,1,0:T(8,128)S(1)}, f32[2,32,1152]{2,1,0:T(8,128)S(1)}, u32[]{:S(2)}, u32[]{:S(2)}) collective-permute-start(f32[2,32,1152]{2,1,0:T(8,128)S(1)} %pad_maximum_fusion.foot_ref.refs_2_), channel_id=1, source_target_pairs={{0,4},{2,6},{4,0},{6,2},{8,12},{10,14},{12,8},{14,10},{16,20},{18,... | collective-permute-start | bytes 884744 | tf_op jit(solution)/shard_map/ppermute | solution.py:429
  21.8 9.1 %collective-permute-start.9 = (f32[2,32,1024]{2,1,0:T(8,128)S(1)}, f32[2,32,1024]{2,1,0:T(8,128)S(1)}, u32[]{:S(2)}, u32[]{:S(2)}) collective-permute-start(f32[2,32,1024]{2,1,0:T(8,128)S(1)} %pad_maximum_fusion.1.refs_5_), channel_id=1, source_target_pairs={{0,4},{2,6},{4,0},{6,2},{8,12},{10,14},{12,8},{14,10},{16,20},{18,... | collective-permute-start | bytes 786440 | tf_op jit(solution)/shard_map/ppermute | solution.py:429
  25.2 10.3 %collective-permute-start.4 = (f32[2,32,1152]{2,1,0:T(8,128)S(1)}, f32[2,32,1152]{2,1,0:T(8,128)S(1)}, u32[]{:S(2)}, u32[]{:S(2)}) collective-permute-start(f32[2,32,1152]{2,1,0:T(8,128)S(1)} %collective-permute-done.3._.refs_3_), channel_id=1, source_target_pairs={{0,8},{2,10},{4,28},{6,30},{8,16},{10,18},{12,4},{14,6},{16,24},{1... | collective-permute-start | bytes 884744 | tf_op jit(solution)/shard_map/ppermute | solution.py:429
  31.0 9.2 %collective-permute-start.10 = (f32[2,32,1024]{2,1,0:T(8,128)S(1)}, f32[2,32,1024]{2,1,0:T(8,128)S(1)}, u32[]{:S(2)}, u32[]{:S(2)}) collective-permute-start(f32[2,32,1024]{2,1,0:T(8,128)S(1)} %collective-permute-done.9.refs_6_), channel_id=1, source_target_pairs={{0,8},{2,10},{4,0},{6,2},{8,16},{10,18},{12,4},{14,6},{16,24},{18,... | collective-permute-start | bytes 786440 | tf_op jit(solution)/shard_map/ppermute | solution.py:429
  37.6 7.0 %collective-permute-start.17 = (f32[2,32,1024]{2,1,0:T(8,128)S(1)}, f32[2,32,1024]{2,1,0:T(8,128)S(1)}, u32[]{:S(2)}, u32[]{:S(2)}) collective-permute-start(f32[2,32,1024]{2,1,0:T(8,128)S(1)} %get-tuple-element.66), channel_id=1, source_target_pairs={{0,4},{2,6},{4,12},{6,14},{8,0},{10,2},{12,20},{14,22},{16,8},{18,... | collective-permute-start | bytes 786440 | tf_op jit(solution)/shard_map/ppermute | solution.py:429
  41.4 26.9 %collective-permute-start.16 = (f32[4,32,2048]{2,1,0:T(8,128)S(1)}, f32[4,32,2048]{2,1,0:T(8,128)S(1)}, u32[]{:S(2)}, u32[]{:S(2)}) collective-permute-start(f32[4,32,2048]{2,1,0:T(8,128)S(1)} %get-tuple-element.63), channel_id=1, source_target_pairs={{0,2},{2,0},{4,6},{6,4},{8,10},{10,8},{12,14},{14,12},{16,18},{18,... | collective-permute-start | bytes 3145736 | tf_op jit(solution)/shard_map/ppermute | solution.py:429
  41.5 8.9 %collective-permute-start.11 = (f32[2,32,1024]{2,1,0:T(8,128)S(1)}, f32[2,32,1024]{2,1,0:T(8,128)S(1)}, u32[]{:S(2)}, u32[]{:S(2)}) collective-permute-start(f32[2,32,1024]{2,1,0:T(8,128)S(1)} %get-tuple-element.60), channel_id=1, source_target_pairs={{0,24},{2,26},{4,12},{6,14},{8,0},{10,2},{12,20},{14,22},{16,8},{1... | collective-permute-start | bytes 786440 | tf_op jit(solution)/shard_map/ppermute | solution.py:429
  44.6 9.2 %collective-permute-start.18 = (f32[2,32,1024]{2,1,0:T(8,128)S(1)}, f32[2,32,1024]{2,1,0:T(8,128)S(1)}, u32[]{:S(2)}, u32[]{:S(2)}) collective-permute-start(f32[2,32,1024]{2,1,0:T(8,128)S(1)} %add.53), channel_id=1, source_target_pairs={{0,4},{2,6},{4,0},{6,2},{8,12},{10,14},{12,8},{14,10},{16,20},{18,... | collective-permute-start | bytes 786440 | tf_op jit(solution)/shard_map/ppermute | solution.py:429
  50.4 9.5 %collective-permute-start.12 = (f32[2,32,1024]{2,1,0:T(8,128)S(1)}, f32[2,32,1024]{2,1,0:T(8,128)S(1)}, u32[]{:S(2)}, u32[]{:S(2)}) collective-permute-start(f32[2,32,1024]{2,1,0:T(8,128)S(1)} %add.48), channel_id=1, source_target_pairs={{0,4},{2,6},{4,0},{6,2},{8,12},{10,14},{12,8},{14,10},{16,20},{18,... | collective-permute-start | bytes 786440 | tf_op jit(solution)/shard_map/ppermute | solution.py:429
  53.9 9.2 %collective-permute-start.20 = (f32[32,1024]{1,0:T(8,128)S(1)}, f32[32,1024]{1,0:T(8,128)S(1)}, u32[]{:S(2)}, u32[]{:S(2)}) collective-permute-start(f32[32,1024]{1,0:T(8,128)S(1)} %get-tuple-element.69), channel_id=1, source_target_pairs={{0,3},{1,2},{2,1},{3,0},{4,7},{5,6},{6,5},{7,4},{8,11},{9,10},{10,... | collective-permute-start | bytes 393224 | tf_op jit(solution)/shard_map/ppermute | solution.py:437
  54.4 8.9 %collective-permute-start.19 = (f32[32,1024]{1,0:T(8,128)S(1)}, f32[32,1024]{1,0:T(8,128)S(1)}, u32[]{:S(2)}, u32[]{:S(2)}) collective-permute-start(f32[32,1024]{1,0:T(8,128)S(1)} %get-tuple-element.69), channel_id=1, source_target_pairs={{0,2},{1,3},{2,0},{3,1},{4,6},{5,7},{6,4},{7,5},{8,10},{9,11},{10,... | collective-permute-start | bytes 393224 | tf_op jit(solution)/shard_map/ppermute | solution.py:437
  55.6 7.0 %collective-permute-start.21 = (f32[32,1024]{1,0:T(8,128)S(1)}, f32[32,1024]{1,0:T(8,128)S(1)}, u32[]{:S(2)}, u32[]{:S(2)}) collective-permute-start(f32[32,1024]{1,0:T(8,128)S(1)} %get-tuple-element.68.refs_4_), channel_id=1, source_target_pairs={{0,1},{1,0},{2,3},{3,2},{4,5},{5,4},{6,7},{7,6},{8,9},{9,8},{10,11... | collective-permute-start | bytes 393224 | tf_op jit(solution)/shard_map/ppermute | solution.py:437
  60.0 7.0 %collective-permute-start.15 = (f32[32,1024]{1,0:T(8,128)S(1)}, f32[32,1024]{1,0:T(8,128)S(1)}, u32[]{:S(2)}, u32[]{:S(2)}) collective-permute-start(f32[32,1024]{1,0:T(8,128)S(1)} %get-tuple-element.70.refs_4_), channel_id=1, source_target_pairs={{0,1},{1,0},{2,3},{3,2},{4,5},{5,4},{6,7},{7,6},{8,9},{9,8},{10,11... | collective-permute-start | bytes 393224 | tf_op jit(solution)/shard_map/ppermute | solution.py:437
  62.6 5.6 %collective-permute-start.14 = (f32[32,1024]{1,0:T(8,128)S(1)}, f32[32,1024]{1,0:T(8,128)S(1)}, u32[]{:S(2)}, u32[]{:S(2)}) collective-permute-start(f32[32,1024]{1,0:T(8,128)S(1)} %get-tuple-element.71), channel_id=1, source_target_pairs={{0,3},{1,2},{2,1},{3,0},{4,7},{5,6},{6,5},{7,4},{8,11},{9,10},{10,... | collective-permute-start | bytes 393224 | tf_op jit(solution)/shard_map/ppermute | solution.py:437
  63.0 5.2 %collective-permute-start.13 = (f32[32,1024]{1,0:T(8,128)S(1)}, f32[32,1024]{1,0:T(8,128)S(1)}, u32[]{:S(2)}, u32[]{:S(2)}) collective-permute-start(f32[32,1024]{1,0:T(8,128)S(1)} %get-tuple-element.71), channel_id=1, source_target_pairs={{0,2},{1,3},{2,0},{3,1},{4,6},{5,7},{6,4},{7,5},{8,10},{9,11},{10,... | collective-permute-start | bytes 393224 | tf_op jit(solution)/shard_map/ppermute | solution.py:437

commit v5 on v4

--- a/solution.py
+++ b/solution.py
@@ -9,6 +9,8 @@
 
 F32, BF16 = jnp.float32, jnp.bfloat16
 CHUNKS = 2
+RAY_HALVES = [[(0, 1)], [(0, 1)]]
+UPDATE_HALVES = [[(0, 1)], [(0,), (1,)]]
 TILE = 512
 LANES = 128
 SUBLANES = 8
@@ -79,23 +81,25 @@
     return out
 
 
-def volume_pieces(dims, zdev, half, offset):
+def volume_pieces(dims, zdev, half, offset, halves):
     odd = lax.rem(lax.axis_index("slab"), 2)
     zb = dims[2]
-    for h in range(2):
+    for i, h in enumerate(halves):
         start = pl.multiple_of(lax.rem(odd + h, 2) * half + offset, LANES)
         for zp in range(zdev // zb):
-            yield h, zp, slice(zp * zb, (zp + 1) * zb), start
-
-
-def rays_kernel(dims, first, half, offset, width, *refs):
+            yield i, zp, slice(zp * zb, (zp + 1) * zb), start
+
+
+def rays_kernel(dims, first, keep, extra, halves, half, offset, width, *refs):
     per, groups, zb, cells = dims
     count = groups * SUBLANES
     if first:
         order_ref, start_ref, len_ref, table_ref, vol_ref, *refs = refs
+    elif extra:
+        start_buf, len_buf, given_ref, vol_ref, *refs = refs
     else:
         given_ref, vol_ref, *refs = refs
-    outs, refs = refs[:2 * groups], refs[2 * groups:]
+    outs, refs = refs[:len(halves) * groups], refs[len(halves) * groups:]
     if first:
         left_ref, buf, sems, table_buf, order_buf, start_buf, len_buf, rows_ref, small_sems = refs
     else:
@@ -111,7 +115,7 @@
         ]
         for copy in small:
             copy.start()
-    for h, zp, slices, start in volume_pieces(dims, zdev, half, offset):
+    for h, zp, slices, start in volume_pieces(dims, zdev, half, offset, halves):
         source = vol_ref.at[slices, :, pl.ds(start, width)]
         copies.append((h, zp, pltpu.make_async_copy(source, buf.at[h, slices], sems.at[h, zp])))
         copies[-1][-1].start()
@@ -123,16 +127,17 @@
         left_ref[...] = left
         small[2].wait()
         small[3].wait()
+    else:
+        left = given_ref[...]
+    if extra:
         shape = (zdev * per, LANES)
         angle, lane = low_bits(iota(shape, 0), per), iota(shape, 1)
         starts = pick(angle, [start_buf[0, a].astype(F32) for a in range(per)])
         lengths = pick(angle, [len_buf[0, a].astype(F32) for a in range(per)])
         for d in range(groups):
             foot = jnp.where(lane == 2 * d, starts, jnp.where(lane == 2 * d + 1, lengths, 0.0))
-            for h in range(2):
+            for h in range(len(halves)):
                 outs[h * groups + d][:, width:] = foot
-    else:
-        left = given_ref[...]
     for h, zp, copy in copies:
         copy.wait()
         for at, size in tiles(width):
@@ -145,36 +150,38 @@
                 )
 
 
-def ray_sums(dims, chunk, offset, width, given, small, table, volume):
+def ray_sums(dims, chunk, halves, offset, width, given, small, table, volume):
     per, groups, zb, cells = dims
     zdev, _, total = volume.shape
-    first = chunk == 0
+    first, keep, extra = given is None, chunk > 0, chunk == 0
     count, all_cells = groups * SUBLANES, table.shape[1]
-    out = jax.ShapeDtypeStruct((zdev * per, width + (LANES if first else 0)), F32)
+    out = jax.ShapeDtypeStruct((zdev * per, width + (LANES if extra else 0)), F32)
     left = jax.ShapeDtypeStruct((2 * count, 2 * zb * cells), BF16)
+    columns = (len(halves), zdev, cells, width)
     assert zb * cells == all_cells
-    sems = pltpu.SemaphoreType.DMA((2, zdev // zb))
-    shapes = [out] * (2 * groups)
-    scratch = [pltpu.VMEM((2, zdev, cells, width), F32), sems]
+    shapes = [out] * (len(halves) * groups)
+    scratch = [] if keep else [pltpu.VMEM(columns, F32)]
+    scratch += [pltpu.SemaphoreType.DMA((len(halves), zdev // zb))]
     args, specs, limit = [given, volume], [IN_VMEM, ANYWHERE], 40
     if first:
         scratch += [pltpu.VMEM(table.shape, F32)] + [pltpu.SMEM(a.shape, a.dtype) for a in small]
         scratch += [pltpu.VMEM((count, all_cells), F32), pltpu.SemaphoreType.DMA((4,))]
         args, specs, limit = [*small, table, volume], [ANYWHERE] * 5, 58
         shapes += [left]
-    if not first:
-        scratch = [sems]
-        shapes += [jax.ShapeDtypeStruct((2, zdev, cells, width), F32)]
-    size = zdev * cells * width * 2
+    elif extra:
+        args, specs, limit = [*small[1:], *args], [IN_SMEM] * 2 + specs, 50
+    if keep:
+        shapes += [jax.ShapeDtypeStruct(columns, F32)]
+    size = zdev * cells * width * len(halves)
     return pl.pallas_call(
-        functools.partial(rays_kernel, dims, first, total // 2, offset, width),
+        functools.partial(rays_kernel, dims, first, keep, extra, halves, total // 2, offset, width),
         in_specs=specs,
         out_specs=[IN_VMEM] * len(shapes),
         out_shape=shapes,
         scratch_shapes=scratch,
         compiler_params=pltpu.CompilerParams(vmem_limit_bytes=limit * MIB),
         cost_estimate=pl.CostEstimate(flops=2 * size * 16, bytes_accessed=size * 4, transcendentals=0),
-        name=f"ray_sums_{chunk}",
+        name=f"ray_sums_{chunk}_{halves[0]}",
     )(*args)
 
 
@@ -227,7 +234,7 @@
 def prepare_kernel(dims, rdev, half, width, order_ref, table_ref, foot_ref, _, vol_ref, kept_ref, left_ref, sems, rows_ref):
     zdev = vol_ref.shape[0]
     copies = []
-    for h, zp, slices, start in volume_pieces(dims, zdev, half, 0):
+    for h, zp, slices, start in volume_pieces(dims, zdev, half, 0, (0, 1)):
         source = vol_ref.at[slices, :, pl.ds(start, width)]
         copies.append(pltpu.make_async_copy(source, kept_ref.at[h, slices], sems.at[h, zp]))
         copies[-1].start()
@@ -339,69 +346,71 @@
     )(*args)
 
 
-def update_kernel(dims, first, last, half, offset, width, *refs):
+def update_kernel(dims, first, halves, half, offset, width, *refs):
     per, groups, zb, cells = dims
     count = groups * SUBLANES
-    left_ref, backs, refs = refs[0], refs[1:1 + 2 * groups], refs[1 + 2 * groups:]
-    backs = [backs[-1], *backs[groups:-1], *backs[:groups]]
+    left_ref, backs, refs = refs[0], refs[len(halves) * groups:0:-1], refs[1 + len(halves) * groups:]
     vol_ref, *refs = refs
     zdev, depth = vol_ref.shape[1], left_ref.shape[2]
-    if last:
-        pieces, refs = refs[:2], refs[2:]
     if not first:
         refs = refs[1:]
-    if last:
-        out_ref, res_ref, buf, sems, res_sems = refs
+    pieces = refs[:-3]
+    if pieces:
+        *pieces, out_ref, res_ref, buf, sems, res_sems = refs
     else:
         out_ref, buf, sems = refs
     odd = lax.rem(lax.axis_index("slab"), 2)
     leaving = []
-    for h, zp, slices, start in volume_pieces(dims, zdev, half, offset):
+    for h, ref in enumerate(pieces):
+        columns = pl.ds(pl.multiple_of(lax.rem(odd + h, 2) * half, LANES), half)
+        leaving.append(pltpu.make_async_copy(ref, res_ref.at[:, :, columns], res_sems.at[h]))
+        leaving[-1].start()
+    held = len(halves) < vol_ref.shape[0]
+    for i, zp, slices, start in volume_pieces(dims, zdev, half, offset, halves):
         rows = slice(zp * SUBLANES, (zp + 1) * SUBLANES)
         left = left_ref[zp]
         for at, size in tiles(width):
             piece = slice(at, at + size)
-            back = jnp.concatenate([backs[h * groups + d][rows, piece] for d in range(groups)], axis=0)
+            back = jnp.concatenate([backs[i * groups + d][rows, piece] for d in range(groups)], axis=0)
             high, low = split(back)
             pad = jnp.zeros((depth - 3 * count, size), BF16)
             change = dot(left, jnp.concatenate([high, low, high, pad], axis=0))
             for z in range(zb):
-                buf[h, zp * zb + z, :, piece] = (
-                    vol_ref[h, zp * zb + z, :, piece] + change[z * cells:(z + 1) * cells]
+                buf[i, zp * zb + z, :, piece] = (
+                    vol_ref[halves[i] if held else i, zp * zb + z, :, piece] + change[z * cells:(z + 1) * cells]
                 )
         leaving.append(
-            pltpu.make_async_copy(buf.at[h, slices], out_ref.at[slices, :, pl.ds(start, width)], sems.at[h, zp])
+            pltpu.make_async_copy(buf.at[i, slices], out_ref.at[slices, :, pl.ds(start, width)], sems.at[i, zp])
         )
         leaving[-1].start()
-    if last:
-        for h, ref in enumerate(pieces):
-            columns = pl.ds(pl.multiple_of(lax.rem(odd + h, 2) * half, LANES), half)
-            leaving.append(pltpu.make_async_copy(ref, res_ref.at[:, :, columns], res_sems.at[h]))
-            leaving[-1].start()
     for copy in leaving:
         copy.wait()
 
 
-def update_step(dims, chunk, offset, width, left, backs, pieces, kept, volume, out):
+def update_step(dims, chunk, halves, offset, width, left, backs, pieces, kept, volume, out):
     per, groups, zb, cells = dims
     zdev, _, total = volume.shape
-    first, last = chunk == 0, chunk == CHUNKS - 1
-    args = [left, *backs[groups:], *backs[1:groups], backs[0], kept]
+    first = out is None
+    args = [left, *backs[::-1], kept]
     shapes = [jax.ShapeDtypeStruct(volume.shape, F32)]
-    scratch = [pltpu.VMEM((2, zdev, cells, width), F32), pltpu.SemaphoreType.DMA((2, zdev // zb))]
-    if last:
-        args += pieces
-        shapes += [jax.ShapeDtypeStruct((*pieces[0].shape[:2], total), F32)]
-        scratch += [pltpu.SemaphoreType.DMA((2,))]
+    scratch = [
+        pltpu.VMEM((len(halves), zdev, cells, width), F32),
+        pltpu.SemaphoreType.DMA((len(halves), zdev // zb)),
+    ]
     specs = [IN_VMEM] * len(args)
     aliases = {}
     if not first:
         aliases = {len(args): 0}
         args += [out]
         specs += [ANYWHERE]
-    size = zdev * cells * width * 2
+    if pieces:
+        args += pieces
+        specs += [IN_VMEM] * 2
+        shapes += [jax.ShapeDtypeStruct((*pieces[0].shape[:2], total), F32)]
+        scratch += [pltpu.SemaphoreType.DMA((2,))]
+    size = zdev * cells * width * len(halves)
     return pl.pallas_call(
-        functools.partial(update_kernel, dims, first, last, total // 2, offset, width),
+        functools.partial(update_kernel, dims, first, halves, total // 2, offset, width),
         in_specs=specs,
         out_specs=[ANYWHERE] * len(shapes),
         out_shape=shapes,
@@ -409,7 +418,7 @@
         input_output_aliases=aliases,
         compiler_params=pltpu.CompilerParams(vmem_limit_bytes=20 * MIB),
         cost_estimate=pl.CostEstimate(flops=2 * size * 48, bytes_accessed=size * 4, transcendentals=0),
-        name=f"update_{chunk}",
+        name=f"update_{chunk}_{halves[0]}",
     )(*args)
 
 
@@ -458,15 +467,18 @@
         lax.dynamic_slice_in_dim(measured, (1 - odd) * half, half, 2).astype(F32), lambda s: s ^ 1
     )
 
-    sums, kept, left = [], [], None
+    sums, kept, left = [], [[] for _ in range(CHUNKS)], None
     for c in range(CHUNKS):
-        parts = ray_sums(
-            dims, c, offsets[c], widths[c], left, (order, foot_start, foot_len), table, volume
-        )
-        if c == 0:
-            left = parts[2 * groups]
-        else:
-            kept.append(parts[2 * groups])
+        parts = []
+        for halves in RAY_HALVES[c]:
+            made = ray_sums(
+                dims, c, halves, offsets[c], widths[c], left, (order, foot_start, foot_len), table, volume
+            )
+            parts += made[:len(halves) * groups]
+            if left is None:
+                left = made[-1]
+            elif c:
+                kept[c] += [(h, made[-1]) for h in halves]
         parts = [spread(parts[h * groups + d], h, d) for h in range(2) for d in range(groups)]
         if c:
             parts, _ = lax.optimization_barrier((parts, sums[-1][0]))
@@ -474,9 +486,9 @@
         near = along(own, facing)
         if c == 0:
             first_columns, update_left = prepare_step(dims, rdev, widths[0], order, table, own, near, volume)
-            kept.append(first_columns)
+            kept[0] = [(h, first_columns) for h in range(2)]
         if c == 1:
-            near, kept[0] = lax.optimization_barrier((near, kept[0]))
+            near, first_columns = lax.optimization_barrier((near, first_columns))
         far = along(near, beyond(c))
         sums.append((own, near, far))
     pieces, given, mats = [], [], None
@@ -491,9 +503,16 @@
         halves = [own[i] + arrived[i] for i in range(2)]
         given.append([spread(halves[h], h, d) for h in range(2) for d in range(groups)])
     pieces = [mine, along(sent, lambda s: s ^ 1)]
-    out = None
+    out, res = None, []
     for c in range(CHUNKS):
-        out, *res = update_step(dims, c, offsets[c], widths[c], update_left, given[c], pieces, kept[c], volume, out)
+        for halves in UPDATE_HALVES[c]:
+            backs = [b for h in halves for b in given[c][h * groups:(h + 1) * groups]]
+            write = c == CHUNKS - 1 and halves[0] == 0
+            out, *made = update_step(
+                dims, c, halves, offsets[c], widths[c], update_left, backs, pieces if write else [],
+                dict(kept[c])[halves[0]], volume, out,
+            )
+            res += made
     return out, res[0]
 
 

time: 72.7 us -> 71.5 us (0.983)
  waiting for transfers between devices: 21.9 us -> 19.9 us
  Pallas kernels: 23.8 us -> 24.6 us
    ppermute x12, waiting for transfers between devices: 6.39 us -> 4.47 us  [spread(): return lax.ppermute(value, ('slab', 'ang'), pairs)]
    pallas_call x4 -> x5, Pallas kernels: 16.4 us -> 17.1 us  [the longest x3 8.7 us: update_step(): pl.pallas_call(functools.partial(update_kernel, dims, first, halves, tota...]
  transfers between devices with their start and end apart: 22 -> 22, of which waited for: 10 -> 9; matrix products, arithmetic and copies ran while one was open for 0% -> 0% of each run, Pallas kernels for 20% -> 25%
where the time goes in v5:
time: 71.5 us; the launch traced here: 71.3 us
  starting transfers between devices  24.8 us (35%)
  Pallas kernels  24.6 us (34%)
  waiting for transfers between devices  19.9 us (28%)
  between operations  0.85 us (1%)
  local copies, waits for them, and re-layouts  0.78 us (1%)
    ppermute x10, waiting for transfers between devices, along(): return lax.ppermute(value, 'slab', pairs)  15.5 us
    ppermute x10, starting transfers between devices, along(): return lax.ppermute(value, 'slab', pairs)  14.6 us
    ppermute x12, starting transfers between devices, spread(): return lax.ppermute(value, ('slab', 'ang'), pairs)  10.2 us
    pallas_call x3, Pallas kernels, update_step(): pl.pallas_call(functools.partial(update_kernel, dims, first, halves, tota...  8.7 us
    pallas_call x2, Pallas kernels, ray_sums(): pl.pallas_call(functools.partial(rays_kernel, dims, first, keep, extra, h...  8.45 us
    ppermute x12, waiting for transfers between devices, spread(): return lax.ppermute(value, ('slab', 'ang'), pairs)  4.47 us
    pallas_call x1, Pallas kernels, prepare_step(): pl.pallas_call(functools.partial(prepare_kernel, dims, rdev, total // 2,...  4.09 us
    pallas_call x2, Pallas kernels, residual_step(): pl.pallas_call(functools.partial(residual_kernel, dims, first, total // 2...  3.32 us
  transfers between devices with their start and end apart: 22, of which 9 were waited for; matrix products, arithmetic and copies ran while one was open for 0% of the time, Pallas kernels for 25%

profile of v5, /device:TPU:0, one launch (start us, length us, event | category | flops | bytes accessed | tf_op | source)
XLA Modules:
  0.0 71.3 jit_solution(18271571431037006012)
XLA Ops:
  0.6 0.0 copy-start.3
  0.6 0.0 copy-start.1
  0.7 0.0 copy-start
  0.7 4.6 %ray_sums_0_0.1 = (f32[32,1152]{1,0:T(8,128)}, f32[32,1152]{1,0:T(8,128)}, f32[32,1152]{1,0:T(8,128)}, f32[32,1152]{1,0:T(8,128)}, bf16[32,512]{1,0:T(8,128)(2,1)}) custom-call(s32[64]{0:T(128)} %refs_0_.3, s32[1,4]{1,0:T(1,128)} %refs_1_.3, s32[1,4]{1,0:T(1,128)} %refs_2_.1, f32[64,256]{1,0:T(8,128)} %refs_1_.4, f32[8,128,4096]{2,1,0:T(8,128)} %refs_1_.5), custom_call_target="tpu_custom_call" | custom-call | flops 67108864 | bytes 8388608 | tf_op jit(solution)/shard_map/ray_sums_0_0/pallas_call | solution.py:176
  5.3 0.0 copy-start.4
  5.3 3.0 %collective-permute-start = (f32[32,1152]{1,0:T(8,128)}, f32[32,1152]{1,0:T(8,128)S(1)}, u32[]{:S(2)}, u32[]{:S(2)}) collective-permute-start(f32[32,1152]{1,0:T(8,128)} %get-tuple-element.37), channel_id=1, source_target_pairs={{0,1},{1,0},{2,3},{3,2},{4,5},{5,4},{6,7},{7,6},{8,9},{9,8},{10,11... | collective-permute-start | bytes 442376 | tf_op jit(solution)/shard_map/ppermute | solution.py:446
  8.4 0.0 copy-done
  8.4 0.1 dynamic-slice_convert_fusion
  8.5 0.1 collective-permute-start.5
  8.5 0.5 collective-permute-start.1
  9.0 0.0 collective-permute-start.2
  9.0 0.0 copy-start.2
  9.0 0.8 %copy-done.2 = bf16[32,512]{1,0:T(8,128)(2,1)S(1)} copy-done((bf16[32,512]{1,0:T(8,128)(2,1)S(1)}, bf16[32,512]{1,0:T(8,128)(2,1)}, u32[]{:S(2)}) %copy-start.2) | copy-done | bytes 32792
  9.8 3.8 %ray_sums_1_0.1 = (f32[32,1024]{1,0:T(8,128)S(1)}, f32[32,1024]{1,0:T(8,128)S(1)}, f32[32,1024]{1,0:T(8,128)S(1)}, f32[32,1024]{1,0:T(8,128)S(1)}, f32[2,8,128,1024]{3,2,1,0:T(8,128)S(1)}) custom-call(bf16[32,512]{1,0:T(8,128)(2,1)S(1)} %copy-done.2, f32[8,128,4096]{2,1,0:T(8,128)} %refs_1_.5), custom_call_target="tpu_custom_call" | custom-call | flops 67108864 | bytes 8388608 | tf_op jit(solution)/shard_map/ray_sums_1_0/pallas_call | solution.py:176
  13.6 1.8 %collective-permute-start.6 = (f32[32,1024]{1,0:T(8,128)S(1)}, f32[32,1024]{1,0:T(8,128)S(1)}, u32[]{:S(2)}, u32[]{:S(2)}) collective-permute-start(f32[32,1024]{1,0:T(8,128)S(1)} %get-tuple-element.48), channel_id=1, source_target_pairs={{0,1},{1,0},{2,3},{3,2},{4,5},{5,4},{6,7},{7,6},{8,9},{9,8},{10,11... | collective-permute-start | bytes 393224 | tf_op jit(solution)/shard_map/ppermute | solution.py:446
  15.4 0.0 collective-permute-done
  15.4 0.2 collective-permute-start.7
  15.6 0.0 copy-done.4
  15.6 0.0 collective-permute-done.1
  15.6 0.3 collective-permute-start.8
  15.9 0.0 collective-permute-done.2
  16.0 1.7 %collective-permute-start.3 = (f32[2,32,1152]{2,1,0:T(8,128)S(1)}, f32[2,32,1152]{2,1,0:T(8,128)S(1)}, u32[]{:S(2)}, u32[]{:S(2)}) collective-permute-start(f32[2,32,1152]{2,1,0:T(8,128)S(1)} %pad_maximum_fusion.foot_ref.refs_2_), channel_id=1, source_target_pairs={{0,4},{2,6},{4,0},{6,2},{8,12},{10,14},{12,8},{14,10},{16,20},{18,... | collective-permute-start | bytes 884744 | tf_op jit(solution)/shard_map/ppermute | solution.py:438
  17.7 2.3 %collective-permute-done.6 = f32[32,1024]{1,0:T(8,128)S(1)} collective-permute-done((f32[32,1024]{1,0:T(8,128)S(1)}, f32[32,1024]{1,0:T(8,128)S(1)}, u32[]{:S(2)}, u32[]{:S(2)}) %collective-permute-start.6) | collective-permute-done | bytes 131104 | tf_op jit(solution)/shard_map/ppermute | solution.py:446
  20.0 0.0 collective-permute-done.7
  20.0 1.8 %collective-permute-done.8 = f32[32,1024]{1,0:T(8,128)S(1)} collective-permute-done((f32[32,1024]{1,0:T(8,128)S(1)}, f32[32,1024]{1,0:T(8,128)S(1)}, u32[]{:S(2)}, u32[]{:S(2)}) %collective-permute-start.8) | collective-permute-done | bytes 131104 | tf_op jit(solution)/shard_map/ppermute | solution.py:446
  21.8 1.9 %collective-permute-start.9 = (f32[2,32,1024]{2,1,0:T(8,128)S(1)}, f32[2,32,1024]{2,1,0:T(8,128)S(1)}, u32[]{:S(2)}, u32[]{:S(2)}) collective-permute-start(f32[2,32,1024]{2,1,0:T(8,128)S(1)} %pad_maximum_fusion.1.refs_5_), channel_id=1, source_target_pairs={{0,4},{2,6},{4,0},{6,2},{8,12},{10,14},{12,8},{14,10},{16,20},{18,... | collective-permute-start | bytes 786440 | tf_op jit(solution)/shard_map/ppermute | solution.py:438
  23.7 1.5 %collective-permute-done.3._.refs_3_ = f32[2,32,1152]{2,1,0:T(8,128)S(1)} collective-permute-done((f32[2,32,1152]{2,1,0:T(8,128)S(1)}, f32[2,32,1152]{2,1,0:T(8,128)S(1)}, u32[]{:S(2)}, u32[]{:S(2)}) %collective-permute-start.3) | collective-permute-done | bytes 294944 | tf_op jit(solution)/shard_map/ppermute | solution.py:438
  25.2 1.7 %collective-permute-start.4 = (f32[2,32,1152]{2,1,0:T(8,128)S(1)}, f32[2,32,1152]{2,1,0:T(8,128)S(1)}, u32[]{:S(2)}, u32[]{:S(2)}) collective-permute-start(f32[2,32,1152]{2,1,0:T(8,128)S(1)} %collective-permute-done.3._.refs_3_), channel_id=1, source_target_pairs={{0,8},{2,10},{4,28},{6,30},{8,16},{10,18},{12,4},{14,6},{16,24},{1... | collective-permute-start | bytes 884744 | tf_op jit(solution)/shard_map/ppermute | solution.py:438
  26.9 0.0 copy-done.3
  26.9 0.0 copy-done.1
  26.9 4.1 %prepare.1 = (f32[2,8,128,1024]{3,2,1,0:T(8,128)S(1)}, bf16[4,256,128]{2,1,0:T(8,128)(2,1)S(1)}) custom-call(s32[64]{0:T(128)S(1)} %copy-done.3, f32[64,256]{1,0:T(8,128)S(1)} %copy-done.1, f32[2,32,1152]{2,1,0:T(8,128)S(1)} %pad_maximum_fusion.foot_ref.refs_2_, f32[2,32,1152]{2,1,0:T(8,128)S(1)} %collective-permute-done.3._.refs_3_, f32[8,128,4096]{2,1,0:T(8,128)} %refs_1_.5), custom_call_target="tpu_custom_call" | custom-call | bytes 8388608 | tf_op jit(solution)/shard_map/prepare/pallas_call | solution.py:250
  31.0 0.0 collective-permute-done.9.refs_6_
  31.0 1.6 %collective-permute-start.10 = (f32[2,32,1024]{2,1,0:T(8,128)S(1)}, f32[2,32,1024]{2,1,0:T(8,128)S(1)}, u32[]{:S(2)}, u32[]{:S(2)}) collective-permute-start(f32[2,32,1024]{2,1,0:T(8,128)S(1)} %collective-permute-done.9.refs_6_), channel_id=1, source_target_pairs={{0,8},{2,10},{4,0},{6,2},{8,16},{10,18},{12,4},{14,6},{16,24},{18,... | collective-permute-start | bytes 786440 | tf_op jit(solution)/shard_map/ppermute | solution.py:438
  32.6 2.8 %collective-permute-done.4.refs_4_ = f32[2,32,1152]{2,1,0:T(8,128)S(1)} collective-permute-done((f32[2,32,1152]{2,1,0:T(8,128)S(1)}, f32[2,32,1152]{2,1,0:T(8,128)S(1)}, u32[]{:S(2)}, u32[]{:S(2)}) %collective-permute-start.4) | collective-permute-done | bytes 294944 | tf_op jit(solution)/shard_map/ppermute | solution.py:438
  35.4 0.0 collective-permute-done.5.refs_6_.refs_9_
  35.4 2.1 %residual_0.1 = (f32[4,32,1024]{2,1,0:T(8,128)S(1)}, f32[4,32,1024]{2,1,0:T(8,128)S(1)}, f32[2,32,1024]{2,1,0:T(8,128)S(1)}, f32[2,32,1024]{2,1,0:T(8,128)S(1)},...) custom-call(s32[64]{0:T(128)S(1)} %copy-done.3, ...), custom_call_target="tpu_custom_call" | custom-call | flops 603979776 | bytes 3670016 | tf_op jit(solution)/shard_map/residual_0/pallas_call | solution.py:336
  37.5 0.8 %collective-permute-start.16 = (f32[2,32,1024]{2,1,0:T(8,128)S(1)}, f32[2,32,1024]{2,1,0:T(8,128)S(1)}, u32[]{:S(2)}, u32[]{:S(2)}) collective-permute-start(f32[2,32,1024]{2,1,0:T(8,128)S(1)} %get-tuple-element.65), channel_id=1, source_target_pairs={{0,4},{2,6},{4,12},{6,14},{8,0},{10,2},{12,20},{14,22},{16,8},{18,... | collective-permute-start | bytes 786440 | tf_op jit(solution)/shard_map/ppermute | solution.py:438
  38.3 1.8 %collective-permute-done.10.refs_7_ = f32[2,32,1024]{2,1,0:T(8,128)S(1)} collective-permute-done((f32[2,32,1024]{2,1,0:T(8,128)S(1)}, f32[2,32,1024]{2,1,0:T(8,128)S(1)}, u32[]{:S(2)}, u32[]{:S(2)}) %collective-permute-start.10) | collective-permute-done | bytes 262176 | tf_op jit(solution)/shard_map/ppermute | solution.py:438
  40.1 1.2 %residual_1.1 = (f32[4,32,2048]{2,1,0:T(8,128)S(1)}, f32[4,32,2048]{2,1,0:T(8,128)S(1)}, f32[2,32,1024]{2,1,0:T(8,128)S(1)}, f32[2,32,1024]{2,1,0:T(8,128)S(1)}, f32[2,32,1024]{2,1,0:T(8,128)S(1)}) custom-call(bf16[256,192]{1,0:T(8,128)(2,1)S(1)} %get-tuple-element.41.refs_0_, bf16[256,192]{1,0:T(8,128)(2,1)S(1)} %get-tuple-element.42.refs_1_, ...), custom_call_target="tpu_custom_call" | custom-call | flops 603979776 | bytes 3670016 | tf_op jit(solution)/shard_map/residual_1/pallas_call | solution.py:336
  41.3 0.1 collective-permute-start.21
  41.4 2.7 %collective-permute-start.11 = (f32[2,32,1024]{2,1,0:T(8,128)S(1)}, f32[2,32,1024]{2,1,0:T(8,128)S(1)}, u32[]{:S(2)}, u32[]{:S(2)}) collective-permute-start(f32[2,32,1024]{2,1,0:T(8,128)S(1)} %get-tuple-element.61), channel_id=1, source_target_pairs={{0,24},{2,26},{4,12},{6,14},{8,0},{10,2},{12,20},{14,22},{16,8},{1... | collective-permute-start | bytes 786440 | tf_op jit(solution)/shard_map/ppermute | solution.py:438
  44.2 0.3 collective-permute-done.16
  44.5 0.6 collective-permute-start.17
  45.1 5.3 %collective-permute-done.11 = f32[2,32,1024]{2,1,0:T(8,128)S(1)} collective-permute-done((f32[2,32,1024]{2,1,0:T(8,128)S(1)}, f32[2,32,1024]{2,1,0:T(8,128)S(1)}, u32[]{:S(2)}, u32[]{:S(2)}) %collective-permute-start.11) | collective-permute-done | bytes 262176 | tf_op jit(solution)/shard_map/ppermute | solution.py:438
  50.4 3.4 %collective-permute-start.12 = (f32[2,32,1024]{2,1,0:T(8,128)S(1)}, f32[2,32,1024]{2,1,0:T(8,128)S(1)}, u32[]{:S(2)}, u32[]{:S(2)}) collective-permute-start(f32[2,32,1024]{2,1,0:T(8,128)S(1)} %add.48), channel_id=1, source_target_pairs={{0,4},{2,6},{4,0},{6,2},{8,12},{10,14},{12,8},{14,10},{16,20},{18,... | collective-permute-start | bytes 786440 | tf_op jit(solution)/shard_map/ppermute | solution.py:438
  53.8 0.0 collective-permute-done.17
  53.8 0.6 collective-permute-start.18
  54.4 1.1 %collective-permute-start.19 = (f32[32,1024]{1,0:T(8,128)S(1)}, f32[32,1024]{1,0:T(8,128)S(1)}, u32[]{:S(2)}, u32[]{:S(2)}) collective-permute-start(f32[32,1024]{1,0:T(8,128)S(1)} %get-tuple-element.71), channel_id=1, source_target_pairs={{0,2},{1,3},{2,0},{3,1},{4,6},{5,7},{6,4},{7,5},{8,10},{9,11},{10,... | collective-permute-start | bytes 393224 | tf_op jit(solution)/shard_map/ppermute | solution.py:446
  55.5 0.5 collective-permute-start.20
  56.0 3.9 %collective-permute-done.12 = f32[2,32,1024]{2,1,0:T(8,128)S(1)} collective-permute-done((f32[2,32,1024]{2,1,0:T(8,128)S(1)}, f32[2,32,1024]{2,1,0:T(8,128)S(1)}, u32[]{:S(2)}, u32[]{:S(2)}) %collective-permute-start.12) | collective-permute-done | bytes 262176 | tf_op jit(solution)/shard_map/ppermute | solution.py:438
  59.9 1.6 %collective-permute-start.15 = (f32[32,1024]{1,0:T(8,128)S(1)}, f32[32,1024]{1,0:T(8,128)S(1)}, u32[]{:S(2)}, u32[]{:S(2)}) collective-permute-start(f32[32,1024]{1,0:T(8,128)S(1)} %get-tuple-element.72.refs_2_), channel_id=1, source_target_pairs={{0,1},{1,0},{2,3},{3,2},{4,5},{5,4},{6,7},{7,6},{8,9},{9,8},{10,11... | collective-permute-start | bytes 393224 | tf_op jit(solution)/shard_map/ppermute | solution.py:446
  61.5 0.0 collective-permute-done.18.refs_1_
  61.5 0.0 collective-permute-start.13
  61.5 0.0 collective-permute-done.19.refs_2_
  61.5 0.6 collective-permute-start.14
  62.1 0.4 collective-permute-done.20.refs_3_
  62.5 3.6 %update_0_0.1.refs_4_ = f32[8,128,4096]{2,1,0:T(8,128)} custom-call(bf16[4,256,128]{2,1,0:T(8,128)(2,1)S(1)} %get-tuple-element.40.refs_0_, f32[32,1024]{1,0:T(8,128)S(1)} %collective-permute-done.18.refs_1_, f32[32,1024]{1,0:T(8,128)S(1)} %collective-permute-done.19.refs_2_, f32[32,1024]{1,0:T(8,128)S(1)} %collective-permute-done.20.refs_3_, ...), custom_call_target="tpu_custom_call" | custom-call | flops 201326592 | bytes 8388608 | tf_op jit(solution)/shard_map/update_0_0/pallas_call | solution.py:412
  66.2 0.0 collective-permute-done.15.refs_1_
  66.2 0.0 collective-permute-done.21.refs_6_
  66.2 2.7 %update_1_0.1 = (f32[8,128,4096]{2,1,0:T(8,128)}, f32[4,32,4096]{2,1,0:T(8,128)}) custom-call(bf16[4,256,128]{2,1,0:T(8,128)(2,1)S(1)} %get-tuple-element.40.refs_0_, f32[32,1024]{1,0:T(8,128)S(1)} %collective-permute-done.15.refs_1_, f32[32,1024]{1,0:T(8,128)S(1)} %get-tuple-element.72.refs_2_, ...), custom_call_target="tpu_custom_call", output_to_operand_aliasing={{0}: (4, {})} | custom-call | flops 100663296 | bytes 4194304 | tf_op jit(solution)/shard_map/update_1_0/pallas_call | solution.py:412
  69.0 0.0 collective-permute-done.13.refs_1_
  69.0 0.0 collective-permute-done.14.refs_2_
  69.0 2.3 %update_1_1.1 = f32[8,128,4096]{2,1,0:T(8,128)} custom-call(bf16[4,256,128]{2,1,0:T(8,128)(2,1)S(1)} %get-tuple-element.40.refs_0_, f32[32,1024]{1,0:T(8,128)S(1)} %collective-permute-done.13.refs_1_, f32[32,1024]{1,0:T(8,128)S(1)} %collective-permute-done.14.refs_2_, ...), custom_call_target="tpu_custom_call", output_to_operand_aliasing={{}: (4, {})} | custom-call | flops 100663296 | bytes 4194304 | tf_op jit(solution)/shard_map/update_1_1/pallas_call | solution.py:412
  (9 shorter events, 0.2 us)
Async XLA Ops:
  0.6 26.3 %copy-start.3 = (s32[64]{0:T(128)S(1)}, s32[64]{0:T(128)}, u32[]{:S(2)}) copy-start(s32[64]{0:T(128)} %refs_0_.3) | copy-start | bytes 772
  0.6 26.3 %copy-start.1 = (f32[64,256]{1,0:T(8,128)S(1)}, f32[64,256]{1,0:T(8,128)}, u32[]{:S(2)}) copy-start(f32[64,256]{1,0:T(8,128)} %refs_1_.4) | copy-start | bytes 196612
  0.7 7.7 %copy-start = (bf16[4,32,4096]{2,1,0:T(8,128)(2,1)S(1)}, bf16[4,32,4096]{2,1,0:T(8,128)(2,1)}, u32[]{:S(2)}) copy-start(bf16[4,32,4096]{2,1,0:T(8,128)(2,1)} %refs_8_.1) | copy-start | bytes 3145732
  5.3 10.3 %copy-start.4 = (f32[32,1152]{1,0:T(8,128)S(1)}, f32[32,1152]{1,0:T(8,128)}, u32[]{:S(2)}) copy-start(f32[32,1152]{1,0:T(8,128)} %get-tuple-element.36) | copy-start | bytes 442372
  5.3 10.1 %collective-permute-start = (f32[32,1152]{1,0:T(8,128)}, f32[32,1152]{1,0:T(8,128)S(1)}, u32[]{:S(2)}, u32[]{:S(2)}) collective-permute-start(f32[32,1152]{1,0:T(8,128)} %get-tuple-element.37), channel_id=1, source_target_pairs={{0,1},{1,0},{2,3},{3,2},{4,5},{5,4},{6,7},{7,6},{8,9},{9,8},{10,11... | collective-permute-start | bytes 442376 | tf_op jit(solution)/shard_map/ppermute | solution.py:446
  8.5 27.0 %collective-permute-start.5 = (f32[4,32,2048]{2,1,0:T(8,128)S(1)}, f32[4,32,2048]{2,1,0:T(8,128)S(1)}, u32[]{:S(2)}, u32[]{:S(2)}) collective-permute-start(f32[4,32,2048]{2,1,0:T(8,128)S(1)} %dynamic-slice_convert_fusion), channel_id=1, source_target_pairs={{0,2},{2,0},{4,6},{6,4},{8,10},{10,8},{12,14},{14,12},{16,18},{18,... | collective-permute-start | bytes 3145736 | tf_op jit(solution)/shard_map/ppermute | solution.py:438
  8.5 7.0 %collective-permute-start.1 = (f32[32,1152]{1,0:T(8,128)}, f32[32,1152]{1,0:T(8,128)S(1)}, u32[]{:S(2)}, u32[]{:S(2)}) collective-permute-start(f32[32,1152]{1,0:T(8,128)} %get-tuple-element.38), channel_id=1, source_target_pairs={{0,2},{1,3},{2,0},{3,1},{4,6},{5,7},{6,4},{7,5},{8,10},{9,11},{10,... | collective-permute-start | bytes 442376 | tf_op jit(solution)/shard_map/ppermute | solution.py:446
  9.0 6.9 %collective-permute-start.2 = (f32[32,1152]{1,0:T(8,128)}, f32[32,1152]{1,0:T(8,128)S(1)}, u32[]{:S(2)}, u32[]{:S(2)}) collective-permute-start(f32[32,1152]{1,0:T(8,128)} %get-tuple-element.39), channel_id=1, source_target_pairs={{0,3},{1,2},{2,1},{3,0},{4,7},{5,6},{6,5},{7,4},{8,11},{9,10},{10,... | collective-permute-start | bytes 442376 | tf_op jit(solution)/shard_map/ppermute | solution.py:446
  9.0 0.8 %copy-start.2 = (bf16[32,512]{1,0:T(8,128)(2,1)S(1)}, bf16[32,512]{1,0:T(8,128)(2,1)}, u32[]{:S(2)}) copy-start(bf16[32,512]{1,0:T(8,128)(2,1)} %get-tuple-element.46.refs_0_) | copy-start | bytes 98308
  13.6 6.4 %collective-permute-start.6 = (f32[32,1024]{1,0:T(8,128)S(1)}, f32[32,1024]{1,0:T(8,128)S(1)}, u32[]{:S(2)}, u32[]{:S(2)}) collective-permute-start(f32[32,1024]{1,0:T(8,128)S(1)} %get-tuple-element.48), channel_id=1, source_target_pairs={{0,1},{1,0},{2,3},{3,2},{4,5},{5,4},{6,7},{7,6},{8,9},{9,8},{10,11... | collective-permute-start | bytes 393224 | tf_op jit(solution)/shard_map/ppermute | solution.py:446
  15.4 4.6 %collective-permute-start.7 = (f32[32,1024]{1,0:T(8,128)S(1)}, f32[32,1024]{1,0:T(8,128)S(1)}, u32[]{:S(2)}, u32[]{:S(2)}) collective-permute-start(f32[32,1024]{1,0:T(8,128)S(1)} %get-tuple-element.49), channel_id=1, source_target_pairs={{0,2},{1,3},{2,0},{3,1},{4,6},{5,7},{6,4},{7,5},{8,10},{9,11},{10,... | collective-permute-start | bytes 393224 | tf_op jit(solution)/shard_map/ppermute | solution.py:446
  15.6 6.2 %collective-permute-start.8 = (f32[32,1024]{1,0:T(8,128)S(1)}, f32[32,1024]{1,0:T(8,128)S(1)}, u32[]{:S(2)}, u32[]{:S(2)}) collective-permute-start(f32[32,1024]{1,0:T(8,128)S(1)} %get-tuple-element.50), channel_id=1, source_target_pairs={{0,3},{1,2},{2,1},{3,0},{4,7},{5,6},{6,5},{7,4},{8,11},{9,10},{10,... | collective-permute-start | bytes 393224 | tf_op jit(solution)/shard_map/ppermute | solution.py:446
  16.0 9.2 %collective-permute-start.3 = (f32[2,32,1152]{2,1,0:T(8,128)S(1)}, f32[2,32,1152]{2,1,0:T(8,128)S(1)}, u32[]{:S(2)}, u32[]{:S(2)}) collective-permute-start(f32[2,32,1152]{2,1,0:T(8,128)S(1)} %pad_maximum_fusion.foot_ref.refs_2_), channel_id=1, source_target_pairs={{0,4},{2,6},{4,0},{6,2},{8,12},{10,14},{12,8},{14,10},{16,20},{18,... | collective-permute-start | bytes 884744 | tf_op jit(solution)/shard_map/ppermute | solution.py:438
  21.8 9.2 %collective-permute-start.9 = (f32[2,32,1024]{2,1,0:T(8,128)S(1)}, f32[2,32,1024]{2,1,0:T(8,128)S(1)}, u32[]{:S(2)}, u32[]{:S(2)}) collective-permute-start(f32[2,32,1024]{2,1,0:T(8,128)S(1)} %pad_maximum_fusion.1.refs_5_), channel_id=1, source_target_pairs={{0,4},{2,6},{4,0},{6,2},{8,12},{10,14},{12,8},{14,10},{16,20},{18,... | collective-permute-start | bytes 786440 | tf_op jit(solution)/shard_map/ppermute | solution.py:438
  25.2 10.3 %collective-permute-start.4 = (f32[2,32,1152]{2,1,0:T(8,128)S(1)}, f32[2,32,1152]{2,1,0:T(8,128)S(1)}, u32[]{:S(2)}, u32[]{:S(2)}) collective-permute-start(f32[2,32,1152]{2,1,0:T(8,128)S(1)} %collective-permute-done.3._.refs_3_), channel_id=1, source_target_pairs={{0,8},{2,10},{4,28},{6,30},{8,16},{10,18},{12,4},{14,6},{16,24},{1... | collective-permute-start | bytes 884744 | tf_op jit(solution)/shard_map/ppermute | solution.py:438
  31.0 9.1 %collective-permute-start.10 = (f32[2,32,1024]{2,1,0:T(8,128)S(1)}, f32[2,32,1024]{2,1,0:T(8,128)S(1)}, u32[]{:S(2)}, u32[]{:S(2)}) collective-permute-start(f32[2,32,1024]{2,1,0:T(8,128)S(1)} %collective-permute-done.9.refs_6_), channel_id=1, source_target_pairs={{0,8},{2,10},{4,0},{6,2},{8,16},{10,18},{12,4},{14,6},{16,24},{18,... | collective-permute-start | bytes 786440 | tf_op jit(solution)/shard_map/ppermute | solution.py:438
  37.5 6.9 %collective-permute-start.16 = (f32[2,32,1024]{2,1,0:T(8,128)S(1)}, f32[2,32,1024]{2,1,0:T(8,128)S(1)}, u32[]{:S(2)}, u32[]{:S(2)}) collective-permute-start(f32[2,32,1024]{2,1,0:T(8,128)S(1)} %get-tuple-element.65), channel_id=1, source_target_pairs={{0,4},{2,6},{4,12},{6,14},{8,0},{10,2},{12,20},{14,22},{16,8},{18,... | collective-permute-start | bytes 786440 | tf_op jit(solution)/shard_map/ppermute | solution.py:438
  41.3 24.9 %collective-permute-start.21 = (f32[4,32,2048]{2,1,0:T(8,128)S(1)}, f32[4,32,2048]{2,1,0:T(8,128)S(1)}, u32[]{:S(2)}, u32[]{:S(2)}) collective-permute-start(f32[4,32,2048]{2,1,0:T(8,128)S(1)} %get-tuple-element.67), channel_id=1, source_target_pairs={{0,2},{2,0},{4,6},{6,4},{8,10},{10,8},{12,14},{14,12},{16,18},{18,... | collective-permute-start | bytes 3145736 | tf_op jit(solution)/shard_map/ppermute | solution.py:438
  41.4 8.9 %collective-permute-start.11 = (f32[2,32,1024]{2,1,0:T(8,128)S(1)}, f32[2,32,1024]{2,1,0:T(8,128)S(1)}, u32[]{:S(2)}, u32[]{:S(2)}) collective-permute-start(f32[2,32,1024]{2,1,0:T(8,128)S(1)} %get-tuple-element.61), channel_id=1, source_target_pairs={{0,24},{2,26},{4,12},{6,14},{8,0},{10,2},{12,20},{14,22},{16,8},{1... | collective-permute-start | bytes 786440 | tf_op jit(solution)/shard_map/ppermute | solution.py:438
  44.5 9.3 %collective-permute-start.17 = (f32[2,32,1024]{2,1,0:T(8,128)S(1)}, f32[2,32,1024]{2,1,0:T(8,128)S(1)}, u32[]{:S(2)}, u32[]{:S(2)}) collective-permute-start(f32[2,32,1024]{2,1,0:T(8,128)S(1)} %add.53), channel_id=1, source_target_pairs={{0,4},{2,6},{4,0},{6,2},{8,12},{10,14},{12,8},{14,10},{16,20},{18,... | collective-permute-start | bytes 786440 | tf_op jit(solution)/shard_map/ppermute | solution.py:438
  50.4 9.5 %collective-permute-start.12 = (f32[2,32,1024]{2,1,0:T(8,128)S(1)}, f32[2,32,1024]{2,1,0:T(8,128)S(1)}, u32[]{:S(2)}, u32[]{:S(2)}) collective-permute-start(f32[2,32,1024]{2,1,0:T(8,128)S(1)} %add.48), channel_id=1, source_target_pairs={{0,4},{2,6},{4,0},{6,2},{8,12},{10,14},{12,8},{14,10},{16,20},{18,... | collective-permute-start | bytes 786440 | tf_op jit(solution)/shard_map/ppermute | solution.py:438
  53.8 7.7 %collective-permute-start.18 = (f32[32,1024]{1,0:T(8,128)S(1)}, f32[32,1024]{1,0:T(8,128)S(1)}, u32[]{:S(2)}, u32[]{:S(2)}) collective-permute-start(f32[32,1024]{1,0:T(8,128)S(1)} %get-tuple-element.71), channel_id=1, source_target_pairs={{0,3},{1,2},{2,1},{3,0},{4,7},{5,6},{6,5},{7,4},{8,11},{9,10},{10,... | collective-permute-start | bytes 393224 | tf_op jit(solution)/shard_map/ppermute | solution.py:446
  54.4 7.2 %collective-permute-start.19 = (f32[32,1024]{1,0:T(8,128)S(1)}, f32[32,1024]{1,0:T(8,128)S(1)}, u32[]{:S(2)}, u32[]{:S(2)}) collective-permute-start(f32[32,1024]{1,0:T(8,128)S(1)} %get-tuple-element.71), channel_id=1, source_target_pairs={{0,2},{1,3},{2,0},{3,1},{4,6},{5,7},{6,4},{7,5},{8,10},{9,11},{10,... | collective-permute-start | bytes 393224 | tf_op jit(solution)/shard_map/ppermute | solution.py:446
  55.5 7.0 %collective-permute-start.20 = (f32[32,1024]{1,0:T(8,128)S(1)}, f32[32,1024]{1,0:T(8,128)S(1)}, u32[]{:S(2)}, u32[]{:S(2)}) collective-permute-start(f32[32,1024]{1,0:T(8,128)S(1)} %get-tuple-element.70.refs_4_), channel_id=1, source_target_pairs={{0,1},{1,0},{2,3},{3,2},{4,5},{5,4},{6,7},{7,6},{8,9},{9,8},{10,11... | collective-permute-start | bytes 393224 | tf_op jit(solution)/shard_map/ppermute | solution.py:446
  59.9 6.3 %collective-permute-start.15 = (f32[32,1024]{1,0:T(8,128)S(1)}, f32[32,1024]{1,0:T(8,128)S(1)}, u32[]{:S(2)}, u32[]{:S(2)}) collective-permute-start(f32[32,1024]{1,0:T(8,128)S(1)} %get-tuple-element.72.refs_2_), channel_id=1, source_target_pairs={{0,1},{1,0},{2,3},{3,2},{4,5},{5,4},{6,7},{7,6},{8,9},{9,8},{10,11... | collective-permute-start | bytes 393224 | tf_op jit(solution)/shard_map/ppermute | solution.py:446
  61.5 7.4 %collective-permute-start.13 = (f32[32,1024]{1,0:T(8,128)S(1)}, f32[32,1024]{1,0:T(8,128)S(1)}, u32[]{:S(2)}, u32[]{:S(2)}) collective-permute-start(f32[32,1024]{1,0:T(8,128)S(1)} %get-tuple-element.73), channel_id=1, source_target_pairs={{0,3},{1,2},{2,1},{3,0},{4,7},{5,6},{6,5},{7,4},{8,11},{9,10},{10,... | collective-permute-start | bytes 393224 | tf_op jit(solution)/shard_map/ppermute | solution.py:446
  61.5 7.4 %collective-permute-start.14 = (f32[32,1024]{1,0:T(8,128)S(1)}, f32[32,1024]{1,0:T(8,128)S(1)}, u32[]{:S(2)}, u32[]{:S(2)}) collective-permute-start(f32[32,1024]{1,0:T(8,128)S(1)} %get-tuple-element.73), channel_id=1, source_target_pairs={{0,2},{1,3},{2,0},{3,1},{4,6},{5,7},{6,4},{7,5},{8,10},{9,11},{10,... | collective-permute-start | bytes 393224 | tf_op jit(solution)/shard_map/ppermute | solution.py:446

commit v6 on v5

--- a/solution.py
+++ b/solution.py
@@ -130,14 +130,14 @@
     else:
         left = given_ref[...]
     if extra:
-        shape = (zdev * per, LANES)
+        shape = (SUBLANES, LANES)
         angle, lane = low_bits(iota(shape, 0), per), iota(shape, 1)
         starts = pick(angle, [start_buf[0, a].astype(F32) for a in range(per)])
         lengths = pick(angle, [len_buf[0, a].astype(F32) for a in range(per)])
         for d in range(groups):
             foot = jnp.where(lane == 2 * d, starts, jnp.where(lane == 2 * d + 1, lengths, 0.0))
             for h in range(len(halves)):
-                outs[h * groups + d][:, width:] = foot
+                outs[h * groups + d][:, zdev // zb * width:] = foot
     for h, zp, copy in copies:
         copy.wait()
         for at, size in tiles(width):
@@ -145,7 +145,7 @@
             product = dot(left, jnp.concatenate([p[0] for p in parts] + [p[1] for p in parts], axis=0))
             sums = product[:count] + product[count:]
             for d in range(groups):
-                outs[h * groups + d][zp * SUBLANES:(zp + 1) * SUBLANES, at:at + size] = (
+                outs[h * groups + d][:, zp * width + at:zp * width + at + size] = (
                     sums[d * SUBLANES:(d + 1) * SUBLANES]
                 )
 
@@ -155,7 +155,7 @@
     zdev, _, total = volume.shape
     first, keep, extra = given is None, chunk > 0, chunk == 0
     count, all_cells = groups * SUBLANES, table.shape[1]
-    out = jax.ShapeDtypeStruct((zdev * per, width + (LANES if extra else 0)), F32)
+    out = jax.ShapeDtypeStruct((SUBLANES, zdev // zb * width + (LANES if extra else 0)), F32)
     left = jax.ShapeDtypeStruct((2 * count, 2 * zb * cells), BF16)
     columns = (len(halves), zdev, cells, width)
     assert zb * cells == all_cells
@@ -238,7 +238,9 @@
         source = vol_ref.at[slices, :, pl.ds(start, width)]
         copies.append(pltpu.make_async_copy(source, kept_ref.at[h, slices], sems.at[h, zp]))
         copies[-1].start()
-    update_weights(dims, zdev, rdev, foot_ref[0, :, width:], order_ref, table_ref, rows_ref, left_ref)
+    batches = zdev // dims[2]
+    foot = jnp.concatenate([foot_ref[0, :, batches * width:]] * batches, axis=0)
+    update_weights(dims, zdev, rdev, foot, order_ref, table_ref, rows_ref, left_ref)
     for copy in copies:
         copy.wait()
 
@@ -281,7 +283,9 @@
         sent_out[:, :, :offset] = sent_before[...]
     outs, refs = refs[:3], refs[3:]
     if first:
-        foot = jnp.concatenate([r[i, :, width:] for r in sums_refs for i in range(2)], axis=0)
+        foot = jnp.concatenate(
+            [r[i, :, zdev // zb * width:] for r in sums_refs for i in range(2) for _ in range(zdev // zb)], axis=0
+        )
         kernel = footprint_matrix(dims, zdev, rdev, foot)
         count, rows = kernel.shape
         kernel_t = kernel.T
@@ -305,7 +309,13 @@
         mine = mine_ref[:, :, pl.ds(pl.multiple_of(start + at, LANES), size)].astype(F32)
         theirs = theirs_ref[:, :, offset + at:offset + at + size]
         measured = jnp.concatenate([m.reshape(per * rdev, size) for m in (mine, theirs)], axis=0)
-        sums = jnp.concatenate([r[i, :, columns] for r in sums_refs for i in range(2)], axis=0)
+        sums = jnp.concatenate(
+            [
+                r[i, :, zp * width + at:zp * width + at + size]
+                for r in sums_refs for i in range(2) for zp in range(zdev // zb)
+            ],
+            axis=0,
+        )
         residual = (measured - dot3(ahead, split(sums))) * inverse
         placed = slice(offset + at, offset + at + size)
         mine_out[:, :, placed] = residual[:per * rdev].reshape(per, rdev, size)

time: 71.5 us -> 71 us (level)
  no operation moved by 1% of the time
where the time goes in v6:
time: 71 us; the launch traced here: 70.8 us
  Pallas kernels  24.5 us (35%)
  starting transfers between devices  24.5 us (35%)
  waiting for transfers between devices  19.8 us (28%)
  between operations  0.84 us (1%)
  local copies, waits for them, and re-layouts  0.78 us (1%)
    ppermute x10, waiting for transfers between devices, along(): return lax.ppermute(value, 'slab', pairs)  15.3 us
    ppermute x10, starting transfers between devices, along(): return lax.ppermute(value, 'slab', pairs)  14.3 us
    ppermute x12, starting transfers between devices, spread(): return lax.ppermute(value, ('slab', 'ang'), pairs)  10.2 us
    pallas_call x3, Pallas kernels, update_step(): pl.pallas_call(functools.partial(update_kernel, dims, first, halves, tota...  8.69 us
    pallas_call x2, Pallas kernels, ray_sums(): pl.pallas_call(functools.partial(rays_kernel, dims, first, keep, extra, h...  8.45 us
    ppermute x12, waiting for transfers between devices, spread(): return lax.ppermute(value, ('slab', 'ang'), pairs)  4.48 us
    pallas_call x1, Pallas kernels, prepare_step(): pl.pallas_call(functools.partial(prepare_kernel, dims, rdev, total // 2,...  4.09 us
    pallas_call x2, Pallas kernels, residual_step(): pl.pallas_call(functools.partial(residual_kernel, dims, first, total // 2...  3.3 us
  transfers between devices with their start and end apart: 22, of which 9 were waited for; matrix products, arithmetic and copies ran while one was open for 0% of the time, Pallas kernels for 25%

profile of v6, /device:TPU:0, one launch (start us, length us, event | category | flops | bytes accessed | tf_op | source)
XLA Modules:
  0.0 70.8 jit_solution(1629849121031216501)
XLA Ops:
  0.6 0.0 copy-start.3
  0.6 0.0 copy-start.1
  0.7 0.0 copy-start
  0.7 4.6 %ray_sums_0_0.1 = (f32[8,4224]{1,0:T(8,128)}, f32[8,4224]{1,0:T(8,128)}, f32[8,4224]{1,0:T(8,128)}, f32[8,4224]{1,0:T(8,128)}, bf16[32,512]{1,0:T(8,128)(2,1)}) custom-call(s32[64]{0:T(128)} %refs_0_.3, s32[1,4]{1,0:T(1,128)} %refs_1_.3, s32[1,4]{1,0:T(1,128)} %refs_2_.1, f32[64,256]{1,0:T(8,128)} %refs_1_.4, f32[8,128,4096]{2,1,0:T(8,128)} %refs_1_.5), custom_call_target="tpu_custom_call" | custom-call | flops 67108864 | bytes 8388608 | tf_op jit(solution)/shard_map/ray_sums_0_0/pallas_call | solution.py:176
  5.3 0.0 copy-start.4
  5.3 3.0 %collective-permute-start = (f32[8,4224]{1,0:T(8,128)}, f32[8,4224]{1,0:T(8,128)S(1)}, u32[]{:S(2)}, u32[]{:S(2)}) collective-permute-start(f32[8,4224]{1,0:T(8,128)} %get-tuple-element.37), channel_id=1, source_target_pairs={{0,1},{1,0},{2,3},{3,2},{4,5},{5,4},{6,7},{7,6},{8,9},{9,8},{10,11... | collective-permute-start | bytes 405512 | tf_op jit(solution)/shard_map/ppermute | solution.py:456
  8.4 0.0 copy-done
  8.4 0.1 dynamic-slice_convert_fusion
  8.5 0.1 collective-permute-start.5
  8.5 0.5 collective-permute-start.1
  9.0 0.0 collective-permute-start.2
  9.0 0.0 copy-start.2
  9.0 0.8 %copy-done.2 = bf16[32,512]{1,0:T(8,128)(2,1)S(1)} copy-done((bf16[32,512]{1,0:T(8,128)(2,1)S(1)}, bf16[32,512]{1,0:T(8,128)(2,1)}, u32[]{:S(2)}) %copy-start.2) | copy-done | bytes 32792
  9.8 3.8 %ray_sums_1_0.1 = (f32[8,4096]{1,0:T(8,128)S(1)}, f32[8,4096]{1,0:T(8,128)S(1)}, f32[8,4096]{1,0:T(8,128)S(1)}, f32[8,4096]{1,0:T(8,128)S(1)}, f32[2,8,128,1024]{3,2,1,0:T(8,128)S(1)}) custom-call(bf16[32,512]{1,0:T(8,128)(2,1)S(1)} %copy-done.2, f32[8,128,4096]{2,1,0:T(8,128)} %refs_1_.5), custom_call_target="tpu_custom_call" | custom-call | flops 67108864 | bytes 8388608 | tf_op jit(solution)/shard_map/ray_sums_1_0/pallas_call | solution.py:176
  13.6 1.8 %collective-permute-start.6 = (f32[8,4096]{1,0:T(8,128)S(1)}, f32[8,4096]{1,0:T(8,128)S(1)}, u32[]{:S(2)}, u32[]{:S(2)}) collective-permute-start(f32[8,4096]{1,0:T(8,128)S(1)} %get-tuple-element.48), channel_id=1, source_target_pairs={{0,1},{1,0},{2,3},{3,2},{4,5},{5,4},{6,7},{7,6},{8,9},{9,8},{10,11... | collective-permute-start | bytes 393224 | tf_op jit(solution)/shard_map/ppermute | solution.py:456
  15.4 0.0 collective-permute-done
  15.4 0.2 collective-permute-start.7
  15.6 0.0 copy-done.4
  15.6 0.0 collective-permute-done.1
  15.6 0.3 collective-permute-start.8
  15.9 0.0 collective-permute-done.2
  16.0 1.7 %collective-permute-start.3 = (f32[2,8,4224]{2,1,0:T(8,128)S(1)}, f32[2,8,4224]{2,1,0:T(8,128)S(1)}, u32[]{:S(2)}, u32[]{:S(2)}) collective-permute-start(f32[2,8,4224]{2,1,0:T(8,128)S(1)} %pad_maximum_fusion.foot_ref.refs_2_), channel_id=1, source_target_pairs={{0,4},{2,6},{4,0},{6,2},{8,12},{10,14},{12,8},{14,10},{16,20},{18,... | collective-permute-start | bytes 811016 | tf_op jit(solution)/shard_map/ppermute | solution.py:448
  17.7 2.3 %collective-permute-done.6 = f32[8,4096]{1,0:T(8,128)S(1)} collective-permute-done((f32[8,4096]{1,0:T(8,128)S(1)}, f32[8,4096]{1,0:T(8,128)S(1)}, u32[]{:S(2)}, u32[]{:S(2)}) %collective-permute-start.6) | collective-permute-done | bytes 131104 | tf_op jit(solution)/shard_map/ppermute | solution.py:456
  20.0 0.0 collective-permute-done.7
  20.0 1.8 %collective-permute-done.8 = f32[8,4096]{1,0:T(8,128)S(1)} collective-permute-done((f32[8,4096]{1,0:T(8,128)S(1)}, f32[8,4096]{1,0:T(8,128)S(1)}, u32[]{:S(2)}, u32[]{:S(2)}) %collective-permute-start.8) | collective-permute-done | bytes 131104 | tf_op jit(solution)/shard_map/ppermute | solution.py:456
  21.8 1.9 %collective-permute-start.9 = (f32[2,8,4096]{2,1,0:T(8,128)S(1)}, f32[2,8,4096]{2,1,0:T(8,128)S(1)}, u32[]{:S(2)}, u32[]{:S(2)}) collective-permute-start(f32[2,8,4096]{2,1,0:T(8,128)S(1)} %pad_maximum_fusion.1.refs_5_), channel_id=1, source_target_pairs={{0,4},{2,6},{4,0},{6,2},{8,12},{10,14},{12,8},{14,10},{16,20},{18,... | collective-permute-start | bytes 786440 | tf_op jit(solution)/shard_map/ppermute | solution.py:448
  23.7 0.9 %collective-permute-done.3._.refs_3_ = f32[2,8,4224]{2,1,0:T(8,128)S(1)} collective-permute-done((f32[2,8,4224]{2,1,0:T(8,128)S(1)}, f32[2,8,4224]{2,1,0:T(8,128)S(1)}, u32[]{:S(2)}, u32[]{:S(2)}) %collective-permute-start.3) | collective-permute-done | bytes 270368 | tf_op jit(solution)/shard_map/ppermute | solution.py:448
  24.6 1.7 %collective-permute-start.4 = (f32[2,8,4224]{2,1,0:T(8,128)S(1)}, f32[2,8,4224]{2,1,0:T(8,128)S(1)}, u32[]{:S(2)}, u32[]{:S(2)}) collective-permute-start(f32[2,8,4224]{2,1,0:T(8,128)S(1)} %collective-permute-done.3._.refs_3_), channel_id=1, source_target_pairs={{0,8},{2,10},{4,28},{6,30},{8,16},{10,18},{12,4},{14,6},{16,24},{1... | collective-permute-start | bytes 811016 | tf_op jit(solution)/shard_map/ppermute | solution.py:448
  26.4 0.0 copy-done.3
  26.4 0.0 copy-done.1
  26.4 4.1 %prepare.1 = (f32[2,8,128,1024]{3,2,1,0:T(8,128)S(1)}, bf16[4,256,128]{2,1,0:T(8,128)(2,1)S(1)}) custom-call(s32[64]{0:T(128)S(1)} %copy-done.3, f32[64,256]{1,0:T(8,128)S(1)} %copy-done.1, f32[2,8,4224]{2,1,0:T(8,128)S(1)} %pad_maximum_fusion.foot_ref.refs_2_, f32[2,8,4224]{2,1,0:T(8,128)S(1)} %collective-permute-done.3._.refs_3_, f32[8,128,4096]{2,1,0:T(8,128)} %refs_1_.5), custom_call_target="tpu_custom_call" | custom-call | bytes 8388608 | tf_op jit(solution)/shard_map/prepare/pallas_call | solution.py:252
  30.5 0.3 collective-permute-done.9.refs_6_
  30.7 1.8 %collective-permute-start.10 = (f32[2,8,4096]{2,1,0:T(8,128)S(1)}, f32[2,8,4096]{2,1,0:T(8,128)S(1)}, u32[]{:S(2)}, u32[]{:S(2)}) collective-permute-start(f32[2,8,4096]{2,1,0:T(8,128)S(1)} %collective-permute-done.9.refs_6_), channel_id=1, source_target_pairs={{0,8},{2,10},{4,0},{6,2},{8,16},{10,18},{12,4},{14,6},{16,24},{18,... | collective-permute-start | bytes 786440 | tf_op jit(solution)/shard_map/ppermute | solution.py:448
  32.6 1.8 %collective-permute-done.4.refs_4_ = f32[2,8,4224]{2,1,0:T(8,128)S(1)} collective-permute-done((f32[2,8,4224]{2,1,0:T(8,128)S(1)}, f32[2,8,4224]{2,1,0:T(8,128)S(1)}, u32[]{:S(2)}, u32[]{:S(2)}) %collective-permute-start.4) | collective-permute-done | bytes 270368 | tf_op jit(solution)/shard_map/ppermute | solution.py:448
  34.4 0.0 collective-permute-done.5.refs_6_.refs_9_
  34.4 2.1 %residual_0.1 = (f32[4,32,1024]{2,1,0:T(8,128)S(1)}, f32[4,32,1024]{2,1,0:T(8,128)S(1)}, f32[2,32,1024]{2,1,0:T(8,128)S(1)}, f32[2,32,1024]{2,1,0:T(8,128)S(1)},...) custom-call(s32[64]{0:T(128)S(1)} %copy-done.3, ...), custom_call_target="tpu_custom_call" | custom-call | flops 603979776 | bytes 3670016 | tf_op jit(solution)/shard_map/residual_0/pallas_call | solution.py:346
  36.4 0.8 %collective-permute-start.16 = (f32[2,32,1024]{2,1,0:T(8,128)S(1)}, f32[2,32,1024]{2,1,0:T(8,128)S(1)}, u32[]{:S(2)}, u32[]{:S(2)}) collective-permute-start(f32[2,32,1024]{2,1,0:T(8,128)S(1)} %get-tuple-element.65), channel_id=1, source_target_pairs={{0,4},{2,6},{4,12},{6,14},{8,0},{10,2},{12,20},{14,22},{16,8},{18,... | collective-permute-start | bytes 786440 | tf_op jit(solution)/shard_map/ppermute | solution.py:448
  37.2 2.3 %collective-permute-done.10.refs_7_ = f32[2,8,4096]{2,1,0:T(8,128)S(1)} collective-permute-done((f32[2,8,4096]{2,1,0:T(8,128)S(1)}, f32[2,8,4096]{2,1,0:T(8,128)S(1)}, u32[]{:S(2)}, u32[]{:S(2)}) %collective-permute-start.10) | collective-permute-done | bytes 262176 | tf_op jit(solution)/shard_map/ppermute | solution.py:448
  39.6 1.2 %residual_1.1 = (f32[4,32,2048]{2,1,0:T(8,128)S(1)}, f32[4,32,2048]{2,1,0:T(8,128)S(1)}, f32[2,32,1024]{2,1,0:T(8,128)S(1)}, f32[2,32,1024]{2,1,0:T(8,128)S(1)}, f32[2,32,1024]{2,1,0:T(8,128)S(1)}) custom-call(bf16[256,192]{1,0:T(8,128)(2,1)S(1)} %get-tuple-element.41.refs_0_, bf16[256,192]{1,0:T(8,128)(2,1)S(1)} %get-tuple-element.42.refs_1_, ...), custom_call_target="tpu_custom_call" | custom-call | flops 603979776 | bytes 3670016 | tf_op jit(solution)/shard_map/residual_1/pallas_call | solution.py:346
  40.8 0.1 collective-permute-start.21
  40.9 3.1 %collective-permute-start.11 = (f32[2,32,1024]{2,1,0:T(8,128)S(1)}, f32[2,32,1024]{2,1,0:T(8,128)S(1)}, u32[]{:S(2)}, u32[]{:S(2)}) collective-permute-start(f32[2,32,1024]{2,1,0:T(8,128)S(1)} %get-tuple-element.61), channel_id=1, source_target_pairs={{0,24},{2,26},{4,12},{6,14},{8,0},{10,2},{12,20},{14,22},{16,8},{1... | collective-permute-start | bytes 786440 | tf_op jit(solution)/shard_map/ppermute | solution.py:448
  44.0 0.0 collective-permute-done.16
  44.0 0.1 collective-permute-start.17
  44.1 6.0 %collective-permute-done.11 = f32[2,32,1024]{2,1,0:T(8,128)S(1)} collective-permute-done((f32[2,32,1024]{2,1,0:T(8,128)S(1)}, f32[2,32,1024]{2,1,0:T(8,128)S(1)}, u32[]{:S(2)}, u32[]{:S(2)}) %collective-permute-start.11) | collective-permute-done | bytes 262176 | tf_op jit(solution)/shard_map/ppermute | solution.py:448
  50.2 3.1 %collective-permute-start.12 = (f32[2,32,1024]{2,1,0:T(8,128)S(1)}, f32[2,32,1024]{2,1,0:T(8,128)S(1)}, u32[]{:S(2)}, u32[]{:S(2)}) collective-permute-start(f32[2,32,1024]{2,1,0:T(8,128)S(1)} %add.48), channel_id=1, source_target_pairs={{0,4},{2,6},{4,0},{6,2},{8,12},{10,14},{12,8},{14,10},{16,20},{18,... | collective-permute-start | bytes 786440 | tf_op jit(solution)/shard_map/ppermute | solution.py:448
  53.2 0.0 collective-permute-done.17
  53.3 0.6 collective-permute-start.18
  53.8 1.1 %collective-permute-start.19 = (f32[32,1024]{1,0:T(8,128)S(1)}, f32[32,1024]{1,0:T(8,128)S(1)}, u32[]{:S(2)}, u32[]{:S(2)}) collective-permute-start(f32[32,1024]{1,0:T(8,128)S(1)} %get-tuple-element.71), channel_id=1, source_target_pairs={{0,2},{1,3},{2,0},{3,1},{4,6},{5,7},{6,4},{7,5},{8,10},{9,11},{10,... | collective-permute-start | bytes 393224 | tf_op jit(solution)/shard_map/ppermute | solution.py:456
  55.0 0.5 collective-permute-start.20
  55.5 3.9 %collective-permute-done.12 = f32[2,32,1024]{2,1,0:T(8,128)S(1)} collective-permute-done((f32[2,32,1024]{2,1,0:T(8,128)S(1)}, f32[2,32,1024]{2,1,0:T(8,128)S(1)}, u32[]{:S(2)}, u32[]{:S(2)}) %collective-permute-start.12) | collective-permute-done | bytes 262176 | tf_op jit(solution)/shard_map/ppermute | solution.py:448
  59.4 1.6 %collective-permute-start.15 = (f32[32,1024]{1,0:T(8,128)S(1)}, f32[32,1024]{1,0:T(8,128)S(1)}, u32[]{:S(2)}, u32[]{:S(2)}) collective-permute-start(f32[32,1024]{1,0:T(8,128)S(1)} %get-tuple-element.72.refs_2_), channel_id=1, source_target_pairs={{0,1},{1,0},{2,3},{3,2},{4,5},{5,4},{6,7},{7,6},{8,9},{9,8},{10,11... | collective-permute-start | bytes 393224 | tf_op jit(solution)/shard_map/ppermute | solution.py:456
  61.0 0.0 collective-permute-done.18.refs_1_
  61.0 0.0 collective-permute-start.13
  61.0 0.0 collective-permute-done.19.refs_2_
  61.0 0.6 collective-permute-start.14
  61.6 0.4 collective-permute-done.20.refs_3_
  62.0 3.6 %update_0_0.1.refs_4_ = f32[8,128,4096]{2,1,0:T(8,128)} custom-call(bf16[4,256,128]{2,1,0:T(8,128)(2,1)S(1)} %get-tuple-element.40.refs_0_, f32[32,1024]{1,0:T(8,128)S(1)} %collective-permute-done.18.refs_1_, f32[32,1024]{1,0:T(8,128)S(1)} %collective-permute-done.19.refs_2_, f32[32,1024]{1,0:T(8,128)S(1)} %collective-permute-done.20.refs_3_, ...), custom_call_target="tpu_custom_call" | custom-call | flops 201326592 | bytes 8388608 | tf_op jit(solution)/shard_map/update_0_0/pallas_call | solution.py:422
  65.7 0.0 collective-permute-done.15.refs_1_
  65.7 0.0 collective-permute-done.21.refs_6_
  65.7 2.7 %update_1_0.1 = (f32[8,128,4096]{2,1,0:T(8,128)}, f32[4,32,4096]{2,1,0:T(8,128)}) custom-call(bf16[4,256,128]{2,1,0:T(8,128)(2,1)S(1)} %get-tuple-element.40.refs_0_, f32[32,1024]{1,0:T(8,128)S(1)} %collective-permute-done.15.refs_1_, f32[32,1024]{1,0:T(8,128)S(1)} %get-tuple-element.72.refs_2_, ...), custom_call_target="tpu_custom_call", output_to_operand_aliasing={{0}: (4, {})} | custom-call | flops 100663296 | bytes 4194304 | tf_op jit(solution)/shard_map/update_1_0/pallas_call | solution.py:422
  68.4 0.0 collective-permute-done.13.refs_1_
  68.4 0.0 collective-permute-done.14.refs_2_
  68.5 2.3 %update_1_1.1 = f32[8,128,4096]{2,1,0:T(8,128)} custom-call(bf16[4,256,128]{2,1,0:T(8,128)(2,1)S(1)} %get-tuple-element.40.refs_0_, f32[32,1024]{1,0:T(8,128)S(1)} %collective-permute-done.13.refs_1_, f32[32,1024]{1,0:T(8,128)S(1)} %collective-permute-done.14.refs_2_, ...), custom_call_target="tpu_custom_call", output_to_operand_aliasing={{}: (4, {})} | custom-call | flops 100663296 | bytes 4194304 | tf_op jit(solution)/shard_map/update_1_1/pallas_call | solution.py:422
  (9 shorter events, 0.3 us)
Async XLA Ops:
  0.6 25.7 %copy-start.3 = (s32[64]{0:T(128)S(1)}, s32[64]{0:T(128)}, u32[]{:S(2)}) copy-start(s32[64]{0:T(128)} %refs_0_.3) | copy-start | bytes 772
  0.6 25.7 %copy-start.1 = (f32[64,256]{1,0:T(8,128)S(1)}, f32[64,256]{1,0:T(8,128)}, u32[]{:S(2)}) copy-start(f32[64,256]{1,0:T(8,128)} %refs_1_.4) | copy-start | bytes 196612
  0.7 7.7 %copy-start = (bf16[4,32,4096]{2,1,0:T(8,128)(2,1)S(1)}, bf16[4,32,4096]{2,1,0:T(8,128)(2,1)}, u32[]{:S(2)}) copy-start(bf16[4,32,4096]{2,1,0:T(8,128)(2,1)} %refs_8_.1) | copy-start | bytes 3145732
  5.3 10.2 %copy-start.4 = (f32[8,4224]{1,0:T(8,128)S(1)}, f32[8,4224]{1,0:T(8,128)}, u32[]{:S(2)}) copy-start(f32[8,4224]{1,0:T(8,128)} %get-tuple-element.36) | copy-start | bytes 405508
  5.3 10.1 %collective-permute-start = (f32[8,4224]{1,0:T(8,128)}, f32[8,4224]{1,0:T(8,128)S(1)}, u32[]{:S(2)}, u32[]{:S(2)}) collective-permute-start(f32[8,4224]{1,0:T(8,128)} %get-tuple-element.37), channel_id=1, source_target_pairs={{0,1},{1,0},{2,3},{3,2},{4,5},{5,4},{6,7},{7,6},{8,9},{9,8},{10,11... | collective-permute-start | bytes 405512 | tf_op jit(solution)/shard_map/ppermute | solution.py:456
  8.5 25.9 %collective-permute-start.5 = (f32[4,32,2048]{2,1,0:T(8,128)S(1)}, f32[4,32,2048]{2,1,0:T(8,128)S(1)}, u32[]{:S(2)}, u32[]{:S(2)}) collective-permute-start(f32[4,32,2048]{2,1,0:T(8,128)S(1)} %dynamic-slice_convert_fusion), channel_id=1, source_target_pairs={{0,2},{2,0},{4,6},{6,4},{8,10},{10,8},{12,14},{14,12},{16,18},{18,... | collective-permute-start | bytes 3145736 | tf_op jit(solution)/shard_map/ppermute | solution.py:448
  8.5 7.0 %collective-permute-start.1 = (f32[8,4224]{1,0:T(8,128)}, f32[8,4224]{1,0:T(8,128)S(1)}, u32[]{:S(2)}, u32[]{:S(2)}) collective-permute-start(f32[8,4224]{1,0:T(8,128)} %get-tuple-element.38), channel_id=1, source_target_pairs={{0,2},{1,3},{2,0},{3,1},{4,6},{5,7},{6,4},{7,5},{8,10},{9,11},{10,... | collective-permute-start | bytes 405512 | tf_op jit(solution)/shard_map/ppermute | solution.py:456
  9.0 6.9 %collective-permute-start.2 = (f32[8,4224]{1,0:T(8,128)}, f32[8,4224]{1,0:T(8,128)S(1)}, u32[]{:S(2)}, u32[]{:S(2)}) collective-permute-start(f32[8,4224]{1,0:T(8,128)} %get-tuple-element.39), channel_id=1, source_target_pairs={{0,3},{1,2},{2,1},{3,0},{4,7},{5,6},{6,5},{7,4},{8,11},{9,10},{10,... | collective-permute-start | bytes 405512 | tf_op jit(solution)/shard_map/ppermute | solution.py:456
  9.0 0.8 %copy-start.2 = (bf16[32,512]{1,0:T(8,128)(2,1)S(1)}, bf16[32,512]{1,0:T(8,128)(2,1)}, u32[]{:S(2)}) copy-start(bf16[32,512]{1,0:T(8,128)(2,1)} %get-tuple-element.46.refs_0_) | copy-start | bytes 98308
  13.6 6.4 %collective-permute-start.6 = (f32[8,4096]{1,0:T(8,128)S(1)}, f32[8,4096]{1,0:T(8,128)S(1)}, u32[]{:S(2)}, u32[]{:S(2)}) collective-permute-start(f32[8,4096]{1,0:T(8,128)S(1)} %get-tuple-element.48), channel_id=1, source_target_pairs={{0,1},{1,0},{2,3},{3,2},{4,5},{5,4},{6,7},{7,6},{8,9},{9,8},{10,11... | collective-permute-start | bytes 393224 | tf_op jit(solution)/shard_map/ppermute | solution.py:456
  15.4 4.6 %collective-permute-start.7 = (f32[8,4096]{1,0:T(8,128)S(1)}, f32[8,4096]{1,0:T(8,128)S(1)}, u32[]{:S(2)}, u32[]{:S(2)}) collective-permute-start(f32[8,4096]{1,0:T(8,128)S(1)} %get-tuple-element.49), channel_id=1, source_target_pairs={{0,2},{1,3},{2,0},{3,1},{4,6},{5,7},{6,4},{7,5},{8,10},{9,11},{10,... | collective-permute-start | bytes 393224 | tf_op jit(solution)/shard_map/ppermute | solution.py:456
  15.6 6.2 %collective-permute-start.8 = (f32[8,4096]{1,0:T(8,128)S(1)}, f32[8,4096]{1,0:T(8,128)S(1)}, u32[]{:S(2)}, u32[]{:S(2)}) collective-permute-start(f32[8,4096]{1,0:T(8,128)S(1)} %get-tuple-element.50), channel_id=1, source_target_pairs={{0,3},{1,2},{2,1},{3,0},{4,7},{5,6},{6,5},{7,4},{8,11},{9,10},{10,... | collective-permute-start | bytes 393224 | tf_op jit(solution)/shard_map/ppermute | solution.py:456
  16.0 8.6 %collective-permute-start.3 = (f32[2,8,4224]{2,1,0:T(8,128)S(1)}, f32[2,8,4224]{2,1,0:T(8,128)S(1)}, u32[]{:S(2)}, u32[]{:S(2)}) collective-permute-start(f32[2,8,4224]{2,1,0:T(8,128)S(1)} %pad_maximum_fusion.foot_ref.refs_2_), channel_id=1, source_target_pairs={{0,4},{2,6},{4,0},{6,2},{8,12},{10,14},{12,8},{14,10},{16,20},{18,... | collective-permute-start | bytes 811016 | tf_op jit(solution)/shard_map/ppermute | solution.py:448
  21.8 8.9 %collective-permute-start.9 = (f32[2,8,4096]{2,1,0:T(8,128)S(1)}, f32[2,8,4096]{2,1,0:T(8,128)S(1)}, u32[]{:S(2)}, u32[]{:S(2)}) collective-permute-start(f32[2,8,4096]{2,1,0:T(8,128)S(1)} %pad_maximum_fusion.1.refs_5_), channel_id=1, source_target_pairs={{0,4},{2,6},{4,0},{6,2},{8,12},{10,14},{12,8},{14,10},{16,20},{18,... | collective-permute-start | bytes 786440 | tf_op jit(solution)/shard_map/ppermute | solution.py:448
  24.6 9.7 %collective-permute-start.4 = (f32[2,8,4224]{2,1,0:T(8,128)S(1)}, f32[2,8,4224]{2,1,0:T(8,128)S(1)}, u32[]{:S(2)}, u32[]{:S(2)}) collective-permute-start(f32[2,8,4224]{2,1,0:T(8,128)S(1)} %collective-permute-done.3._.refs_3_), channel_id=1, source_target_pairs={{0,8},{2,10},{4,28},{6,30},{8,16},{10,18},{12,4},{14,6},{16,24},{1... | collective-permute-start | bytes 811016 | tf_op jit(solution)/shard_map/ppermute | solution.py:448
  30.7 8.8 %collective-permute-start.10 = (f32[2,8,4096]{2,1,0:T(8,128)S(1)}, f32[2,8,4096]{2,1,0:T(8,128)S(1)}, u32[]{:S(2)}, u32[]{:S(2)}) collective-permute-start(f32[2,8,4096]{2,1,0:T(8,128)S(1)} %collective-permute-done.9.refs_6_), channel_id=1, source_target_pairs={{0,8},{2,10},{4,0},{6,2},{8,16},{10,18},{12,4},{14,6},{16,24},{18,... | collective-permute-start | bytes 786440 | tf_op jit(solution)/shard_map/ppermute | solution.py:448
  36.4 7.5 %collective-permute-start.16 = (f32[2,32,1024]{2,1,0:T(8,128)S(1)}, f32[2,32,1024]{2,1,0:T(8,128)S(1)}, u32[]{:S(2)}, u32[]{:S(2)}) collective-permute-start(f32[2,32,1024]{2,1,0:T(8,128)S(1)} %get-tuple-element.65), channel_id=1, source_target_pairs={{0,4},{2,6},{4,12},{6,14},{8,0},{10,2},{12,20},{14,22},{16,8},{18,... | collective-permute-start | bytes 786440 | tf_op jit(solution)/shard_map/ppermute | solution.py:448
  40.8 24.9 %collective-permute-start.21 = (f32[4,32,2048]{2,1,0:T(8,128)S(1)}, f32[4,32,2048]{2,1,0:T(8,128)S(1)}, u32[]{:S(2)}, u32[]{:S(2)}) collective-permute-start(f32[4,32,2048]{2,1,0:T(8,128)S(1)} %get-tuple-element.67), channel_id=1, source_target_pairs={{0,2},{2,0},{4,6},{6,4},{8,10},{10,8},{12,14},{14,12},{16,18},{18,... | collective-permute-start | bytes 3145736 | tf_op jit(solution)/shard_map/ppermute | solution.py:448
  40.9 9.2 %collective-permute-start.11 = (f32[2,32,1024]{2,1,0:T(8,128)S(1)}, f32[2,32,1024]{2,1,0:T(8,128)S(1)}, u32[]{:S(2)}, u32[]{:S(2)}) collective-permute-start(f32[2,32,1024]{2,1,0:T(8,128)S(1)} %get-tuple-element.61), channel_id=1, source_target_pairs={{0,24},{2,26},{4,12},{6,14},{8,0},{10,2},{12,20},{14,22},{16,8},{1... | collective-permute-start | bytes 786440 | tf_op jit(solution)/shard_map/ppermute | solution.py:448
  44.0 9.2 %collective-permute-start.17 = (f32[2,32,1024]{2,1,0:T(8,128)S(1)}, f32[2,32,1024]{2,1,0:T(8,128)S(1)}, u32[]{:S(2)}, u32[]{:S(2)}) collective-permute-start(f32[2,32,1024]{2,1,0:T(8,128)S(1)} %add.53), channel_id=1, source_target_pairs={{0,4},{2,6},{4,0},{6,2},{8,12},{10,14},{12,8},{14,10},{16,20},{18,... | collective-permute-start | bytes 786440 | tf_op jit(solution)/shard_map/ppermute | solution.py:448
  50.2 9.2 %collective-permute-start.12 = (f32[2,32,1024]{2,1,0:T(8,128)S(1)}, f32[2,32,1024]{2,1,0:T(8,128)S(1)}, u32[]{:S(2)}, u32[]{:S(2)}) collective-permute-start(f32[2,32,1024]{2,1,0:T(8,128)S(1)} %add.48), channel_id=1, source_target_pairs={{0,4},{2,6},{4,0},{6,2},{8,12},{10,14},{12,8},{14,10},{16,20},{18,... | collective-permute-start | bytes 786440 | tf_op jit(solution)/shard_map/ppermute | solution.py:448
  53.3 7.7 %collective-permute-start.18 = (f32[32,1024]{1,0:T(8,128)S(1)}, f32[32,1024]{1,0:T(8,128)S(1)}, u32[]{:S(2)}, u32[]{:S(2)}) collective-permute-start(f32[32,1024]{1,0:T(8,128)S(1)} %get-tuple-element.71), channel_id=1, source_target_pairs={{0,3},{1,2},{2,1},{3,0},{4,7},{5,6},{6,5},{7,4},{8,11},{9,10},{10,... | collective-permute-start | bytes 393224 | tf_op jit(solution)/shard_map/ppermute | solution.py:456
  53.8 7.2 %collective-permute-start.19 = (f32[32,1024]{1,0:T(8,128)S(1)}, f32[32,1024]{1,0:T(8,128)S(1)}, u32[]{:S(2)}, u32[]{:S(2)}) collective-permute-start(f32[32,1024]{1,0:T(8,128)S(1)} %get-tuple-element.71), channel_id=1, source_target_pairs={{0,2},{1,3},{2,0},{3,1},{4,6},{5,7},{6,4},{7,5},{8,10},{9,11},{10,... | collective-permute-start | bytes 393224 | tf_op jit(solution)/shard_map/ppermute | solution.py:456
  55.0 7.0 %collective-permute-start.20 = (f32[32,1024]{1,0:T(8,128)S(1)}, f32[32,1024]{1,0:T(8,128)S(1)}, u32[]{:S(2)}, u32[]{:S(2)}) collective-permute-start(f32[32,1024]{1,0:T(8,128)S(1)} %get-tuple-element.70.refs_4_), channel_id=1, source_target_pairs={{0,1},{1,0},{2,3},{3,2},{4,5},{5,4},{6,7},{7,6},{8,9},{9,8},{10,11... | collective-permute-start | bytes 393224 | tf_op jit(solution)/shard_map/ppermute | solution.py:456
  59.4 6.3 %collective-permute-start.15 = (f32[32,1024]{1,0:T(8,128)S(1)}, f32[32,1024]{1,0:T(8,128)S(1)}, u32[]{:S(2)}, u32[]{:S(2)}) collective-permute-start(f32[32,1024]{1,0:T(8,128)S(1)} %get-tuple-element.72.refs_2_), channel_id=1, source_target_pairs={{0,1},{1,0},{2,3},{3,2},{4,5},{5,4},{6,7},{7,6},{8,9},{9,8},{10,11... | collective-permute-start | bytes 393224 | tf_op jit(solution)/shard_map/ppermute | solution.py:456
  61.0 7.4 %collective-permute-start.13 = (f32[32,1024]{1,0:T(8,128)S(1)}, f32[32,1024]{1,0:T(8,128)S(1)}, u32[]{:S(2)}, u32[]{:S(2)}) collective-permute-start(f32[32,1024]{1,0:T(8,128)S(1)} %get-tuple-element.73), channel_id=1, source_target_pairs={{0,3},{1,2},{2,1},{3,0},{4,7},{5,6},{6,5},{7,4},{8,11},{9,10},{10,... | collective-permute-start | bytes 393224 | tf_op jit(solution)/shard_map/ppermute | solution.py:456
  61.0 7.4 %collective-permute-start.14 = (f32[32,1024]{1,0:T(8,128)S(1)}, f32[32,1024]{1,0:T(8,128)S(1)}, u32[]{:S(2)}, u32[]{:S(2)}) collective-permute-start(f32[32,1024]{1,0:T(8,128)S(1)} %get-tuple-element.73), channel_id=1, source_target_pairs={{0,2},{1,3},{2,0},{3,1},{4,6},{5,7},{6,4},{7,5},{8,10},{9,11},{10,... | collective-permute-start | bytes 393224 | tf_op jit(solution)/shard_map/ppermute | solution.py:456

commit v7 on v6

--- a/solution.py
+++ b/solution.py
@@ -234,7 +234,7 @@
 def prepare_kernel(dims, rdev, half, width, order_ref, table_ref, foot_ref, _, vol_ref, kept_ref, left_ref, sems, rows_ref):
     zdev = vol_ref.shape[0]
     copies = []
-    for h, zp, slices, start in volume_pieces(dims, zdev, half, 0, (0, 1)):
+    for h, zp, slices, start in volume_pieces(dims, zdev, half, 0, (0,)):
         source = vol_ref.at[slices, :, pl.ds(start, width)]
         copies.append(pltpu.make_async_copy(source, kept_ref.at[h, slices], sems.at[h, zp]))
         copies[-1].start()
@@ -254,17 +254,51 @@
         in_specs=[IN_SMEM, IN_VMEM, IN_VMEM, ANYWHERE, ANYWHERE],
         out_specs=[IN_VMEM, IN_VMEM],
         out_shape=[
-            jax.ShapeDtypeStruct((2, zdev, cells, width), F32),
+            jax.ShapeDtypeStruct((1, zdev, cells, width), F32),
             jax.ShapeDtypeStruct((zdev // zb, zb * cells, depth), BF16),
         ],
         scratch_shapes=[
-            pltpu.SemaphoreType.DMA((2, zdev // zb)),
+            pltpu.SemaphoreType.DMA((1, zdev // zb)),
             pltpu.VMEM((groups * SUBLANES, table.shape[1]), F32),
         ],
         compiler_params=pltpu.CompilerParams(vmem_limit_bytes=40 * MIB),
         cost_estimate=pl.CostEstimate(flops=0, bytes_accessed=8 * zdev * cells * width, transcendentals=0),
         name="prepare",
     )(order, table, own, after, volume)
+
+
+def residual_columns(half, which):
+    odd = lax.rem(lax.axis_index("slab"), 2)
+    return pl.ds(pl.multiple_of(lax.rem(odd + which, 2) * half, LANES), half)
+
+
+def load_kernel(dims, half, width, _, vol_ref, mine_ref, kept_ref, res_ref, sems, res_sem):
+    copies = []
+    for h, zp, slices, start in volume_pieces(dims, vol_ref.shape[0], half, 0, (1,)):
+        source = vol_ref.at[slices, :, pl.ds(start, width)]
+        copies.append(pltpu.make_async_copy(source, kept_ref.at[h, slices], sems.at[h, zp]))
+        copies[-1].start()
+    copies.append(pltpu.make_async_copy(mine_ref, res_ref.at[:, :, residual_columns(half, 0)], res_sem))
+    copies[-1].start()
+    for copy in copies:
+        copy.wait()
+
+
+def load_step(dims, width, after, volume, mine):
+    zdev, cells, total = volume.shape
+    return pl.pallas_call(
+        functools.partial(load_kernel, dims, total // 2, width),
+        in_specs=[ANYWHERE, ANYWHERE, IN_VMEM],
+        out_specs=[IN_VMEM, ANYWHERE],
+        out_shape=[
+            jax.ShapeDtypeStruct((1, zdev, cells, width), F32),
+            jax.ShapeDtypeStruct((*mine.shape[:2], total), F32),
+        ],
+        scratch_shapes=[pltpu.SemaphoreType.DMA((1, zdev // dims[2])), pltpu.SemaphoreType.DMA],
+        compiler_params=pltpu.CompilerParams(vmem_limit_bytes=40 * MIB),
+        cost_estimate=pl.CostEstimate(flops=0, bytes_accessed=4 * zdev * cells * width, transcendentals=0),
+        name="load",
+    )(after, volume, mine)
 
 
 def residual_kernel(dims, first, half, rdev, zdev, offset, width, *refs):
@@ -356,26 +390,22 @@
     )(*args)
 
 
-def update_kernel(dims, first, halves, half, offset, width, *refs):
+def update_kernel(dims, first, parts, halves, half, offset, width, *refs):
     per, groups, zb, cells = dims
     count = groups * SUBLANES
     left_ref, backs, refs = refs[0], refs[len(halves) * groups:0:-1], refs[1 + len(halves) * groups:]
-    vol_ref, *refs = refs
-    zdev, depth = vol_ref.shape[1], left_ref.shape[2]
+    vols, refs = refs[:parts], refs[parts:]
+    zdev, depth = vols[0].shape[1], left_ref.shape[2]
     if not first:
         refs = refs[1:]
-    pieces = refs[:-3]
-    if pieces:
-        *pieces, out_ref, res_ref, buf, sems, res_sems = refs
+    leaving = []
+    if len(refs) > 3:
+        theirs_ref, _, out_ref, res_ref, buf, sems, res_sem = refs
+        leaving.append(pltpu.make_async_copy(theirs_ref, res_ref.at[:, :, residual_columns(half, 1)], res_sem))
+        leaving[0].start()
     else:
         out_ref, buf, sems = refs
-    odd = lax.rem(lax.axis_index("slab"), 2)
-    leaving = []
-    for h, ref in enumerate(pieces):
-        columns = pl.ds(pl.multiple_of(lax.rem(odd + h, 2) * half, LANES), half)
-        leaving.append(pltpu.make_async_copy(ref, res_ref.at[:, :, columns], res_sems.at[h]))
-        leaving[-1].start()
-    held = len(halves) < vol_ref.shape[0]
+    whole = vols[0].shape[0] == 2
     for i, zp, slices, start in volume_pieces(dims, zdev, half, offset, halves):
         rows = slice(zp * SUBLANES, (zp + 1) * SUBLANES)
         left = left_ref[zp]
@@ -387,7 +417,7 @@
             change = dot(left, jnp.concatenate([high, low, high, pad], axis=0))
             for z in range(zb):
                 buf[i, zp * zb + z, :, piece] = (
-                    vol_ref[halves[i] if held else i, zp * zb + z, :, piece] + change[z * cells:(z + 1) * cells]
+                    vols[0 if whole else i][halves[i] if whole else 0, zp * zb + z, :, piece] + change[z * cells:(z + 1) * cells]
                 )
         leaving.append(
             pltpu.make_async_copy(buf.at[i, slices], out_ref.at[slices, :, pl.ds(start, width)], sems.at[i, zp])
@@ -401,7 +431,7 @@
     per, groups, zb, cells = dims
     zdev, _, total = volume.shape
     first = out is None
-    args = [left, *backs[::-1], kept]
+    args = [left, *backs[::-1], *kept]
     shapes = [jax.ShapeDtypeStruct(volume.shape, F32)]
     scratch = [
         pltpu.VMEM((len(halves), zdev, cells, width), F32),
@@ -414,13 +444,14 @@
         args += [out]
         specs += [ANYWHERE]
     if pieces:
+        aliases[len(args) + 1] = 1
         args += pieces
-        specs += [IN_VMEM] * 2
-        shapes += [jax.ShapeDtypeStruct((*pieces[0].shape[:2], total), F32)]
-        scratch += [pltpu.SemaphoreType.DMA((2,))]
+        specs += [IN_VMEM, ANYWHERE]
+        shapes += [jax.ShapeDtypeStruct(pieces[1].shape, F32)]
+        scratch += [pltpu.SemaphoreType.DMA]
     size = zdev * cells * width * len(halves)
     return pl.pallas_call(
-        functools.partial(update_kernel, dims, first, halves, total // 2, offset, width),
+        functools.partial(update_kernel, dims, first, len(kept), halves, total // 2, offset, width),
         in_specs=specs,
         out_specs=[ANYWHERE] * len(shapes),
         out_shape=shapes,
@@ -488,7 +519,7 @@
             if left is None:
                 left = made[-1]
             elif c:
-                kept[c] += [(h, made[-1]) for h in halves]
+                kept[c] = [made[-1]]
         parts = [spread(parts[h * groups + d], h, d) for h in range(2) for d in range(groups)]
         if c:
             parts, _ = lax.optimization_barrier((parts, sums[-1][0]))
@@ -496,9 +527,9 @@
         near = along(own, facing)
         if c == 0:
             first_columns, update_left = prepare_step(dims, rdev, widths[0], order, table, own, near, volume)
-            kept[0] = [(h, first_columns) for h in range(2)]
         if c == 1:
             near, first_columns = lax.optimization_barrier((near, first_columns))
+            kept[0] = [first_columns]
         far = along(near, beyond(c))
         sums.append((own, near, far))
     pieces, given, mats = [], [], None
@@ -508,22 +539,30 @@
         )
         pieces = [mine, sent]
         mats = rest if c == 0 else mats
-        near = near + along(far, back_from_beyond(c))
+        returned = along(far, back_from_beyond(c))
+        if c == 1:
+            other_columns, res = load_step(dims, widths[0], near_before, volume, mine)
+            returned, other_columns = lax.optimization_barrier((returned, other_columns))
+            kept[0].append(other_columns)
+        near = near + returned
         arrived = along(near, facing)
+        if c == 0:
+            near_before = near
         halves = [own[i] + arrived[i] for i in range(2)]
         given.append([spread(halves[h], h, d) for h in range(2) for d in range(groups)])
-    pieces = [mine, along(sent, lambda s: s ^ 1)]
-    out, res = None, []
+    pieces = [along(sent, lambda s: s ^ 1), res]
+    out = None
     for c in range(CHUNKS):
         for halves in UPDATE_HALVES[c]:
             backs = [b for h in halves for b in given[c][h * groups:(h + 1) * groups]]
             write = c == CHUNKS - 1 and halves[0] == 0
-            out, *made = update_step(
+            made = update_step(
                 dims, c, halves, offsets[c], widths[c], update_left, backs, pieces if write else [],
-                dict(kept[c])[halves[0]], volume, out,
+                kept[c], volume, out,
             )
-            res += made
-    return out, res[0]
+            out = made[0]
+            res = made[1] if write else res
+    return out, res
 
 
 def solution(mesh):

time: 71 us -> 74.4 us (1.048)
  local copies, waits for them, and re-layouts: 0.78 us -> 4.4 us
  waiting for transfers between devices: 19.8 us -> 17.9 us
  Pallas kernels: 24.5 us -> 26.4 us
    unnamed x10 -> x16, local copies, waits for them, and re-layouts: 0.78 us -> 4.4 us
    pallas_call x3 -> x4, Pallas kernels: 8.69 us -> 11.8 us  [the longest x3 9.17 us: update_step(): pl.pallas_call(functools.partial(update_kernel, dims, first, len(kept), h...]
    ppermute x10, waiting for transfers between devices: 15.3 us -> 14 us  [along(): return lax.ppermute(value, 'slab', pairs)]
    pallas_call x1, Pallas kernels: 4.09 us -> 2.8 us  [prepare_step(): pl.pallas_call(functools.partial(prepare_kernel, dims, rdev, total // 2,...]
  transfers between devices with their start and end apart: 22 -> 22, of which waited for: 9 -> 10; matrix products, arithmetic and copies ran while one was open for 0% -> 0% of each run, Pallas kernels for 25% -> 26%
where the time goes in v7:
time: 74.4 us; the launch traced here: 74.2 us
  Pallas kernels  26.4 us (35%)
  starting transfers between devices  24.3 us (33%)
  waiting for transfers between devices  17.9 us (24%)
  local copies, waits for them, and re-layouts  4.4 us (6%)
  between operations  0.83 us (1%)
    ppermute x10, starting transfers between devices, along(): return lax.ppermute(value, 'slab', pairs)  14.4 us
    ppermute x10, waiting for transfers between devices, along(): return lax.ppermute(value, 'slab', pairs)  14 us
    ppermute x12, starting transfers between devices, spread(): return lax.ppermute(value, ('slab', 'ang'), pairs)  9.86 us
    pallas_call x3, Pallas kernels, update_step(): pl.pallas_call(functools.partial(update_kernel, dims, first, len(kept), h...  9.17 us
    pallas_call x2, Pallas kernels, ray_sums(): pl.pallas_call(functools.partial(rays_kernel, dims, first, keep, extra, h...  8.46 us
    unnamed x16, local copies, waits for them, and re-layouts  4.4 us
    ppermute x12, waiting for transfers between devices, spread(): return lax.ppermute(value, ('slab', 'ang'), pairs)  3.93 us
    pallas_call x2, Pallas kernels, residual_step(): pl.pallas_call(functools.partial(residual_kernel, dims, first, total // 2...  3.3 us
  transfers between devices with their start and end apart: 22, of which 10 were waited for; matrix products, arithmetic and copies ran while one was open for 0% of the time, Pallas kernels for 26%

profile of v7, /device:TPU:0, one launch (start us, length us, event | category | flops | bytes accessed | tf_op | source)
XLA Modules:
  0.0 74.2 jit_solution(2713504933373334297)
XLA Ops:
  0.6 4.6 %ray_sums_0_0.1 = (f32[8,4224]{1,0:T(8,128)}, f32[8,4224]{1,0:T(8,128)}, f32[8,4224]{1,0:T(8,128)}, f32[8,4224]{1,0:T(8,128)}, bf16[32,512]{1,0:T(8,128)(2,1)}) custom-call(s32[64]{0:T(128)} %refs_0_.3, s32[1,4]{1,0:T(1,128)} %refs_1_.3, s32[1,4]{1,0:T(1,128)} %refs_2_.1, f32[64,256]{1,0:T(8,128)} %refs_1_.4, f32[8,128,4096]{2,1,0:T(8,128)} %vol_ref.3), custom_call_target="tpu_custom_call" | custom-call | flops 67108864 | bytes 8388608 | tf_op jit(solution)/shard_map/ray_sums_0_0/pallas_call | solution.py:176
  5.2 3.0 %collective-permute-start = (f32[8,4224]{1,0:T(8,128)}, f32[8,4224]{1,0:T(8,128)S(1)}, u32[]{:S(2)}, u32[]{:S(2)}) collective-permute-start(f32[8,4224]{1,0:T(8,128)} %get-tuple-element.42), channel_id=1, source_target_pairs={{0,1},{1,0},{2,3},{3,2},{4,5},{5,4},{6,7},{7,6},{8,9},{9,8},{10,11... | collective-permute-start | bytes 405512 | tf_op jit(solution)/shard_map/ppermute | solution.py:487
  8.2 0.0 collective-permute-start.1
  8.2 0.2 collective-permute-start.2
  8.4 0.0 copy-start.3
  8.4 0.8 %copy-done.3 = bf16[32,512]{1,0:T(8,128)(2,1)S(1)} copy-done((bf16[32,512]{1,0:T(8,128)(2,1)S(1)}, bf16[32,512]{1,0:T(8,128)(2,1)}, u32[]{:S(2)}) %copy-start.3) | copy-done | bytes 32792
  9.2 3.9 %ray_sums_1_0.1 = (f32[8,4096]{1,0:T(8,128)S(1)}, f32[8,4096]{1,0:T(8,128)S(1)}, f32[8,4096]{1,0:T(8,128)S(1)}, f32[8,4096]{1,0:T(8,128)S(1)}, f32[2,8,128,1024]{3,2,1,0:T(8,128)S(1)}) custom-call(bf16[32,512]{1,0:T(8,128)(2,1)S(1)} %copy-done.3, f32[8,128,4096]{2,1,0:T(8,128)} %vol_ref.3), custom_call_target="tpu_custom_call" | custom-call | flops 67108864 | bytes 8388608 | tf_op jit(solution)/shard_map/ray_sums_1_0/pallas_call | solution.py:176
  13.1 0.0 copy-start
  13.1 3.3 %copy-done = f32[2,8,128,1024]{3,2,1,0:T(8,128)} copy-done((f32[2,8,128,1024]{3,2,1,0:T(8,128)}, f32[2,8,128,1024]{3,2,1,0:T(8,128)S(1)}, u32[]{:S(2)}) %copy-start) | copy-done | bytes 8388632
  16.4 1.9 %collective-permute-start.6 = (f32[8,4096]{1,0:T(8,128)S(1)}, f32[8,4096]{1,0:T(8,128)S(1)}, u32[]{:S(2)}, u32[]{:S(2)}) collective-permute-start(f32[8,4096]{1,0:T(8,128)S(1)} %get-tuple-element.53), channel_id=1, source_target_pairs={{0,1},{1,0},{2,3},{3,2},{4,5},{5,4},{6,7},{7,6},{8,9},{9,8},{10,11... | collective-permute-start | bytes 393224 | tf_op jit(solution)/shard_map/ppermute | solution.py:487
  18.3 0.0 collective-permute-start.7
  18.3 0.0 copy-done.1
  18.4 0.1 dynamic-slice_convert_fusion
  18.4 0.0 collective-permute-done
  18.5 0.3 collective-permute-start.8
  18.7 0.0 copy-done.5
  18.8 0.0 collective-permute-done.1
  18.8 0.4 collective-permute-start.5
  19.2 0.0 collective-permute-done.2
  19.2 1.7 %collective-permute-start.3 = (f32[2,8,4224]{2,1,0:T(8,128)S(1)}, f32[2,8,4224]{2,1,0:T(8,128)S(1)}, u32[]{:S(2)}, u32[]{:S(2)}) collective-permute-start(f32[2,8,4224]{2,1,0:T(8,128)S(1)} %pad_maximum_fusion.foot_ref.refs_2_), channel_id=1, source_target_pairs={{0,4},{2,6},{4,0},{6,2},{8,12},{10,14},{12,8},{14,10},{16,20},{18,... | collective-permute-start | bytes 811016 | tf_op jit(solution)/shard_map/ppermute | solution.py:479
  20.9 1.8 %collective-permute-done.6 = f32[8,4096]{1,0:T(8,128)S(1)} collective-permute-done((f32[8,4096]{1,0:T(8,128)S(1)}, f32[8,4096]{1,0:T(8,128)S(1)}, u32[]{:S(2)}, u32[]{:S(2)}) %collective-permute-start.6) | collective-permute-done | bytes 131104 | tf_op jit(solution)/shard_map/ppermute | solution.py:487
  22.7 0.0 collective-permute-done.7
  22.7 1.7 %collective-permute-done.8 = f32[8,4096]{1,0:T(8,128)S(1)} collective-permute-done((f32[8,4096]{1,0:T(8,128)S(1)}, f32[8,4096]{1,0:T(8,128)S(1)}, u32[]{:S(2)}, u32[]{:S(2)}) %collective-permute-start.8) | collective-permute-done | bytes 131104 | tf_op jit(solution)/shard_map/ppermute | solution.py:487
  24.5 1.5 %collective-permute-start.9 = (f32[2,8,4096]{2,1,0:T(8,128)S(1)}, f32[2,8,4096]{2,1,0:T(8,128)S(1)}, u32[]{:S(2)}, u32[]{:S(2)}) collective-permute-start(f32[2,8,4096]{2,1,0:T(8,128)S(1)} %pad_maximum_fusion.1.refs_5_), channel_id=1, source_target_pairs={{0,4},{2,6},{4,0},{6,2},{8,12},{10,14},{12,8},{14,10},{16,20},{18,... | collective-permute-start | bytes 786440 | tf_op jit(solution)/shard_map/ppermute | solution.py:479
  26.0 2.2 %collective-permute-done.3._.refs_3_ = f32[2,8,4224]{2,1,0:T(8,128)S(1)} collective-permute-done((f32[2,8,4224]{2,1,0:T(8,128)S(1)}, f32[2,8,4224]{2,1,0:T(8,128)S(1)}, u32[]{:S(2)}, u32[]{:S(2)}) %collective-permute-start.3) | collective-permute-done | bytes 270368 | tf_op jit(solution)/shard_map/ppermute | solution.py:479
  28.2 2.0 %collective-permute-start.4 = (f32[2,8,4224]{2,1,0:T(8,128)S(1)}, f32[2,8,4224]{2,1,0:T(8,128)S(1)}, u32[]{:S(2)}, u32[]{:S(2)}) collective-permute-start(f32[2,8,4224]{2,1,0:T(8,128)S(1)} %collective-permute-done.3._.refs_3_), channel_id=1, source_target_pairs={{0,8},{2,10},{4,28},{6,30},{8,16},{10,18},{12,4},{14,6},{16,24},{1... | collective-permute-start | bytes 811016 | tf_op jit(solution)/shard_map/ppermute | solution.py:479
  30.1 0.0 copy-done.2
  30.2 0.0 copy-done.4
  30.2 2.8 %prepare.1 = (f32[1,8,128,1024]{3,2,1,0:T(8,128)S(1)}, bf16[4,256,128]{2,1,0:T(8,128)(2,1)S(1)}) custom-call(s32[64]{0:T(128)S(1)} %copy-done.4, f32[64,256]{1,0:T(8,128)S(1)} %copy-done.2, f32[2,8,4224]{2,1,0:T(8,128)S(1)} %pad_maximum_fusion.foot_ref.refs_2_, f32[2,8,4224]{2,1,0:T(8,128)S(1)} %collective-permute-done.3._.refs_3_, f32[8,128,4096]{2,1,0:T(8,128)} %vol_ref.3), custom_call_target="tpu_custom_call" | custom-call | bytes 8388608 | tf_op jit(solution)/shard_map/prepare/pallas_call | solution.py:252
  33.0 0.7 collective-permute-done.9.refs_6_
  33.6 1.8 %collective-permute-start.10 = (f32[2,8,4096]{2,1,0:T(8,128)S(1)}, f32[2,8,4096]{2,1,0:T(8,128)S(1)}, u32[]{:S(2)}, u32[]{:S(2)}) collective-permute-start(f32[2,8,4096]{2,1,0:T(8,128)S(1)} %collective-permute-done.9.refs_6_), channel_id=1, source_target_pairs={{0,8},{2,10},{4,0},{6,2},{8,16},{10,18},{12,4},{14,6},{16,24},{18,... | collective-permute-start | bytes 786440 | tf_op jit(solution)/shard_map/ppermute | solution.py:479
  35.5 2.8 %collective-permute-done.4.refs_4_ = f32[2,8,4224]{2,1,0:T(8,128)S(1)} collective-permute-done((f32[2,8,4224]{2,1,0:T(8,128)S(1)}, f32[2,8,4224]{2,1,0:T(8,128)S(1)}, u32[]{:S(2)}, u32[]{:S(2)}) %collective-permute-start.4) | collective-permute-done | bytes 270368 | tf_op jit(solution)/shard_map/ppermute | solution.py:479
  38.2 0.0 collective-permute-done.5.refs_6_.refs_9_
  38.2 2.0 %residual_0.1 = (f32[4,32,1024]{2,1,0:T(8,128)S(1)}, f32[4,32,1024]{2,1,0:T(8,128)S(1)}, f32[2,32,1024]{2,1,0:T(8,128)S(1)}, f32[2,32,1024]{2,1,0:T(8,128)S(1)},...) custom-call(s32[64]{0:T(128)S(1)} %copy-done.4, ...), custom_call_target="tpu_custom_call" | custom-call | flops 603979776 | bytes 3670016 | tf_op jit(solution)/shard_map/residual_0/pallas_call | solution.py:380
  40.3 0.8 %collective-permute-start.12 = (f32[2,32,1024]{2,1,0:T(8,128)S(1)}, f32[2,32,1024]{2,1,0:T(8,128)S(1)}, u32[]{:S(2)}, u32[]{:S(2)}) collective-permute-start(f32[2,32,1024]{2,1,0:T(8,128)S(1)} %get-tuple-element.68), channel_id=1, source_target_pairs={{0,4},{2,6},{4,12},{6,14},{8,0},{10,2},{12,20},{14,22},{16,8},{18,... | collective-permute-start | bytes 786440 | tf_op jit(solution)/shard_map/ppermute | solution.py:479
  41.1 1.0 %collective-permute-done.10.refs_7_ = f32[2,8,4096]{2,1,0:T(8,128)S(1)} collective-permute-done((f32[2,8,4096]{2,1,0:T(8,128)S(1)}, f32[2,8,4096]{2,1,0:T(8,128)S(1)}, u32[]{:S(2)}, u32[]{:S(2)}) %collective-permute-start.10) | collective-permute-done | bytes 262176 | tf_op jit(solution)/shard_map/ppermute | solution.py:479
  42.1 1.3 %residual_1.1 = (f32[4,32,2048]{2,1,0:T(8,128)S(1)}, f32[4,32,2048]{2,1,0:T(8,128)S(1)}, f32[2,32,1024]{2,1,0:T(8,128)S(1)}, f32[2,32,1024]{2,1,0:T(8,128)S(1)}, f32[2,32,1024]{2,1,0:T(8,128)S(1)}) custom-call(bf16[256,192]{1,0:T(8,128)(2,1)S(1)} %get-tuple-element.46.refs_0_, bf16[256,192]{1,0:T(8,128)(2,1)S(1)} %get-tuple-element.47.refs_1_, ...), custom_call_target="tpu_custom_call" | custom-call | flops 603979776 | bytes 3670016 | tf_op jit(solution)/shard_map/residual_1/pallas_call | solution.py:380
  43.4 0.1 collective-permute-start.21
  43.5 3.5 %collective-permute-start.11 = (f32[2,32,1024]{2,1,0:T(8,128)S(1)}, f32[2,32,1024]{2,1,0:T(8,128)S(1)}, u32[]{:S(2)}, u32[]{:S(2)}) collective-permute-start(f32[2,32,1024]{2,1,0:T(8,128)S(1)} %get-tuple-element.66), channel_id=1, source_target_pairs={{0,24},{2,26},{4,12},{6,14},{8,0},{10,2},{12,20},{14,22},{16,8},{1... | collective-permute-start | bytes 786440 | tf_op jit(solution)/shard_map/ppermute | solution.py:479
  47.0 1.0 %collective-permute-done.12 = f32[2,32,1024]{2,1,0:T(8,128)S(1)} collective-permute-done((f32[2,32,1024]{2,1,0:T(8,128)S(1)}, f32[2,32,1024]{2,1,0:T(8,128)S(1)}, u32[]{:S(2)}, u32[]{:S(2)}) %collective-permute-start.12) | collective-permute-done | bytes 262176 | tf_op jit(solution)/shard_map/ppermute | solution.py:479
  48.0 0.1 collective-permute-start.17
  48.1 2.6 %load.1 = (f32[1,8,128,1024]{3,2,1,0:T(8,128)S(1)}, f32[4,32,4096]{2,1,0:T(8,128)}) custom-call(f32[2,32,1024]{2,1,0:T(8,128)S(1)} %add.48._, f32[8,128,4096]{2,1,0:T(8,128)} %vol_ref.3, f32[4,32,2048]{2,1,0:T(8,128)S(1)} %get-tuple-element.69.mine_ref), custom_call_target="tpu_custom_call" | custom-call | bytes 4194304 | tf_op jit(solution)/shard_map/load/pallas_call | solution.py:289
  50.7 2.4 %collective-permute-done.11 = f32[2,32,1024]{2,1,0:T(8,128)S(1)} collective-permute-done((f32[2,32,1024]{2,1,0:T(8,128)S(1)}, f32[2,32,1024]{2,1,0:T(8,128)S(1)}, u32[]{:S(2)}, u32[]{:S(2)}) %collective-permute-start.11) | collective-permute-done | bytes 262176 | tf_op jit(solution)/shard_map/ppermute | solution.py:479
  53.2 2.6 %collective-permute-start.13 = (f32[2,32,1024]{2,1,0:T(8,128)S(1)}, f32[2,32,1024]{2,1,0:T(8,128)S(1)}, u32[]{:S(2)}, u32[]{:S(2)}) collective-permute-start(f32[2,32,1024]{2,1,0:T(8,128)S(1)} %add.49), channel_id=1, source_target_pairs={{0,4},{2,6},{4,0},{6,2},{8,12},{10,14},{12,8},{14,10},{16,20},{18,... | collective-permute-start | bytes 786440 | tf_op jit(solution)/shard_map/ppermute | solution.py:479
  55.8 0.0 collective-permute-done.17
  55.8 0.6 collective-permute-start.18
  56.4 1.1 %collective-permute-start.19 = (f32[32,1024]{1,0:T(8,128)S(1)}, f32[32,1024]{1,0:T(8,128)S(1)}, u32[]{:S(2)}, u32[]{:S(2)}) collective-permute-start(f32[32,1024]{1,0:T(8,128)S(1)} %get-tuple-element.81), channel_id=1, source_target_pairs={{0,2},{1,3},{2,0},{3,1},{4,6},{5,7},{6,4},{7,5},{8,10},{9,11},{10,... | collective-permute-start | bytes 393224 | tf_op jit(solution)/shard_map/ppermute | solution.py:487
  57.5 0.5 collective-permute-start.20
  58.0 3.9 %collective-permute-done.13 = f32[2,32,1024]{2,1,0:T(8,128)S(1)} collective-permute-done((f32[2,32,1024]{2,1,0:T(8,128)S(1)}, f32[2,32,1024]{2,1,0:T(8,128)S(1)}, u32[]{:S(2)}, u32[]{:S(2)}) %collective-permute-start.13) | collective-permute-done | bytes 262176 | tf_op jit(solution)/shard_map/ppermute | solution.py:479
  62.0 1.6 %collective-permute-start.16 = (f32[32,1024]{1,0:T(8,128)S(1)}, f32[32,1024]{1,0:T(8,128)S(1)}, u32[]{:S(2)}, u32[]{:S(2)}) collective-permute-start(f32[32,1024]{1,0:T(8,128)S(1)} %get-tuple-element.82.refs_2_), channel_id=1, source_target_pairs={{0,1},{1,0},{2,3},{3,2},{4,5},{5,4},{6,7},{7,6},{8,9},{9,8},{10,11... | collective-permute-start | bytes 393224 | tf_op jit(solution)/shard_map/ppermute | solution.py:487
  63.6 0.0 collective-permute-done.18.refs_1_
  63.6 0.0 collective-permute-start.14
  63.6 0.0 collective-permute-done.19.refs_2_
  63.6 0.6 collective-permute-start.15
  64.2 0.4 collective-permute-done.20.refs_3_
  64.6 4.2 %update_0_0.1.refs_4_ = f32[8,128,4096]{2,1,0:T(8,128)} custom-call(bf16[4,256,128]{2,1,0:T(8,128)(2,1)S(1)} %get-tuple-element.45.refs_0_, f32[32,1024]{1,0:T(8,128)S(1)} %collective-permute-done.18.refs_1_, f32[32,1024]{1,0:T(8,128)S(1)} %collective-permute-done.19.refs_2_, f32[32,1024]{1,0:T(8,128)S(1)} %collective-permute-done.20.refs_3_, ...), custom_call_target="tpu_custom_call" | custom-call | flops 201326592 | bytes 8388608 | tf_op jit(solution)/shard_map/update_0_0/pallas_call | solution.py:453
  68.8 0.0 collective-permute-done.16.refs_1_
  68.8 0.0 collective-permute-done.21.refs_5_
  68.8 0.0 slice-done
  68.8 0.3 slice-done.1
  69.2 2.7 %update_1_0.1 = (f32[8,128,4096]{2,1,0:T(8,128)}, f32[4,32,4096]{2,1,0:T(8,128)}) custom-call(bf16[4,256,128]{2,1,0:T(8,128)(2,1)S(1)} %get-tuple-element.45.refs_0_, f32[32,1024]{1,0:T(8,128)S(1)} %collective-permute-done.16.refs_1_, f32[32,1024]{1,0:T(8,128)S(1)} %get-tuple-element.82.refs_2_, ...), custom_call_target="tpu_custom_call", output_to_operand_aliasing={{0}: (4, {}), {1}: (6, {})} | custom-call | flops 100663296 | bytes 4194304 | tf_op jit(solution)/shard_map/update_1_0/pallas_call | solution.py:453
  71.8 0.0 collective-permute-done.14.refs_1_
  71.8 0.0 collective-permute-done.15.refs_2_
  71.9 2.3 %update_1_1.1 = f32[8,128,4096]{2,1,0:T(8,128)} custom-call(bf16[4,256,128]{2,1,0:T(8,128)(2,1)S(1)} %get-tuple-element.45.refs_0_, f32[32,1024]{1,0:T(8,128)S(1)} %collective-permute-done.14.refs_1_, f32[32,1024]{1,0:T(8,128)S(1)} %collective-permute-done.15.refs_2_, f32[2,8,128,1024]{3,2,1,0:T(8,128)S(1)} %bitcast.17, ...), custom_call_target="tpu_custom_call", output_to_operand_aliasing={{}: (4, {})} | custom-call | flops 100663296 | bytes 4194304 | tf_op jit(solution)/shard_map/update_1_1/pallas_call | solution.py:453
  (16 shorter events, 0.3 us)
Async XLA Ops:
  5.2 13.3 %collective-permute-start = (f32[8,4224]{1,0:T(8,128)}, f32[8,4224]{1,0:T(8,128)S(1)}, u32[]{:S(2)}, u32[]{:S(2)}) collective-permute-start(f32[8,4224]{1,0:T(8,128)} %get-tuple-element.42), channel_id=1, source_target_pairs={{0,1},{1,0},{2,3},{3,2},{4,5},{5,4},{6,7},{7,6},{8,9},{9,8},{10,11... | collective-permute-start | bytes 405512 | tf_op jit(solution)/shard_map/ppermute | solution.py:487
  8.2 10.5 %collective-permute-start.1 = (f32[8,4224]{1,0:T(8,128)}, f32[8,4224]{1,0:T(8,128)S(1)}, u32[]{:S(2)}, u32[]{:S(2)}) collective-permute-start(f32[8,4224]{1,0:T(8,128)} %get-tuple-element.43), channel_id=1, source_target_pairs={{0,2},{1,3},{2,0},{3,1},{4,6},{5,7},{6,4},{7,5},{8,10},{9,11},{10,... | collective-permute-start | bytes 405512 | tf_op jit(solution)/shard_map/ppermute | solution.py:487
  8.2 10.9 %collective-permute-start.2 = (f32[8,4224]{1,0:T(8,128)}, f32[8,4224]{1,0:T(8,128)S(1)}, u32[]{:S(2)}, u32[]{:S(2)}) collective-permute-start(f32[8,4224]{1,0:T(8,128)} %get-tuple-element.44), channel_id=1, source_target_pairs={{0,3},{1,2},{2,1},{3,0},{4,7},{5,6},{6,5},{7,4},{8,11},{9,10},{10,... | collective-permute-start | bytes 405512 | tf_op jit(solution)/shard_map/ppermute | solution.py:487
  8.4 0.8 %copy-start.3 = (bf16[32,512]{1,0:T(8,128)(2,1)S(1)}, bf16[32,512]{1,0:T(8,128)(2,1)}, u32[]{:S(2)}) copy-start(bf16[32,512]{1,0:T(8,128)(2,1)} %get-tuple-element.51.refs_0_) | copy-start | bytes 98308
  9.2 9.2 %copy-start.1 = (bf16[4,32,4096]{2,1,0:T(8,128)(2,1)S(1)}, bf16[4,32,4096]{2,1,0:T(8,128)(2,1)}, u32[]{:S(2)}) copy-start(bf16[4,32,4096]{2,1,0:T(8,128)(2,1)} %refs_8_.1) | copy-start | bytes 3145732
  9.2 9.5 %copy-start.5 = (f32[8,4224]{1,0:T(8,128)S(1)}, f32[8,4224]{1,0:T(8,128)}, u32[]{:S(2)}) copy-start(f32[8,4224]{1,0:T(8,128)} %get-tuple-element.41) | copy-start | bytes 405508
  9.2 21.0 %copy-start.2 = (f32[64,256]{1,0:T(8,128)S(1)}, f32[64,256]{1,0:T(8,128)}, u32[]{:S(2)}) copy-start(f32[64,256]{1,0:T(8,128)} %refs_1_.4) | copy-start | bytes 196612
  9.2 21.0 %copy-start.4 = (s32[64]{0:T(128)S(1)}, s32[64]{0:T(128)}, u32[]{:S(2)}) copy-start(s32[64]{0:T(128)} %refs_0_.3) | copy-start | bytes 772
  13.1 3.3 %copy-start = (f32[2,8,128,1024]{3,2,1,0:T(8,128)}, f32[2,8,128,1024]{3,2,1,0:T(8,128)S(1)}, u32[]{:S(2)}) copy-start(f32[2,8,128,1024]{3,2,1,0:T(8,128)S(1)} %get-tuple-element.72.refs_3_) | copy-start | bytes 25165828
  16.4 6.2 %collective-permute-start.6 = (f32[8,4096]{1,0:T(8,128)S(1)}, f32[8,4096]{1,0:T(8,128)S(1)}, u32[]{:S(2)}, u32[]{:S(2)}) collective-permute-start(f32[8,4096]{1,0:T(8,128)S(1)} %get-tuple-element.53), channel_id=1, source_target_pairs={{0,1},{1,0},{2,3},{3,2},{4,5},{5,4},{6,7},{7,6},{8,9},{9,8},{10,11... | collective-permute-start | bytes 393224 | tf_op jit(solution)/shard_map/ppermute | solution.py:487
  18.3 4.3 %collective-permute-start.7 = (f32[8,4096]{1,0:T(8,128)S(1)}, f32[8,4096]{1,0:T(8,128)S(1)}, u32[]{:S(2)}, u32[]{:S(2)}) collective-permute-start(f32[8,4096]{1,0:T(8,128)S(1)} %get-tuple-element.54), channel_id=1, source_target_pairs={{0,2},{1,3},{2,0},{3,1},{4,6},{5,7},{6,4},{7,5},{8,10},{9,11},{10,... | collective-permute-start | bytes 393224 | tf_op jit(solution)/shard_map/ppermute | solution.py:487
  18.5 5.9 %collective-permute-start.8 = (f32[8,4096]{1,0:T(8,128)S(1)}, f32[8,4096]{1,0:T(8,128)S(1)}, u32[]{:S(2)}, u32[]{:S(2)}) collective-permute-start(f32[8,4096]{1,0:T(8,128)S(1)} %get-tuple-element.55), channel_id=1, source_target_pairs={{0,3},{1,2},{2,1},{3,0},{4,7},{5,6},{6,5},{7,4},{8,11},{9,10},{10,... | collective-permute-start | bytes 393224 | tf_op jit(solution)/shard_map/ppermute | solution.py:487
  18.8 19.5 %collective-permute-start.5 = (f32[4,32,2048]{2,1,0:T(8,128)S(1)}, f32[4,32,2048]{2,1,0:T(8,128)S(1)}, u32[]{:S(2)}, u32[]{:S(2)}) collective-permute-start(f32[4,32,2048]{2,1,0:T(8,128)S(1)} %dynamic-slice_convert_fusion), channel_id=1, source_target_pairs={{0,2},{2,0},{4,6},{6,4},{8,10},{10,8},{12,14},{14,12},{16,18},{18,... | collective-permute-start | bytes 3145736 | tf_op jit(solution)/shard_map/ppermute | solution.py:479
  19.2 9.0 %collective-permute-start.3 = (f32[2,8,4224]{2,1,0:T(8,128)S(1)}, f32[2,8,4224]{2,1,0:T(8,128)S(1)}, u32[]{:S(2)}, u32[]{:S(2)}) collective-permute-start(f32[2,8,4224]{2,1,0:T(8,128)S(1)} %pad_maximum_fusion.foot_ref.refs_2_), channel_id=1, source_target_pairs={{0,4},{2,6},{4,0},{6,2},{8,12},{10,14},{12,8},{14,10},{16,20},{18,... | collective-permute-start | bytes 811016 | tf_op jit(solution)/shard_map/ppermute | solution.py:479
  24.5 9.2 %collective-permute-start.9 = (f32[2,8,4096]{2,1,0:T(8,128)S(1)}, f32[2,8,4096]{2,1,0:T(8,128)S(1)}, u32[]{:S(2)}, u32[]{:S(2)}) collective-permute-start(f32[2,8,4096]{2,1,0:T(8,128)S(1)} %pad_maximum_fusion.1.refs_5_), channel_id=1, source_target_pairs={{0,4},{2,6},{4,0},{6,2},{8,12},{10,14},{12,8},{14,10},{16,20},{18,... | collective-permute-start | bytes 786440 | tf_op jit(solution)/shard_map/ppermute | solution.py:479
  28.2 10.0 %collective-permute-start.4 = (f32[2,8,4224]{2,1,0:T(8,128)S(1)}, f32[2,8,4224]{2,1,0:T(8,128)S(1)}, u32[]{:S(2)}, u32[]{:S(2)}) collective-permute-start(f32[2,8,4224]{2,1,0:T(8,128)S(1)} %collective-permute-done.3._.refs_3_), channel_id=1, source_target_pairs={{0,8},{2,10},{4,28},{6,30},{8,16},{10,18},{12,4},{14,6},{16,24},{1... | collective-permute-start | bytes 811016 | tf_op jit(solution)/shard_map/ppermute | solution.py:479
  33.6 8.5 %collective-permute-start.10 = (f32[2,8,4096]{2,1,0:T(8,128)S(1)}, f32[2,8,4096]{2,1,0:T(8,128)S(1)}, u32[]{:S(2)}, u32[]{:S(2)}) collective-permute-start(f32[2,8,4096]{2,1,0:T(8,128)S(1)} %collective-permute-done.9.refs_6_), channel_id=1, source_target_pairs={{0,8},{2,10},{4,0},{6,2},{8,16},{10,18},{12,4},{14,6},{16,24},{18,... | collective-permute-start | bytes 786440 | tf_op jit(solution)/shard_map/ppermute | solution.py:479
  40.3 7.7 %collective-permute-start.12 = (f32[2,32,1024]{2,1,0:T(8,128)S(1)}, f32[2,32,1024]{2,1,0:T(8,128)S(1)}, u32[]{:S(2)}, u32[]{:S(2)}) collective-permute-start(f32[2,32,1024]{2,1,0:T(8,128)S(1)} %get-tuple-element.68), channel_id=1, source_target_pairs={{0,4},{2,6},{4,12},{6,14},{8,0},{10,2},{12,20},{14,22},{16,8},{18,... | collective-permute-start | bytes 786440 | tf_op jit(solution)/shard_map/ppermute | solution.py:479
  43.4 25.4 %collective-permute-start.21 = (f32[4,32,2048]{2,1,0:T(8,128)S(1)}, f32[4,32,2048]{2,1,0:T(8,128)S(1)}, u32[]{:S(2)}, u32[]{:S(2)}) collective-permute-start(f32[4,32,2048]{2,1,0:T(8,128)S(1)} %get-tuple-element.76), channel_id=1, source_target_pairs={{0,2},{2,0},{4,6},{6,4},{8,10},{10,8},{12,14},{14,12},{16,18},{18,... | collective-permute-start | bytes 3145736 | tf_op jit(solution)/shard_map/ppermute | solution.py:479
  43.5 9.7 %collective-permute-start.11 = (f32[2,32,1024]{2,1,0:T(8,128)S(1)}, f32[2,32,1024]{2,1,0:T(8,128)S(1)}, u32[]{:S(2)}, u32[]{:S(2)}) collective-permute-start(f32[2,32,1024]{2,1,0:T(8,128)S(1)} %get-tuple-element.66), channel_id=1, source_target_pairs={{0,24},{2,26},{4,12},{6,14},{8,0},{10,2},{12,20},{14,22},{16,8},{1... | collective-permute-start | bytes 786440 | tf_op jit(solution)/shard_map/ppermute | solution.py:479
  48.0 7.8 %collective-permute-start.17 = (f32[2,32,1024]{2,1,0:T(8,128)S(1)}, f32[2,32,1024]{2,1,0:T(8,128)S(1)}, u32[]{:S(2)}, u32[]{:S(2)}) collective-permute-start(f32[2,32,1024]{2,1,0:T(8,128)S(1)} %add.48._), channel_id=1, source_target_pairs={{0,4},{2,6},{4,0},{6,2},{8,12},{10,14},{12,8},{14,10},{16,20},{18,... | collective-permute-start | bytes 786440 | tf_op jit(solution)/shard_map/ppermute | solution.py:479
  53.2 8.8 %collective-permute-start.13 = (f32[2,32,1024]{2,1,0:T(8,128)S(1)}, f32[2,32,1024]{2,1,0:T(8,128)S(1)}, u32[]{:S(2)}, u32[]{:S(2)}) collective-permute-start(f32[2,32,1024]{2,1,0:T(8,128)S(1)} %add.49), channel_id=1, source_target_pairs={{0,4},{2,6},{4,0},{6,2},{8,12},{10,14},{12,8},{14,10},{16,20},{18,... | collective-permute-start | bytes 786440 | tf_op jit(solution)/shard_map/ppermute | solution.py:479
  55.8 7.7 %collective-permute-start.18 = (f32[32,1024]{1,0:T(8,128)S(1)}, f32[32,1024]{1,0:T(8,128)S(1)}, u32[]{:S(2)}, u32[]{:S(2)}) collective-permute-start(f32[32,1024]{1,0:T(8,128)S(1)} %get-tuple-element.81), channel_id=1, source_target_pairs={{0,3},{1,2},{2,1},{3,0},{4,7},{5,6},{6,5},{7,4},{8,11},{9,10},{10,... | collective-permute-start | bytes 393224 | tf_op jit(solution)/shard_map/ppermute | solution.py:487
  56.4 7.2 %collective-permute-start.19 = (f32[32,1024]{1,0:T(8,128)S(1)}, f32[32,1024]{1,0:T(8,128)S(1)}, u32[]{:S(2)}, u32[]{:S(2)}) collective-permute-start(f32[32,1024]{1,0:T(8,128)S(1)} %get-tuple-element.81), channel_id=1, source_target_pairs={{0,2},{1,3},{2,0},{3,1},{4,6},{5,7},{6,4},{7,5},{8,10},{9,11},{10,... | collective-permute-start | bytes 393224 | tf_op jit(solution)/shard_map/ppermute | solution.py:487
  57.5 7.0 %collective-permute-start.20 = (f32[32,1024]{1,0:T(8,128)S(1)}, f32[32,1024]{1,0:T(8,128)S(1)}, u32[]{:S(2)}, u32[]{:S(2)}) collective-permute-start(f32[32,1024]{1,0:T(8,128)S(1)} %get-tuple-element.80.refs_4_), channel_id=1, source_target_pairs={{0,1},{1,0},{2,3},{3,2},{4,5},{5,4},{6,7},{7,6},{8,9},{9,8},{10,11... | collective-permute-start | bytes 393224 | tf_op jit(solution)/shard_map/ppermute | solution.py:487
  61.9 6.9 %slice-start = ((s8[8388608]{0:T(1024)(128)(4,1)}), s8[4194304]{0:T(1024)(128)(4,1)S(1)}, s32[]{:S(2)}) async-start(s8[8388608]{0:T(1024)(128)(4,1)} %bitcast.16), calls=%async_computation | async-start | bytes 8388608
  62.0 6.8 %collective-permute-start.16 = (f32[32,1024]{1,0:T(8,128)S(1)}, f32[32,1024]{1,0:T(8,128)S(1)}, u32[]{:S(2)}, u32[]{:S(2)}) collective-permute-start(f32[32,1024]{1,0:T(8,128)S(1)} %get-tuple-element.82.refs_2_), channel_id=1, source_target_pairs={{0,1},{1,0},{2,3},{3,2},{4,5},{5,4},{6,7},{7,6},{8,9},{9,8},{10,11... | collective-permute-start | bytes 393224 | tf_op jit(solution)/shard_map/ppermute | solution.py:487
  63.6 8.3 %collective-permute-start.14 = (f32[32,1024]{1,0:T(8,128)S(1)}, f32[32,1024]{1,0:T(8,128)S(1)}, u32[]{:S(2)}, u32[]{:S(2)}) collective-permute-start(f32[32,1024]{1,0:T(8,128)S(1)} %get-tuple-element.83), channel_id=1, source_target_pairs={{0,3},{1,2},{2,1},{3,0},{4,7},{5,6},{6,5},{7,4},{8,11},{9,10},{10,... | collective-permute-start | bytes 393224 | tf_op jit(solution)/shard_map/ppermute | solution.py:487
  63.6 8.3 %collective-permute-start.15 = (f32[32,1024]{1,0:T(8,128)S(1)}, f32[32,1024]{1,0:T(8,128)S(1)}, u32[]{:S(2)}, u32[]{:S(2)}) collective-permute-start(f32[32,1024]{1,0:T(8,128)S(1)} %get-tuple-element.83), channel_id=1, source_target_pairs={{0,2},{1,3},{2,0},{3,1},{4,6},{5,7},{6,4},{7,5},{8,10},{9,11},{10,... | collective-permute-start | bytes 393224 | tf_op jit(solution)/shard_map/ppermute | solution.py:487
  64.6 4.6 %slice-start.1 = ((s8[8388608]{0:T(1024)(128)(4,1)}), s8[4194304]{0:T(1024)(128)(4,1)S(1)}, s32[]{:S(2)}) async-start(s8[8388608]{0:T(1024)(128)(4,1)} %bitcast.16), calls=%async_computation.1 | async-start | bytes 8388608

commit v8 on v7

--- a/solution.py
+++ b/solution.py
@@ -261,7 +261,7 @@
             pltpu.SemaphoreType.DMA((1, zdev // zb)),
             pltpu.VMEM((groups * SUBLANES, table.shape[1]), F32),
         ],
-        compiler_params=pltpu.CompilerParams(vmem_limit_bytes=40 * MIB),
+        compiler_params=pltpu.CompilerParams(vmem_limit_bytes=36 * MIB),
         cost_estimate=pl.CostEstimate(flops=0, bytes_accessed=8 * zdev * cells * width, transcendentals=0),
         name="prepare",
     )(order, table, own, after, volume)
@@ -295,7 +295,7 @@
             jax.ShapeDtypeStruct((*mine.shape[:2], total), F32),
         ],
         scratch_shapes=[pltpu.SemaphoreType.DMA((1, zdev // dims[2])), pltpu.SemaphoreType.DMA],
-        compiler_params=pltpu.CompilerParams(vmem_limit_bytes=40 * MIB),
+        compiler_params=pltpu.CompilerParams(vmem_limit_bytes=33 * MIB),
         cost_estimate=pl.CostEstimate(flops=0, bytes_accessed=4 * zdev * cells * width, transcendentals=0),
         name="load",
     )(after, volume, mine)
@@ -475,7 +475,7 @@
     offsets = [sum(widths[:c]) for c in range(CHUNKS)]
 
     def along(value, to):
-        pairs = [(s, to(s)) for s in range(slabs)]
+        pairs = [(s, to(s)) for s in range(slabs) if to(s) is not None]
         return lax.ppermute(value, "slab", pairs)
 
     def spread(value, other, d):
@@ -494,7 +494,7 @@
             there = s + 4 if up(s) else s - 4
             if 0 <= there < slabs:
                 return there
-            return there % slabs if busy else facing(s)
+            return None if busy else facing(s)
         return to
 
     def beyond(c):

time: 74.4 us -> 75.8 us (1.019)
  starting transfers between devices: 24.3 us -> 26.1 us
    ppermute x10, starting transfers between devices: 14.4 us -> 16.3 us  [along(): return lax.ppermute(value, 'slab', pairs)]
  transfers between devices with their start and end apart: 22 -> 22, of which waited for: 10 -> 8; matrix products, arithmetic and copies ran while one was open for 0% -> 0% of each run, Pallas kernels for 26% -> 26%
where the time goes in v8:
time: 75.8 us; the launch traced here: 75.5 us
  Pallas kernels  26.3 us (35%)
  starting transfers between devices  26.1 us (34%)
  waiting for transfers between devices  17.5 us (23%)
  local copies, waits for them, and re-layouts  4.38 us (6%)
  between operations  0.87 us (1%)
    ppermute x10, starting transfers between devices, along(): return lax.ppermute(value, 'slab', pairs)  16.3 us
    ppermute x10, waiting for transfers between devices, along(): return lax.ppermute(value, 'slab', pairs)  14 us
    ppermute x12, starting transfers between devices, spread(): return lax.ppermute(value, ('slab', 'ang'), pairs)  9.86 us
    pallas_call x3, Pallas kernels, update_step(): pl.pallas_call(functools.partial(update_kernel, dims, first, len(kept), h...  9.16 us
    pallas_call x2, Pallas kernels, ray_sums(): pl.pallas_call(functools.partial(rays_kernel, dims, first, keep, extra, h...  8.46 us
    unnamed x16, local copies, waits for them, and re-layouts  4.38 us
    ppermute x12, waiting for transfers between devices, spread(): return lax.ppermute(value, ('slab', 'ang'), pairs)  3.53 us
    pallas_call x2, Pallas kernels, residual_step(): pl.pallas_call(functools.partial(residual_kernel, dims, first, total // 2...  3.27 us
  transfers between devices with their start and end apart: 22, of which 8 were waited for; matrix products, arithmetic and copies ran while one was open for 0% of the time, Pallas kernels for 26%

profile of v8, /device:TPU:0, one launch (start us, length us, event | category | flops | bytes accessed | tf_op | source)
XLA Modules:
  0.0 75.5 jit_solution(526552747386793321)
XLA Ops:
  0.6 4.6 %ray_sums_0_0.1 = (f32[8,4224]{1,0:T(8,128)}, f32[8,4224]{1,0:T(8,128)}, f32[8,4224]{1,0:T(8,128)}, f32[8,4224]{1,0:T(8,128)}, bf16[32,512]{1,0:T(8,128)(2,1)}) custom-call(s32[64]{0:T(128)} %refs_0_.3, s32[1,4]{1,0:T(1,128)} %refs_1_.3, s32[1,4]{1,0:T(1,128)} %refs_2_.1, f32[64,256]{1,0:T(8,128)} %refs_1_.4, f32[8,128,4096]{2,1,0:T(8,128)} %vol_ref.3), custom_call_target="tpu_custom_call" | custom-call | flops 67108864 | bytes 8388608 | tf_op jit(solution)/shard_map/ray_sums_0_0/pallas_call | solution.py:176
  5.2 3.0 %collective-permute-start = (f32[8,4224]{1,0:T(8,128)}, f32[8,4224]{1,0:T(8,128)S(1)}, u32[]{:S(2)}, u32[]{:S(2)}) collective-permute-start(f32[8,4224]{1,0:T(8,128)} %get-tuple-element.42), channel_id=1, source_target_pairs={{0,1},{1,0},{2,3},{3,2},{4,5},{5,4},{6,7},{7,6},{8,9},{9,8},{10,11... | collective-permute-start | bytes 405512 | tf_op jit(solution)/shard_map/ppermute | solution.py:487
  8.2 0.0 collective-permute-start.1
  8.2 0.2 collective-permute-start.2
  8.4 0.0 copy-start.3
  8.4 0.8 %copy-done.3 = bf16[32,512]{1,0:T(8,128)(2,1)S(1)} copy-done((bf16[32,512]{1,0:T(8,128)(2,1)S(1)}, bf16[32,512]{1,0:T(8,128)(2,1)}, u32[]{:S(2)}) %copy-start.3) | copy-done | bytes 32792
  9.2 3.9 %ray_sums_1_0.1 = (f32[8,4096]{1,0:T(8,128)S(1)}, f32[8,4096]{1,0:T(8,128)S(1)}, f32[8,4096]{1,0:T(8,128)S(1)}, f32[8,4096]{1,0:T(8,128)S(1)}, f32[2,8,128,1024]{3,2,1,0:T(8,128)S(1)}) custom-call(bf16[32,512]{1,0:T(8,128)(2,1)S(1)} %copy-done.3, f32[8,128,4096]{2,1,0:T(8,128)} %vol_ref.3), custom_call_target="tpu_custom_call" | custom-call | flops 67108864 | bytes 8388608 | tf_op jit(solution)/shard_map/ray_sums_1_0/pallas_call | solution.py:176
  13.1 0.0 copy-start
  13.1 3.3 %copy-done = f32[2,8,128,1024]{3,2,1,0:T(8,128)} copy-done((f32[2,8,128,1024]{3,2,1,0:T(8,128)}, f32[2,8,128,1024]{3,2,1,0:T(8,128)S(1)}, u32[]{:S(2)}) %copy-start) | copy-done | bytes 8388632
  16.4 1.9 %collective-permute-start.6 = (f32[8,4096]{1,0:T(8,128)S(1)}, f32[8,4096]{1,0:T(8,128)S(1)}, u32[]{:S(2)}, u32[]{:S(2)}) collective-permute-start(f32[8,4096]{1,0:T(8,128)S(1)} %get-tuple-element.53), channel_id=1, source_target_pairs={{0,1},{1,0},{2,3},{3,2},{4,5},{5,4},{6,7},{7,6},{8,9},{9,8},{10,11... | collective-permute-start | bytes 393224 | tf_op jit(solution)/shard_map/ppermute | solution.py:487
  18.3 0.0 collective-permute-start.7
  18.3 0.0 copy-done.1
  18.4 0.1 dynamic-slice_convert_fusion
  18.4 0.0 collective-permute-done
  18.5 0.3 collective-permute-start.8
  18.7 0.0 copy-done.5
  18.8 0.0 collective-permute-done.1
  18.8 0.4 collective-permute-start.5
  19.2 0.0 collective-permute-done.2
  19.2 1.7 %collective-permute-start.3 = (f32[2,8,4224]{2,1,0:T(8,128)S(1)}, f32[2,8,4224]{2,1,0:T(8,128)S(1)}, u32[]{:S(2)}, u32[]{:S(2)}) collective-permute-start(f32[2,8,4224]{2,1,0:T(8,128)S(1)} %pad_maximum_fusion.foot_ref.refs_2_), channel_id=1, source_target_pairs={{0,4},{2,6},{4,0},{6,2},{8,12},{10,14},{12,8},{14,10},{16,20},{18,... | collective-permute-start | bytes 811016 | tf_op jit(solution)/shard_map/ppermute | solution.py:479
  20.9 1.8 %collective-permute-done.6 = f32[8,4096]{1,0:T(8,128)S(1)} collective-permute-done((f32[8,4096]{1,0:T(8,128)S(1)}, f32[8,4096]{1,0:T(8,128)S(1)}, u32[]{:S(2)}, u32[]{:S(2)}) %collective-permute-start.6) | collective-permute-done | bytes 131104 | tf_op jit(solution)/shard_map/ppermute | solution.py:487
  22.7 0.0 collective-permute-done.7
  22.7 1.7 %collective-permute-done.8 = f32[8,4096]{1,0:T(8,128)S(1)} collective-permute-done((f32[8,4096]{1,0:T(8,128)S(1)}, f32[8,4096]{1,0:T(8,128)S(1)}, u32[]{:S(2)}, u32[]{:S(2)}) %collective-permute-start.8) | collective-permute-done | bytes 131104 | tf_op jit(solution)/shard_map/ppermute | solution.py:487
  24.5 1.5 %collective-permute-start.9 = (f32[2,8,4096]{2,1,0:T(8,128)S(1)}, f32[2,8,4096]{2,1,0:T(8,128)S(1)}, u32[]{:S(2)}, u32[]{:S(2)}) collective-permute-start(f32[2,8,4096]{2,1,0:T(8,128)S(1)} %pad_maximum_fusion.1.refs_5_), channel_id=1, source_target_pairs={{0,4},{2,6},{4,0},{6,2},{8,12},{10,14},{12,8},{14,10},{16,20},{18,... | collective-permute-start | bytes 786440 | tf_op jit(solution)/shard_map/ppermute | solution.py:479
  26.0 2.2 %collective-permute-done.3._.refs_3_ = f32[2,8,4224]{2,1,0:T(8,128)S(1)} collective-permute-done((f32[2,8,4224]{2,1,0:T(8,128)S(1)}, f32[2,8,4224]{2,1,0:T(8,128)S(1)}, u32[]{:S(2)}, u32[]{:S(2)}) %collective-permute-start.3) | collective-permute-done | bytes 270368 | tf_op jit(solution)/shard_map/ppermute | solution.py:479
  28.2 3.9 %collective-permute-start.4 = (f32[2,8,4224]{2,1,0:T(8,128)S(1)}, f32[2,8,4224]{2,1,0:T(8,128)S(1)}, u32[]{:S(2)}, u32[]{:S(2)}) collective-permute-start(f32[2,8,4224]{2,1,0:T(8,128)S(1)} %collective-permute-done.3._.refs_3_), channel_id=1, source_target_pairs={{0,8},{2,10},{8,16},{10,18},{12,4},{14,6},{16,24},{18,26},{20,12},... | collective-permute-start | bytes 811016 | tf_op jit(solution)/shard_map/ppermute | solution.py:479
  32.1 0.0 copy-done.2
  32.1 0.0 copy-done.4
  32.1 2.8 %prepare.1 = (f32[1,8,128,1024]{3,2,1,0:T(8,128)S(1)}, bf16[4,256,128]{2,1,0:T(8,128)(2,1)S(1)}) custom-call(s32[64]{0:T(128)S(1)} %copy-done.4, f32[64,256]{1,0:T(8,128)S(1)} %copy-done.2, f32[2,8,4224]{2,1,0:T(8,128)S(1)} %pad_maximum_fusion.foot_ref.refs_2_, f32[2,8,4224]{2,1,0:T(8,128)S(1)} %collective-permute-done.3._.refs_3_, f32[8,128,4096]{2,1,0:T(8,128)} %vol_ref.3), custom_call_target="tpu_custom_call" | custom-call | bytes 8388608 | tf_op jit(solution)/shard_map/prepare/pallas_call | solution.py:252
  34.9 0.0 collective-permute-done.9.refs_6_
  34.9 1.6 %collective-permute-start.10 = (f32[2,8,4096]{2,1,0:T(8,128)S(1)}, f32[2,8,4096]{2,1,0:T(8,128)S(1)}, u32[]{:S(2)}, u32[]{:S(2)}) collective-permute-start(f32[2,8,4096]{2,1,0:T(8,128)S(1)} %collective-permute-done.9.refs_6_), channel_id=1, source_target_pairs={{0,8},{2,10},{4,0},{6,2},{8,16},{10,18},{12,4},{14,6},{16,24},{18,... | collective-permute-start | bytes 786440 | tf_op jit(solution)/shard_map/ppermute | solution.py:479
  36.5 2.3 %collective-permute-done.4.refs_4_ = f32[2,8,4224]{2,1,0:T(8,128)S(1)} collective-permute-done((f32[2,8,4224]{2,1,0:T(8,128)S(1)}, f32[2,8,4224]{2,1,0:T(8,128)S(1)}, u32[]{:S(2)}, u32[]{:S(2)}) %collective-permute-start.4) | collective-permute-done | bytes 270368 | tf_op jit(solution)/shard_map/ppermute | solution.py:479
  38.8 0.0 collective-permute-done.5.refs_6_.refs_9_
  38.8 2.0 %residual_0.1 = (f32[4,32,1024]{2,1,0:T(8,128)S(1)}, f32[4,32,1024]{2,1,0:T(8,128)S(1)}, f32[2,32,1024]{2,1,0:T(8,128)S(1)}, f32[2,32,1024]{2,1,0:T(8,128)S(1)},...) custom-call(s32[64]{0:T(128)S(1)} %copy-done.4, ...), custom_call_target="tpu_custom_call" | custom-call | flops 603979776 | bytes 3670016 | tf_op jit(solution)/shard_map/residual_0/pallas_call | solution.py:380
  40.9 2.6 %collective-permute-start.12 = (f32[2,32,1024]{2,1,0:T(8,128)S(1)}, f32[2,32,1024]{2,1,0:T(8,128)S(1)}, u32[]{:S(2)}, u32[]{:S(2)}) collective-permute-start(f32[2,32,1024]{2,1,0:T(8,128)S(1)} %get-tuple-element.68), channel_id=1, source_target_pairs={{0,4},{2,6},{4,12},{6,14},{8,0},{10,2},{12,20},{14,22},{16,8},{18,... | collective-permute-start | bytes 786440 | tf_op jit(solution)/shard_map/ppermute | solution.py:479
  43.5 0.0 collective-permute-done.10.refs_7_
  43.5 1.2 %residual_1.1 = (f32[4,32,2048]{2,1,0:T(8,128)S(1)}, f32[4,32,2048]{2,1,0:T(8,128)S(1)}, f32[2,32,1024]{2,1,0:T(8,128)S(1)}, f32[2,32,1024]{2,1,0:T(8,128)S(1)}, f32[2,32,1024]{2,1,0:T(8,128)S(1)}) custom-call(bf16[256,192]{1,0:T(8,128)(2,1)S(1)} %get-tuple-element.46.refs_0_, bf16[256,192]{1,0:T(8,128)(2,1)S(1)} %get-tuple-element.47.refs_1_, ...), custom_call_target="tpu_custom_call" | custom-call | flops 603979776 | bytes 3670016 | tf_op jit(solution)/shard_map/residual_1/pallas_call | solution.py:380
  44.7 0.1 collective-permute-start.21
  44.8 1.3 %collective-permute-start.11 = (f32[2,32,1024]{2,1,0:T(8,128)S(1)}, f32[2,32,1024]{2,1,0:T(8,128)S(1)}, u32[]{:S(2)}, u32[]{:S(2)}) collective-permute-start(f32[2,32,1024]{2,1,0:T(8,128)S(1)} %get-tuple-element.66), channel_id=1, source_target_pairs={{4,12},{6,14},{8,0},{10,2},{12,20},{14,22},{16,8},{18,10},{20,28},... | collective-permute-start | bytes 786440 | tf_op jit(solution)/shard_map/ppermute | solution.py:479
  46.1 1.7 %collective-permute-done.12 = f32[2,32,1024]{2,1,0:T(8,128)S(1)} collective-permute-done((f32[2,32,1024]{2,1,0:T(8,128)S(1)}, f32[2,32,1024]{2,1,0:T(8,128)S(1)}, u32[]{:S(2)}, u32[]{:S(2)}) %collective-permute-start.12) | collective-permute-done | bytes 262176 | tf_op jit(solution)/shard_map/ppermute | solution.py:479
  47.8 2.4 %collective-permute-start.17 = (f32[2,32,1024]{2,1,0:T(8,128)S(1)}, f32[2,32,1024]{2,1,0:T(8,128)S(1)}, u32[]{:S(2)}, u32[]{:S(2)}) collective-permute-start(f32[2,32,1024]{2,1,0:T(8,128)S(1)} %add.48._), channel_id=1, source_target_pairs={{0,4},{2,6},{4,0},{6,2},{8,12},{10,14},{12,8},{14,10},{16,20},{18,... | collective-permute-start | bytes 786440 | tf_op jit(solution)/shard_map/ppermute | solution.py:479
  50.3 2.6 %load.1 = (f32[1,8,128,1024]{3,2,1,0:T(8,128)S(1)}, f32[4,32,4096]{2,1,0:T(8,128)}) custom-call(f32[2,32,1024]{2,1,0:T(8,128)S(1)} %add.48._, f32[8,128,4096]{2,1,0:T(8,128)} %vol_ref.3, f32[4,32,2048]{2,1,0:T(8,128)S(1)} %get-tuple-element.69.mine_ref), custom_call_target="tpu_custom_call" | custom-call | bytes 4194304 | tf_op jit(solution)/shard_map/load/pallas_call | solution.py:289
  52.9 2.7 %collective-permute-done.11 = f32[2,32,1024]{2,1,0:T(8,128)S(1)} collective-permute-done((f32[2,32,1024]{2,1,0:T(8,128)S(1)}, f32[2,32,1024]{2,1,0:T(8,128)S(1)}, u32[]{:S(2)}, u32[]{:S(2)}) %collective-permute-start.11) | collective-permute-done | bytes 262176 | tf_op jit(solution)/shard_map/ppermute | solution.py:479
  55.6 0.8 %collective-permute-start.13 = (f32[2,32,1024]{2,1,0:T(8,128)S(1)}, f32[2,32,1024]{2,1,0:T(8,128)S(1)}, u32[]{:S(2)}, u32[]{:S(2)}) collective-permute-start(f32[2,32,1024]{2,1,0:T(8,128)S(1)} %add.49), channel_id=1, source_target_pairs={{0,4},{2,6},{4,0},{6,2},{8,12},{10,14},{12,8},{14,10},{16,20},{18,... | collective-permute-start | bytes 786440 | tf_op jit(solution)/shard_map/ppermute | solution.py:479
  56.4 0.5 collective-permute-done.17
  57.0 0.9 %collective-permute-start.18 = (f32[32,1024]{1,0:T(8,128)S(1)}, f32[32,1024]{1,0:T(8,128)S(1)}, u32[]{:S(2)}, u32[]{:S(2)}) collective-permute-start(f32[32,1024]{1,0:T(8,128)S(1)} %get-tuple-element.81), channel_id=1, source_target_pairs={{0,3},{1,2},{2,1},{3,0},{4,7},{5,6},{6,5},{7,4},{8,11},{9,10},{10,... | collective-permute-start | bytes 393224 | tf_op jit(solution)/shard_map/ppermute | solution.py:487
  57.9 0.8 %collective-permute-start.19 = (f32[32,1024]{1,0:T(8,128)S(1)}, f32[32,1024]{1,0:T(8,128)S(1)}, u32[]{:S(2)}, u32[]{:S(2)}) collective-permute-start(f32[32,1024]{1,0:T(8,128)S(1)} %get-tuple-element.81), channel_id=1, source_target_pairs={{0,2},{1,3},{2,0},{3,1},{4,6},{5,7},{6,4},{7,5},{8,10},{9,11},{10,... | collective-permute-start | bytes 393224 | tf_op jit(solution)/shard_map/ppermute | solution.py:487
  58.7 0.5 collective-permute-start.20
  59.2 4.5 %collective-permute-done.13 = f32[2,32,1024]{2,1,0:T(8,128)S(1)} collective-permute-done((f32[2,32,1024]{2,1,0:T(8,128)S(1)}, f32[2,32,1024]{2,1,0:T(8,128)S(1)}, u32[]{:S(2)}, u32[]{:S(2)}) %collective-permute-start.13) | collective-permute-done | bytes 262176 | tf_op jit(solution)/shard_map/ppermute | solution.py:479
  63.8 1.6 %collective-permute-start.16 = (f32[32,1024]{1,0:T(8,128)S(1)}, f32[32,1024]{1,0:T(8,128)S(1)}, u32[]{:S(2)}, u32[]{:S(2)}) collective-permute-start(f32[32,1024]{1,0:T(8,128)S(1)} %get-tuple-element.82.refs_2_), channel_id=1, source_target_pairs={{0,1},{1,0},{2,3},{3,2},{4,5},{5,4},{6,7},{7,6},{8,9},{9,8},{10,11... | collective-permute-start | bytes 393224 | tf_op jit(solution)/shard_map/ppermute | solution.py:487
  65.4 0.0 collective-permute-done.18.refs_1_
  65.4 0.0 collective-permute-start.14
  65.4 0.0 collective-permute-done.19.refs_2_
  65.4 0.6 collective-permute-start.15
  66.0 0.0 collective-permute-done.20.refs_3_
  66.0 4.2 %update_0_0.1.refs_4_ = f32[8,128,4096]{2,1,0:T(8,128)} custom-call(bf16[4,256,128]{2,1,0:T(8,128)(2,1)S(1)} %get-tuple-element.45.refs_0_, f32[32,1024]{1,0:T(8,128)S(1)} %collective-permute-done.18.refs_1_, f32[32,1024]{1,0:T(8,128)S(1)} %collective-permute-done.19.refs_2_, f32[32,1024]{1,0:T(8,128)S(1)} %collective-permute-done.20.refs_3_, ...), custom_call_target="tpu_custom_call" | custom-call | flops 201326592 | bytes 8388608 | tf_op jit(solution)/shard_map/update_0_0/pallas_call | solution.py:453
  70.2 0.0 collective-permute-done.16.refs_1_
  70.2 0.0 collective-permute-done.21.refs_5_
  70.2 0.0 slice-done
  70.2 0.3 slice-done.1
  70.5 2.7 %update_1_0.1 = (f32[8,128,4096]{2,1,0:T(8,128)}, f32[4,32,4096]{2,1,0:T(8,128)}) custom-call(bf16[4,256,128]{2,1,0:T(8,128)(2,1)S(1)} %get-tuple-element.45.refs_0_, f32[32,1024]{1,0:T(8,128)S(1)} %collective-permute-done.16.refs_1_, f32[32,1024]{1,0:T(8,128)S(1)} %get-tuple-element.82.refs_2_, ...), custom_call_target="tpu_custom_call", output_to_operand_aliasing={{0}: (4, {}), {1}: (6, {})} | custom-call | flops 100663296 | bytes 4194304 | tf_op jit(solution)/shard_map/update_1_0/pallas_call | solution.py:453
  73.2 0.0 collective-permute-done.14.refs_1_
  73.2 0.0 collective-permute-done.15.refs_2_
  73.2 2.3 %update_1_1.1 = f32[8,128,4096]{2,1,0:T(8,128)} custom-call(bf16[4,256,128]{2,1,0:T(8,128)(2,1)S(1)} %get-tuple-element.45.refs_0_, f32[32,1024]{1,0:T(8,128)S(1)} %collective-permute-done.14.refs_1_, f32[32,1024]{1,0:T(8,128)S(1)} %collective-permute-done.15.refs_2_, f32[2,8,128,1024]{3,2,1,0:T(8,128)S(1)} %bitcast.17, ...), custom_call_target="tpu_custom_call", output_to_operand_aliasing={{}: (4, {})} | custom-call | flops 100663296 | bytes 4194304 | tf_op jit(solution)/shard_map/update_1_1/pallas_call | solution.py:453
  (16 shorter events, 0.3 us)
Async XLA Ops:
  5.2 13.3 %collective-permute-start = (f32[8,4224]{1,0:T(8,128)}, f32[8,4224]{1,0:T(8,128)S(1)}, u32[]{:S(2)}, u32[]{:S(2)}) collective-permute-start(f32[8,4224]{1,0:T(8,128)} %get-tuple-element.42), channel_id=1, source_target_pairs={{0,1},{1,0},{2,3},{3,2},{4,5},{5,4},{6,7},{7,6},{8,9},{9,8},{10,11... | collective-permute-start | bytes 405512 | tf_op jit(solution)/shard_map/ppermute | solution.py:487
  8.2 10.5 %collective-permute-start.1 = (f32[8,4224]{1,0:T(8,128)}, f32[8,4224]{1,0:T(8,128)S(1)}, u32[]{:S(2)}, u32[]{:S(2)}) collective-permute-start(f32[8,4224]{1,0:T(8,128)} %get-tuple-element.43), channel_id=1, source_target_pairs={{0,2},{1,3},{2,0},{3,1},{4,6},{5,7},{6,4},{7,5},{8,10},{9,11},{10,... | collective-permute-start | bytes 405512 | tf_op jit(solution)/shard_map/ppermute | solution.py:487
  8.2 10.9 %collective-permute-start.2 = (f32[8,4224]{1,0:T(8,128)}, f32[8,4224]{1,0:T(8,128)S(1)}, u32[]{:S(2)}, u32[]{:S(2)}) collective-permute-start(f32[8,4224]{1,0:T(8,128)} %get-tuple-element.44), channel_id=1, source_target_pairs={{0,3},{1,2},{2,1},{3,0},{4,7},{5,6},{6,5},{7,4},{8,11},{9,10},{10,... | collective-permute-start | bytes 405512 | tf_op jit(solution)/shard_map/ppermute | solution.py:487
  8.4 0.8 %copy-start.3 = (bf16[32,512]{1,0:T(8,128)(2,1)S(1)}, bf16[32,512]{1,0:T(8,128)(2,1)}, u32[]{:S(2)}) copy-start(bf16[32,512]{1,0:T(8,128)(2,1)} %get-tuple-element.51.refs_0_) | copy-start | bytes 98308
  9.2 9.2 %copy-start.1 = (bf16[4,32,4096]{2,1,0:T(8,128)(2,1)S(1)}, bf16[4,32,4096]{2,1,0:T(8,128)(2,1)}, u32[]{:S(2)}) copy-start(bf16[4,32,4096]{2,1,0:T(8,128)(2,1)} %refs_8_.1) | copy-start | bytes 3145732
  9.2 9.5 %copy-start.5 = (f32[8,4224]{1,0:T(8,128)S(1)}, f32[8,4224]{1,0:T(8,128)}, u32[]{:S(2)}) copy-start(f32[8,4224]{1,0:T(8,128)} %get-tuple-element.41) | copy-start | bytes 405508
  9.2 22.9 %copy-start.2 = (f32[64,256]{1,0:T(8,128)S(1)}, f32[64,256]{1,0:T(8,128)}, u32[]{:S(2)}) copy-start(f32[64,256]{1,0:T(8,128)} %refs_1_.4) | copy-start | bytes 196612
  9.2 22.9 %copy-start.4 = (s32[64]{0:T(128)S(1)}, s32[64]{0:T(128)}, u32[]{:S(2)}) copy-start(s32[64]{0:T(128)} %refs_0_.3) | copy-start | bytes 772
  13.1 3.3 %copy-start = (f32[2,8,128,1024]{3,2,1,0:T(8,128)}, f32[2,8,128,1024]{3,2,1,0:T(8,128)S(1)}, u32[]{:S(2)}) copy-start(f32[2,8,128,1024]{3,2,1,0:T(8,128)S(1)} %get-tuple-element.72.refs_3_) | copy-start | bytes 25165828
  16.4 6.2 %collective-permute-start.6 = (f32[8,4096]{1,0:T(8,128)S(1)}, f32[8,4096]{1,0:T(8,128)S(1)}, u32[]{:S(2)}, u32[]{:S(2)}) collective-permute-start(f32[8,4096]{1,0:T(8,128)S(1)} %get-tuple-element.53), channel_id=1, source_target_pairs={{0,1},{1,0},{2,3},{3,2},{4,5},{5,4},{6,7},{7,6},{8,9},{9,8},{10,11... | collective-permute-start | bytes 393224 | tf_op jit(solution)/shard_map/ppermute | solution.py:487
  18.3 4.3 %collective-permute-start.7 = (f32[8,4096]{1,0:T(8,128)S(1)}, f32[8,4096]{1,0:T(8,128)S(1)}, u32[]{:S(2)}, u32[]{:S(2)}) collective-permute-start(f32[8,4096]{1,0:T(8,128)S(1)} %get-tuple-element.54), channel_id=1, source_target_pairs={{0,2},{1,3},{2,0},{3,1},{4,6},{5,7},{6,4},{7,5},{8,10},{9,11},{10,... | collective-permute-start | bytes 393224 | tf_op jit(solution)/shard_map/ppermute | solution.py:487
  18.5 5.9 %collective-permute-start.8 = (f32[8,4096]{1,0:T(8,128)S(1)}, f32[8,4096]{1,0:T(8,128)S(1)}, u32[]{:S(2)}, u32[]{:S(2)}) collective-permute-start(f32[8,4096]{1,0:T(8,128)S(1)} %get-tuple-element.55), channel_id=1, source_target_pairs={{0,3},{1,2},{2,1},{3,0},{4,7},{5,6},{6,5},{7,4},{8,11},{9,10},{10,... | collective-permute-start | bytes 393224 | tf_op jit(solution)/shard_map/ppermute | solution.py:487
  18.8 20.1 %collective-permute-start.5 = (f32[4,32,2048]{2,1,0:T(8,128)S(1)}, f32[4,32,2048]{2,1,0:T(8,128)S(1)}, u32[]{:S(2)}, u32[]{:S(2)}) collective-permute-start(f32[4,32,2048]{2,1,0:T(8,128)S(1)} %dynamic-slice_convert_fusion), channel_id=1, source_target_pairs={{0,2},{2,0},{4,6},{6,4},{8,10},{10,8},{12,14},{14,12},{16,18},{18,... | collective-permute-start | bytes 3145736 | tf_op jit(solution)/shard_map/ppermute | solution.py:479
  19.2 9.0 %collective-permute-start.3 = (f32[2,8,4224]{2,1,0:T(8,128)S(1)}, f32[2,8,4224]{2,1,0:T(8,128)S(1)}, u32[]{:S(2)}, u32[]{:S(2)}) collective-permute-start(f32[2,8,4224]{2,1,0:T(8,128)S(1)} %pad_maximum_fusion.foot_ref.refs_2_), channel_id=1, source_target_pairs={{0,4},{2,6},{4,0},{6,2},{8,12},{10,14},{12,8},{14,10},{16,20},{18,... | collective-permute-start | bytes 811016 | tf_op jit(solution)/shard_map/ppermute | solution.py:479
  24.5 10.5 %collective-permute-start.9 = (f32[2,8,4096]{2,1,0:T(8,128)S(1)}, f32[2,8,4096]{2,1,0:T(8,128)S(1)}, u32[]{:S(2)}, u32[]{:S(2)}) collective-permute-start(f32[2,8,4096]{2,1,0:T(8,128)S(1)} %pad_maximum_fusion.1.refs_5_), channel_id=1, source_target_pairs={{0,4},{2,6},{4,0},{6,2},{8,12},{10,14},{12,8},{14,10},{16,20},{18,... | collective-permute-start | bytes 786440 | tf_op jit(solution)/shard_map/ppermute | solution.py:479
  28.2 10.7 %collective-permute-start.4 = (f32[2,8,4224]{2,1,0:T(8,128)S(1)}, f32[2,8,4224]{2,1,0:T(8,128)S(1)}, u32[]{:S(2)}, u32[]{:S(2)}) collective-permute-start(f32[2,8,4224]{2,1,0:T(8,128)S(1)} %collective-permute-done.3._.refs_3_), channel_id=1, source_target_pairs={{0,8},{2,10},{8,16},{10,18},{12,4},{14,6},{16,24},{18,26},{20,12},... | collective-permute-start | bytes 811016 | tf_op jit(solution)/shard_map/ppermute | solution.py:479
  34.9 8.6 %collective-permute-start.10 = (f32[2,8,4096]{2,1,0:T(8,128)S(1)}, f32[2,8,4096]{2,1,0:T(8,128)S(1)}, u32[]{:S(2)}, u32[]{:S(2)}) collective-permute-start(f32[2,8,4096]{2,1,0:T(8,128)S(1)} %collective-permute-done.9.refs_6_), channel_id=1, source_target_pairs={{0,8},{2,10},{4,0},{6,2},{8,16},{10,18},{12,4},{14,6},{16,24},{18,... | collective-permute-start | bytes 786440 | tf_op jit(solution)/shard_map/ppermute | solution.py:479
  40.9 6.9 %collective-permute-start.12 = (f32[2,32,1024]{2,1,0:T(8,128)S(1)}, f32[2,32,1024]{2,1,0:T(8,128)S(1)}, u32[]{:S(2)}, u32[]{:S(2)}) collective-permute-start(f32[2,32,1024]{2,1,0:T(8,128)S(1)} %get-tuple-element.68), channel_id=1, source_target_pairs={{0,4},{2,6},{4,12},{6,14},{8,0},{10,2},{12,20},{14,22},{16,8},{18,... | collective-permute-start | bytes 786440 | tf_op jit(solution)/shard_map/ppermute | solution.py:479
  44.7 25.5 %collective-permute-start.21 = (f32[4,32,2048]{2,1,0:T(8,128)S(1)}, f32[4,32,2048]{2,1,0:T(8,128)S(1)}, u32[]{:S(2)}, u32[]{:S(2)}) collective-permute-start(f32[4,32,2048]{2,1,0:T(8,128)S(1)} %get-tuple-element.76), channel_id=1, source_target_pairs={{0,2},{2,0},{4,6},{6,4},{8,10},{10,8},{12,14},{14,12},{16,18},{18,... | collective-permute-start | bytes 3145736 | tf_op jit(solution)/shard_map/ppermute | solution.py:479
  44.8 10.8 %collective-permute-start.11 = (f32[2,32,1024]{2,1,0:T(8,128)S(1)}, f32[2,32,1024]{2,1,0:T(8,128)S(1)}, u32[]{:S(2)}, u32[]{:S(2)}) collective-permute-start(f32[2,32,1024]{2,1,0:T(8,128)S(1)} %get-tuple-element.66), channel_id=1, source_target_pairs={{4,12},{6,14},{8,0},{10,2},{12,20},{14,22},{16,8},{18,10},{20,28},... | collective-permute-start | bytes 786440 | tf_op jit(solution)/shard_map/ppermute | solution.py:479
  47.8 9.1 %collective-permute-start.17 = (f32[2,32,1024]{2,1,0:T(8,128)S(1)}, f32[2,32,1024]{2,1,0:T(8,128)S(1)}, u32[]{:S(2)}, u32[]{:S(2)}) collective-permute-start(f32[2,32,1024]{2,1,0:T(8,128)S(1)} %add.48._), channel_id=1, source_target_pairs={{0,4},{2,6},{4,0},{6,2},{8,12},{10,14},{12,8},{14,10},{16,20},{18,... | collective-permute-start | bytes 786440 | tf_op jit(solution)/shard_map/ppermute | solution.py:479
  55.6 8.1 %collective-permute-start.13 = (f32[2,32,1024]{2,1,0:T(8,128)S(1)}, f32[2,32,1024]{2,1,0:T(8,128)S(1)}, u32[]{:S(2)}, u32[]{:S(2)}) collective-permute-start(f32[2,32,1024]{2,1,0:T(8,128)S(1)} %add.49), channel_id=1, source_target_pairs={{0,4},{2,6},{4,0},{6,2},{8,12},{10,14},{12,8},{14,10},{16,20},{18,... | collective-permute-start | bytes 786440 | tf_op jit(solution)/shard_map/ppermute | solution.py:479
  57.0 8.4 %collective-permute-start.18 = (f32[32,1024]{1,0:T(8,128)S(1)}, f32[32,1024]{1,0:T(8,128)S(1)}, u32[]{:S(2)}, u32[]{:S(2)}) collective-permute-start(f32[32,1024]{1,0:T(8,128)S(1)} %get-tuple-element.81), channel_id=1, source_target_pairs={{0,3},{1,2},{2,1},{3,0},{4,7},{5,6},{6,5},{7,4},{8,11},{9,10},{10,... | collective-permute-start | bytes 393224 | tf_op jit(solution)/shard_map/ppermute | solution.py:487
  57.9 7.5 %collective-permute-start.19 = (f32[32,1024]{1,0:T(8,128)S(1)}, f32[32,1024]{1,0:T(8,128)S(1)}, u32[]{:S(2)}, u32[]{:S(2)}) collective-permute-start(f32[32,1024]{1,0:T(8,128)S(1)} %get-tuple-element.81), channel_id=1, source_target_pairs={{0,2},{1,3},{2,0},{3,1},{4,6},{5,7},{6,4},{7,5},{8,10},{9,11},{10,... | collective-permute-start | bytes 393224 | tf_op jit(solution)/shard_map/ppermute | solution.py:487
  58.7 7.3 %collective-permute-start.20 = (f32[32,1024]{1,0:T(8,128)S(1)}, f32[32,1024]{1,0:T(8,128)S(1)}, u32[]{:S(2)}, u32[]{:S(2)}) collective-permute-start(f32[32,1024]{1,0:T(8,128)S(1)} %get-tuple-element.80.refs_4_), channel_id=1, source_target_pairs={{0,1},{1,0},{2,3},{3,2},{4,5},{5,4},{6,7},{7,6},{8,9},{9,8},{10,11... | collective-permute-start | bytes 393224 | tf_op jit(solution)/shard_map/ppermute | solution.py:487
  63.7 6.5 %slice-start = ((s8[8388608]{0:T(1024)(128)(4,1)}), s8[4194304]{0:T(1024)(128)(4,1)S(1)}, s32[]{:S(2)}) async-start(s8[8388608]{0:T(1024)(128)(4,1)} %bitcast.16), calls=%async_computation | async-start | bytes 8388608
  63.8 6.4 %collective-permute-start.16 = (f32[32,1024]{1,0:T(8,128)S(1)}, f32[32,1024]{1,0:T(8,128)S(1)}, u32[]{:S(2)}, u32[]{:S(2)}) collective-permute-start(f32[32,1024]{1,0:T(8,128)S(1)} %get-tuple-element.82.refs_2_), channel_id=1, source_target_pairs={{0,1},{1,0},{2,3},{3,2},{4,5},{5,4},{6,7},{7,6},{8,9},{9,8},{10,11... | collective-permute-start | bytes 393224 | tf_op jit(solution)/shard_map/ppermute | solution.py:487
  65.4 7.8 %collective-permute-start.14 = (f32[32,1024]{1,0:T(8,128)S(1)}, f32[32,1024]{1,0:T(8,128)S(1)}, u32[]{:S(2)}, u32[]{:S(2)}) collective-permute-start(f32[32,1024]{1,0:T(8,128)S(1)} %get-tuple-element.83), channel_id=1, source_target_pairs={{0,3},{1,2},{2,1},{3,0},{4,7},{5,6},{6,5},{7,4},{8,11},{9,10},{10,... | collective-permute-start | bytes 393224 | tf_op jit(solution)/shard_map/ppermute | solution.py:487
  65.4 7.8 %collective-permute-start.15 = (f32[32,1024]{1,0:T(8,128)S(1)}, f32[32,1024]{1,0:T(8,128)S(1)}, u32[]{:S(2)}, u32[]{:S(2)}) collective-permute-start(f32[32,1024]{1,0:T(8,128)S(1)} %get-tuple-element.83), channel_id=1, source_target_pairs={{0,2},{1,3},{2,0},{3,1},{4,6},{5,7},{6,4},{7,5},{8,10},{9,11},{10,... | collective-permute-start | bytes 393224 | tf_op jit(solution)/shard_map/ppermute | solution.py:487
  66.0 4.5 %slice-start.1 = ((s8[8388608]{0:T(1024)(128)(4,1)}), s8[4194304]{0:T(1024)(128)(4,1)S(1)}, s32[]{:S(2)}) async-start(s8[8388608]{0:T(1024)(128)(4,1)} %bitcast.16), calls=%async_computation.1 | async-start | bytes 8388608

commit v9 on v6

--- a/solution.py
+++ b/solution.py
@@ -205,11 +205,11 @@
     row = (row_slab * rdev + low_bits(row_id, rdev)).astype(F32)
     shape = (foot.shape[0], rows)
     same_angle = low_bits(iota(shape, 0), per) == low_bits(over(iota(shape, 1), rdev), per)
-    beyond = slab + jnp.where(low_bits(slab, 4) < 2, -2, 2)
-    there = jnp.logical_and(beyond >= 0, beyond < lax.axis_size("slab"))
-    known = jnp.where(there, foot.shape[0], foot.shape[0] // 3 * 2)
-    meets = jnp.logical_and(same_angle, iota(shape, 0) < known)
-    return jnp.where(meets, hat_weights(dims, zdev, foot[:, 0:1], foot[:, 1:2], row), 0.0)
+    return jnp.where(same_angle, hat_weights(dims, zdev, foot[:, 0:1], foot[:, 1:2], row), 0.0)
+
+
+def footprints(ref, batches, width):
+    return jnp.concatenate([ref[i, :, batches * width:] for i in range(2) for _ in range(batches)], axis=0)
 
 
 def update_weights(dims, zdev, rdev, foot, order_ref, table_ref, rows_ref, out_ref):
@@ -231,7 +231,10 @@
         out_ref[zp] = stacked.T.astype(BF16)
 
 
-def prepare_kernel(dims, rdev, half, width, order_ref, table_ref, foot_ref, _, vol_ref, kept_ref, left_ref, sems, rows_ref):
+def prepare_kernel(
+    dims, rdev, half, width, order_ref, table_ref, own_ref, near_ref, vol_ref,
+    kept_ref, left_ref, ahead_high, ahead_low, back_high, back_low, cover_ref, sems, rows_ref,
+):
     zdev = vol_ref.shape[0]
     copies = []
     for h, zp, slices, start in volume_pieces(dims, zdev, half, 0, (0, 1)):
@@ -239,8 +242,13 @@
         copies.append(pltpu.make_async_copy(source, kept_ref.at[h, slices], sems.at[h, zp]))
         copies[-1].start()
     batches = zdev // dims[2]
-    foot = jnp.concatenate([foot_ref[0, :, batches * width:]] * batches, axis=0)
-    update_weights(dims, zdev, rdev, foot, order_ref, table_ref, rows_ref, left_ref)
+    own = footprints(own_ref, batches, width)
+    kernel = footprint_matrix(dims, zdev, rdev, jnp.concatenate([own, footprints(near_ref, batches, width)], axis=0))
+    back_high[...], back_low[...] = split(kernel)
+    kernel_t = kernel.T
+    ahead_high[...], ahead_low[...] = split(kernel_t)
+    cover_ref[...] = jnp.broadcast_to(jnp.sum(kernel_t, axis=1, keepdims=True), cover_ref.shape)
+    update_weights(dims, zdev, rdev, own[:own.shape[0] // 2], order_ref, table_ref, rows_ref, left_ref)
     for copy in copies:
         copy.wait()
 
@@ -249,13 +257,19 @@
     per, groups, zb, cells = dims
     zdev, _, total = volume.shape
     depth = -(-3 * groups * SUBLANES // LANES) * LANES
+    count, rows = 4 * zdev * per, 2 * per * rdev
     return pl.pallas_call(
         functools.partial(prepare_kernel, dims, rdev, total // 2, width),
-        in_specs=[IN_SMEM, IN_VMEM, IN_VMEM, ANYWHERE, ANYWHERE],
-        out_specs=[IN_VMEM, IN_VMEM],
+        in_specs=[IN_SMEM, IN_VMEM, IN_VMEM, IN_VMEM, ANYWHERE],
+        out_specs=[IN_VMEM] * 7,
         out_shape=[
             jax.ShapeDtypeStruct((2, zdev, cells, width), F32),
             jax.ShapeDtypeStruct((zdev // zb, zb * cells, depth), BF16),
+            jax.ShapeDtypeStruct((rows, count), BF16),
+            jax.ShapeDtypeStruct((rows, count), BF16),
+            jax.ShapeDtypeStruct((count, rows), BF16),
+            jax.ShapeDtypeStruct((count, rows), BF16),
+            jax.ShapeDtypeStruct((rows, LANES), F32),
         ],
         scratch_shapes=[
             pltpu.SemaphoreType.DMA((2, zdev // zb)),
@@ -272,6 +286,7 @@
     block = zdev * per
     if first:
         order_ref, table_ref, *refs = refs
+        known, known_cover, refs = refs[:4], refs[4], refs[5:]
     else:
         mats, inverse_ref, refs = refs[:4], refs[4], refs[5:]
     sums_refs, (mine_ref, theirs_ref), refs = refs[:3], refs[3:5], refs[5:]
@@ -281,24 +296,28 @@
     if not first:
         mine_out[:, :, :offset] = mine_before[...]
         sent_out[:, :, :offset] = sent_before[...]
-    outs, refs = refs[:3], refs[3:]
-    if first:
-        foot = jnp.concatenate(
-            [r[i, :, zdev // zb * width:] for r in sums_refs for i in range(2) for _ in range(zdev // zb)], axis=0
-        )
-        kernel = footprint_matrix(dims, zdev, rdev, foot)
-        count, rows = kernel.shape
+    outs = refs[:1 if first else 3]
+    refs = refs[len(outs):]
+    if first:
+        slab = lax.axis_index("slab")
+        beyond = slab + jnp.where(low_bits(slab, 4) < 2, -2, 2)
+        there = jnp.logical_and(beyond >= 0, beyond < lax.axis_size("slab"))
+        kernel = footprint_matrix(dims, zdev, rdev, footprints(sums_refs[2], zdev // zb, width))
+        kernel = jnp.where(there, kernel, 0.0)
+        rows = kernel.shape[1]
         kernel_t = kernel.T
-        cover = jnp.sum(kernel_t, axis=1, keepdims=True)
+        cover = known_cover[:, 0:1] + jnp.sum(kernel_t, axis=1, keepdims=True)
         angle = low_bits(over(iota((rows, 1), 0), rdev), per)
         path = jnp.zeros((rows, 1), F32)
         for a in range(per):
             at = order_ref[lax.axis_index("ang") * per + a]
             path = jnp.where(angle == a, jnp.sum(table_ref[pl.ds(at, 1), :], axis=1, keepdims=True), path)
         inverse = 1.0 / jnp.maximum(path * cover, 0.25)
-        ahead, back = split(kernel_t), split(kernel)
+        ahead = [jnp.concatenate([k[...], far], axis=1) for k, far in zip(known[:2], split(kernel_t))]
+        back = [jnp.concatenate([k[...], far], axis=0) for k, far in zip(known[2:], split(kernel))]
         for ref, value in zip(refs, (*ahead, *back)):
             ref[...] = value
+        back = split(kernel)
         refs[4][...] = jnp.broadcast_to(inverse, (rows, LANES))
     else:
         ahead, back = (mats[0][...], mats[1][...]), (mats[2][...], mats[3][...])
@@ -334,9 +353,9 @@
     count, rows = 6 * block, 2 * per * rdev
     given = jax.ShapeDtypeStruct((2, block, width), F32)
     piece = jax.ShapeDtypeStruct((per, rdev, offset + width), F32)
-    shapes = [piece, piece, given, given, given]
-    if first:
-        args, specs = [order, table], [IN_SMEM, IN_VMEM]
+    shapes = [piece, piece] + [given] * (1 if first else 3)
+    if first:
+        args, specs = [order, table, *mats], [IN_SMEM] + [IN_VMEM] * (1 + len(mats))
         ahead, back = jax.ShapeDtypeStruct((rows, count), BF16), jax.ShapeDtypeStruct((count, rows), BF16)
         shapes += [ahead, ahead, back, back, jax.ShapeDtypeStruct((rows, LANES), F32)]
     else:
@@ -354,6 +373,34 @@
         ),
         name=f"residual_{chunk}",
     )(*args)
+
+
+def back_kernel(high_ref, low_ref, mine_ref, sent_ref, *outs):
+    block, width = outs[0].shape[1:]
+    back = high_ref[:4 * block], low_ref[:4 * block]
+    for at, size in tiles(width):
+        columns = slice(at, at + size)
+        rows = mine_ref.shape[0] * mine_ref.shape[1]
+        residual = jnp.concatenate([r[:, :, columns].reshape(rows, size) for r in (mine_ref, sent_ref)], axis=0)
+        given = dot3(back, split(residual))
+        for i, ref in enumerate(outs):
+            for j in range(2):
+                ref[j, :, columns] = given[(2 * i + j) * block:(2 * i + j + 1) * block]
+
+
+def back_step(high, low, mine, sent, far):
+    given = jax.ShapeDtypeStruct(far.shape, F32)
+    return pl.pallas_call(
+        back_kernel,
+        in_specs=[IN_VMEM] * 4,
+        out_specs=[IN_VMEM] * 2,
+        out_shape=[given, given],
+        compiler_params=pltpu.CompilerParams(vmem_limit_bytes=30 * MIB),
+        cost_estimate=pl.CostEstimate(
+            flops=6 * high.size * far.shape[2], bytes_accessed=8 * mine.size, transcendentals=0
+        ),
+        name="back_0",
+    )(high, low, mine, sent)
 
 
 def update_kernel(dims, first, halves, half, offset, width, *refs):
@@ -495,19 +542,23 @@
         own = jnp.stack([sum(parts[:groups]), sum(parts[groups:])])
         near = along(own, facing)
         if c == 0:
-            first_columns, update_left = prepare_step(dims, rdev, widths[0], order, table, own, near, volume)
+            first_columns, update_left, *mats = prepare_step(dims, rdev, widths[0], order, table, own, near, volume)
             kept[0] = [(h, first_columns) for h in range(2)]
         if c == 1:
             near, first_columns = lax.optimization_barrier((near, first_columns))
         far = along(near, beyond(c))
         sums.append((own, near, far))
-    pieces, given, mats = [], [], None
+    pieces, given = [], []
     for c in range(CHUNKS):
-        mine, sent, own, near, far, *rest = residual_step(
+        mine, sent, *made = residual_step(
             dims, zdev, c, offsets[c], widths[c], mats, pieces, order, table, sums[c], measured, theirs
         )
+        if c == 0:
+            far, *mats = made
+            own, near = back_step(mats[2], mats[3], mine, sent, far)
+        else:
+            own, near, far = made
         pieces = [mine, sent]
-        mats = rest if c == 0 else mats
         near = near + along(far, back_from_beyond(c))
         arrived = along(near, facing)
         halves = [own[i] + arrived[i] for i in range(2)]

time: 71 us -> 71.4 us (level)
  transfers between devices with their start and end apart: 22 -> 22, of which waited for: 9 -> 8; matrix products, arithmetic and copies ran while one was open for 0% -> 1% of each run, Pallas kernels for 25% -> 26%
where the time goes in v9:
time: 71.4 us; the launch traced here: 71.2 us
  Pallas kernels  25.1 us (35%)
  starting transfers between devices  24.4 us (34%)
  waiting for transfers between devices  19.7 us (28%)
  between operations  0.86 us (1%)
  local copies, waits for them, and re-layouts  0.78 us (1%)
    ppermute x10, waiting for transfers between devices, along(): return lax.ppermute(value, 'slab', pairs)  15.2 us
    ppermute x10, starting transfers between devices, along(): return lax.ppermute(value, 'slab', pairs)  14.2 us
    ppermute x12, starting transfers between devices, spread(): return lax.ppermute(value, ('slab', 'ang'), pairs)  10.2 us
    pallas_call x3, Pallas kernels, update_step(): pl.pallas_call(functools.partial(update_kernel, dims, first, halves, tota...  8.7 us
    pallas_call x2, Pallas kernels, ray_sums(): pl.pallas_call(functools.partial(rays_kernel, dims, first, keep, extra, h...  8.45 us
    pallas_call x1, Pallas kernels, prepare_step(): pl.pallas_call(functools.partial(prepare_kernel, dims, rdev, total // 2,...  4.49 us
    ppermute x12, waiting for transfers between devices, spread(): return lax.ppermute(value, ('slab', 'ang'), pairs)  4.48 us
    pallas_call x2, Pallas kernels, residual_step(): pl.pallas_call(functools.partial(residual_kernel, dims, first, total // 2...  3.08 us
  transfers between devices with their start and end apart: 22, of which 8 were waited for; matrix products, arithmetic and copies ran while one was open for 1% of the time, Pallas kernels for 26%

profile of v9, /device:TPU:0, one launch (start us, length us, event | category | flops | bytes accessed | tf_op | source)
XLA Modules:
  0.0 71.2 jit_solution(17922781844420211996)
XLA Ops:
  0.6 0.0 copy-start.3
  0.6 0.0 copy-start.1
  0.7 0.0 copy-start
  0.7 4.6 %ray_sums_0_0.1 = (f32[8,4224]{1,0:T(8,128)}, f32[8,4224]{1,0:T(8,128)}, f32[8,4224]{1,0:T(8,128)}, f32[8,4224]{1,0:T(8,128)}, bf16[32,512]{1,0:T(8,128)(2,1)}) custom-call(s32[64]{0:T(128)} %refs_0_.3, s32[1,4]{1,0:T(1,128)} %refs_1_.3, s32[1,4]{1,0:T(1,128)} %refs_2_.1, f32[64,256]{1,0:T(8,128)} %refs_1_.4, f32[8,128,4096]{2,1,0:T(8,128)} %refs_1_.5), custom_call_target="tpu_custom_call" | custom-call | flops 67108864 | bytes 8388608 | tf_op jit(solution)/shard_map/ray_sums_0_0/pallas_call | solution.py:176
  5.3 0.0 copy-start.4
  5.3 3.0 %collective-permute-start = (f32[8,4224]{1,0:T(8,128)}, f32[8,4224]{1,0:T(8,128)S(1)}, u32[]{:S(2)}, u32[]{:S(2)}) collective-permute-start(f32[8,4224]{1,0:T(8,128)} %get-tuple-element.42), channel_id=1, source_target_pairs={{0,1},{1,0},{2,3},{3,2},{4,5},{5,4},{6,7},{7,6},{8,9},{9,8},{10,11... | collective-permute-start | bytes 405512 | tf_op jit(solution)/shard_map/ppermute | solution.py:503
  8.4 0.0 copy-done
  8.4 0.1 dynamic-slice_convert_fusion
  8.5 0.1 collective-permute-start.5
  8.5 0.5 collective-permute-start.1
  9.0 0.0 collective-permute-start.2
  9.0 0.0 copy-start.2
  9.0 0.8 %copy-done.2 = bf16[32,512]{1,0:T(8,128)(2,1)S(1)} copy-done((bf16[32,512]{1,0:T(8,128)(2,1)S(1)}, bf16[32,512]{1,0:T(8,128)(2,1)}, u32[]{:S(2)}) %copy-start.2) | copy-done | bytes 32792
  9.8 3.8 %ray_sums_1_0.1 = (f32[8,4096]{1,0:T(8,128)S(1)}, f32[8,4096]{1,0:T(8,128)S(1)}, f32[8,4096]{1,0:T(8,128)S(1)}, f32[8,4096]{1,0:T(8,128)S(1)}, f32[2,8,128,1024]{3,2,1,0:T(8,128)S(1)}) custom-call(bf16[32,512]{1,0:T(8,128)(2,1)S(1)} %copy-done.2, f32[8,128,4096]{2,1,0:T(8,128)} %refs_1_.5), custom_call_target="tpu_custom_call" | custom-call | flops 67108864 | bytes 8388608 | tf_op jit(solution)/shard_map/ray_sums_1_0/pallas_call | solution.py:176
  13.6 1.8 %collective-permute-start.6 = (f32[8,4096]{1,0:T(8,128)S(1)}, f32[8,4096]{1,0:T(8,128)S(1)}, u32[]{:S(2)}, u32[]{:S(2)}) collective-permute-start(f32[8,4096]{1,0:T(8,128)S(1)} %get-tuple-element.58), channel_id=1, source_target_pairs={{0,1},{1,0},{2,3},{3,2},{4,5},{5,4},{6,7},{7,6},{8,9},{9,8},{10,11... | collective-permute-start | bytes 393224 | tf_op jit(solution)/shard_map/ppermute | solution.py:503
  15.4 0.0 collective-permute-done
  15.4 0.2 collective-permute-start.7
  15.6 0.0 copy-done.4
  15.6 0.0 collective-permute-done.1
  15.6 0.3 collective-permute-start.8
  15.9 0.0 collective-permute-done.2
  16.0 1.7 %collective-permute-start.3 = (f32[2,8,4224]{2,1,0:T(8,128)S(1)}, f32[2,8,4224]{2,1,0:T(8,128)S(1)}, u32[]{:S(2)}, u32[]{:S(2)}) collective-permute-start(f32[2,8,4224]{2,1,0:T(8,128)S(1)} %pad_maximum_fusion.own_ref.refs_7_), channel_id=1, source_target_pairs={{0,4},{2,6},{4,0},{6,2},{8,12},{10,14},{12,8},{14,10},{16,20},{18,... | collective-permute-start | bytes 811016 | tf_op jit(solution)/shard_map/ppermute | solution.py:495
  17.7 2.3 %collective-permute-done.6 = f32[8,4096]{1,0:T(8,128)S(1)} collective-permute-done((f32[8,4096]{1,0:T(8,128)S(1)}, f32[8,4096]{1,0:T(8,128)S(1)}, u32[]{:S(2)}, u32[]{:S(2)}) %collective-permute-start.6) | collective-permute-done | bytes 131104 | tf_op jit(solution)/shard_map/ppermute | solution.py:503
  20.0 0.0 collective-permute-done.7
  20.0 1.8 %collective-permute-done.8 = f32[8,4096]{1,0:T(8,128)S(1)} collective-permute-done((f32[8,4096]{1,0:T(8,128)S(1)}, f32[8,4096]{1,0:T(8,128)S(1)}, u32[]{:S(2)}, u32[]{:S(2)}) %collective-permute-start.8) | collective-permute-done | bytes 131104 | tf_op jit(solution)/shard_map/ppermute | solution.py:503
  21.8 1.9 %collective-permute-start.9 = (f32[2,8,4096]{2,1,0:T(8,128)S(1)}, f32[2,8,4096]{2,1,0:T(8,128)S(1)}, u32[]{:S(2)}, u32[]{:S(2)}) collective-permute-start(f32[2,8,4096]{2,1,0:T(8,128)S(1)} %pad_maximum_fusion.1.refs_5_), channel_id=1, source_target_pairs={{0,4},{2,6},{4,0},{6,2},{8,12},{10,14},{12,8},{14,10},{16,20},{18,... | collective-permute-start | bytes 786440 | tf_op jit(solution)/shard_map/ppermute | solution.py:495
  23.7 0.9 %collective-permute-done.3.near_ref.refs_8_ = f32[2,8,4224]{2,1,0:T(8,128)S(1)} collective-permute-done((f32[2,8,4224]{2,1,0:T(8,128)S(1)}, f32[2,8,4224]{2,1,0:T(8,128)S(1)}, u32[]{:S(2)}, u32[]{:S(2)}) %collective-permute-start.3) | collective-permute-done | bytes 270368 | tf_op jit(solution)/shard_map/ppermute | solution.py:495
  24.6 1.7 %collective-permute-start.4 = (f32[2,8,4224]{2,1,0:T(8,128)S(1)}, f32[2,8,4224]{2,1,0:T(8,128)S(1)}, u32[]{:S(2)}, u32[]{:S(2)}) collective-permute-start(f32[2,8,4224]{2,1,0:T(8,128)S(1)} %collective-permute-done.3.near_ref.refs_8_), channel_id=1, source_target_pairs={{0,8},{2,10},{4,28},{6,30},{8,16},{10,18},{12,4},{14,6},{16,24},{1... | collective-permute-start | bytes 811016 | tf_op jit(solution)/shard_map/ppermute | solution.py:495
  26.4 0.0 copy-done.3
  26.4 0.0 copy-done.1
  26.4 4.5 %prepare.1 = (f32[2,8,128,1024]{3,2,1,0:T(8,128)S(1)}, bf16[4,256,128]{2,1,0:T(8,128)(2,1)S(1)}, bf16[256,128]{1,0:T(8,128)(2,1)S(1)}, bf16[256,128]{1,0:T(8,128...) custom-call(s32[64]{0:T(128)S(1)} %copy-done.3, ...), custom_call_target="tpu_custom_call" | custom-call | bytes 8388608 | tf_op jit(solution)/shard_map/prepare/pallas_call | solution.py:261
  30.9 0.0 collective-permute-done.9.refs_6_
  30.9 1.7 %collective-permute-start.10 = (f32[2,8,4096]{2,1,0:T(8,128)S(1)}, f32[2,8,4096]{2,1,0:T(8,128)S(1)}, u32[]{:S(2)}, u32[]{:S(2)}) collective-permute-start(f32[2,8,4096]{2,1,0:T(8,128)S(1)} %collective-permute-done.9.refs_6_), channel_id=1, source_target_pairs={{0,8},{2,10},{4,0},{6,2},{8,16},{10,18},{12,4},{14,6},{16,24},{18,... | collective-permute-start | bytes 786440 | tf_op jit(solution)/shard_map/ppermute | solution.py:495
  32.6 1.8 %collective-permute-done.4.refs_9_ = f32[2,8,4224]{2,1,0:T(8,128)S(1)} collective-permute-done((f32[2,8,4224]{2,1,0:T(8,128)S(1)}, f32[2,8,4224]{2,1,0:T(8,128)S(1)}, u32[]{:S(2)}, u32[]{:S(2)}) %collective-permute-start.4) | collective-permute-done | bytes 270368 | tf_op jit(solution)/shard_map/ppermute | solution.py:495
  34.4 0.0 collective-permute-done.5.refs_11_.refs_9_
  34.4 1.9 %residual_0.1 = (f32[4,32,1024]{2,1,0:T(8,128)S(1)}, f32[4,32,1024]{2,1,0:T(8,128)S(1)}, f32[2,32,1024]{2,1,0:T(8,128)S(1)}, bf16[256,192]{1,0:T(8,128)(2,1)S(1)...) custom-call(s32[64]{0:T(128)S(1)} %copy-done.3, ...), custom_call_target="tpu_custom_call" | custom-call | flops 603979776 | bytes 3670016 | tf_op jit(solution)/shard_map/residual_0/pallas_call | solution.py:365
  36.2 0.8 %collective-permute-start.16 = (f32[2,32,1024]{2,1,0:T(8,128)S(1)}, f32[2,32,1024]{2,1,0:T(8,128)S(1)}, u32[]{:S(2)}, u32[]{:S(2)}) collective-permute-start(f32[2,32,1024]{2,1,0:T(8,128)S(1)} %get-tuple-element.75), channel_id=1, source_target_pairs={{0,4},{2,6},{4,12},{6,14},{8,0},{10,2},{12,20},{14,22},{16,8},{18,... | collective-permute-start | bytes 786440 | tf_op jit(solution)/shard_map/ppermute | solution.py:495
  37.0 2.9 %collective-permute-done.10.refs_7_ = f32[2,8,4096]{2,1,0:T(8,128)S(1)} collective-permute-done((f32[2,8,4096]{2,1,0:T(8,128)S(1)}, f32[2,8,4096]{2,1,0:T(8,128)S(1)}, u32[]{:S(2)}, u32[]{:S(2)}) %collective-permute-start.10) | collective-permute-done | bytes 262176 | tf_op jit(solution)/shard_map/ppermute | solution.py:495
  40.0 1.2 %residual_1.1 = (f32[4,32,2048]{2,1,0:T(8,128)S(1)}, f32[4,32,2048]{2,1,0:T(8,128)S(1)}, f32[2,32,1024]{2,1,0:T(8,128)S(1)}, f32[2,32,1024]{2,1,0:T(8,128)S(1)}, f32[2,32,1024]{2,1,0:T(8,128)S(1)}) custom-call(bf16[256,192]{1,0:T(8,128)(2,1)S(1)} %get-tuple-element.51.refs_0_, bf16[256,192]{1,0:T(8,128)(2,1)S(1)} %get-tuple-element.52.refs_1_, ...), custom_call_target="tpu_custom_call" | custom-call | flops 603979776 | bytes 3670016 | tf_op jit(solution)/shard_map/residual_1/pallas_call | solution.py:365
  41.2 0.1 collective-permute-start.21
  41.3 2.7 %collective-permute-start.11 = (f32[2,32,1024]{2,1,0:T(8,128)S(1)}, f32[2,32,1024]{2,1,0:T(8,128)S(1)}, u32[]{:S(2)}, u32[]{:S(2)}) collective-permute-start(f32[2,32,1024]{2,1,0:T(8,128)S(1)} %get-tuple-element.71), channel_id=1, source_target_pairs={{0,24},{2,26},{4,12},{6,14},{8,0},{10,2},{12,20},{14,22},{16,8},{1... | collective-permute-start | bytes 786440 | tf_op jit(solution)/shard_map/ppermute | solution.py:495
  44.0 0.4 back_0.1
  44.4 0.0 collective-permute-done.16
  44.4 0.1 collective-permute-start.17
  44.5 5.6 %collective-permute-done.11 = f32[2,32,1024]{2,1,0:T(8,128)S(1)} collective-permute-done((f32[2,32,1024]{2,1,0:T(8,128)S(1)}, f32[2,32,1024]{2,1,0:T(8,128)S(1)}, u32[]{:S(2)}, u32[]{:S(2)}) %collective-permute-start.11) | collective-permute-done | bytes 262176 | tf_op jit(solution)/shard_map/ppermute | solution.py:495
  50.2 3.5 %collective-permute-start.12 = (f32[2,32,1024]{2,1,0:T(8,128)S(1)}, f32[2,32,1024]{2,1,0:T(8,128)S(1)}, u32[]{:S(2)}, u32[]{:S(2)}) collective-permute-start(f32[2,32,1024]{2,1,0:T(8,128)S(1)} %add.48), channel_id=1, source_target_pairs={{0,4},{2,6},{4,0},{6,2},{8,12},{10,14},{12,8},{14,10},{16,20},{18,... | collective-permute-start | bytes 786440 | tf_op jit(solution)/shard_map/ppermute | solution.py:495
  53.6 0.0 collective-permute-done.17
  53.7 0.6 collective-permute-start.18
  54.2 1.1 %collective-permute-start.19 = (f32[32,1024]{1,0:T(8,128)S(1)}, f32[32,1024]{1,0:T(8,128)S(1)}, u32[]{:S(2)}, u32[]{:S(2)}) collective-permute-start(f32[32,1024]{1,0:T(8,128)S(1)} %get-tuple-element.81), channel_id=1, source_target_pairs={{0,2},{1,3},{2,0},{3,1},{4,6},{5,7},{6,4},{7,5},{8,10},{9,11},{10,... | collective-permute-start | bytes 393224 | tf_op jit(solution)/shard_map/ppermute | solution.py:503
  55.4 0.5 collective-permute-start.20
  55.9 3.9 %collective-permute-done.12 = f32[2,32,1024]{2,1,0:T(8,128)S(1)} collective-permute-done((f32[2,32,1024]{2,1,0:T(8,128)S(1)}, f32[2,32,1024]{2,1,0:T(8,128)S(1)}, u32[]{:S(2)}, u32[]{:S(2)}) %collective-permute-start.12) | collective-permute-done | bytes 262176 | tf_op jit(solution)/shard_map/ppermute | solution.py:495
  59.8 1.6 %collective-permute-start.15 = (f32[32,1024]{1,0:T(8,128)S(1)}, f32[32,1024]{1,0:T(8,128)S(1)}, u32[]{:S(2)}, u32[]{:S(2)}) collective-permute-start(f32[32,1024]{1,0:T(8,128)S(1)} %get-tuple-element.82.refs_2_), channel_id=1, source_target_pairs={{0,1},{1,0},{2,3},{3,2},{4,5},{5,4},{6,7},{7,6},{8,9},{9,8},{10,11... | collective-permute-start | bytes 393224 | tf_op jit(solution)/shard_map/ppermute | solution.py:503
  61.4 0.0 collective-permute-done.18.refs_1_
  61.4 0.0 collective-permute-start.13
  61.4 0.0 collective-permute-done.19.refs_2_
  61.4 0.6 collective-permute-start.14
  62.0 0.4 collective-permute-done.20.refs_3_
  62.4 3.6 %update_0_0.1.refs_4_ = f32[8,128,4096]{2,1,0:T(8,128)} custom-call(bf16[4,256,128]{2,1,0:T(8,128)(2,1)S(1)} %get-tuple-element.45.refs_0_, f32[32,1024]{1,0:T(8,128)S(1)} %collective-permute-done.18.refs_1_, f32[32,1024]{1,0:T(8,128)S(1)} %collective-permute-done.19.refs_2_, f32[32,1024]{1,0:T(8,128)S(1)} %collective-permute-done.20.refs_3_, ...), custom_call_target="tpu_custom_call" | custom-call | flops 201326592 | bytes 8388608 | tf_op jit(solution)/shard_map/update_0_0/pallas_call | solution.py:469
  66.1 0.0 collective-permute-done.15.refs_1_
  66.1 0.0 collective-permute-done.21.refs_6_
  66.1 2.7 %update_1_0.1 = (f32[8,128,4096]{2,1,0:T(8,128)}, f32[4,32,4096]{2,1,0:T(8,128)}) custom-call(bf16[4,256,128]{2,1,0:T(8,128)(2,1)S(1)} %get-tuple-element.45.refs_0_, f32[32,1024]{1,0:T(8,128)S(1)} %collective-permute-done.15.refs_1_, f32[32,1024]{1,0:T(8,128)S(1)} %get-tuple-element.82.refs_2_, ...), custom_call_target="tpu_custom_call", output_to_operand_aliasing={{0}: (4, {})} | custom-call | flops 100663296 | bytes 4194304 | tf_op jit(solution)/shard_map/update_1_0/pallas_call | solution.py:469
  68.8 0.0 collective-permute-done.13.refs_1_
  68.9 0.0 collective-permute-done.14.refs_2_
  68.9 2.3 %update_1_1.1 = f32[8,128,4096]{2,1,0:T(8,128)} custom-call(bf16[4,256,128]{2,1,0:T(8,128)(2,1)S(1)} %get-tuple-element.45.refs_0_, f32[32,1024]{1,0:T(8,128)S(1)} %collective-permute-done.13.refs_1_, f32[32,1024]{1,0:T(8,128)S(1)} %collective-permute-done.14.refs_2_, ...), custom_call_target="tpu_custom_call", output_to_operand_aliasing={{}: (4, {})} | custom-call | flops 100663296 | bytes 4194304 | tf_op jit(solution)/shard_map/update_1_1/pallas_call | solution.py:469
  (9 shorter events, 0.3 us)
Async XLA Ops:
  0.6 25.7 %copy-start.3 = (s32[64]{0:T(128)S(1)}, s32[64]{0:T(128)}, u32[]{:S(2)}) copy-start(s32[64]{0:T(128)} %refs_0_.3) | copy-start | bytes 772
  0.6 25.7 %copy-start.1 = (f32[64,256]{1,0:T(8,128)S(1)}, f32[64,256]{1,0:T(8,128)}, u32[]{:S(2)}) copy-start(f32[64,256]{1,0:T(8,128)} %refs_1_.4) | copy-start | bytes 196612
  0.7 7.7 %copy-start = (bf16[4,32,4096]{2,1,0:T(8,128)(2,1)S(1)}, bf16[4,32,4096]{2,1,0:T(8,128)(2,1)}, u32[]{:S(2)}) copy-start(bf16[4,32,4096]{2,1,0:T(8,128)(2,1)} %refs_8_.1) | copy-start | bytes 3145732
  5.3 10.2 %copy-start.4 = (f32[8,4224]{1,0:T(8,128)S(1)}, f32[8,4224]{1,0:T(8,128)}, u32[]{:S(2)}) copy-start(f32[8,4224]{1,0:T(8,128)} %get-tuple-element.41) | copy-start | bytes 405508
  5.3 10.1 %collective-permute-start = (f32[8,4224]{1,0:T(8,128)}, f32[8,4224]{1,0:T(8,128)S(1)}, u32[]{:S(2)}, u32[]{:S(2)}) collective-permute-start(f32[8,4224]{1,0:T(8,128)} %get-tuple-element.42), channel_id=1, source_target_pairs={{0,1},{1,0},{2,3},{3,2},{4,5},{5,4},{6,7},{7,6},{8,9},{9,8},{10,11... | collective-permute-start | bytes 405512 | tf_op jit(solution)/shard_map/ppermute | solution.py:503
  8.5 25.9 %collective-permute-start.5 = (f32[4,32,2048]{2,1,0:T(8,128)S(1)}, f32[4,32,2048]{2,1,0:T(8,128)S(1)}, u32[]{:S(2)}, u32[]{:S(2)}) collective-permute-start(f32[4,32,2048]{2,1,0:T(8,128)S(1)} %dynamic-slice_convert_fusion), channel_id=1, source_target_pairs={{0,2},{2,0},{4,6},{6,4},{8,10},{10,8},{12,14},{14,12},{16,18},{18,... | collective-permute-start | bytes 3145736 | tf_op jit(solution)/shard_map/ppermute | solution.py:495
  8.5 7.0 %collective-permute-start.1 = (f32[8,4224]{1,0:T(8,128)}, f32[8,4224]{1,0:T(8,128)S(1)}, u32[]{:S(2)}, u32[]{:S(2)}) collective-permute-start(f32[8,4224]{1,0:T(8,128)} %get-tuple-element.43), channel_id=1, source_target_pairs={{0,2},{1,3},{2,0},{3,1},{4,6},{5,7},{6,4},{7,5},{8,10},{9,11},{10,... | collective-permute-start | bytes 405512 | tf_op jit(solution)/shard_map/ppermute | solution.py:503
  9.0 6.9 %collective-permute-start.2 = (f32[8,4224]{1,0:T(8,128)}, f32[8,4224]{1,0:T(8,128)S(1)}, u32[]{:S(2)}, u32[]{:S(2)}) collective-permute-start(f32[8,4224]{1,0:T(8,128)} %get-tuple-element.44), channel_id=1, source_target_pairs={{0,3},{1,2},{2,1},{3,0},{4,7},{5,6},{6,5},{7,4},{8,11},{9,10},{10,... | collective-permute-start | bytes 405512 | tf_op jit(solution)/shard_map/ppermute | solution.py:503
  9.0 0.8 %copy-start.2 = (bf16[32,512]{1,0:T(8,128)(2,1)S(1)}, bf16[32,512]{1,0:T(8,128)(2,1)}, u32[]{:S(2)}) copy-start(bf16[32,512]{1,0:T(8,128)(2,1)} %get-tuple-element.56.refs_0_) | copy-start | bytes 98308
  13.6 6.4 %collective-permute-start.6 = (f32[8,4096]{1,0:T(8,128)S(1)}, f32[8,4096]{1,0:T(8,128)S(1)}, u32[]{:S(2)}, u32[]{:S(2)}) collective-permute-start(f32[8,4096]{1,0:T(8,128)S(1)} %get-tuple-element.58), channel_id=1, source_target_pairs={{0,1},{1,0},{2,3},{3,2},{4,5},{5,4},{6,7},{7,6},{8,9},{9,8},{10,11... | collective-permute-start | bytes 393224 | tf_op jit(solution)/shard_map/ppermute | solution.py:503
  15.4 4.6 %collective-permute-start.7 = (f32[8,4096]{1,0:T(8,128)S(1)}, f32[8,4096]{1,0:T(8,128)S(1)}, u32[]{:S(2)}, u32[]{:S(2)}) collective-permute-start(f32[8,4096]{1,0:T(8,128)S(1)} %get-tuple-element.59), channel_id=1, source_target_pairs={{0,2},{1,3},{2,0},{3,1},{4,6},{5,7},{6,4},{7,5},{8,10},{9,11},{10,... | collective-permute-start | bytes 393224 | tf_op jit(solution)/shard_map/ppermute | solution.py:503
  15.6 6.2 %collective-permute-start.8 = (f32[8,4096]{1,0:T(8,128)S(1)}, f32[8,4096]{1,0:T(8,128)S(1)}, u32[]{:S(2)}, u32[]{:S(2)}) collective-permute-start(f32[8,4096]{1,0:T(8,128)S(1)} %get-tuple-element.60), channel_id=1, source_target_pairs={{0,3},{1,2},{2,1},{3,0},{4,7},{5,6},{6,5},{7,4},{8,11},{9,10},{10,... | collective-permute-start | bytes 393224 | tf_op jit(solution)/shard_map/ppermute | solution.py:503
  16.0 8.7 %collective-permute-start.3 = (f32[2,8,4224]{2,1,0:T(8,128)S(1)}, f32[2,8,4224]{2,1,0:T(8,128)S(1)}, u32[]{:S(2)}, u32[]{:S(2)}) collective-permute-start(f32[2,8,4224]{2,1,0:T(8,128)S(1)} %pad_maximum_fusion.own_ref.refs_7_), channel_id=1, source_target_pairs={{0,4},{2,6},{4,0},{6,2},{8,12},{10,14},{12,8},{14,10},{16,20},{18,... | collective-permute-start | bytes 811016 | tf_op jit(solution)/shard_map/ppermute | solution.py:495
  21.8 9.0 %collective-permute-start.9 = (f32[2,8,4096]{2,1,0:T(8,128)S(1)}, f32[2,8,4096]{2,1,0:T(8,128)S(1)}, u32[]{:S(2)}, u32[]{:S(2)}) collective-permute-start(f32[2,8,4096]{2,1,0:T(8,128)S(1)} %pad_maximum_fusion.1.refs_5_), channel_id=1, source_target_pairs={{0,4},{2,6},{4,0},{6,2},{8,12},{10,14},{12,8},{14,10},{16,20},{18,... | collective-permute-start | bytes 786440 | tf_op jit(solution)/shard_map/ppermute | solution.py:495
  24.6 9.7 %collective-permute-start.4 = (f32[2,8,4224]{2,1,0:T(8,128)S(1)}, f32[2,8,4224]{2,1,0:T(8,128)S(1)}, u32[]{:S(2)}, u32[]{:S(2)}) collective-permute-start(f32[2,8,4224]{2,1,0:T(8,128)S(1)} %collective-permute-done.3.near_ref.refs_8_), channel_id=1, source_target_pairs={{0,8},{2,10},{4,28},{6,30},{8,16},{10,18},{12,4},{14,6},{16,24},{1... | collective-permute-start | bytes 811016 | tf_op jit(solution)/shard_map/ppermute | solution.py:495
  30.9 9.1 %collective-permute-start.10 = (f32[2,8,4096]{2,1,0:T(8,128)S(1)}, f32[2,8,4096]{2,1,0:T(8,128)S(1)}, u32[]{:S(2)}, u32[]{:S(2)}) collective-permute-start(f32[2,8,4096]{2,1,0:T(8,128)S(1)} %collective-permute-done.9.refs_6_), channel_id=1, source_target_pairs={{0,8},{2,10},{4,0},{6,2},{8,16},{10,18},{12,4},{14,6},{16,24},{18,... | collective-permute-start | bytes 786440 | tf_op jit(solution)/shard_map/ppermute | solution.py:495
  36.2 8.2 %collective-permute-start.16 = (f32[2,32,1024]{2,1,0:T(8,128)S(1)}, f32[2,32,1024]{2,1,0:T(8,128)S(1)}, u32[]{:S(2)}, u32[]{:S(2)}) collective-permute-start(f32[2,32,1024]{2,1,0:T(8,128)S(1)} %get-tuple-element.75), channel_id=1, source_target_pairs={{0,4},{2,6},{4,12},{6,14},{8,0},{10,2},{12,20},{14,22},{16,8},{18,... | collective-permute-start | bytes 786440 | tf_op jit(solution)/shard_map/ppermute | solution.py:495
  41.2 24.9 %collective-permute-start.21 = (f32[4,32,2048]{2,1,0:T(8,128)S(1)}, f32[4,32,2048]{2,1,0:T(8,128)S(1)}, u32[]{:S(2)}, u32[]{:S(2)}) collective-permute-start(f32[4,32,2048]{2,1,0:T(8,128)S(1)} %get-tuple-element.77), channel_id=1, source_target_pairs={{0,2},{2,0},{4,6},{6,4},{8,10},{10,8},{12,14},{14,12},{16,18},{18,... | collective-permute-start | bytes 3145736 | tf_op jit(solution)/shard_map/ppermute | solution.py:495
  41.3 8.9 %collective-permute-start.11 = (f32[2,32,1024]{2,1,0:T(8,128)S(1)}, f32[2,32,1024]{2,1,0:T(8,128)S(1)}, u32[]{:S(2)}, u32[]{:S(2)}) collective-permute-start(f32[2,32,1024]{2,1,0:T(8,128)S(1)} %get-tuple-element.71), channel_id=1, source_target_pairs={{0,24},{2,26},{4,12},{6,14},{8,0},{10,2},{12,20},{14,22},{16,8},{1... | collective-permute-start | bytes 786440 | tf_op jit(solution)/shard_map/ppermute | solution.py:495
  44.4 9.2 %collective-permute-start.17 = (f32[2,32,1024]{2,1,0:T(8,128)S(1)}, f32[2,32,1024]{2,1,0:T(8,128)S(1)}, u32[]{:S(2)}, u32[]{:S(2)}) collective-permute-start(f32[2,32,1024]{2,1,0:T(8,128)S(1)} %add.53), channel_id=1, source_target_pairs={{0,4},{2,6},{4,0},{6,2},{8,12},{10,14},{12,8},{14,10},{16,20},{18,... | collective-permute-start | bytes 786440 | tf_op jit(solution)/shard_map/ppermute | solution.py:495
  50.2 9.6 %collective-permute-start.12 = (f32[2,32,1024]{2,1,0:T(8,128)S(1)}, f32[2,32,1024]{2,1,0:T(8,128)S(1)}, u32[]{:S(2)}, u32[]{:S(2)}) collective-permute-start(f32[2,32,1024]{2,1,0:T(8,128)S(1)} %add.48), channel_id=1, source_target_pairs={{0,4},{2,6},{4,0},{6,2},{8,12},{10,14},{12,8},{14,10},{16,20},{18,... | collective-permute-start | bytes 786440 | tf_op jit(solution)/shard_map/ppermute | solution.py:495
  53.7 7.7 %collective-permute-start.18 = (f32[32,1024]{1,0:T(8,128)S(1)}, f32[32,1024]{1,0:T(8,128)S(1)}, u32[]{:S(2)}, u32[]{:S(2)}) collective-permute-start(f32[32,1024]{1,0:T(8,128)S(1)} %get-tuple-element.81), channel_id=1, source_target_pairs={{0,3},{1,2},{2,1},{3,0},{4,7},{5,6},{6,5},{7,4},{8,11},{9,10},{10,... | collective-permute-start | bytes 393224 | tf_op jit(solution)/shard_map/ppermute | solution.py:503
  54.2 7.1 %collective-permute-start.19 = (f32[32,1024]{1,0:T(8,128)S(1)}, f32[32,1024]{1,0:T(8,128)S(1)}, u32[]{:S(2)}, u32[]{:S(2)}) collective-permute-start(f32[32,1024]{1,0:T(8,128)S(1)} %get-tuple-element.81), channel_id=1, source_target_pairs={{0,2},{1,3},{2,0},{3,1},{4,6},{5,7},{6,4},{7,5},{8,10},{9,11},{10,... | collective-permute-start | bytes 393224 | tf_op jit(solution)/shard_map/ppermute | solution.py:503
  55.4 7.0 %collective-permute-start.20 = (f32[32,1024]{1,0:T(8,128)S(1)}, f32[32,1024]{1,0:T(8,128)S(1)}, u32[]{:S(2)}, u32[]{:S(2)}) collective-permute-start(f32[32,1024]{1,0:T(8,128)S(1)} %get-tuple-element.80.refs_4_), channel_id=1, source_target_pairs={{0,1},{1,0},{2,3},{3,2},{4,5},{5,4},{6,7},{7,6},{8,9},{9,8},{10,11... | collective-permute-start | bytes 393224 | tf_op jit(solution)/shard_map/ppermute | solution.py:503
  59.8 6.3 %collective-permute-start.15 = (f32[32,1024]{1,0:T(8,128)S(1)}, f32[32,1024]{1,0:T(8,128)S(1)}, u32[]{:S(2)}, u32[]{:S(2)}) collective-permute-start(f32[32,1024]{1,0:T(8,128)S(1)} %get-tuple-element.82.refs_2_), channel_id=1, source_target_pairs={{0,1},{1,0},{2,3},{3,2},{4,5},{5,4},{6,7},{7,6},{8,9},{9,8},{10,11... | collective-permute-start | bytes 393224 | tf_op jit(solution)/shard_map/ppermute | solution.py:503
  61.4 7.5 %collective-permute-start.13 = (f32[32,1024]{1,0:T(8,128)S(1)}, f32[32,1024]{1,0:T(8,128)S(1)}, u32[]{:S(2)}, u32[]{:S(2)}) collective-permute-start(f32[32,1024]{1,0:T(8,128)S(1)} %get-tuple-element.83), channel_id=1, source_target_pairs={{0,3},{1,2},{2,1},{3,0},{4,7},{5,6},{6,5},{7,4},{8,11},{9,10},{10,... | collective-permute-start | bytes 393224 | tf_op jit(solution)/shard_map/ppermute | solution.py:503
  61.4 7.5 %collective-permute-start.14 = (f32[32,1024]{1,0:T(8,128)S(1)}, f32[32,1024]{1,0:T(8,128)S(1)}, u32[]{:S(2)}, u32[]{:S(2)}) collective-permute-start(f32[32,1024]{1,0:T(8,128)S(1)} %get-tuple-element.83), channel_id=1, source_target_pairs={{0,2},{1,3},{2,0},{3,1},{4,6},{5,7},{6,4},{7,5},{8,10},{9,11},{10,... | collective-permute-start | bytes 393224 | tf_op jit(solution)/shard_map/ppermute | solution.py:503

commit v10 on v6

--- a/solution.py
+++ b/solution.py
@@ -261,7 +261,7 @@
             pltpu.SemaphoreType.DMA((2, zdev // zb)),
             pltpu.VMEM((groups * SUBLANES, table.shape[1]), F32),
         ],
-        compiler_params=pltpu.CompilerParams(vmem_limit_bytes=40 * MIB),
+        compiler_params=pltpu.CompilerParams(vmem_limit_bytes=32 * MIB),
         cost_estimate=pl.CostEstimate(flops=0, bytes_accessed=8 * zdev * cells * width, transcendentals=0),
         name="prepare",
     )(order, table, own, after, volume)
@@ -494,11 +494,6 @@
             parts, _ = lax.optimization_barrier((parts, sums[-1][0]))
         own = jnp.stack([sum(parts[:groups]), sum(parts[groups:])])
         near = along(own, facing)
-        if c == 0:
-            first_columns, update_left = prepare_step(dims, rdev, widths[0], order, table, own, near, volume)
-            kept[0] = [(h, first_columns) for h in range(2)]
-        if c == 1:
-            near, first_columns = lax.optimization_barrier((near, first_columns))
         far = along(near, beyond(c))
         sums.append((own, near, far))
     pieces, given, mats = [], [], None
@@ -508,7 +503,15 @@
         )
         pieces = [mine, sent]
         mats = rest if c == 0 else mats
-        near = near + along(far, back_from_beyond(c))
+        returned = along(far, back_from_beyond(c))
+        if c == 1:
+            first_columns, update_left = prepare_step(
+                dims, rdev, widths[0], order, table, sums[0][0], near_before, volume
+            )
+            returned, first_columns = lax.optimization_barrier((returned, first_columns))
+            kept[0] = [(h, first_columns) for h in range(2)]
+        near = near + returned
+        near_before = near
         arrived = along(near, facing)
         halves = [own[i] + arrived[i] for i in range(2)]
         given.append([spread(halves[h], h, d) for h in range(2) for d in range(groups)])

time: 71 us -> 74.1 us (1.044)
  local copies, waits for them, and re-layouts: 0.78 us -> 4.37 us
  waiting for transfers between devices: 19.8 us -> 19 us
    unnamed x10 -> x16, local copies, waits for them, and re-layouts: 0.78 us -> 4.37 us
  transfers between devices with their start and end apart: 22 -> 22, of which waited for: 9 -> 10; matrix products, arithmetic and copies ran while one was open for 0% -> 0% of each run, Pallas kernels for 25% -> 25%
where the time goes in v10:
time: 74.1 us; the launch traced here: 73.9 us
  Pallas kernels  25.1 us (34%)
  starting transfers between devices  24.2 us (33%)
  waiting for transfers between devices  19 us (26%)
  local copies, waits for them, and re-layouts  4.37 us (6%)
  between operations  0.86 us (1%)
    ppermute x10, waiting for transfers between devices, along(): return lax.ppermute(value, 'slab', pairs)  15 us
    ppermute x10, starting transfers between devices, along(): return lax.ppermute(value, 'slab', pairs)  14.4 us
    ppermute x12, starting transfers between devices, spread(): return lax.ppermute(value, ('slab', 'ang'), pairs)  9.86 us
    pallas_call x3, Pallas kernels, update_step(): pl.pallas_call(functools.partial(update_kernel, dims, first, halves, tota...  9.23 us
    pallas_call x2, Pallas kernels, ray_sums(): pl.pallas_call(functools.partial(rays_kernel, dims, first, keep, extra, h...  8.47 us
    unnamed x16, local copies, waits for them, and re-layouts  4.37 us
    pallas_call x1, Pallas kernels, prepare_step(): pl.pallas_call(functools.partial(prepare_kernel, dims, rdev, total // 2,...  4.09 us
    ppermute x12, waiting for transfers between devices, spread(): return lax.ppermute(value, ('slab', 'ang'), pairs)  3.97 us
  transfers between devices with their start and end apart: 22, of which 10 were waited for; matrix products, arithmetic and copies ran while one was open for 0% of the time, Pallas kernels for 25%

profile of v10, /device:TPU:0, one launch (start us, length us, event | category | flops | bytes accessed | tf_op | source)
XLA Modules:
  0.0 73.9 jit_solution(774187062326818947)
XLA Ops:
  0.6 0.0 copy-start.4
  0.6 0.0 copy-start.2
  0.7 0.0 copy-start.1
  0.7 4.6 %ray_sums_0_0.1 = (f32[8,4224]{1,0:T(8,128)}, f32[8,4224]{1,0:T(8,128)}, f32[8,4224]{1,0:T(8,128)}, f32[8,4224]{1,0:T(8,128)}, bf16[32,512]{1,0:T(8,128)(2,1)}) custom-call(s32[64]{0:T(128)} %order_ref.1, s32[1,4]{1,0:T(1,128)} %refs_1_.3, s32[1,4]{1,0:T(1,128)} %refs_2_.1, f32[64,256]{1,0:T(8,128)} %table_ref.1, f32[8,128,4096]{2,1,0:T(8,128)} %refs_1_.5), custom_call_target="tpu_custom_call" | custom-call | flops 67108864 | bytes 8388608 | tf_op jit(solution)/shard_map/ray_sums_0_0/pallas_call | solution.py:176
  5.3 3.0 %collective-permute-start = (f32[8,4224]{1,0:T(8,128)}, f32[8,4224]{1,0:T(8,128)S(1)}, u32[]{:S(2)}, u32[]{:S(2)}) collective-permute-start(f32[8,4224]{1,0:T(8,128)} %get-tuple-element.38), channel_id=1, source_target_pairs={{0,1},{1,0},{2,3},{3,2},{4,5},{5,4},{6,7},{7,6},{8,9},{9,8},{10,11... | collective-permute-start | bytes 405512 | tf_op jit(solution)/shard_map/ppermute | solution.py:456
  8.3 0.0 collective-permute-start.1
  8.3 0.2 collective-permute-start.2
  8.6 0.8 %copy-done.3 = bf16[32,512]{1,0:T(8,128)(2,1)S(1)} copy-done((bf16[32,512]{1,0:T(8,128)(2,1)S(1)}, bf16[32,512]{1,0:T(8,128)(2,1)}, u32[]{:S(2)}) %copy-start.3) | copy-done | bytes 32792
  9.3 3.8 %ray_sums_1_0.1 = (f32[8,4096]{1,0:T(8,128)S(1)}, f32[8,4096]{1,0:T(8,128)S(1)}, f32[8,4096]{1,0:T(8,128)S(1)}, f32[8,4096]{1,0:T(8,128)S(1)}, f32[2,8,128,1024]{3,2,1,0:T(8,128)S(1)}) custom-call(bf16[32,512]{1,0:T(8,128)(2,1)S(1)} %copy-done.3, f32[8,128,4096]{2,1,0:T(8,128)} %refs_1_.5), custom_call_target="tpu_custom_call" | custom-call | flops 67108864 | bytes 8388608 | tf_op jit(solution)/shard_map/ray_sums_1_0/pallas_call | solution.py:176
  13.1 0.0 copy-start
  13.2 3.3 %copy-done = f32[2,8,128,1024]{3,2,1,0:T(8,128)} copy-done((f32[2,8,128,1024]{3,2,1,0:T(8,128)}, f32[2,8,128,1024]{3,2,1,0:T(8,128)S(1)}, u32[]{:S(2)}) %copy-start) | copy-done | bytes 8388632
  16.4 1.9 %collective-permute-start.7 = (f32[8,4096]{1,0:T(8,128)S(1)}, f32[8,4096]{1,0:T(8,128)S(1)}, u32[]{:S(2)}, u32[]{:S(2)}) collective-permute-start(f32[8,4096]{1,0:T(8,128)S(1)} %get-tuple-element.51), channel_id=1, source_target_pairs={{0,1},{1,0},{2,3},{3,2},{4,5},{5,4},{6,7},{7,6},{8,9},{9,8},{10,11... | collective-permute-start | bytes 393224 | tf_op jit(solution)/shard_map/ppermute | solution.py:456
  18.4 0.0 collective-permute-start.8
  18.4 0.1 dynamic-slice_convert_fusion
  18.5 0.0 collective-permute-done
  18.5 0.3 collective-permute-start.9
  18.8 0.0 copy-done.5
  18.8 0.0 collective-permute-done.1
  18.8 0.4 collective-permute-start.5
  19.2 0.0 collective-permute-done.2
  19.2 1.7 %collective-permute-start.3 = (f32[2,8,4224]{2,1,0:T(8,128)S(1)}, f32[2,8,4224]{2,1,0:T(8,128)S(1)}, u32[]{:S(2)}, u32[]{:S(2)}) collective-permute-start(f32[2,8,4224]{2,1,0:T(8,128)S(1)} %pad_maximum_fusion.refs_2_.foot_ref), channel_id=1, source_target_pairs={{0,4},{2,6},{4,0},{6,2},{8,12},{10,14},{12,8},{14,10},{16,20},{18,... | collective-permute-start | bytes 811016 | tf_op jit(solution)/shard_map/ppermute | solution.py:448
  20.9 1.8 %collective-permute-done.7 = f32[8,4096]{1,0:T(8,128)S(1)} collective-permute-done((f32[8,4096]{1,0:T(8,128)S(1)}, f32[8,4096]{1,0:T(8,128)S(1)}, u32[]{:S(2)}, u32[]{:S(2)}) %collective-permute-start.7) | collective-permute-done | bytes 131104 | tf_op jit(solution)/shard_map/ppermute | solution.py:456
  22.7 0.0 collective-permute-done.8
  22.7 1.7 %collective-permute-done.9 = f32[8,4096]{1,0:T(8,128)S(1)} collective-permute-done((f32[8,4096]{1,0:T(8,128)S(1)}, f32[8,4096]{1,0:T(8,128)S(1)}, u32[]{:S(2)}, u32[]{:S(2)}) %collective-permute-start.9) | collective-permute-done | bytes 131104 | tf_op jit(solution)/shard_map/ppermute | solution.py:456
  24.5 1.5 %collective-permute-start.10 = (f32[2,8,4096]{2,1,0:T(8,128)S(1)}, f32[2,8,4096]{2,1,0:T(8,128)S(1)}, u32[]{:S(2)}, u32[]{:S(2)}) collective-permute-start(f32[2,8,4096]{2,1,0:T(8,128)S(1)} %pad_maximum_fusion.1.refs_5_), channel_id=1, source_target_pairs={{0,4},{2,6},{4,0},{6,2},{8,12},{10,14},{12,8},{14,10},{16,20},{18,... | collective-permute-start | bytes 786440 | tf_op jit(solution)/shard_map/ppermute | solution.py:448
  26.0 2.2 %collective-permute-done.3.refs_3_ = f32[2,8,4224]{2,1,0:T(8,128)S(1)} collective-permute-done((f32[2,8,4224]{2,1,0:T(8,128)S(1)}, f32[2,8,4224]{2,1,0:T(8,128)S(1)}, u32[]{:S(2)}, u32[]{:S(2)}) %collective-permute-start.3) | collective-permute-done | bytes 270368 | tf_op jit(solution)/shard_map/ppermute | solution.py:448
  28.2 2.0 %collective-permute-start.4 = (f32[2,8,4224]{2,1,0:T(8,128)S(1)}, f32[2,8,4224]{2,1,0:T(8,128)S(1)}, u32[]{:S(2)}, u32[]{:S(2)}) collective-permute-start(f32[2,8,4224]{2,1,0:T(8,128)S(1)} %collective-permute-done.3.refs_3_), channel_id=1, source_target_pairs={{0,8},{2,10},{4,28},{6,30},{8,16},{10,18},{12,4},{14,6},{16,24},{1... | collective-permute-start | bytes 811016 | tf_op jit(solution)/shard_map/ppermute | solution.py:448
  30.2 3.5 %collective-permute-done.10.refs_6_ = f32[2,8,4096]{2,1,0:T(8,128)S(1)} collective-permute-done((f32[2,8,4096]{2,1,0:T(8,128)S(1)}, f32[2,8,4096]{2,1,0:T(8,128)S(1)}, u32[]{:S(2)}, u32[]{:S(2)}) %collective-permute-start.10) | collective-permute-done | bytes 262176 | tf_op jit(solution)/shard_map/ppermute | solution.py:448
  33.7 1.8 %collective-permute-start.11 = (f32[2,8,4096]{2,1,0:T(8,128)S(1)}, f32[2,8,4096]{2,1,0:T(8,128)S(1)}, u32[]{:S(2)}, u32[]{:S(2)}) collective-permute-start(f32[2,8,4096]{2,1,0:T(8,128)S(1)} %collective-permute-done.10.refs_6_), channel_id=1, source_target_pairs={{0,8},{2,10},{4,0},{6,2},{8,16},{10,18},{12,4},{14,6},{16,24},{18,... | collective-permute-start | bytes 786440 | tf_op jit(solution)/shard_map/ppermute | solution.py:448
  35.5 2.8 %collective-permute-done.4.refs_4_ = f32[2,8,4224]{2,1,0:T(8,128)S(1)} collective-permute-done((f32[2,8,4224]{2,1,0:T(8,128)S(1)}, f32[2,8,4224]{2,1,0:T(8,128)S(1)}, u32[]{:S(2)}, u32[]{:S(2)}) %collective-permute-start.4) | collective-permute-done | bytes 270368 | tf_op jit(solution)/shard_map/ppermute | solution.py:448
  38.2 0.0 collective-permute-done.5.refs_6_.refs_9_
  38.2 0.0 copy-done.2
  38.2 2.1 %residual_0.1 = (f32[4,32,1024]{2,1,0:T(8,128)S(1)}, f32[4,32,1024]{2,1,0:T(8,128)S(1)}, f32[2,32,1024]{2,1,0:T(8,128)S(1)}, f32[2,32,1024]{2,1,0:T(8,128)S(1)},...) custom-call(s32[64]{0:T(128)S(1)} %copy-done.4, ...), custom_call_target="tpu_custom_call" | custom-call | flops 603979776 | bytes 3670016 | tf_op jit(solution)/shard_map/residual_0/pallas_call | solution.py:346
  40.3 0.8 %collective-permute-start.6 = (f32[2,32,1024]{2,1,0:T(8,128)S(1)}, f32[2,32,1024]{2,1,0:T(8,128)S(1)}, u32[]{:S(2)}, u32[]{:S(2)}) collective-permute-start(f32[2,32,1024]{2,1,0:T(8,128)S(1)} %get-tuple-element.42), channel_id=1, source_target_pairs={{0,4},{2,6},{4,12},{6,14},{8,0},{10,2},{12,20},{14,22},{16,8},{18,... | collective-permute-start | bytes 786440 | tf_op jit(solution)/shard_map/ppermute | solution.py:448
  41.1 0.7 collective-permute-done.11.refs_7_
  41.8 1.2 %residual_1.1 = (f32[4,32,2048]{2,1,0:T(8,128)S(1)}, f32[4,32,2048]{2,1,0:T(8,128)S(1)}, f32[2,32,1024]{2,1,0:T(8,128)S(1)}, f32[2,32,1024]{2,1,0:T(8,128)S(1)}, f32[2,32,1024]{2,1,0:T(8,128)S(1)}) custom-call(bf16[256,192]{1,0:T(8,128)(2,1)S(1)} %get-tuple-element.44.refs_0_, bf16[256,192]{1,0:T(8,128)(2,1)S(1)} %get-tuple-element.45.refs_1_, ...), custom_call_target="tpu_custom_call" | custom-call | flops 603979776 | bytes 3670016 | tf_op jit(solution)/shard_map/residual_1/pallas_call | solution.py:346
  43.0 0.1 collective-permute-start.21
  43.1 3.8 %collective-permute-start.12 = (f32[2,32,1024]{2,1,0:T(8,128)S(1)}, f32[2,32,1024]{2,1,0:T(8,128)S(1)}, u32[]{:S(2)}, u32[]{:S(2)}) collective-permute-start(f32[2,32,1024]{2,1,0:T(8,128)S(1)} %get-tuple-element.62), channel_id=1, source_target_pairs={{0,24},{2,26},{4,12},{6,14},{8,0},{10,2},{12,20},{14,22},{16,8},{1... | collective-permute-start | bytes 786440 | tf_op jit(solution)/shard_map/ppermute | solution.py:448
  47.0 1.4 %collective-permute-done.6 = f32[2,32,1024]{2,1,0:T(8,128)S(1)} collective-permute-done((f32[2,32,1024]{2,1,0:T(8,128)S(1)}, f32[2,32,1024]{2,1,0:T(8,128)S(1)}, u32[]{:S(2)}, u32[]{:S(2)}) %collective-permute-start.6) | collective-permute-done | bytes 262176 | tf_op jit(solution)/shard_map/ppermute | solution.py:448
  48.4 0.1 collective-permute-start.17
  48.5 4.1 %prepare.1 = (f32[2,8,128,1024]{3,2,1,0:T(8,128)S(1)}, bf16[4,256,128]{2,1,0:T(8,128)(2,1)S(1)}) custom-call(s32[64]{0:T(128)S(1)} %copy-done.4, f32[64,256]{1,0:T(8,128)S(1)} %copy-done.2, f32[2,8,4224]{2,1,0:T(8,128)S(1)} %pad_maximum_fusion.refs_2_.foot_ref, f32[2,32,1024]{2,1,0:T(8,128)S(1)} %add.46._, f32[8,128,4096]{2,1,0:T(8,128)} %refs_1_.5), custom_call_target="tpu_custom_call" | custom-call | bytes 8388608 | tf_op jit(solution)/shard_map/prepare/pallas_call | solution.py:252
  52.6 0.0 slice-start
  52.6 0.5 collective-permute-done.12
  53.2 2.2 %collective-permute-start.13 = (f32[2,32,1024]{2,1,0:T(8,128)S(1)}, f32[2,32,1024]{2,1,0:T(8,128)S(1)}, u32[]{:S(2)}, u32[]{:S(2)}) collective-permute-start(f32[2,32,1024]{2,1,0:T(8,128)S(1)} %add.49), channel_id=1, source_target_pairs={{0,4},{2,6},{4,0},{6,2},{8,12},{10,14},{12,8},{14,10},{16,20},{18,... | collective-permute-start | bytes 786440 | tf_op jit(solution)/shard_map/ppermute | solution.py:448
  55.4 0.0 collective-permute-done.17
  55.5 0.5 collective-permute-start.18
  56.0 1.2 %collective-permute-start.19 = (f32[32,1024]{1,0:T(8,128)S(1)}, f32[32,1024]{1,0:T(8,128)S(1)}, u32[]{:S(2)}, u32[]{:S(2)}) collective-permute-start(f32[32,1024]{1,0:T(8,128)S(1)} %get-tuple-element.73), channel_id=1, source_target_pairs={{0,2},{1,3},{2,0},{3,1},{4,6},{5,7},{6,4},{7,5},{8,10},{9,11},{10,... | collective-permute-start | bytes 393224 | tf_op jit(solution)/shard_map/ppermute | solution.py:456
  57.2 0.5 collective-permute-start.20
  57.7 3.9 %collective-permute-done.13 = f32[2,32,1024]{2,1,0:T(8,128)S(1)} collective-permute-done((f32[2,32,1024]{2,1,0:T(8,128)S(1)}, f32[2,32,1024]{2,1,0:T(8,128)S(1)}, u32[]{:S(2)}, u32[]{:S(2)}) %collective-permute-start.13) | collective-permute-done | bytes 262176 | tf_op jit(solution)/shard_map/ppermute | solution.py:448
  61.6 1.6 %collective-permute-start.16 = (f32[32,1024]{1,0:T(8,128)S(1)}, f32[32,1024]{1,0:T(8,128)S(1)}, u32[]{:S(2)}, u32[]{:S(2)}) collective-permute-start(f32[32,1024]{1,0:T(8,128)S(1)} %get-tuple-element.74.refs_2_), channel_id=1, source_target_pairs={{0,1},{1,0},{2,3},{3,2},{4,5},{5,4},{6,7},{7,6},{8,9},{9,8},{10,11... | collective-permute-start | bytes 393224 | tf_op jit(solution)/shard_map/ppermute | solution.py:456
  63.2 0.0 collective-permute-done.18.refs_1_
  63.2 0.0 collective-permute-start.14
  63.2 0.0 collective-permute-done.19.refs_2_
  63.2 0.6 collective-permute-start.15
  63.8 0.4 collective-permute-done.20.refs_3_
  64.2 4.2 %update_0_0.1.refs_4_ = f32[8,128,4096]{2,1,0:T(8,128)} custom-call(bf16[4,256,128]{2,1,0:T(8,128)(2,1)S(1)} %get-tuple-element.43.refs_0_, f32[32,1024]{1,0:T(8,128)S(1)} %collective-permute-done.18.refs_1_, f32[32,1024]{1,0:T(8,128)S(1)} %collective-permute-done.19.refs_2_, f32[32,1024]{1,0:T(8,128)S(1)} %collective-permute-done.20.refs_3_, ...), custom_call_target="tpu_custom_call" | custom-call | flops 201326592 | bytes 8388608 | tf_op jit(solution)/shard_map/update_0_0/pallas_call | solution.py:422
  68.4 0.0 collective-permute-done.16.refs_1_
  68.4 0.0 collective-permute-done.21.refs_6_
  68.5 0.0 slice-done
  68.5 0.3 slice-done.1
  68.8 2.7 %update_1_0.1 = (f32[8,128,4096]{2,1,0:T(8,128)}, f32[4,32,4096]{2,1,0:T(8,128)}) custom-call(bf16[4,256,128]{2,1,0:T(8,128)(2,1)S(1)} %get-tuple-element.43.refs_0_, f32[32,1024]{1,0:T(8,128)S(1)} %collective-permute-done.16.refs_1_, f32[32,1024]{1,0:T(8,128)S(1)} %get-tuple-element.74.refs_2_, ...), custom_call_target="tpu_custom_call", output_to_operand_aliasing={{0}: (4, {})} | custom-call | flops 100663296 | bytes 4194304 | tf_op jit(solution)/shard_map/update_1_0/pallas_call | solution.py:422
  71.5 0.0 collective-permute-done.14.refs_1_
  71.5 0.0 collective-permute-done.15.refs_2_
  71.5 2.3 %update_1_1.1 = f32[8,128,4096]{2,1,0:T(8,128)} custom-call(bf16[4,256,128]{2,1,0:T(8,128)(2,1)S(1)} %get-tuple-element.43.refs_0_, f32[32,1024]{1,0:T(8,128)S(1)} %collective-permute-done.14.refs_1_, f32[32,1024]{1,0:T(8,128)S(1)} %collective-permute-done.15.refs_2_, f32[2,8,128,1024]{3,2,1,0:T(8,128)S(1)} %bitcast.17, ...), custom_call_target="tpu_custom_call", output_to_operand_aliasing={{}: (4, {})} | custom-call | flops 100663296 | bytes 4194304 | tf_op jit(solution)/shard_map/update_1_1/pallas_call | solution.py:422
  (15 shorter events, 0.3 us)
Async XLA Ops:
  0.6 37.6 %copy-start.4 = (s32[64]{0:T(128)S(1)}, s32[64]{0:T(128)}, u32[]{:S(2)}) copy-start(s32[64]{0:T(128)} %order_ref.1) | copy-start | bytes 772
  0.6 37.6 %copy-start.2 = (f32[64,256]{1,0:T(8,128)S(1)}, f32[64,256]{1,0:T(8,128)}, u32[]{:S(2)}) copy-start(f32[64,256]{1,0:T(8,128)} %table_ref.1) | copy-start | bytes 196612
  0.7 17.7 %copy-start.1 = (bf16[4,32,4096]{2,1,0:T(8,128)(2,1)S(1)}, bf16[4,32,4096]{2,1,0:T(8,128)(2,1)}, u32[]{:S(2)}) copy-start(bf16[4,32,4096]{2,1,0:T(8,128)(2,1)} %refs_8_.1) | copy-start | bytes 3145732
  5.3 13.2 %collective-permute-start = (f32[8,4224]{1,0:T(8,128)}, f32[8,4224]{1,0:T(8,128)S(1)}, u32[]{:S(2)}, u32[]{:S(2)}) collective-permute-start(f32[8,4224]{1,0:T(8,128)} %get-tuple-element.38), channel_id=1, source_target_pairs={{0,1},{1,0},{2,3},{3,2},{4,5},{5,4},{6,7},{7,6},{8,9},{9,8},{10,11... | collective-permute-start | bytes 405512 | tf_op jit(solution)/shard_map/ppermute | solution.py:456
  8.3 10.4 %collective-permute-start.1 = (f32[8,4224]{1,0:T(8,128)}, f32[8,4224]{1,0:T(8,128)S(1)}, u32[]{:S(2)}, u32[]{:S(2)}) collective-permute-start(f32[8,4224]{1,0:T(8,128)} %get-tuple-element.39), channel_id=1, source_target_pairs={{0,2},{1,3},{2,0},{3,1},{4,6},{5,7},{6,4},{7,5},{8,10},{9,11},{10,... | collective-permute-start | bytes 405512 | tf_op jit(solution)/shard_map/ppermute | solution.py:456
  8.3 10.8 %collective-permute-start.2 = (f32[8,4224]{1,0:T(8,128)}, f32[8,4224]{1,0:T(8,128)S(1)}, u32[]{:S(2)}, u32[]{:S(2)}) collective-permute-start(f32[8,4224]{1,0:T(8,128)} %get-tuple-element.40), channel_id=1, source_target_pairs={{0,3},{1,2},{2,1},{3,0},{4,7},{5,6},{6,5},{7,4},{8,11},{9,10},{10,... | collective-permute-start | bytes 405512 | tf_op jit(solution)/shard_map/ppermute | solution.py:456
  8.5 0.8 %copy-start.3 = (bf16[32,512]{1,0:T(8,128)(2,1)S(1)}, bf16[32,512]{1,0:T(8,128)(2,1)}, u32[]{:S(2)}) copy-start(bf16[32,512]{1,0:T(8,128)(2,1)} %get-tuple-element.49.refs_0_) | copy-start | bytes 98308
  9.3 9.4 %copy-start.5 = (f32[8,4224]{1,0:T(8,128)S(1)}, f32[8,4224]{1,0:T(8,128)}, u32[]{:S(2)}) copy-start(f32[8,4224]{1,0:T(8,128)} %get-tuple-element.37) | copy-start | bytes 405508
  13.1 3.3 %copy-start = (f32[2,8,128,1024]{3,2,1,0:T(8,128)}, f32[2,8,128,1024]{3,2,1,0:T(8,128)S(1)}, u32[]{:S(2)}) copy-start(f32[2,8,128,1024]{3,2,1,0:T(8,128)S(1)} %get-tuple-element.65.refs_3_) | copy-start | bytes 25165828
  16.4 6.2 %collective-permute-start.7 = (f32[8,4096]{1,0:T(8,128)S(1)}, f32[8,4096]{1,0:T(8,128)S(1)}, u32[]{:S(2)}, u32[]{:S(2)}) collective-permute-start(f32[8,4096]{1,0:T(8,128)S(1)} %get-tuple-element.51), channel_id=1, source_target_pairs={{0,1},{1,0},{2,3},{3,2},{4,5},{5,4},{6,7},{7,6},{8,9},{9,8},{10,11... | collective-permute-start | bytes 393224 | tf_op jit(solution)/shard_map/ppermute | solution.py:456
  18.4 4.3 %collective-permute-start.8 = (f32[8,4096]{1,0:T(8,128)S(1)}, f32[8,4096]{1,0:T(8,128)S(1)}, u32[]{:S(2)}, u32[]{:S(2)}) collective-permute-start(f32[8,4096]{1,0:T(8,128)S(1)} %get-tuple-element.52), channel_id=1, source_target_pairs={{0,2},{1,3},{2,0},{3,1},{4,6},{5,7},{6,4},{7,5},{8,10},{9,11},{10,... | collective-permute-start | bytes 393224 | tf_op jit(solution)/shard_map/ppermute | solution.py:456
  18.5 5.9 %collective-permute-start.9 = (f32[8,4096]{1,0:T(8,128)S(1)}, f32[8,4096]{1,0:T(8,128)S(1)}, u32[]{:S(2)}, u32[]{:S(2)}) collective-permute-start(f32[8,4096]{1,0:T(8,128)S(1)} %get-tuple-element.53), channel_id=1, source_target_pairs={{0,3},{1,2},{2,1},{3,0},{4,7},{5,6},{6,5},{7,4},{8,11},{9,10},{10,... | collective-permute-start | bytes 393224 | tf_op jit(solution)/shard_map/ppermute | solution.py:456
  18.8 19.5 %collective-permute-start.5 = (f32[4,32,2048]{2,1,0:T(8,128)S(1)}, f32[4,32,2048]{2,1,0:T(8,128)S(1)}, u32[]{:S(2)}, u32[]{:S(2)}) collective-permute-start(f32[4,32,2048]{2,1,0:T(8,128)S(1)} %dynamic-slice_convert_fusion), channel_id=1, source_target_pairs={{0,2},{2,0},{4,6},{6,4},{8,10},{10,8},{12,14},{14,12},{16,18},{18,... | collective-permute-start | bytes 3145736 | tf_op jit(solution)/shard_map/ppermute | solution.py:448
  19.2 9.0 %collective-permute-start.3 = (f32[2,8,4224]{2,1,0:T(8,128)S(1)}, f32[2,8,4224]{2,1,0:T(8,128)S(1)}, u32[]{:S(2)}, u32[]{:S(2)}) collective-permute-start(f32[2,8,4224]{2,1,0:T(8,128)S(1)} %pad_maximum_fusion.refs_2_.foot_ref), channel_id=1, source_target_pairs={{0,4},{2,6},{4,0},{6,2},{8,12},{10,14},{12,8},{14,10},{16,20},{18,... | collective-permute-start | bytes 811016 | tf_op jit(solution)/shard_map/ppermute | solution.py:448
  24.5 9.2 %collective-permute-start.10 = (f32[2,8,4096]{2,1,0:T(8,128)S(1)}, f32[2,8,4096]{2,1,0:T(8,128)S(1)}, u32[]{:S(2)}, u32[]{:S(2)}) collective-permute-start(f32[2,8,4096]{2,1,0:T(8,128)S(1)} %pad_maximum_fusion.1.refs_5_), channel_id=1, source_target_pairs={{0,4},{2,6},{4,0},{6,2},{8,12},{10,14},{12,8},{14,10},{16,20},{18,... | collective-permute-start | bytes 786440 | tf_op jit(solution)/shard_map/ppermute | solution.py:448
  28.2 10.0 %collective-permute-start.4 = (f32[2,8,4224]{2,1,0:T(8,128)S(1)}, f32[2,8,4224]{2,1,0:T(8,128)S(1)}, u32[]{:S(2)}, u32[]{:S(2)}) collective-permute-start(f32[2,8,4224]{2,1,0:T(8,128)S(1)} %collective-permute-done.3.refs_3_), channel_id=1, source_target_pairs={{0,8},{2,10},{4,28},{6,30},{8,16},{10,18},{12,4},{14,6},{16,24},{1... | collective-permute-start | bytes 811016 | tf_op jit(solution)/shard_map/ppermute | solution.py:448
  33.7 8.1 %collective-permute-start.11 = (f32[2,8,4096]{2,1,0:T(8,128)S(1)}, f32[2,8,4096]{2,1,0:T(8,128)S(1)}, u32[]{:S(2)}, u32[]{:S(2)}) collective-permute-start(f32[2,8,4096]{2,1,0:T(8,128)S(1)} %collective-permute-done.10.refs_6_), channel_id=1, source_target_pairs={{0,8},{2,10},{4,0},{6,2},{8,16},{10,18},{12,4},{14,6},{16,24},{18,... | collective-permute-start | bytes 786440 | tf_op jit(solution)/shard_map/ppermute | solution.py:448
  40.3 8.1 %collective-permute-start.6 = (f32[2,32,1024]{2,1,0:T(8,128)S(1)}, f32[2,32,1024]{2,1,0:T(8,128)S(1)}, u32[]{:S(2)}, u32[]{:S(2)}) collective-permute-start(f32[2,32,1024]{2,1,0:T(8,128)S(1)} %get-tuple-element.42), channel_id=1, source_target_pairs={{0,4},{2,6},{4,12},{6,14},{8,0},{10,2},{12,20},{14,22},{16,8},{18,... | collective-permute-start | bytes 786440 | tf_op jit(solution)/shard_map/ppermute | solution.py:448
  43.0 25.4 %collective-permute-start.21 = (f32[4,32,2048]{2,1,0:T(8,128)S(1)}, f32[4,32,2048]{2,1,0:T(8,128)S(1)}, u32[]{:S(2)}, u32[]{:S(2)}) collective-permute-start(f32[4,32,2048]{2,1,0:T(8,128)S(1)} %get-tuple-element.69), channel_id=1, source_target_pairs={{0,2},{2,0},{4,6},{6,4},{8,10},{10,8},{12,14},{14,12},{16,18},{18,... | collective-permute-start | bytes 3145736 | tf_op jit(solution)/shard_map/ppermute | solution.py:448
  43.1 10.0 %collective-permute-start.12 = (f32[2,32,1024]{2,1,0:T(8,128)S(1)}, f32[2,32,1024]{2,1,0:T(8,128)S(1)}, u32[]{:S(2)}, u32[]{:S(2)}) collective-permute-start(f32[2,32,1024]{2,1,0:T(8,128)S(1)} %get-tuple-element.62), channel_id=1, source_target_pairs={{0,24},{2,26},{4,12},{6,14},{8,0},{10,2},{12,20},{14,22},{16,8},{1... | collective-permute-start | bytes 786440 | tf_op jit(solution)/shard_map/ppermute | solution.py:448
  48.4 7.0 %collective-permute-start.17 = (f32[2,32,1024]{2,1,0:T(8,128)S(1)}, f32[2,32,1024]{2,1,0:T(8,128)S(1)}, u32[]{:S(2)}, u32[]{:S(2)}) collective-permute-start(f32[2,32,1024]{2,1,0:T(8,128)S(1)} %add.46._), channel_id=1, source_target_pairs={{0,4},{2,6},{4,0},{6,2},{8,12},{10,14},{12,8},{14,10},{16,20},{18,... | collective-permute-start | bytes 786440 | tf_op jit(solution)/shard_map/ppermute | solution.py:448
  52.6 15.8 %slice-start = ((s8[8388608]{0:T(1024)(128)(4,1)}), s8[4194304]{0:T(1024)(128)(4,1)S(1)}, s32[]{:S(2)}) async-start(s8[8388608]{0:T(1024)(128)(4,1)} %bitcast.16), calls=%async_computation | async-start | bytes 8388608
  53.2 8.4 %collective-permute-start.13 = (f32[2,32,1024]{2,1,0:T(8,128)S(1)}, f32[2,32,1024]{2,1,0:T(8,128)S(1)}, u32[]{:S(2)}, u32[]{:S(2)}) collective-permute-start(f32[2,32,1024]{2,1,0:T(8,128)S(1)} %add.49), channel_id=1, source_target_pairs={{0,4},{2,6},{4,0},{6,2},{8,12},{10,14},{12,8},{14,10},{16,20},{18,... | collective-permute-start | bytes 786440 | tf_op jit(solution)/shard_map/ppermute | solution.py:448
  55.5 7.7 %collective-permute-start.18 = (f32[32,1024]{1,0:T(8,128)S(1)}, f32[32,1024]{1,0:T(8,128)S(1)}, u32[]{:S(2)}, u32[]{:S(2)}) collective-permute-start(f32[32,1024]{1,0:T(8,128)S(1)} %get-tuple-element.73), channel_id=1, source_target_pairs={{0,3},{1,2},{2,1},{3,0},{4,7},{5,6},{6,5},{7,4},{8,11},{9,10},{10,... | collective-permute-start | bytes 393224 | tf_op jit(solution)/shard_map/ppermute | solution.py:456
  56.0 7.2 %collective-permute-start.19 = (f32[32,1024]{1,0:T(8,128)S(1)}, f32[32,1024]{1,0:T(8,128)S(1)}, u32[]{:S(2)}, u32[]{:S(2)}) collective-permute-start(f32[32,1024]{1,0:T(8,128)S(1)} %get-tuple-element.73), channel_id=1, source_target_pairs={{0,2},{1,3},{2,0},{3,1},{4,6},{5,7},{6,4},{7,5},{8,10},{9,11},{10,... | collective-permute-start | bytes 393224 | tf_op jit(solution)/shard_map/ppermute | solution.py:456
  57.2 7.0 %collective-permute-start.20 = (f32[32,1024]{1,0:T(8,128)S(1)}, f32[32,1024]{1,0:T(8,128)S(1)}, u32[]{:S(2)}, u32[]{:S(2)}) collective-permute-start(f32[32,1024]{1,0:T(8,128)S(1)} %get-tuple-element.72.refs_4_), channel_id=1, source_target_pairs={{0,1},{1,0},{2,3},{3,2},{4,5},{5,4},{6,7},{7,6},{8,9},{9,8},{10,11... | collective-permute-start | bytes 393224 | tf_op jit(solution)/shard_map/ppermute | solution.py:456
  61.6 6.9 %collective-permute-start.16 = (f32[32,1024]{1,0:T(8,128)S(1)}, f32[32,1024]{1,0:T(8,128)S(1)}, u32[]{:S(2)}, u32[]{:S(2)}) collective-permute-start(f32[32,1024]{1,0:T(8,128)S(1)} %get-tuple-element.74.refs_2_), channel_id=1, source_target_pairs={{0,1},{1,0},{2,3},{3,2},{4,5},{5,4},{6,7},{7,6},{8,9},{9,8},{10,11... | collective-permute-start | bytes 393224 | tf_op jit(solution)/shard_map/ppermute | solution.py:456
  63.2 8.4 %collective-permute-start.14 = (f32[32,1024]{1,0:T(8,128)S(1)}, f32[32,1024]{1,0:T(8,128)S(1)}, u32[]{:S(2)}, u32[]{:S(2)}) collective-permute-start(f32[32,1024]{1,0:T(8,128)S(1)} %get-tuple-element.75), channel_id=1, source_target_pairs={{0,3},{1,2},{2,1},{3,0},{4,7},{5,6},{6,5},{7,4},{8,11},{9,10},{10,... | collective-permute-start | bytes 393224 | tf_op jit(solution)/shard_map/ppermute | solution.py:456
  63.2 8.4 %collective-permute-start.15 = (f32[32,1024]{1,0:T(8,128)S(1)}, f32[32,1024]{1,0:T(8,128)S(1)}, u32[]{:S(2)}, u32[]{:S(2)}) collective-permute-start(f32[32,1024]{1,0:T(8,128)S(1)} %get-tuple-element.75), channel_id=1, source_target_pairs={{0,2},{1,3},{2,0},{3,1},{4,6},{5,7},{6,4},{7,5},{8,10},{9,11},{10,... | collective-permute-start | bytes 393224 | tf_op jit(solution)/shard_map/ppermute | solution.py:456
  64.2 4.5 %slice-start.1 = ((s8[8388608]{0:T(1024)(128)(4,1)}), s8[4194304]{0:T(1024)(128)(4,1)S(1)}, s32[]{:S(2)}) async-start(s8[8388608]{0:T(1024)(128)(4,1)} %bitcast.16), calls=%async_computation.1 | async-start | bytes 8388608

commit v11 on v5

--- a/solution.py
+++ b/solution.py
@@ -346,10 +346,16 @@
     )(*args)
 
 
+def operand_order(halves, groups):
+    at = list(range(len(halves) * groups))
+    return at[1:groups] + at[groups + 1:] + at[groups:groups + 1] + at[:1]
+
+
 def update_kernel(dims, first, halves, half, offset, width, *refs):
     per, groups, zb, cells = dims
     count = groups * SUBLANES
-    left_ref, backs, refs = refs[0], refs[len(halves) * groups:0:-1], refs[1 + len(halves) * groups:]
+    left_ref, given, refs = refs[0], refs[1:1 + len(halves) * groups], refs[1 + len(halves) * groups:]
+    backs = dict(zip(operand_order(halves, groups), given))
     vol_ref, *refs = refs
     zdev, depth = vol_ref.shape[1], left_ref.shape[2]
     if not first:
@@ -391,7 +397,7 @@
     per, groups, zb, cells = dims
     zdev, _, total = volume.shape
     first = out is None
-    args = [left, *backs[::-1], kept]
+    args = [left, *(backs[i] for i in operand_order(halves, groups)), kept]
     shapes = [jax.ShapeDtypeStruct(volume.shape, F32)]
     scratch = [
         pltpu.VMEM((len(halves), zdev, cells, width), F32),
@@ -430,7 +436,7 @@
     zb = SUBLANES // per
     dims = (per, groups, zb, cells)
     each = half // CHUNKS
-    widths = [each] * CHUNKS
+    widths = [each - LANES] + [each] * (CHUNKS - 2) + [each + LANES]
     offsets = [sum(widths[:c]) for c in range(CHUNKS)]
 
     def along(value, to):

time: 71.5 us -> 72 us (level)
  waiting for transfers between devices: 19.9 us -> 22 us
  starting transfers between devices: 24.8 us -> 23.2 us
    ppermute x12, waiting for transfers between devices: 4.47 us -> 6.23 us  [spread(): return lax.ppermute(value, ('slab', 'ang'), pairs)]
    ppermute x10, starting transfers between devices: 14.6 us -> 13.6 us  [along(): return lax.ppermute(value, 'slab', pairs)]
  transfers between devices with their start and end apart: 22 -> 22, of which waited for: 9 -> 10; matrix products, arithmetic and copies ran while one was open for 0% -> 0% of each run, Pallas kernels for 25% -> 25%
where the time goes in v11:
time: 72 us; the launch traced here: 71.8 us
  Pallas kernels  24.7 us (34%)
  starting transfers between devices  23.2 us (32%)
  waiting for transfers between devices  22 us (31%)
  between operations  0.85 us (1%)
  local copies, waits for them, and re-layouts  0.78 us (1%)
    ppermute x10, waiting for transfers between devices, along(): return lax.ppermute(value, 'slab', pairs)  15.7 us
    ppermute x10, starting transfers between devices, along(): return lax.ppermute(value, 'slab', pairs)  13.6 us
    ppermute x12, starting transfers between devices, spread(): return lax.ppermute(value, ('slab', 'ang'), pairs)  9.6 us
    pallas_call x3, Pallas kernels, update_step(): pl.pallas_call(functools.partial(update_kernel, dims, first, halves, tota...  8.76 us
    pallas_call x2, Pallas kernels, ray_sums(): pl.pallas_call(functools.partial(rays_kernel, dims, first, keep, extra, h...  8.45 us
    ppermute x12, waiting for transfers between devices, spread(): return lax.ppermute(value, ('slab', 'ang'), pairs)  6.23 us
    pallas_call x1, Pallas kernels, prepare_step(): pl.pallas_call(functools.partial(prepare_kernel, dims, rdev, total // 2,...  3.78 us
    pallas_call x2, Pallas kernels, residual_step(): pl.pallas_call(functools.partial(residual_kernel, dims, first, total // 2...  3.7 us
  transfers between devices with their start and end apart: 22, of which 10 were waited for; matrix products, arithmetic and copies ran while one was open for 0% of the time, Pallas kernels for 25%

profile of v11, /device:TPU:0, one launch (start us, length us, event | category | flops | bytes accessed | tf_op | source)
XLA Modules:
  0.0 71.8 jit_solution(16316269420335366460)
XLA Ops:
  0.6 0.0 copy-start.3
  0.6 0.0 copy-start.1
  0.7 0.0 copy-start
  0.7 4.3 %ray_sums_0_0.1 = (f32[32,1024]{1,0:T(8,128)}, f32[32,1024]{1,0:T(8,128)}, f32[32,1024]{1,0:T(8,128)}, f32[32,1024]{1,0:T(8,128)}, bf16[32,512]{1,0:T(8,128)(2,1)}) custom-call(s32[64]{0:T(128)} %refs_0_.3, s32[1,4]{1,0:T(1,128)} %refs_1_.3, s32[1,4]{1,0:T(1,128)} %refs_2_.1, f32[64,256]{1,0:T(8,128)} %refs_1_.4, f32[8,128,4096]{2,1,0:T(8,128)} %refs_1_.5), custom_call_target="tpu_custom_call" | custom-call | flops 58720256 | bytes 7340032 | tf_op jit(solution)/shard_map/ray_sums_0_0/pallas_call | solution.py:176
  5.0 0.0 copy-start.4
  5.0 3.0 %collective-permute-start = (f32[32,1024]{1,0:T(8,128)}, f32[32,1024]{1,0:T(8,128)S(1)}, u32[]{:S(2)}, u32[]{:S(2)}) collective-permute-start(f32[32,1024]{1,0:T(8,128)} %get-tuple-element.37), channel_id=1, source_target_pairs={{0,1},{1,0},{2,3},{3,2},{4,5},{5,4},{6,7},{7,6},{8,9},{9,8},{10,11... | collective-permute-start | bytes 393224 | tf_op jit(solution)/shard_map/ppermute | solution.py:452
  8.0 0.0 copy-done
  8.0 0.1 dynamic-slice_convert_fusion
  8.1 0.1 collective-permute-start.5
  8.2 0.5 collective-permute-start.1
  8.7 0.0 collective-permute-start.2
  8.7 0.0 copy-start.2
  8.7 0.8 %copy-done.2 = bf16[32,512]{1,0:T(8,128)(2,1)S(1)} copy-done((bf16[32,512]{1,0:T(8,128)(2,1)S(1)}, bf16[32,512]{1,0:T(8,128)(2,1)}, u32[]{:S(2)}) %copy-start.2) | copy-done | bytes 32792
  9.5 4.1 %ray_sums_1_0.1 = (f32[32,1152]{1,0:T(8,128)S(1)}, f32[32,1152]{1,0:T(8,128)S(1)}, f32[32,1152]{1,0:T(8,128)S(1)}, f32[32,1152]{1,0:T(8,128)S(1)}, f32[2,8,128,1152]{3,2,1,0:T(8,128)S(1)}) custom-call(bf16[32,512]{1,0:T(8,128)(2,1)S(1)} %copy-done.2, f32[8,128,4096]{2,1,0:T(8,128)} %refs_1_.5), custom_call_target="tpu_custom_call" | custom-call | flops 75497472 | bytes 9437184 | tf_op jit(solution)/shard_map/ray_sums_1_0/pallas_call | solution.py:176
  13.6 1.8 %collective-permute-start.6 = (f32[32,1152]{1,0:T(8,128)S(1)}, f32[32,1152]{1,0:T(8,128)S(1)}, u32[]{:S(2)}, u32[]{:S(2)}) collective-permute-start(f32[32,1152]{1,0:T(8,128)S(1)} %get-tuple-element.48), channel_id=1, source_target_pairs={{0,1},{1,0},{2,3},{3,2},{4,5},{5,4},{6,7},{7,6},{8,9},{9,8},{10,11... | collective-permute-start | bytes 442376 | tf_op jit(solution)/shard_map/ppermute | solution.py:452
  15.4 0.0 collective-permute-done
  15.4 0.2 collective-permute-start.7
  15.6 0.0 copy-done.4
  15.6 0.0 collective-permute-done.1
  15.6 0.3 collective-permute-start.8
  15.9 0.0 collective-permute-done.2
  16.0 1.7 %collective-permute-start.3 = (f32[2,32,1024]{2,1,0:T(8,128)S(1)}, f32[2,32,1024]{2,1,0:T(8,128)S(1)}, u32[]{:S(2)}, u32[]{:S(2)}) collective-permute-start(f32[2,32,1024]{2,1,0:T(8,128)S(1)} %pad_maximum_fusion.1.foot_ref.refs_2_), channel_id=1, source_target_pairs={{0,4},{2,6},{4,0},{6,2},{8,12},{10,14},{12,8},{14,10},{16,20},{18,... | collective-permute-start | bytes 786440 | tf_op jit(solution)/shard_map/ppermute | solution.py:444
  17.7 2.6 %collective-permute-done.6 = f32[32,1152]{1,0:T(8,128)S(1)} collective-permute-done((f32[32,1152]{1,0:T(8,128)S(1)}, f32[32,1152]{1,0:T(8,128)S(1)}, u32[]{:S(2)}, u32[]{:S(2)}) %collective-permute-start.6) | collective-permute-done | bytes 147488 | tf_op jit(solution)/shard_map/ppermute | solution.py:452
  20.3 0.0 collective-permute-done.7
  20.3 2.1 %collective-permute-done.8 = f32[32,1152]{1,0:T(8,128)S(1)} collective-permute-done((f32[32,1152]{1,0:T(8,128)S(1)}, f32[32,1152]{1,0:T(8,128)S(1)}, u32[]{:S(2)}, u32[]{:S(2)}) %collective-permute-start.8) | collective-permute-done | bytes 147488 | tf_op jit(solution)/shard_map/ppermute | solution.py:452
  22.5 1.9 %collective-permute-start.9 = (f32[2,32,1152]{2,1,0:T(8,128)S(1)}, f32[2,32,1152]{2,1,0:T(8,128)S(1)}, u32[]{:S(2)}, u32[]{:S(2)}) collective-permute-start(f32[2,32,1152]{2,1,0:T(8,128)S(1)} %pad_maximum_fusion.refs_5_), channel_id=1, source_target_pairs={{0,4},{2,6},{4,0},{6,2},{8,12},{10,14},{12,8},{14,10},{16,20},{18,... | collective-permute-start | bytes 884744 | tf_op jit(solution)/shard_map/ppermute | solution.py:444
  24.4 0.1 collective-permute-done.3._.refs_3_
  24.5 1.7 %collective-permute-start.4 = (f32[2,32,1024]{2,1,0:T(8,128)S(1)}, f32[2,32,1024]{2,1,0:T(8,128)S(1)}, u32[]{:S(2)}, u32[]{:S(2)}) collective-permute-start(f32[2,32,1024]{2,1,0:T(8,128)S(1)} %collective-permute-done.3._.refs_3_), channel_id=1, source_target_pairs={{0,8},{2,10},{4,28},{6,30},{8,16},{10,18},{12,4},{14,6},{16,24},{1... | collective-permute-start | bytes 786440 | tf_op jit(solution)/shard_map/ppermute | solution.py:444
  26.2 0.0 copy-done.3
  26.2 0.0 copy-done.1
  26.2 3.8 %prepare.1 = (f32[2,8,128,896]{3,2,1,0:T(8,128)S(1)}, bf16[4,256,128]{2,1,0:T(8,128)(2,1)S(1)}) custom-call(s32[64]{0:T(128)S(1)} %copy-done.3, f32[64,256]{1,0:T(8,128)S(1)} %copy-done.1, f32[2,32,1024]{2,1,0:T(8,128)S(1)} %pad_maximum_fusion.1.foot_ref.refs_2_, f32[2,32,1024]{2,1,0:T(8,128)S(1)} %collective-permute-done.3._.refs_3_, f32[8,128,4096]{2,1,0:T(8,128)} %refs_1_.5), custom_call_target="tpu_custom_call" | custom-call | bytes 7340032 | tf_op jit(solution)/shard_map/prepare/pallas_call | solution.py:250
  30.0 2.2 %collective-permute-done.9.refs_6_ = f32[2,32,1152]{2,1,0:T(8,128)S(1)} collective-permute-done((f32[2,32,1152]{2,1,0:T(8,128)S(1)}, f32[2,32,1152]{2,1,0:T(8,128)S(1)}, u32[]{:S(2)}, u32[]{:S(2)}) %collective-permute-start.9) | collective-permute-done | bytes 294944 | tf_op jit(solution)/shard_map/ppermute | solution.py:444
  32.2 1.8 %collective-permute-start.10 = (f32[2,32,1152]{2,1,0:T(8,128)S(1)}, f32[2,32,1152]{2,1,0:T(8,128)S(1)}, u32[]{:S(2)}, u32[]{:S(2)}) collective-permute-start(f32[2,32,1152]{2,1,0:T(8,128)S(1)} %collective-permute-done.9.refs_6_), channel_id=1, source_target_pairs={{0,8},{2,10},{4,0},{6,2},{8,16},{10,18},{12,4},{14,6},{16,24},{18,... | collective-permute-start | bytes 884744 | tf_op jit(solution)/shard_map/ppermute | solution.py:444
  34.0 0.8 %collective-permute-done.4.refs_4_ = f32[2,32,1024]{2,1,0:T(8,128)S(1)} collective-permute-done((f32[2,32,1024]{2,1,0:T(8,128)S(1)}, f32[2,32,1024]{2,1,0:T(8,128)S(1)}, u32[]{:S(2)}, u32[]{:S(2)}) %collective-permute-start.4) | collective-permute-done | bytes 262176 | tf_op jit(solution)/shard_map/ppermute | solution.py:444
  34.8 0.0 collective-permute-done.5.refs_6_.refs_9_
  34.8 2.1 %residual_0.1 = (f32[4,32,896]{2,1,0:T(8,128)S(1)}, f32[4,32,896]{2,1,0:T(8,128)S(1)}, f32[2,32,896]{2,1,0:T(8,128)S(1)}, f32[2,32,896]{2,1,0:T(8,128)S(1)}, f32...) custom-call(s32[64]{0:T(128)S(1)} %copy-done.3, ...), custom_call_target="tpu_custom_call" | custom-call | flops 528482304 | bytes 3211264 | tf_op jit(solution)/shard_map/residual_0/pallas_call | solution.py:336
  36.9 0.1 collective-permute-start.16
  36.9 3.9 %collective-permute-done.10.refs_7_ = f32[2,32,1152]{2,1,0:T(8,128)S(1)} collective-permute-done((f32[2,32,1152]{2,1,0:T(8,128)S(1)}, f32[2,32,1152]{2,1,0:T(8,128)S(1)}, u32[]{:S(2)}, u32[]{:S(2)}) %collective-permute-start.10) | collective-permute-done | bytes 294944 | tf_op jit(solution)/shard_map/ppermute | solution.py:444
  40.9 1.6 %residual_1.1 = (f32[4,32,2048]{2,1,0:T(8,128)S(1)}, f32[4,32,2048]{2,1,0:T(8,128)S(1)}, f32[2,32,1152]{2,1,0:T(8,128)S(1)}, f32[2,32,1152]{2,1,0:T(8,128)S(1)}, f32[2,32,1152]{2,1,0:T(8,128)S(1)}) custom-call(bf16[256,192]{1,0:T(8,128)(2,1)S(1)} %get-tuple-element.41.refs_0_, bf16[256,192]{1,0:T(8,128)(2,1)S(1)} %get-tuple-element.42.refs_1_, ...), custom_call_target="tpu_custom_call" | custom-call | flops 679477248 | bytes 4128768 | tf_op jit(solution)/shard_map/residual_1/pallas_call | solution.py:336
  42.5 3.9 %collective-permute-start.11 = (f32[2,32,1152]{2,1,0:T(8,128)S(1)}, f32[2,32,1152]{2,1,0:T(8,128)S(1)}, u32[]{:S(2)}, u32[]{:S(2)}) collective-permute-start(f32[2,32,1152]{2,1,0:T(8,128)S(1)} %get-tuple-element.61), channel_id=1, source_target_pairs={{0,24},{2,26},{4,12},{6,14},{8,0},{10,2},{12,20},{14,22},{16,8},{1... | collective-permute-start | bytes 884744 | tf_op jit(solution)/shard_map/ppermute | solution.py:444
  46.4 0.0 collective-permute-done.16
  46.4 0.1 collective-permute-start.17
  46.5 0.1 collective-permute-start.21
  46.6 5.2 %collective-permute-done.11 = f32[2,32,1152]{2,1,0:T(8,128)S(1)} collective-permute-done((f32[2,32,1152]{2,1,0:T(8,128)S(1)}, f32[2,32,1152]{2,1,0:T(8,128)S(1)}, u32[]{:S(2)}, u32[]{:S(2)}) %collective-permute-start.11) | collective-permute-done | bytes 294944 | tf_op jit(solution)/shard_map/ppermute | solution.py:444
  51.8 2.3 %collective-permute-start.12 = (f32[2,32,1152]{2,1,0:T(8,128)S(1)}, f32[2,32,1152]{2,1,0:T(8,128)S(1)}, u32[]{:S(2)}, u32[]{:S(2)}) collective-permute-start(f32[2,32,1152]{2,1,0:T(8,128)S(1)} %add.48), channel_id=1, source_target_pairs={{0,4},{2,6},{4,0},{6,2},{8,12},{10,14},{12,8},{14,10},{16,20},{18,... | collective-permute-start | bytes 884744 | tf_op jit(solution)/shard_map/ppermute | solution.py:444
  54.1 0.0 collective-permute-done.17
  54.1 1.6 %collective-permute-start.18 = (f32[32,896]{1,0:T(8,128)S(1)}, f32[32,896]{1,0:T(8,128)S(1)}, u32[]{:S(2)}, u32[]{:S(2)}) collective-permute-start(f32[32,896]{1,0:T(8,128)S(1)} %get-tuple-element.73.refs_4_), channel_id=1, source_target_pairs={{0,1},{1,0},{2,3},{3,2},{4,5},{5,4},{6,7},{7,6},{8,9},{9,8},{10,11... | collective-permute-start | bytes 344072 | tf_op jit(solution)/shard_map/ppermute | solution.py:452
  55.7 0.0 collective-permute-start.19
  55.7 3.6 %collective-permute-done.12 = f32[2,32,1152]{2,1,0:T(8,128)S(1)} collective-permute-done((f32[2,32,1152]{2,1,0:T(8,128)S(1)}, f32[2,32,1152]{2,1,0:T(8,128)S(1)}, u32[]{:S(2)}, u32[]{:S(2)}) %collective-permute-start.12) | collective-permute-done | bytes 294944 | tf_op jit(solution)/shard_map/ppermute | solution.py:444
  59.4 1.6 %collective-permute-start.15 = (f32[32,1152]{1,0:T(8,128)S(1)}, f32[32,1152]{1,0:T(8,128)S(1)}, u32[]{:S(2)}, u32[]{:S(2)}) collective-permute-start(f32[32,1152]{1,0:T(8,128)S(1)} %get-tuple-element.70.refs_2_), channel_id=1, source_target_pairs={{0,1},{1,0},{2,3},{3,2},{4,5},{5,4},{6,7},{7,6},{8,9},{9,8},{10,11... | collective-permute-start | bytes 442376 | tf_op jit(solution)/shard_map/ppermute | solution.py:452
  60.9 0.0 collective-permute-start.13
  60.9 0.0 collective-permute-done.18.refs_1_
  60.9 0.6 collective-permute-start.14
  61.6 0.1 collective-permute-done.19.refs_2_
  61.7 0.0 collective-permute-start.20
  61.7 1.3 %collective-permute-done.20.refs_3_ = f32[32,896]{1,0:T(8,128)S(1)} collective-permute-done((f32[32,896]{1,0:T(8,128)S(1)}, f32[32,896]{1,0:T(8,128)S(1)}, u32[]{:S(2)}, u32[]{:S(2)}) %collective-permute-start.20) | collective-permute-done | bytes 114720 | tf_op jit(solution)/shard_map/ppermute | solution.py:452
  63.0 3.3 %update_0_0.1.refs_4_ = f32[8,128,4096]{2,1,0:T(8,128)} custom-call(bf16[4,256,128]{2,1,0:T(8,128)(2,1)S(1)} %get-tuple-element.40.refs_0_, f32[32,896]{1,0:T(8,128)S(1)} %collective-permute-done.18.refs_1_, f32[32,896]{1,0:T(8,128)S(1)} %collective-permute-done.19.refs_2_, f32[32,896]{1,0:T(8,128)S(1)} %collective-permute-done.20.refs_3_, ...), custom_call_target="tpu_custom_call" | custom-call | flops 176160768 | bytes 7340032 | tf_op jit(solution)/shard_map/update_0_0/pallas_call | solution.py:418
  66.4 0.0 collective-permute-done.15.refs_1_
  66.4 0.0 collective-permute-done.21.refs_6_
  66.4 2.9 %update_1_0.1 = (f32[8,128,4096]{2,1,0:T(8,128)}, f32[4,32,4096]{2,1,0:T(8,128)}) custom-call(bf16[4,256,128]{2,1,0:T(8,128)(2,1)S(1)} %get-tuple-element.40.refs_0_, f32[32,1152]{1,0:T(8,128)S(1)} %collective-permute-done.15.refs_1_, f32[32,1152]{1,0:T(8,128)S(1)} %get-tuple-element.70.refs_2_, ...), custom_call_target="tpu_custom_call", output_to_operand_aliasing={{0}: (4, {})} | custom-call | flops 113246208 | bytes 4718592 | tf_op jit(solution)/shard_map/update_1_0/pallas_call | solution.py:418
  69.3 0.0 collective-permute-done.13.refs_1_
  69.3 0.0 collective-permute-done.14.refs_2_
  69.3 2.5 %update_1_1.1 = f32[8,128,4096]{2,1,0:T(8,128)} custom-call(bf16[4,256,128]{2,1,0:T(8,128)(2,1)S(1)} %get-tuple-element.40.refs_0_, f32[32,1152]{1,0:T(8,128)S(1)} %collective-permute-done.13.refs_1_, f32[32,1152]{1,0:T(8,128)S(1)} %collective-permute-done.14.refs_2_, ...), custom_call_target="tpu_custom_call", output_to_operand_aliasing={{}: (4, {})} | custom-call | flops 113246208 | bytes 4718592 | tf_op jit(solution)/shard_map/update_1_1/pallas_call | solution.py:418
  (9 shorter events, 0.2 us)
Async XLA Ops:
  0.6 25.6 %copy-start.3 = (s32[64]{0:T(128)S(1)}, s32[64]{0:T(128)}, u32[]{:S(2)}) copy-start(s32[64]{0:T(128)} %refs_0_.3) | copy-start | bytes 772
  0.6 25.5 %copy-start.1 = (f32[64,256]{1,0:T(8,128)S(1)}, f32[64,256]{1,0:T(8,128)}, u32[]{:S(2)}) copy-start(f32[64,256]{1,0:T(8,128)} %refs_1_.4) | copy-start | bytes 196612
  0.7 7.4 %copy-start = (bf16[4,32,4096]{2,1,0:T(8,128)(2,1)S(1)}, bf16[4,32,4096]{2,1,0:T(8,128)(2,1)}, u32[]{:S(2)}) copy-start(bf16[4,32,4096]{2,1,0:T(8,128)(2,1)} %refs_8_.1) | copy-start | bytes 3145732
  5.0 10.6 %copy-start.4 = (f32[32,1024]{1,0:T(8,128)S(1)}, f32[32,1024]{1,0:T(8,128)}, u32[]{:S(2)}) copy-start(f32[32,1024]{1,0:T(8,128)} %get-tuple-element.36) | copy-start | bytes 393220
  5.0 10.4 %collective-permute-start = (f32[32,1024]{1,0:T(8,128)}, f32[32,1024]{1,0:T(8,128)S(1)}, u32[]{:S(2)}, u32[]{:S(2)}) collective-permute-start(f32[32,1024]{1,0:T(8,128)} %get-tuple-element.37), channel_id=1, source_target_pairs={{0,1},{1,0},{2,3},{3,2},{4,5},{5,4},{6,7},{7,6},{8,9},{9,8},{10,11... | collective-permute-start | bytes 393224 | tf_op jit(solution)/shard_map/ppermute | solution.py:452
  8.1 26.6 %collective-permute-start.5 = (f32[4,32,2048]{2,1,0:T(8,128)S(1)}, f32[4,32,2048]{2,1,0:T(8,128)S(1)}, u32[]{:S(2)}, u32[]{:S(2)}) collective-permute-start(f32[4,32,2048]{2,1,0:T(8,128)S(1)} %dynamic-slice_convert_fusion), channel_id=1, source_target_pairs={{0,2},{2,0},{4,6},{6,4},{8,10},{10,8},{12,14},{14,12},{16,18},{18,... | collective-permute-start | bytes 3145736 | tf_op jit(solution)/shard_map/ppermute | solution.py:444
  8.2 7.4 %collective-permute-start.1 = (f32[32,1024]{1,0:T(8,128)}, f32[32,1024]{1,0:T(8,128)S(1)}, u32[]{:S(2)}, u32[]{:S(2)}) collective-permute-start(f32[32,1024]{1,0:T(8,128)} %get-tuple-element.38), channel_id=1, source_target_pairs={{0,2},{1,3},{2,0},{3,1},{4,6},{5,7},{6,4},{7,5},{8,10},{9,11},{10,... | collective-permute-start | bytes 393224 | tf_op jit(solution)/shard_map/ppermute | solution.py:452
  8.7 7.2 %collective-permute-start.2 = (f32[32,1024]{1,0:T(8,128)}, f32[32,1024]{1,0:T(8,128)S(1)}, u32[]{:S(2)}, u32[]{:S(2)}) collective-permute-start(f32[32,1024]{1,0:T(8,128)} %get-tuple-element.39), channel_id=1, source_target_pairs={{0,3},{1,2},{2,1},{3,0},{4,7},{5,6},{6,5},{7,4},{8,11},{9,10},{10,... | collective-permute-start | bytes 393224 | tf_op jit(solution)/shard_map/ppermute | solution.py:452
  8.7 0.8 %copy-start.2 = (bf16[32,512]{1,0:T(8,128)(2,1)S(1)}, bf16[32,512]{1,0:T(8,128)(2,1)}, u32[]{:S(2)}) copy-start(bf16[32,512]{1,0:T(8,128)(2,1)} %get-tuple-element.46.refs_0_) | copy-start | bytes 98308
  13.6 6.7 %collective-permute-start.6 = (f32[32,1152]{1,0:T(8,128)S(1)}, f32[32,1152]{1,0:T(8,128)S(1)}, u32[]{:S(2)}, u32[]{:S(2)}) collective-permute-start(f32[32,1152]{1,0:T(8,128)S(1)} %get-tuple-element.48), channel_id=1, source_target_pairs={{0,1},{1,0},{2,3},{3,2},{4,5},{5,4},{6,7},{7,6},{8,9},{9,8},{10,11... | collective-permute-start | bytes 442376 | tf_op jit(solution)/shard_map/ppermute | solution.py:452
  15.4 5.0 %collective-permute-start.7 = (f32[32,1152]{1,0:T(8,128)S(1)}, f32[32,1152]{1,0:T(8,128)S(1)}, u32[]{:S(2)}, u32[]{:S(2)}) collective-permute-start(f32[32,1152]{1,0:T(8,128)S(1)} %get-tuple-element.49), channel_id=1, source_target_pairs={{0,2},{1,3},{2,0},{3,1},{4,6},{5,7},{6,4},{7,5},{8,10},{9,11},{10,... | collective-permute-start | bytes 442376 | tf_op jit(solution)/shard_map/ppermute | solution.py:452
  15.6 6.9 %collective-permute-start.8 = (f32[32,1152]{1,0:T(8,128)S(1)}, f32[32,1152]{1,0:T(8,128)S(1)}, u32[]{:S(2)}, u32[]{:S(2)}) collective-permute-start(f32[32,1152]{1,0:T(8,128)S(1)} %get-tuple-element.50), channel_id=1, source_target_pairs={{0,3},{1,2},{2,1},{3,0},{4,7},{5,6},{6,5},{7,4},{8,11},{9,10},{10,... | collective-permute-start | bytes 442376 | tf_op jit(solution)/shard_map/ppermute | solution.py:452
  16.0 8.5 %collective-permute-start.3 = (f32[2,32,1024]{2,1,0:T(8,128)S(1)}, f32[2,32,1024]{2,1,0:T(8,128)S(1)}, u32[]{:S(2)}, u32[]{:S(2)}) collective-permute-start(f32[2,32,1024]{2,1,0:T(8,128)S(1)} %pad_maximum_fusion.1.foot_ref.refs_2_), channel_id=1, source_target_pairs={{0,4},{2,6},{4,0},{6,2},{8,12},{10,14},{12,8},{14,10},{16,20},{18,... | collective-permute-start | bytes 786440 | tf_op jit(solution)/shard_map/ppermute | solution.py:444
  22.5 9.6 %collective-permute-start.9 = (f32[2,32,1152]{2,1,0:T(8,128)S(1)}, f32[2,32,1152]{2,1,0:T(8,128)S(1)}, u32[]{:S(2)}, u32[]{:S(2)}) collective-permute-start(f32[2,32,1152]{2,1,0:T(8,128)S(1)} %pad_maximum_fusion.refs_5_), channel_id=1, source_target_pairs={{0,4},{2,6},{4,0},{6,2},{8,12},{10,14},{12,8},{14,10},{16,20},{18,... | collective-permute-start | bytes 884744 | tf_op jit(solution)/shard_map/ppermute | solution.py:444
  24.5 10.3 %collective-permute-start.4 = (f32[2,32,1024]{2,1,0:T(8,128)S(1)}, f32[2,32,1024]{2,1,0:T(8,128)S(1)}, u32[]{:S(2)}, u32[]{:S(2)}) collective-permute-start(f32[2,32,1024]{2,1,0:T(8,128)S(1)} %collective-permute-done.3._.refs_3_), channel_id=1, source_target_pairs={{0,8},{2,10},{4,28},{6,30},{8,16},{10,18},{12,4},{14,6},{16,24},{1... | collective-permute-start | bytes 786440 | tf_op jit(solution)/shard_map/ppermute | solution.py:444
  32.2 8.7 %collective-permute-start.10 = (f32[2,32,1152]{2,1,0:T(8,128)S(1)}, f32[2,32,1152]{2,1,0:T(8,128)S(1)}, u32[]{:S(2)}, u32[]{:S(2)}) collective-permute-start(f32[2,32,1152]{2,1,0:T(8,128)S(1)} %collective-permute-done.9.refs_6_), channel_id=1, source_target_pairs={{0,8},{2,10},{4,0},{6,2},{8,16},{10,18},{12,4},{14,6},{16,24},{18,... | collective-permute-start | bytes 884744 | tf_op jit(solution)/shard_map/ppermute | solution.py:444
  36.9 9.5 %collective-permute-start.16 = (f32[2,32,896]{2,1,0:T(8,128)S(1)}, f32[2,32,896]{2,1,0:T(8,128)S(1)}, u32[]{:S(2)}, u32[]{:S(2)}) collective-permute-start(f32[2,32,896]{2,1,0:T(8,128)S(1)} %get-tuple-element.65), channel_id=1, source_target_pairs={{0,4},{2,6},{4,12},{6,14},{8,0},{10,2},{12,20},{14,22},{16,8},{18,... | collective-permute-start | bytes 688136 | tf_op jit(solution)/shard_map/ppermute | solution.py:444
  42.5 9.3 %collective-permute-start.11 = (f32[2,32,1152]{2,1,0:T(8,128)S(1)}, f32[2,32,1152]{2,1,0:T(8,128)S(1)}, u32[]{:S(2)}, u32[]{:S(2)}) collective-permute-start(f32[2,32,1152]{2,1,0:T(8,128)S(1)} %get-tuple-element.61), channel_id=1, source_target_pairs={{0,24},{2,26},{4,12},{6,14},{8,0},{10,2},{12,20},{14,22},{16,8},{1... | collective-permute-start | bytes 884744 | tf_op jit(solution)/shard_map/ppermute | solution.py:444
  46.4 7.7 %collective-permute-start.17 = (f32[2,32,896]{2,1,0:T(8,128)S(1)}, f32[2,32,896]{2,1,0:T(8,128)S(1)}, u32[]{:S(2)}, u32[]{:S(2)}) collective-permute-start(f32[2,32,896]{2,1,0:T(8,128)S(1)} %add.53), channel_id=1, source_target_pairs={{0,4},{2,6},{4,0},{6,2},{8,12},{10,14},{12,8},{14,10},{16,20},{18,... | collective-permute-start | bytes 688136 | tf_op jit(solution)/shard_map/ppermute | solution.py:444
  46.5 19.9 %collective-permute-start.21 = (f32[4,32,2048]{2,1,0:T(8,128)S(1)}, f32[4,32,2048]{2,1,0:T(8,128)S(1)}, u32[]{:S(2)}, u32[]{:S(2)}) collective-permute-start(f32[4,32,2048]{2,1,0:T(8,128)S(1)} %get-tuple-element.67), channel_id=1, source_target_pairs={{0,2},{2,0},{4,6},{6,4},{8,10},{10,8},{12,14},{14,12},{16,18},{18,... | collective-permute-start | bytes 3145736 | tf_op jit(solution)/shard_map/ppermute | solution.py:444
  51.8 7.5 %collective-permute-start.12 = (f32[2,32,1152]{2,1,0:T(8,128)S(1)}, f32[2,32,1152]{2,1,0:T(8,128)S(1)}, u32[]{:S(2)}, u32[]{:S(2)}) collective-permute-start(f32[2,32,1152]{2,1,0:T(8,128)S(1)} %add.48), channel_id=1, source_target_pairs={{0,4},{2,6},{4,0},{6,2},{8,12},{10,14},{12,8},{14,10},{16,20},{18,... | collective-permute-start | bytes 884744 | tf_op jit(solution)/shard_map/ppermute | solution.py:444
  54.1 6.8 %collective-permute-start.18 = (f32[32,896]{1,0:T(8,128)S(1)}, f32[32,896]{1,0:T(8,128)S(1)}, u32[]{:S(2)}, u32[]{:S(2)}) collective-permute-start(f32[32,896]{1,0:T(8,128)S(1)} %get-tuple-element.73.refs_4_), channel_id=1, source_target_pairs={{0,1},{1,0},{2,3},{3,2},{4,5},{5,4},{6,7},{7,6},{8,9},{9,8},{10,11... | collective-permute-start | bytes 344072 | tf_op jit(solution)/shard_map/ppermute | solution.py:452
  55.7 6.0 %collective-permute-start.19 = (f32[32,896]{1,0:T(8,128)S(1)}, f32[32,896]{1,0:T(8,128)S(1)}, u32[]{:S(2)}, u32[]{:S(2)}) collective-permute-start(f32[32,896]{1,0:T(8,128)S(1)} %get-tuple-element.72), channel_id=1, source_target_pairs={{0,3},{1,2},{2,1},{3,0},{4,7},{5,6},{6,5},{7,4},{8,11},{9,10},{10,... | collective-permute-start | bytes 344072 | tf_op jit(solution)/shard_map/ppermute | solution.py:452
  59.4 7.0 %collective-permute-start.15 = (f32[32,1152]{1,0:T(8,128)S(1)}, f32[32,1152]{1,0:T(8,128)S(1)}, u32[]{:S(2)}, u32[]{:S(2)}) collective-permute-start(f32[32,1152]{1,0:T(8,128)S(1)} %get-tuple-element.70.refs_2_), channel_id=1, source_target_pairs={{0,1},{1,0},{2,3},{3,2},{4,5},{5,4},{6,7},{7,6},{8,9},{9,8},{10,11... | collective-permute-start | bytes 442376 | tf_op jit(solution)/shard_map/ppermute | solution.py:452
  60.9 8.4 %collective-permute-start.13 = (f32[32,1152]{1,0:T(8,128)S(1)}, f32[32,1152]{1,0:T(8,128)S(1)}, u32[]{:S(2)}, u32[]{:S(2)}) collective-permute-start(f32[32,1152]{1,0:T(8,128)S(1)} %get-tuple-element.71), channel_id=1, source_target_pairs={{0,3},{1,2},{2,1},{3,0},{4,7},{5,6},{6,5},{7,4},{8,11},{9,10},{10,... | collective-permute-start | bytes 442376 | tf_op jit(solution)/shard_map/ppermute | solution.py:452
  60.9 8.4 %collective-permute-start.14 = (f32[32,1152]{1,0:T(8,128)S(1)}, f32[32,1152]{1,0:T(8,128)S(1)}, u32[]{:S(2)}, u32[]{:S(2)}) collective-permute-start(f32[32,1152]{1,0:T(8,128)S(1)} %get-tuple-element.71), channel_id=1, source_target_pairs={{0,2},{1,3},{2,0},{3,1},{4,6},{5,7},{6,4},{7,5},{8,10},{9,11},{10,... | collective-permute-start | bytes 442376 | tf_op jit(solution)/shard_map/ppermute | solution.py:452
  61.7 1.3 %collective-permute-start.20 = (f32[32,896]{1,0:T(8,128)S(1)}, f32[32,896]{1,0:T(8,128)S(1)}, u32[]{:S(2)}, u32[]{:S(2)}) collective-permute-start(f32[32,896]{1,0:T(8,128)S(1)} %get-tuple-element.72), channel_id=1, source_target_pairs={{0,2},{1,3},{2,0},{3,1},{4,6},{5,7},{6,4},{7,5},{8,10},{9,11},{10,... | collective-permute-start | bytes 344072 | tf_op jit(solution)/shard_map/ppermute | solution.py:452

commit v12 on v6

--- a/solution.py
+++ b/solution.py
@@ -95,10 +95,8 @@
     count = groups * SUBLANES
     if first:
         order_ref, start_ref, len_ref, table_ref, vol_ref, *refs = refs
-    elif extra:
-        start_buf, len_buf, given_ref, vol_ref, *refs = refs
-    else:
-        given_ref, vol_ref, *refs = refs
+    else:
+        order_ref, table_ref, vol_ref, *refs, rows_ref = refs
     outs, refs = refs[:len(halves) * groups], refs[len(halves) * groups:]
     if first:
         left_ref, buf, sems, table_buf, order_buf, start_buf, len_buf, rows_ref, small_sems = refs
@@ -128,7 +126,8 @@
         small[2].wait()
         small[3].wait()
     else:
-        left = given_ref[...]
+        both = jnp.concatenate(split(slice_weights(dims, 1, order_ref, table_ref, rows_ref)), axis=0)
+        left = jnp.concatenate([both, both], axis=1)
     if extra:
         shape = (SUBLANES, LANES)
         angle, lane = low_bits(iota(shape, 0), per), iota(shape, 1)
@@ -162,14 +161,14 @@
     shapes = [out] * (len(halves) * groups)
     scratch = [] if keep else [pltpu.VMEM(columns, F32)]
     scratch += [pltpu.SemaphoreType.DMA((len(halves), zdev // zb))]
-    args, specs, limit = [given, volume], [IN_VMEM, ANYWHERE], 40
     if first:
         scratch += [pltpu.VMEM(table.shape, F32)] + [pltpu.SMEM(a.shape, a.dtype) for a in small]
         scratch += [pltpu.VMEM((count, all_cells), F32), pltpu.SemaphoreType.DMA((4,))]
         args, specs, limit = [*small, table, volume], [ANYWHERE] * 5, 58
         shapes += [left]
-    elif extra:
-        args, specs, limit = [*small[1:], *args], [IN_SMEM] * 2 + specs, 50
+    else:
+        scratch += [pltpu.VMEM((count, all_cells), F32)]
+        args, specs, limit = [small[0], table, volume], [IN_SMEM, IN_VMEM, ANYWHERE], 40
     if keep:
         shapes += [jax.ShapeDtypeStruct(columns, F32)]
     size = zdev * cells * width * len(halves)
@@ -487,6 +486,7 @@
             parts += made[:len(halves) * groups]
             if left is None:
                 left = made[-1]
+                parts[0], table = lax.optimization_barrier((parts[0], table))
             elif c:
                 kept[c] += [(h, made[-1]) for h in halves]
         parts = [spread(parts[h * groups + d], h, d) for h in range(2) for d in range(groups)]

time: 71 us -> 70.8 us (level)
  local copies, waits for them, and re-layouts: 0.78 us -> 0.02 us
    unnamed x10 -> x8, local copies, waits for them, and re-layouts: 0.78 us -> 0.02 us
  transfers between devices with their start and end apart: 22 -> 22, of which waited for: 9 -> 9; matrix products, arithmetic and copies ran while one was open for 0% -> 0% of each run, Pallas kernels for 25% -> 26%
where the time goes in v12:
time: 70.8 us; the launch traced here: 70.6 us
  Pallas kernels  25.1 us (35%)
  starting transfers between devices  24.5 us (35%)
  waiting for transfers between devices  19.8 us (28%)
  between operations  0.84 us (1%)
    ppermute x10, waiting for transfers between devices, along(): return lax.ppermute(value, 'slab', pairs)  15.3 us
    ppermute x10, starting transfers between devices, along(): return lax.ppermute(value, 'slab', pairs)  14.3 us
    ppermute x12, starting transfers between devices, spread(): return lax.ppermute(value, ('slab', 'ang'), pairs)  10.2 us
    pallas_call x2, Pallas kernels, ray_sums(): pl.pallas_call(functools.partial(rays_kernel, dims, first, keep, extra, h...  9.06 us
    pallas_call x3, Pallas kernels, update_step(): pl.pallas_call(functools.partial(update_kernel, dims, first, halves, tota...  8.7 us
    ppermute x12, waiting for transfers between devices, spread(): return lax.ppermute(value, ('slab', 'ang'), pairs)  4.46 us
    pallas_call x1, Pallas kernels, prepare_step(): pl.pallas_call(functools.partial(prepare_kernel, dims, rdev, total // 2,...  4.08 us
    pallas_call x2, Pallas kernels, residual_step(): pl.pallas_call(functools.partial(residual_kernel, dims, first, total // 2...  3.3 us
  transfers between devices with their start and end apart: 22, of which 9 were waited for; matrix products, arithmetic and copies ran while one was open for 0% of the time, Pallas kernels for 26%

profile of v12, /device:TPU:0, one launch (start us, length us, event | category | flops | bytes accessed | tf_op | source)
XLA Modules:
  0.0 70.6 jit_solution(13352010123409807892)
XLA Ops:
  0.6 0.0 copy-start.2
  0.6 0.0 copy-start.1
  0.7 0.0 copy-start
  0.7 4.6 %ray_sums_0_0.1 = (f32[8,4224]{1,0:T(8,128)}, f32[8,4224]{1,0:T(8,128)}, f32[8,4224]{1,0:T(8,128)}, f32[8,4224]{1,0:T(8,128)}, bf16[32,512]{1,0:T(8,128)(2,1)}) custom-call(s32[64]{0:T(128)} %refs_0_.5, s32[1,4]{1,0:T(1,128)} %refs_1_.1, s32[1,4]{1,0:T(1,128)} %refs_2_.2, f32[64,256]{1,0:T(8,128)} %refs_1_.3, f32[8,128,4096]{2,1,0:T(8,128)} %refs_2_.3), custom_call_target="tpu_custom_call" | custom-call | flops 67108864 | bytes 8388608 | tf_op jit(solution)/shard_map/ray_sums_0_0/pallas_call | solution.py:175
  5.3 0.0 copy-start.3
  5.3 3.0 %collective-permute-start = (f32[8,4224]{1,0:T(8,128)}, f32[8,4224]{1,0:T(8,128)S(1)}, u32[]{:S(2)}, u32[]{:S(2)}) collective-permute-start(f32[8,4224]{1,0:T(8,128)} %get-tuple-element.40), channel_id=1, source_target_pairs={{0,1},{1,0},{2,3},{3,2},{4,5},{5,4},{6,7},{7,6},{8,9},{9,8},{10,11... | collective-permute-start | bytes 405512 | tf_op jit(solution)/shard_map/ppermute | solution.py:455
  8.4 0.0 copy-done
  8.4 0.1 dynamic-slice_convert_fusion
  8.5 0.1 collective-permute-start.5
  8.5 0.5 collective-permute-start.1
  9.0 0.0 collective-permute-start.2
  9.0 0.0 copy-done.2
  9.0 0.0 copy-done.1
  9.1 4.4 %ray_sums_1_0.1 = (f32[8,4096]{1,0:T(8,128)S(1)}, f32[8,4096]{1,0:T(8,128)S(1)}, f32[8,4096]{1,0:T(8,128)S(1)}, f32[8,4096]{1,0:T(8,128)S(1)}, f32[2,8,128,1024]{3,2,1,0:T(8,128)S(1)}) custom-call(s32[64]{0:T(128)S(1)} %copy-done.2, f32[64,256]{1,0:T(8,128)S(1)} %copy-done.1, f32[8,128,4096]{2,1,0:T(8,128)} %refs_2_.3), custom_call_target="tpu_custom_call" | custom-call | flops 67108864 | bytes 8388608 | tf_op jit(solution)/shard_map/ray_sums_1_0/pallas_call | solution.py:175
  13.5 1.8 %collective-permute-start.6 = (f32[8,4096]{1,0:T(8,128)S(1)}, f32[8,4096]{1,0:T(8,128)S(1)}, u32[]{:S(2)}, u32[]{:S(2)}) collective-permute-start(f32[8,4096]{1,0:T(8,128)S(1)} %get-tuple-element.50), channel_id=1, source_target_pairs={{0,1},{1,0},{2,3},{3,2},{4,5},{5,4},{6,7},{7,6},{8,9},{9,8},{10,11... | collective-permute-start | bytes 393224 | tf_op jit(solution)/shard_map/ppermute | solution.py:455
  15.2 0.0 collective-permute-done
  15.2 0.2 collective-permute-start.7
  15.4 0.0 copy-done.3
  15.4 0.0 collective-permute-done.1
  15.4 0.3 collective-permute-start.8
  15.8 0.0 collective-permute-done.2
  15.8 1.7 %collective-permute-start.3 = (f32[2,8,4224]{2,1,0:T(8,128)S(1)}, f32[2,8,4224]{2,1,0:T(8,128)S(1)}, u32[]{:S(2)}, u32[]{:S(2)}) collective-permute-start(f32[2,8,4224]{2,1,0:T(8,128)S(1)} %pad_maximum_fusion.foot_ref.refs_2_), channel_id=1, source_target_pairs={{0,4},{2,6},{4,0},{6,2},{8,12},{10,14},{12,8},{14,10},{16,20},{18,... | collective-permute-start | bytes 811016 | tf_op jit(solution)/shard_map/ppermute | solution.py:447
  17.6 2.3 %collective-permute-done.6 = f32[8,4096]{1,0:T(8,128)S(1)} collective-permute-done((f32[8,4096]{1,0:T(8,128)S(1)}, f32[8,4096]{1,0:T(8,128)S(1)}, u32[]{:S(2)}, u32[]{:S(2)}) %collective-permute-start.6) | collective-permute-done | bytes 131104 | tf_op jit(solution)/shard_map/ppermute | solution.py:455
  19.8 0.0 collective-permute-done.7
  19.9 1.8 %collective-permute-done.8 = f32[8,4096]{1,0:T(8,128)S(1)} collective-permute-done((f32[8,4096]{1,0:T(8,128)S(1)}, f32[8,4096]{1,0:T(8,128)S(1)}, u32[]{:S(2)}, u32[]{:S(2)}) %collective-permute-start.8) | collective-permute-done | bytes 131104 | tf_op jit(solution)/shard_map/ppermute | solution.py:455
  21.7 1.9 %collective-permute-start.9 = (f32[2,8,4096]{2,1,0:T(8,128)S(1)}, f32[2,8,4096]{2,1,0:T(8,128)S(1)}, u32[]{:S(2)}, u32[]{:S(2)}) collective-permute-start(f32[2,8,4096]{2,1,0:T(8,128)S(1)} %pad_maximum_fusion.1.refs_5_), channel_id=1, source_target_pairs={{0,4},{2,6},{4,0},{6,2},{8,12},{10,14},{12,8},{14,10},{16,20},{18,... | collective-permute-start | bytes 786440 | tf_op jit(solution)/shard_map/ppermute | solution.py:447
  23.5 0.9 %collective-permute-done.3._.refs_3_ = f32[2,8,4224]{2,1,0:T(8,128)S(1)} collective-permute-done((f32[2,8,4224]{2,1,0:T(8,128)S(1)}, f32[2,8,4224]{2,1,0:T(8,128)S(1)}, u32[]{:S(2)}, u32[]{:S(2)}) %collective-permute-start.3) | collective-permute-done | bytes 270368 | tf_op jit(solution)/shard_map/ppermute | solution.py:447
  24.5 1.7 %collective-permute-start.4 = (f32[2,8,4224]{2,1,0:T(8,128)S(1)}, f32[2,8,4224]{2,1,0:T(8,128)S(1)}, u32[]{:S(2)}, u32[]{:S(2)}) collective-permute-start(f32[2,8,4224]{2,1,0:T(8,128)S(1)} %collective-permute-done.3._.refs_3_), channel_id=1, source_target_pairs={{0,8},{2,10},{4,28},{6,30},{8,16},{10,18},{12,4},{14,6},{16,24},{1... | collective-permute-start | bytes 811016 | tf_op jit(solution)/shard_map/ppermute | solution.py:447
  26.2 4.1 %prepare.1 = (f32[2,8,128,1024]{3,2,1,0:T(8,128)S(1)}, bf16[4,256,128]{2,1,0:T(8,128)(2,1)S(1)}) custom-call(s32[64]{0:T(128)S(1)} %copy-done.2, f32[64,256]{1,0:T(8,128)S(1)} %copy-done.1, f32[2,8,4224]{2,1,0:T(8,128)S(1)} %pad_maximum_fusion.foot_ref.refs_2_, f32[2,8,4224]{2,1,0:T(8,128)S(1)} %collective-permute-done.3._.refs_3_, f32[8,128,4096]{2,1,0:T(8,128)} %refs_2_.3), custom_call_target="tpu_custom_call" | custom-call | bytes 8388608 | tf_op jit(solution)/shard_map/prepare/pallas_call | solution.py:251
  30.3 0.3 collective-permute-done.9.refs_6_
  30.6 1.8 %collective-permute-start.10 = (f32[2,8,4096]{2,1,0:T(8,128)S(1)}, f32[2,8,4096]{2,1,0:T(8,128)S(1)}, u32[]{:S(2)}, u32[]{:S(2)}) collective-permute-start(f32[2,8,4096]{2,1,0:T(8,128)S(1)} %collective-permute-done.9.refs_6_), channel_id=1, source_target_pairs={{0,8},{2,10},{4,0},{6,2},{8,16},{10,18},{12,4},{14,6},{16,24},{18,... | collective-permute-start | bytes 786440 | tf_op jit(solution)/shard_map/ppermute | solution.py:447
  32.4 1.8 %collective-permute-done.4.refs_4_ = f32[2,8,4224]{2,1,0:T(8,128)S(1)} collective-permute-done((f32[2,8,4224]{2,1,0:T(8,128)S(1)}, f32[2,8,4224]{2,1,0:T(8,128)S(1)}, u32[]{:S(2)}, u32[]{:S(2)}) %collective-permute-start.4) | collective-permute-done | bytes 270368 | tf_op jit(solution)/shard_map/ppermute | solution.py:447
  34.2 0.0 collective-permute-done.5.refs_6_.refs_9_
  34.2 2.1 %residual_0.1 = (f32[4,32,1024]{2,1,0:T(8,128)S(1)}, f32[4,32,1024]{2,1,0:T(8,128)S(1)}, f32[2,32,1024]{2,1,0:T(8,128)S(1)}, f32[2,32,1024]{2,1,0:T(8,128)S(1)},...) custom-call(s32[64]{0:T(128)S(1)} %copy-done.2, ...), custom_call_target="tpu_custom_call" | custom-call | flops 603979776 | bytes 3670016 | tf_op jit(solution)/shard_map/residual_0/pallas_call | solution.py:345
  36.3 0.8 %collective-permute-start.16 = (f32[2,32,1024]{2,1,0:T(8,128)S(1)}, f32[2,32,1024]{2,1,0:T(8,128)S(1)}, u32[]{:S(2)}, u32[]{:S(2)}) collective-permute-start(f32[2,32,1024]{2,1,0:T(8,128)S(1)} %get-tuple-element.67), channel_id=1, source_target_pairs={{0,4},{2,6},{4,12},{6,14},{8,0},{10,2},{12,20},{14,22},{16,8},{18,... | collective-permute-start | bytes 786440 | tf_op jit(solution)/shard_map/ppermute | solution.py:447
  37.1 2.3 %collective-permute-done.10.refs_7_ = f32[2,8,4096]{2,1,0:T(8,128)S(1)} collective-permute-done((f32[2,8,4096]{2,1,0:T(8,128)S(1)}, f32[2,8,4096]{2,1,0:T(8,128)S(1)}, u32[]{:S(2)}, u32[]{:S(2)}) %collective-permute-start.10) | collective-permute-done | bytes 262176 | tf_op jit(solution)/shard_map/ppermute | solution.py:447
  39.4 1.2 %residual_1.1 = (f32[4,32,2048]{2,1,0:T(8,128)S(1)}, f32[4,32,2048]{2,1,0:T(8,128)S(1)}, f32[2,32,1024]{2,1,0:T(8,128)S(1)}, f32[2,32,1024]{2,1,0:T(8,128)S(1)}, f32[2,32,1024]{2,1,0:T(8,128)S(1)}) custom-call(bf16[256,192]{1,0:T(8,128)(2,1)S(1)} %get-tuple-element.44.refs_0_, bf16[256,192]{1,0:T(8,128)(2,1)S(1)} %get-tuple-element.45.refs_1_, ...), custom_call_target="tpu_custom_call" | custom-call | flops 603979776 | bytes 3670016 | tf_op jit(solution)/shard_map/residual_1/pallas_call | solution.py:345
  40.7 0.1 collective-permute-start.21
  40.7 3.1 %collective-permute-start.11 = (f32[2,32,1024]{2,1,0:T(8,128)S(1)}, f32[2,32,1024]{2,1,0:T(8,128)S(1)}, u32[]{:S(2)}, u32[]{:S(2)}) collective-permute-start(f32[2,32,1024]{2,1,0:T(8,128)S(1)} %get-tuple-element.63), channel_id=1, source_target_pairs={{0,24},{2,26},{4,12},{6,14},{8,0},{10,2},{12,20},{14,22},{16,8},{1... | collective-permute-start | bytes 786440 | tf_op jit(solution)/shard_map/ppermute | solution.py:447
  43.8 0.0 collective-permute-done.16
  43.9 0.1 collective-permute-start.17
  43.9 6.0 %collective-permute-done.11 = f32[2,32,1024]{2,1,0:T(8,128)S(1)} collective-permute-done((f32[2,32,1024]{2,1,0:T(8,128)S(1)}, f32[2,32,1024]{2,1,0:T(8,128)S(1)}, u32[]{:S(2)}, u32[]{:S(2)}) %collective-permute-start.11) | collective-permute-done | bytes 262176 | tf_op jit(solution)/shard_map/ppermute | solution.py:447
  50.0 3.1 %collective-permute-start.12 = (f32[2,32,1024]{2,1,0:T(8,128)S(1)}, f32[2,32,1024]{2,1,0:T(8,128)S(1)}, u32[]{:S(2)}, u32[]{:S(2)}) collective-permute-start(f32[2,32,1024]{2,1,0:T(8,128)S(1)} %add.48), channel_id=1, source_target_pairs={{0,4},{2,6},{4,0},{6,2},{8,12},{10,14},{12,8},{14,10},{16,20},{18,... | collective-permute-start | bytes 786440 | tf_op jit(solution)/shard_map/ppermute | solution.py:447
  53.1 0.0 collective-permute-done.17
  53.1 0.6 collective-permute-start.18
  53.7 1.1 %collective-permute-start.19 = (f32[32,1024]{1,0:T(8,128)S(1)}, f32[32,1024]{1,0:T(8,128)S(1)}, u32[]{:S(2)}, u32[]{:S(2)}) collective-permute-start(f32[32,1024]{1,0:T(8,128)S(1)} %get-tuple-element.73), channel_id=1, source_target_pairs={{0,2},{1,3},{2,0},{3,1},{4,6},{5,7},{6,4},{7,5},{8,10},{9,11},{10,... | collective-permute-start | bytes 393224 | tf_op jit(solution)/shard_map/ppermute | solution.py:455
  54.8 0.5 collective-permute-start.20
  55.3 3.9 %collective-permute-done.12 = f32[2,32,1024]{2,1,0:T(8,128)S(1)} collective-permute-done((f32[2,32,1024]{2,1,0:T(8,128)S(1)}, f32[2,32,1024]{2,1,0:T(8,128)S(1)}, u32[]{:S(2)}, u32[]{:S(2)}) %collective-permute-start.12) | collective-permute-done | bytes 262176 | tf_op jit(solution)/shard_map/ppermute | solution.py:447
  59.3 1.6 %collective-permute-start.15 = (f32[32,1024]{1,0:T(8,128)S(1)}, f32[32,1024]{1,0:T(8,128)S(1)}, u32[]{:S(2)}, u32[]{:S(2)}) collective-permute-start(f32[32,1024]{1,0:T(8,128)S(1)} %get-tuple-element.74.refs_2_), channel_id=1, source_target_pairs={{0,1},{1,0},{2,3},{3,2},{4,5},{5,4},{6,7},{7,6},{8,9},{9,8},{10,11... | collective-permute-start | bytes 393224 | tf_op jit(solution)/shard_map/ppermute | solution.py:455
  60.8 0.0 collective-permute-done.18.refs_1_
  60.8 0.0 collective-permute-start.13
  60.8 0.0 collective-permute-done.19.refs_2_
  60.9 0.6 collective-permute-start.14
  61.5 0.4 collective-permute-done.20.refs_3_
  61.9 3.6 %update_0_0.1.refs_4_ = f32[8,128,4096]{2,1,0:T(8,128)} custom-call(bf16[4,256,128]{2,1,0:T(8,128)(2,1)S(1)} %get-tuple-element.43.refs_0_, f32[32,1024]{1,0:T(8,128)S(1)} %collective-permute-done.18.refs_1_, f32[32,1024]{1,0:T(8,128)S(1)} %collective-permute-done.19.refs_2_, f32[32,1024]{1,0:T(8,128)S(1)} %collective-permute-done.20.refs_3_, ...), custom_call_target="tpu_custom_call" | custom-call | flops 201326592 | bytes 8388608 | tf_op jit(solution)/shard_map/update_0_0/pallas_call | solution.py:421
  65.5 0.0 collective-permute-done.15.refs_1_
  65.5 0.0 collective-permute-done.21.refs_6_
  65.5 2.7 %update_1_0.1 = (f32[8,128,4096]{2,1,0:T(8,128)}, f32[4,32,4096]{2,1,0:T(8,128)}) custom-call(bf16[4,256,128]{2,1,0:T(8,128)(2,1)S(1)} %get-tuple-element.43.refs_0_, f32[32,1024]{1,0:T(8,128)S(1)} %collective-permute-done.15.refs_1_, f32[32,1024]{1,0:T(8,128)S(1)} %get-tuple-element.74.refs_2_, ...), custom_call_target="tpu_custom_call", output_to_operand_aliasing={{0}: (4, {})} | custom-call | flops 100663296 | bytes 4194304 | tf_op jit(solution)/shard_map/update_1_0/pallas_call | solution.py:421
  68.3 0.0 collective-permute-done.13.refs_1_
  68.3 0.0 collective-permute-done.14.refs_2_
  68.3 2.3 %update_1_1.1 = f32[8,128,4096]{2,1,0:T(8,128)} custom-call(bf16[4,256,128]{2,1,0:T(8,128)(2,1)S(1)} %get-tuple-element.43.refs_0_, f32[32,1024]{1,0:T(8,128)S(1)} %collective-permute-done.13.refs_1_, f32[32,1024]{1,0:T(8,128)S(1)} %collective-permute-done.14.refs_2_, ...), custom_call_target="tpu_custom_call", output_to_operand_aliasing={{}: (4, {})} | custom-call | flops 100663296 | bytes 4194304 | tf_op jit(solution)/shard_map/update_1_1/pallas_call | solution.py:421
  (9 shorter events, 0.3 us)
Async XLA Ops:
  0.6 8.4 %copy-start.2 = (s32[64]{0:T(128)S(1)}, s32[64]{0:T(128)}, u32[]{:S(2)}) copy-start(s32[64]{0:T(128)} %refs_0_.5) | copy-start | bytes 772
  0.6 8.4 %copy-start.1 = (f32[64,256]{1,0:T(8,128)S(1)}, f32[64,256]{1,0:T(8,128)}, u32[]{:S(2)}) copy-start(f32[64,256]{1,0:T(8,128)} %refs_1_.3) | copy-start | bytes 196612
  0.7 7.7 %copy-start = (bf16[4,32,4096]{2,1,0:T(8,128)(2,1)S(1)}, bf16[4,32,4096]{2,1,0:T(8,128)(2,1)}, u32[]{:S(2)}) copy-start(bf16[4,32,4096]{2,1,0:T(8,128)(2,1)} %refs_8_.1) | copy-start | bytes 3145732
  5.3 10.1 %copy-start.3 = (f32[8,4224]{1,0:T(8,128)S(1)}, f32[8,4224]{1,0:T(8,128)}, u32[]{:S(2)}) copy-start(f32[8,4224]{1,0:T(8,128)} %get-tuple-element.39) | copy-start | bytes 405508
  5.3 9.9 %collective-permute-start = (f32[8,4224]{1,0:T(8,128)}, f32[8,4224]{1,0:T(8,128)S(1)}, u32[]{:S(2)}, u32[]{:S(2)}) collective-permute-start(f32[8,4224]{1,0:T(8,128)} %get-tuple-element.40), channel_id=1, source_target_pairs={{0,1},{1,0},{2,3},{3,2},{4,5},{5,4},{6,7},{7,6},{8,9},{9,8},{10,11... | collective-permute-start | bytes 405512 | tf_op jit(solution)/shard_map/ppermute | solution.py:455
  8.5 25.8 %collective-permute-start.5 = (f32[4,32,2048]{2,1,0:T(8,128)S(1)}, f32[4,32,2048]{2,1,0:T(8,128)S(1)}, u32[]{:S(2)}, u32[]{:S(2)}) collective-permute-start(f32[4,32,2048]{2,1,0:T(8,128)S(1)} %dynamic-slice_convert_fusion), channel_id=1, source_target_pairs={{0,2},{2,0},{4,6},{6,4},{8,10},{10,8},{12,14},{14,12},{16,18},{18,... | collective-permute-start | bytes 3145736 | tf_op jit(solution)/shard_map/ppermute | solution.py:447
  8.5 6.9 %collective-permute-start.1 = (f32[8,4224]{1,0:T(8,128)}, f32[8,4224]{1,0:T(8,128)S(1)}, u32[]{:S(2)}, u32[]{:S(2)}) collective-permute-start(f32[8,4224]{1,0:T(8,128)} %get-tuple-element.41), channel_id=1, source_target_pairs={{0,2},{1,3},{2,0},{3,1},{4,6},{5,7},{6,4},{7,5},{8,10},{9,11},{10,... | collective-permute-start | bytes 405512 | tf_op jit(solution)/shard_map/ppermute | solution.py:455
  9.0 6.7 %collective-permute-start.2 = (f32[8,4224]{1,0:T(8,128)}, f32[8,4224]{1,0:T(8,128)S(1)}, u32[]{:S(2)}, u32[]{:S(2)}) collective-permute-start(f32[8,4224]{1,0:T(8,128)} %get-tuple-element.42), channel_id=1, source_target_pairs={{0,3},{1,2},{2,1},{3,0},{4,7},{5,6},{6,5},{7,4},{8,11},{9,10},{10,... | collective-permute-start | bytes 405512 | tf_op jit(solution)/shard_map/ppermute | solution.py:455
  13.5 6.4 %collective-permute-start.6 = (f32[8,4096]{1,0:T(8,128)S(1)}, f32[8,4096]{1,0:T(8,128)S(1)}, u32[]{:S(2)}, u32[]{:S(2)}) collective-permute-start(f32[8,4096]{1,0:T(8,128)S(1)} %get-tuple-element.50), channel_id=1, source_target_pairs={{0,1},{1,0},{2,3},{3,2},{4,5},{5,4},{6,7},{7,6},{8,9},{9,8},{10,11... | collective-permute-start | bytes 393224 | tf_op jit(solution)/shard_map/ppermute | solution.py:455
  15.2 4.6 %collective-permute-start.7 = (f32[8,4096]{1,0:T(8,128)S(1)}, f32[8,4096]{1,0:T(8,128)S(1)}, u32[]{:S(2)}, u32[]{:S(2)}) collective-permute-start(f32[8,4096]{1,0:T(8,128)S(1)} %get-tuple-element.51), channel_id=1, source_target_pairs={{0,2},{1,3},{2,0},{3,1},{4,6},{5,7},{6,4},{7,5},{8,10},{9,11},{10,... | collective-permute-start | bytes 393224 | tf_op jit(solution)/shard_map/ppermute | solution.py:455
  15.4 6.2 %collective-permute-start.8 = (f32[8,4096]{1,0:T(8,128)S(1)}, f32[8,4096]{1,0:T(8,128)S(1)}, u32[]{:S(2)}, u32[]{:S(2)}) collective-permute-start(f32[8,4096]{1,0:T(8,128)S(1)} %get-tuple-element.52), channel_id=1, source_target_pairs={{0,3},{1,2},{2,1},{3,0},{4,7},{5,6},{6,5},{7,4},{8,11},{9,10},{10,... | collective-permute-start | bytes 393224 | tf_op jit(solution)/shard_map/ppermute | solution.py:455
  15.8 8.6 %collective-permute-start.3 = (f32[2,8,4224]{2,1,0:T(8,128)S(1)}, f32[2,8,4224]{2,1,0:T(8,128)S(1)}, u32[]{:S(2)}, u32[]{:S(2)}) collective-permute-start(f32[2,8,4224]{2,1,0:T(8,128)S(1)} %pad_maximum_fusion.foot_ref.refs_2_), channel_id=1, source_target_pairs={{0,4},{2,6},{4,0},{6,2},{8,12},{10,14},{12,8},{14,10},{16,20},{18,... | collective-permute-start | bytes 811016 | tf_op jit(solution)/shard_map/ppermute | solution.py:447
  21.7 8.9 %collective-permute-start.9 = (f32[2,8,4096]{2,1,0:T(8,128)S(1)}, f32[2,8,4096]{2,1,0:T(8,128)S(1)}, u32[]{:S(2)}, u32[]{:S(2)}) collective-permute-start(f32[2,8,4096]{2,1,0:T(8,128)S(1)} %pad_maximum_fusion.1.refs_5_), channel_id=1, source_target_pairs={{0,4},{2,6},{4,0},{6,2},{8,12},{10,14},{12,8},{14,10},{16,20},{18,... | collective-permute-start | bytes 786440 | tf_op jit(solution)/shard_map/ppermute | solution.py:447
  24.5 9.7 %collective-permute-start.4 = (f32[2,8,4224]{2,1,0:T(8,128)S(1)}, f32[2,8,4224]{2,1,0:T(8,128)S(1)}, u32[]{:S(2)}, u32[]{:S(2)}) collective-permute-start(f32[2,8,4224]{2,1,0:T(8,128)S(1)} %collective-permute-done.3._.refs_3_), channel_id=1, source_target_pairs={{0,8},{2,10},{4,28},{6,30},{8,16},{10,18},{12,4},{14,6},{16,24},{1... | collective-permute-start | bytes 811016 | tf_op jit(solution)/shard_map/ppermute | solution.py:447
  30.6 8.8 %collective-permute-start.10 = (f32[2,8,4096]{2,1,0:T(8,128)S(1)}, f32[2,8,4096]{2,1,0:T(8,128)S(1)}, u32[]{:S(2)}, u32[]{:S(2)}) collective-permute-start(f32[2,8,4096]{2,1,0:T(8,128)S(1)} %collective-permute-done.9.refs_6_), channel_id=1, source_target_pairs={{0,8},{2,10},{4,0},{6,2},{8,16},{10,18},{12,4},{14,6},{16,24},{18,... | collective-permute-start | bytes 786440 | tf_op jit(solution)/shard_map/ppermute | solution.py:447
  36.3 7.5 %collective-permute-start.16 = (f32[2,32,1024]{2,1,0:T(8,128)S(1)}, f32[2,32,1024]{2,1,0:T(8,128)S(1)}, u32[]{:S(2)}, u32[]{:S(2)}) collective-permute-start(f32[2,32,1024]{2,1,0:T(8,128)S(1)} %get-tuple-element.67), channel_id=1, source_target_pairs={{0,4},{2,6},{4,12},{6,14},{8,0},{10,2},{12,20},{14,22},{16,8},{18,... | collective-permute-start | bytes 786440 | tf_op jit(solution)/shard_map/ppermute | solution.py:447
  40.7 24.9 %collective-permute-start.21 = (f32[4,32,2048]{2,1,0:T(8,128)S(1)}, f32[4,32,2048]{2,1,0:T(8,128)S(1)}, u32[]{:S(2)}, u32[]{:S(2)}) collective-permute-start(f32[4,32,2048]{2,1,0:T(8,128)S(1)} %get-tuple-element.69), channel_id=1, source_target_pairs={{0,2},{2,0},{4,6},{6,4},{8,10},{10,8},{12,14},{14,12},{16,18},{18,... | collective-permute-start | bytes 3145736 | tf_op jit(solution)/shard_map/ppermute | solution.py:447
  40.7 9.3 %collective-permute-start.11 = (f32[2,32,1024]{2,1,0:T(8,128)S(1)}, f32[2,32,1024]{2,1,0:T(8,128)S(1)}, u32[]{:S(2)}, u32[]{:S(2)}) collective-permute-start(f32[2,32,1024]{2,1,0:T(8,128)S(1)} %get-tuple-element.63), channel_id=1, source_target_pairs={{0,24},{2,26},{4,12},{6,14},{8,0},{10,2},{12,20},{14,22},{16,8},{1... | collective-permute-start | bytes 786440 | tf_op jit(solution)/shard_map/ppermute | solution.py:447
  43.9 9.2 %collective-permute-start.17 = (f32[2,32,1024]{2,1,0:T(8,128)S(1)}, f32[2,32,1024]{2,1,0:T(8,128)S(1)}, u32[]{:S(2)}, u32[]{:S(2)}) collective-permute-start(f32[2,32,1024]{2,1,0:T(8,128)S(1)} %add.53), channel_id=1, source_target_pairs={{0,4},{2,6},{4,0},{6,2},{8,12},{10,14},{12,8},{14,10},{16,20},{18,... | collective-permute-start | bytes 786440 | tf_op jit(solution)/shard_map/ppermute | solution.py:447
  50.0 9.2 %collective-permute-start.12 = (f32[2,32,1024]{2,1,0:T(8,128)S(1)}, f32[2,32,1024]{2,1,0:T(8,128)S(1)}, u32[]{:S(2)}, u32[]{:S(2)}) collective-permute-start(f32[2,32,1024]{2,1,0:T(8,128)S(1)} %add.48), channel_id=1, source_target_pairs={{0,4},{2,6},{4,0},{6,2},{8,12},{10,14},{12,8},{14,10},{16,20},{18,... | collective-permute-start | bytes 786440 | tf_op jit(solution)/shard_map/ppermute | solution.py:447
  53.1 7.7 %collective-permute-start.18 = (f32[32,1024]{1,0:T(8,128)S(1)}, f32[32,1024]{1,0:T(8,128)S(1)}, u32[]{:S(2)}, u32[]{:S(2)}) collective-permute-start(f32[32,1024]{1,0:T(8,128)S(1)} %get-tuple-element.73), channel_id=1, source_target_pairs={{0,3},{1,2},{2,1},{3,0},{4,7},{5,6},{6,5},{7,4},{8,11},{9,10},{10,... | collective-permute-start | bytes 393224 | tf_op jit(solution)/shard_map/ppermute | solution.py:455
  53.7 7.2 %collective-permute-start.19 = (f32[32,1024]{1,0:T(8,128)S(1)}, f32[32,1024]{1,0:T(8,128)S(1)}, u32[]{:S(2)}, u32[]{:S(2)}) collective-permute-start(f32[32,1024]{1,0:T(8,128)S(1)} %get-tuple-element.73), channel_id=1, source_target_pairs={{0,2},{1,3},{2,0},{3,1},{4,6},{5,7},{6,4},{7,5},{8,10},{9,11},{10,... | collective-permute-start | bytes 393224 | tf_op jit(solution)/shard_map/ppermute | solution.py:455
  54.8 7.0 %collective-permute-start.20 = (f32[32,1024]{1,0:T(8,128)S(1)}, f32[32,1024]{1,0:T(8,128)S(1)}, u32[]{:S(2)}, u32[]{:S(2)}) collective-permute-start(f32[32,1024]{1,0:T(8,128)S(1)} %get-tuple-element.72.refs_4_), channel_id=1, source_target_pairs={{0,1},{1,0},{2,3},{3,2},{4,5},{5,4},{6,7},{7,6},{8,9},{9,8},{10,11... | collective-permute-start | bytes 393224 | tf_op jit(solution)/shard_map/ppermute | solution.py:455
  59.3 6.3 %collective-permute-start.15 = (f32[32,1024]{1,0:T(8,128)S(1)}, f32[32,1024]{1,0:T(8,128)S(1)}, u32[]{:S(2)}, u32[]{:S(2)}) collective-permute-start(f32[32,1024]{1,0:T(8,128)S(1)} %get-tuple-element.74.refs_2_), channel_id=1, source_target_pairs={{0,1},{1,0},{2,3},{3,2},{4,5},{5,4},{6,7},{7,6},{8,9},{9,8},{10,11... | collective-permute-start | bytes 393224 | tf_op jit(solution)/shard_map/ppermute | solution.py:455
  60.8 7.4 %collective-permute-start.13 = (f32[32,1024]{1,0:T(8,128)S(1)}, f32[32,1024]{1,0:T(8,128)S(1)}, u32[]{:S(2)}, u32[]{:S(2)}) collective-permute-start(f32[32,1024]{1,0:T(8,128)S(1)} %get-tuple-element.75), channel_id=1, source_target_pairs={{0,3},{1,2},{2,1},{3,0},{4,7},{5,6},{6,5},{7,4},{8,11},{9,10},{10,... | collective-permute-start | bytes 393224 | tf_op jit(solution)/shard_map/ppermute | solution.py:455
  60.9 7.5 %collective-permute-start.14 = (f32[32,1024]{1,0:T(8,128)S(1)}, f32[32,1024]{1,0:T(8,128)S(1)}, u32[]{:S(2)}, u32[]{:S(2)}) collective-permute-start(f32[32,1024]{1,0:T(8,128)S(1)} %get-tuple-element.75), channel_id=1, source_target_pairs={{0,2},{1,3},{2,0},{3,1},{4,6},{5,7},{6,4},{7,5},{8,10},{9,11},{10,... | collective-permute-start | bytes 393224 | tf_op jit(solution)/shard_map/ppermute | solution.py:455
